TPU v7x, 32 devices: a whole 2x2x4 slice. The times are simulated.
32 devices in a mesh: groups: 2 (over y), mesh: 4 (over z), band: 2 (over x), width: 2 (over core).
Axes of the slice: x: 2, y: 2, z: 4, core: 2. Of those that a mesh axis runs over, the one named last changes fastest.
Arguments:
- grid_latent: bfloat16 [8192, 512], P(('groups', 'mesh', 'band')), parts along dimension 0, may hold values from -6 to 6
- mesh_latent: bfloat16 [5120, 512], P(('groups', 'mesh', 'band')), parts along dimension 0, may hold values from -6 to 6
- grid_edge: bfloat16 [12288, 512], P(('groups', 'mesh', 'band')), parts along dimension 0, may hold values from -6 to 6
- mesh_edge: bfloat16 [12288, 512], P(('groups', 'mesh', 'band')), parts along dimension 0, may hold values from -6 to 6
- encoder_slot: int32 [12288], P(('groups', 'mesh', 'band')), parts along dimension 0, may hold values from 0 to 639, as said below
- encoder_target: int32 [12288], P(('groups', 'mesh', 'band')), parts along dimension 0, may hold values from 0 to 319
- halo_down: int32 [1024], P(('groups', 'mesh', 'band')), parts along dimension 0, may hold values from 0 to 511
- halo_up: int32 [1024], P(('groups', 'mesh', 'band')), parts along dimension 0, may hold values from 0 to 511
- send_lists: int32 [16, 8, 8], P(('groups', 'mesh', 'band')), parts along dimension 0, may hold values from -1 to 319, as said below
- mesh_slot: int32 [12288], P(('groups', 'mesh', 'band')), parts along dimension 0, may hold values from 0 to 63, as said below
- mesh_target: int32 [12288], P(('groups', 'mesh', 'band')), parts along dimension 0, may hold values from 0 to 319
- edge_mats: bfloat16 [3, 3, 512, 512], P(None, None, 'mesh', 'width'), may hold values from -0.15625 to 0.15625
- node_mats: bfloat16 [3, 2, 512, 512], P(None, None, 'mesh', 'width'), may hold values from -0.1875 to 0.1875
- edge_back: bfloat16 [3, 512, 512], P(None, 'width', 'mesh'), may hold values from -0.25 to 0.25
- node_back: bfloat16 [3, 512, 512], P(None, 'width', 'mesh'), may hold values from -0.25 to 0.25
Outputs:
- mesh_out: bfloat16 [5120, 512], P(('groups', 'mesh', 'band')), parts along dimension 0
There are 2 independent parts, one for each index of `groups`. A program takes and returns all parts, laid end to end along the dimension named above; an argument that names none is the same for every part. Nothing has to cross between parts.
Inputs may be any that keep to these rules, and one draw needn't show every extreme that they name: `encoder_slot`: for an edge of device d (rows d * 768 to (d + 1) * 768 - 1): a value below 512 is one of d's own grid nodes; 512 + j with j < 64 names entry j of the halo_up list of device d - 1; 576 + j names entry j of the halo_down list of device d + 1. Device 0 names nothing of a lower and the last device nothing of an upper device; every entry of an existing neighbour's list is named by some edge of d. In each send_lists[p, q, :] the live entries (0 or more) come first, the rest are -1. Device p has 8 live entries for itself and for the four devices at most two indices away along mesh+band, counted around the loop, and between 2 and 4 for every other device. `mesh_slot`: for an edge of device q, slot s names entry s % 8 of send_lists[s // 8, q, :], which is always live; every live entry sent to q is named by some edge of q.
All inputs are finite; a program needn't handle non-finite values.
Results may differ from a plain program's by a relative error of at most 0.02.
Values may be sent and summed in bfloat16 or wider, within the bound.
No kernel may reach another device: no remote copies, remote signals or barrier semaphores. Data moves between devices by JAX's collectives and lax.ppermute only.
A program may use at most 64 MiB of HBM per device.

v0:
```python
import jax
import jax.numpy as jnp
from jax import lax
from jax.sharding import PartitionSpec as P


def padded(cells, sides, width):
    for axis, dim in sides:
        count = lax.axis_size(axis)
        ends = count - 1
        head = lax.slice_in_dim(cells, 0, width, axis=dim)
        tail = lax.slice_in_dim(cells, cells.shape[dim] - width, cells.shape[dim], axis=dim)
        cells = jnp.concatenate(
            [
                lax.ppermute(tail, axis, [(i, (i + 1) % count) for i in range(ends)]),
                cells,
                lax.ppermute(head, axis, [((i + 1) % count, i) for i in range(ends)]),
            ],
            axis=dim,
        )
    return cells


def normalize(total):
    row_mean = jnp.mean(total, axis=1, keepdims=True)
    row_meansq = jnp.mean(total * total, axis=1, keepdims=True)
    return (total - row_mean) * lax.rsqrt(row_meansq - row_mean * row_mean + 1e-05)


def finish(partial_value, residual):
    total = lax.psum(partial_value.astype(jnp.bfloat16), "width").astype(jnp.float32)
    normed = normalize(total)
    message = normed.astype(jnp.bfloat16)
    updated = (residual.astype(jnp.float32) + normed).astype(jnp.bfloat16)
    return (message, updated)


def grid_table(grid_latent, send_mat, halo_down, halo_up):
    halo_rows = halo_down.shape[0]
    outgoing = jnp.concatenate([grid_latent[halo_down], grid_latent[halo_up]], axis=0)
    extended = padded(outgoing, ((("mesh", "band"), 0),), halo_rows)
    whole_rows = jnp.concatenate(
        [grid_latent, extended[:halo_rows], extended[extended.shape[0] - halo_rows :]], axis=0
    )
    send_table = jnp.dot(whole_rows, send_mat, preferred_element_type=jnp.float32).astype(
        jnp.bfloat16
    )
    return send_table


def mesh_table(node_rows, send_mat, send_lists):
    row_list = send_lists[0]
    is_live = (row_list >= 0)[:, :, None]
    row_index = jnp.maximum(row_list, 0)
    nothing = jnp.zeros((), jnp.bfloat16)
    packed = jnp.where(is_live, node_rows[row_index], nothing)
    projected = jnp.einsum(
        "pcd,dh->pch",
        lax.all_to_all(packed, ("mesh", "band"), split_axis=0, concat_axis=0, tiled=True),
        send_mat,
        preferred_element_type=jnp.float32,
    ).astype(jnp.bfloat16)
    return projected.reshape(-1, projected.shape[2])


def edge_update(send_table, send_slot, node_rows, target_ids, edge_rows, edge_mats, edge_back):
    recv_proj = jnp.dot(node_rows, edge_mats[1], preferred_element_type=jnp.float32)
    preact = jnp.dot(edge_rows, edge_mats[2], preferred_element_type=jnp.float32)
    preact = preact + send_table[send_slot].astype(jnp.float32) + recv_proj[target_ids]
    edge_hidden = jax.nn.silu(preact).astype(jnp.bfloat16)
    partial_value = jnp.dot(edge_hidden, edge_back, preferred_element_type=jnp.float32)
    message, updated = finish(partial_value, edge_rows)
    node_ids = jnp.arange(node_rows.shape[0], dtype=jnp.int32)
    onehot = (target_ids[None, :] == node_ids[:, None]).astype(jnp.bfloat16)
    incoming = jnp.dot(onehot, message, preferred_element_type=jnp.float32).astype(jnp.bfloat16)
    return (incoming, updated)


def node_update(node_rows, incoming, node_mats, node_back):
    node_pre = jnp.dot(node_rows, node_mats[0], preferred_element_type=jnp.float32)
    node_pre = node_pre + jnp.dot(incoming, node_mats[1], preferred_element_type=jnp.float32)
    node_hidden = jax.nn.silu(node_pre).astype(jnp.bfloat16)
    partial_value = jnp.dot(node_hidden, node_back, preferred_element_type=jnp.float32)
    unused, updated = finish(partial_value, node_rows)
    return updated


def on_device(
    grid_latent,
    mesh_latent,
    grid_edge,
    mesh_edge,
    encoder_slot,
    encoder_target,
    halo_down,
    halo_up,
    send_lists,
    mesh_slot,
    mesh_target,
    edge_mats,
    node_mats,
    edge_back,
    node_back,
):
    node_rows = mesh_latent
    edge_rows = mesh_edge
    block_count = edge_mats.shape[0]
    for block_id in range(block_count):
        block_edge, block_node, block_eback, block_nback = (
            lax.all_gather(edge_mats[block_id], "mesh", axis=1, tiled=True),
            lax.all_gather(node_mats[block_id], "mesh", axis=1, tiled=True),
            lax.all_gather(edge_back[block_id], "mesh", axis=1, tiled=True),
            lax.all_gather(node_back[block_id], "mesh", axis=1, tiled=True),
        )
        if block_id == 0:
            send_table = grid_table(grid_latent, block_edge[0], halo_down, halo_up)
            incoming, unused = edge_update(
                send_table,
                encoder_slot,
                node_rows,
                encoder_target,
                grid_edge,
                block_edge,
                block_eback,
            )
        else:
            keep_edges = block_id + 1 < block_count
            send_table = mesh_table(node_rows, block_edge[0], send_lists)
            incoming, edge_next = edge_update(
                send_table, mesh_slot, node_rows, mesh_target, edge_rows, block_edge, block_eback
            )
            if keep_edges:
                edge_rows = edge_next
        node_rows = node_update(node_rows, incoming, block_node, block_nback)
    return node_rows


def solution(mesh):
    return jax.shard_map(
        on_device,
        mesh=mesh,
        in_specs=(
            P(("groups", "mesh", "band"), None),
            P(("groups", "mesh", "band"), None),
            P(("groups", "mesh", "band"), None),
            P(("groups", "mesh", "band"), None),
            P(("groups", "mesh", "band")),
            P(("groups", "mesh", "band")),
            P(("groups", "mesh", "band")),
            P(("groups", "mesh", "band")),
            P(("groups", "mesh", "band"), None, None),
            P(("groups", "mesh", "band")),
            P(("groups", "mesh", "band")),
            P(None, None, "mesh", "width"),
            P(None, None, "mesh", "width"),
            P(None, "width", "mesh"),
            P(None, "width", "mesh"),
        ),
        out_specs=P(("groups", "mesh", "band"), None),
        check_vma=False,
    )
```

profile of v0, /device:TPU:0, one launch (start us, length us, event | category | flops | bytes accessed | tf_op | source)
XLA Modules:
  0.0 290.5 jit_solution(10745261586246817201)
XLA Ops:
  6.5 0.8 compare_select_fusion.5
  7.4 2.4 gather_fusion
  9.8 5.5 %collective-permute-start = (bf16[64,512]{1,0:T(8,128)(2,1)}, bf16[64,512]{1,0:T(8,128)(2,1)}, u32[]{:S(2)}, u32[]{:S(2)}) collective-permute-start(bf16[64,512]{1,0:T(8,128)(2,1)} %gather_fusion), channel_id=1, source_target_pairs={{0,2},{2,4},{4,6},{6,8},{8,10},{10,12},{12,14},{1,3},{3,5},{5,7},{... | collective-permute-start | bytes 196616 | tf_op jit(solution)/shard_map/ppermute | solution.py:15
  15.2 0.7 compare_select_fusion.4
  15.9 1.3 gather_fusion.1
  17.2 1.3 collective-permute-start.1
  18.5 0.8 fusion.94
  19.3 21.5 %all-gather.1 = bf16[1,3,512,256]{3,2,1,0:T(8,128)(2,1)S(1)} all-gather(bf16[1,3,128,256]{3,2,1,0:T(8,128)(2,1)S(1)} %get-tuple-element.18), channel_id=3, replica_groups=mesh['groups'=2,'mesh'=4,'band'=2,'width'=2] {'mesh'}, dimensions={2}, use_global_device_ids=true | all-gather | bytes 983040 | tf_op jit(solution)/shard_map/all_gather | solution.py:110
  40.9 0.6 pad_clamp_fusion.4
  41.5 0.7 fusion.97
  42.1 0.7 fusion.95
  42.9 0.7 fusion.96
  43.7 0.6 compare_select_fusion.1
  44.3 0.2 fusion.82
  44.6 2.1 gather_fusion.3
  46.7 13.7 %all-gather.2 = bf16[1,256,512]{2,1,0:T(8,128)(2,1)} all-gather(bf16[1,256,128]{2,1,0:T(8,128)(2,1)} %get-tuple-element.27), channel_id=4, replica_groups=mesh['groups'=2,'mesh'=4,'band'=2,'width'=2] {'mesh'}, dimensions={2}, use_global_device_ids=true | all-gather | bytes 327680 | tf_op jit(solution)/shard_map/all_gather | solution.py:112
  60.4 1.2 convolution_convert_fusion.9
  61.6 2.7 gather_fusion.2
  64.3 2.8 convolution_convert_fusion.2
  67.1 0.8 copy-done.19
  67.9 13.0 %all-gather.3 = bf16[1,256,512]{2,1,0:T(8,128)(2,1)S(1)} all-gather(bf16[1,256,128]{2,1,0:T(8,128)(2,1)S(1)} %copy-done.19), channel_id=5, replica_groups=mesh['groups'=2,'mesh'=4,'band'=2,'width'=2] {'mesh'}, dimensions={2}, use_global_device_ids=true | all-gather | bytes 327680 | tf_op jit(solution)/shard_map/all_gather | solution.py:113
  80.9 14.9 %all-gather = bf16[1,2,512,256]{3,2,1,0:T(8,128)(2,1)S(1)} all-gather(bf16[1,2,128,256]{3,2,1,0:T(8,128)(2,1)S(1)} %copy-done.11), channel_id=2, replica_groups=mesh['groups'=2,'mesh'=4,'band'=2,'width'=2] {'mesh'}, dimensions={2}, use_global_device_ids=true | all-gather | bytes 655360 | tf_op jit(solution)/shard_map/all_gather | solution.py:111
  96.1 1.5 convert_reduce_fusion.2
  97.6 0.8 multiply_convert_fusion.5
  98.4 1.0 convolution_convert_fusion.7
  99.5 14.5 %all-gather.6 = bf16[1,256,512]{2,1,0:T(8,128)(2,1)} all-gather(bf16[1,256,128]{2,1,0:T(8,128)(2,1)S(1)} %copy-done.18), channel_id=8, replica_groups=mesh['groups'=2,'mesh'=4,'band'=2,'width'=2] {'mesh'}, dimensions={2}, use_global_device_ids=true | all-gather | bytes 327680 | tf_op jit(solution)/shard_map/all_gather | solution.py:112
  114.0 15.6 %all-gather.5 = bf16[1,3,512,256]{3,2,1,0:T(8,128)(2,1)S(1)} all-gather(bf16[1,3,128,256]{3,2,1,0:T(8,128)(2,1)S(1)} %copy-done.7), channel_id=7, replica_groups=mesh['groups'=2,'mesh'=4,'band'=2,'width'=2] {'mesh'}, dimensions={2}, use_global_device_ids=true | all-gather | bytes 983040 | tf_op jit(solution)/shard_map/all_gather | solution.py:110
  129.6 1.2 convert_reduce_fusion.5
  130.8 1.2 fusion.48
  132.0 0.7 gather_fusion.4
  132.7 0.7 bitcast_select_fusion.1
  133.4 3.4 %all-to-all-start = ((bf16[8,8,512]{2,1,0:T(8,128)(2,1)}), bf16[8,8,512]{2,1,0:T(8,128)(2,1)S(1)}, u32[]{:S(2)}, u32[]{:S(2)}) async-start(bf16[8,8,512]{2,1,0:T(8,128)(2,1)} %bitcast_select_fusion.1), calls=%async_computation | async-start | bytes 131072 | tf_op jit(solution)/shard_map/all_to_all | solution.py:59
  137.1 2.1 gather_fusion.6
  139.2 4.9 %all-to-all-done = bf16[8,8,512]{2,1,0:T(8,128)(2,1)S(1)} async-done(((bf16[8,8,512]{2,1,0:T(8,128)(2,1)}), bf16[8,8,512]{2,1,0:T(8,128)(2,1)S(1)}, u32[]{:S(2)}, u32[]{:S(2)}) %all-to-all-start) | async-done | bytes 65568 | tf_op jit(solution)/shard_map/all_to_all | solution.py:59
  144.2 2.7 gather_fusion.5
  146.9 3.0 %convolution_convert_fusion.1 = bf16[768,512]{1,0:T(8,128)(2,1)} fusion(f32[768,256]{1,0:T(8,128)S(1)} %gather_fusion.6, bf16[768,512]{1,0:T(8,128)(2,1)} %param.18, bf16[768,256]{1,0:T(8,128)(2,1)S(1)} %gather_fusion.5, bf16[1,3,512,256]{3,2,1,0:T(8,128)(2,1)S(1)} %all-gather.5, bf16[1,256,512]{2,1,0:T(8,128)(2,1)S(1)} %copy-done.14), kind=kOutput, calls=%fused_computation.31 | convolution fusion | flops 404619264 | bytes 3276800 | tf_op jit(solution)/shard_map/dot_general | solution.py:71
  149.9 0.8 copy-done.17
  150.7 12.9 %all-gather.7 = bf16[1,256,512]{2,1,0:T(8,128)(2,1)S(1)} all-gather(bf16[1,256,128]{2,1,0:T(8,128)(2,1)S(1)} %copy-done.17), channel_id=9, replica_groups=mesh['groups'=2,'mesh'=4,'band'=2,'width'=2] {'mesh'}, dimensions={2}, use_global_device_ids=true | all-gather | bytes 327680 | tf_op jit(solution)/shard_map/all_gather | solution.py:113
  163.6 14.9 %all-gather.4 = bf16[1,2,512,256]{3,2,1,0:T(8,128)(2,1)S(1)} all-gather(bf16[1,2,128,256]{3,2,1,0:T(8,128)(2,1)S(1)} %copy-done.10), channel_id=6, replica_groups=mesh['groups'=2,'mesh'=4,'band'=2,'width'=2] {'mesh'}, dimensions={2}, use_global_device_ids=true | all-gather | bytes 655360 | tf_op jit(solution)/shard_map/all_gather | solution.py:111
  178.4 0.2 fusion.81
  178.7 1.5 convert_reduce_fusion.1
  180.3 0.8 multiply_convert_fusion.4
  181.1 1.0 convolution_convert_fusion.5
  182.1 14.5 %all-gather.10 = bf16[1,256,512]{2,1,0:T(8,128)(2,1)} all-gather(bf16[1,256,128]{2,1,0:T(8,128)(2,1)S(1)} %copy-done.16), channel_id=12, replica_groups=mesh['groups'=2,'mesh'=4,'band'=2,'width'=2] {'mesh'}, dimensions={2}, use_global_device_ids=true | all-gather | bytes 327680 | tf_op jit(solution)/shard_map/all_gather | solution.py:112
  196.5 15.6 %all-gather.9 = bf16[1,3,512,256]{3,2,1,0:T(8,128)(2,1)S(1)} all-gather(bf16[1,3,128,256]{3,2,1,0:T(8,128)(2,1)S(1)} %copy-done.6), channel_id=11, replica_groups=mesh['groups'=2,'mesh'=4,'band'=2,'width'=2] {'mesh'}, dimensions={2}, use_global_device_ids=true | all-gather | bytes 983040 | tf_op jit(solution)/shard_map/all_gather | solution.py:110
  212.1 1.2 convert_reduce_fusion.4
  213.3 1.2 fusion.52
  214.5 0.7 gather_fusion.7
  215.2 0.7 bitcast_select_fusion
  215.9 3.4 %all-to-all-start.1 = ((bf16[8,8,512]{2,1,0:T(8,128)(2,1)}), bf16[8,8,512]{2,1,0:T(8,128)(2,1)S(1)}, u32[]{:S(2)}, u32[]{:S(2)}) async-start(bf16[8,8,512]{2,1,0:T(8,128)(2,1)} %bitcast_select_fusion), calls=%async_computation.1 | async-start | bytes 131072 | tf_op jit(solution)/shard_map/all_to_all | solution.py:59
  219.5 0.2 fusion.78
  219.8 2.1 gather_fusion.9
  221.9 4.5 %all-to-all-done.1 = bf16[8,8,512]{2,1,0:T(8,128)(2,1)S(1)} async-done(((bf16[8,8,512]{2,1,0:T(8,128)(2,1)}), bf16[8,8,512]{2,1,0:T(8,128)(2,1)S(1)}, u32[]{:S(2)}, u32[]{:S(2)}) %all-to-all-start.1) | async-done | bytes 65568 | tf_op jit(solution)/shard_map/all_to_all | solution.py:59
  226.6 2.7 gather_fusion.8
  229.3 3.3 %convolution_convert_fusion = bf16[768,512]{1,0:T(8,128)(2,1)} fusion(f32[768,256]{1,0:T(8,128)S(1)} %gather_fusion.9, bf16[768,512]{1,0:T(8,128)(2,1)} %all-reduce.11.cloned.1.call-done, bf16[768,512]{1,0:T(8,128)(2,1)} %param.18, bf16[768,256]{1,0:T(8,128)(2,1)S(1)} %gather_fusion.8, f32[768]{0:T(1024)S(1)} %get-tuple-element.32, ...), kind=kOutput, calls=%fused_computation.30 | convolution fusion | flops 406978560 | bytes 4071424 | tf_op jit(solution)/shard_map/dot_general | solution.py:71
  232.6 0.8 copy-done.15
  233.4 12.9 %all-gather.11 = bf16[1,256,512]{2,1,0:T(8,128)(2,1)S(1)} all-gather(bf16[1,256,128]{2,1,0:T(8,128)(2,1)S(1)} %copy-done.15), channel_id=13, replica_groups=mesh['groups'=2,'mesh'=4,'band'=2,'width'=2] {'mesh'}, dimensions={2}, use_global_device_ids=true | all-gather | bytes 327680 | tf_op jit(solution)/shard_map/all_gather | solution.py:113
  246.2 14.7 %all-gather.8 = bf16[1,2,512,256]{3,2,1,0:T(8,128)(2,1)S(1)} all-gather(bf16[1,2,128,256]{3,2,1,0:T(8,128)(2,1)S(1)} %copy-done.9), channel_id=10, replica_groups=mesh['groups'=2,'mesh'=4,'band'=2,'width'=2] {'mesh'}, dimensions={2}, use_global_device_ids=true | all-gather | bytes 655360 | tf_op jit(solution)/shard_map/all_gather | solution.py:111
  261.2 1.5 convert_reduce_fusion
  262.7 0.8 multiply_convert_fusion.3
  263.5 1.0 convolution_convert_fusion.3
  264.5 16.1 %all-reduce.17.cloned.1.call-done = bf16[320,512]{1,0:T(8,128)(2,1)} async-done(((bf16[320,512]{1,0:T(8,128)(2,1)}), bf16[320,512]{1,0:T(8,128)(2,1)}) %all-reduce.17.cloned.1.call-update) | async-done | bytes 327696 | tf_op jit(solution)/shard_map/psum | solution.py:31
  280.6 1.2 convert_reduce_fusion.3
  281.8 1.9 fusion.56
  (101 shorter events, 1.9 us)
Async XLA Ops:
  6.5 57.7 %copy-start = (bf16[768,512]{1,0:T(8,128)(2,1)S(1)}, bf16[768,512]{1,0:T(8,128)(2,1)}, u32[]{:S(2)}) copy-start(bf16[768,512]{1,0:T(8,128)(2,1)} %param.17) | copy-start | bytes 2359300
  6.5 9.4 %copy-start.2 = (bf16[512,512]{1,0:T(8,128)(2,1)S(1)}, bf16[512,512]{1,0:T(8,128)(2,1)}, u32[]{:S(2)}) copy-start(bf16[512,512]{1,0:T(8,128)(2,1)} %param.15) | copy-start | bytes 1572868
  6.5 12.0 %copy-start.8 = (bf16[3,3,128,256]{3,2,1,0:T(8,128)(2,1)S(1)}, bf16[3,3,128,256]{3,2,1,0:T(8,128)(2,1)}, u32[]{:S(2)}) copy-start(bf16[3,3,128,256]{3,2,1,0:T(8,128)(2,1)} %param.26) | copy-start | bytes 1769476
  6.5 89.6 %all-reduce.7.cloned.1.call-start = ((), (), s32[]{:S(2)}) async-start(), calls=%async_computation.2 | async-start | bytes 1572864 | tf_op jit(solution)/shard_map/psum | solution.py:31
  9.8 50.6 %collective-permute-start = (bf16[64,512]{1,0:T(8,128)(2,1)}, bf16[64,512]{1,0:T(8,128)(2,1)}, u32[]{:S(2)}, u32[]{:S(2)}) collective-permute-start(bf16[64,512]{1,0:T(8,128)(2,1)} %gather_fusion), channel_id=1, source_target_pairs={{0,2},{2,4},{4,6},{6,8},{8,10},{10,12},{12,14},{1,3},{3,5},{5,7},{... | collective-permute-start | bytes 196616 | tf_op jit(solution)/shard_map/ppermute | solution.py:15
  17.2 43.1 %collective-permute-start.1 = (bf16[64,512]{1,0:T(8,128)(2,1)}, bf16[64,512]{1,0:T(8,128)(2,1)}, u32[]{:S(2)}, u32[]{:S(2)}) collective-permute-start(bf16[64,512]{1,0:T(8,128)(2,1)} %gather_fusion.1), channel_id=1, source_target_pairs={{2,0},{4,2},{6,4},{8,6},{10,8},{12,10},{14,12},{3,1},{5,3},{7,5},{... | collective-permute-start | bytes 196616 | tf_op jit(solution)/shard_map/ppermute | solution.py:17
  19.3 21.5 %copy-start.27 = (s32[768]{0:T(1024)S(1)}, s32[768]{0:T(1024)}, u32[]{:S(2)}) copy-start(s32[768]{0:T(1024)} %param.20) | copy-start | bytes 9220
  19.3 21.5 %copy-start.25 = (s32[768]{0:T(1024)S(1)}, s32[768]{0:T(1024)}, u32[]{:S(2)}) copy-start(s32[768]{0:T(1024)} %param.19) | copy-start | bytes 9220
  19.3 22.1 %copy-start.20 = (bf16[3,256,128]{2,1,0:T(8,128)(2,1)S(1)}, bf16[3,256,128]{2,1,0:T(8,128)(2,1)}, u32[]{:S(2)}) copy-start(bf16[3,256,128]{2,1,0:T(8,128)(2,1)} %param.28) | copy-start | bytes 589828
  19.3 22.8 %copy-start.12 = (bf16[3,2,128,256]{3,2,1,0:T(8,128)(2,1)S(1)}, bf16[3,2,128,256]{3,2,1,0:T(8,128)(2,1)}, u32[]{:S(2)}) copy-start(bf16[3,2,128,256]{3,2,1,0:T(8,128)(2,1)} %param.27) | copy-start | bytes 1179652
  40.8 2.1 copy-start.21
  41.5 2.1 copy-start.29
  41.5 2.1 copy-start.22
  41.5 2.2 copy-start.26
  41.5 2.8 copy-start.1
  60.4 1.2 copy-start.24
  67.0 0.8 copy-start.19
  67.0 13.9 %copy-start.23 = (s32[768]{0:T(1024)S(1)}, s32[768]{0:T(1024)}, u32[]{:S(2)}) copy-start(s32[768]{0:T(1024)} %compare_select_fusion.1) | copy-start | bytes 9220
  67.0 13.9 %copy-start.11 = (bf16[1,2,128,256]{3,2,1,0:T(8,128)(2,1)S(1)}, bf16[1,2,128,256]{3,2,1,0:T(8,128)(2,1)}, u32[]{:S(2)}) copy-start(bf16[1,2,128,256]{3,2,1,0:T(8,128)(2,1)} %get-tuple-element.21) | copy-start | bytes 393220
  67.1 62.5 %all-reduce.9.cloned.1.call-start = ((), (), s32[]{:S(2)}) async-start(), calls=%async_computation.3 | async-start | bytes 655360 | tf_op jit(solution)/shard_map/psum | solution.py:31
  95.8 1.8 copy-start.28
  96.1 1.5 copy-start.4
  98.4 1.0 copy-start.18
  98.4 15.6 %copy-start.7 = (bf16[1,3,128,256]{3,2,1,0:T(8,128)(2,1)S(1)}, bf16[1,3,128,256]{3,2,1,0:T(8,128)(2,1)}, u32[]{:S(2)}) copy-start(bf16[1,3,128,256]{3,2,1,0:T(8,128)(2,1)} %get-tuple-element.19) | copy-start | bytes 589828
  133.4 10.6 %all-to-all-start = ((bf16[8,8,512]{2,1,0:T(8,128)(2,1)}), bf16[8,8,512]{2,1,0:T(8,128)(2,1)S(1)}, u32[]{:S(2)}, u32[]{:S(2)}) async-start(bf16[8,8,512]{2,1,0:T(8,128)(2,1)} %bitcast_select_fusion.1), calls=%async_computation | async-start | bytes 131072 | tf_op jit(solution)/shard_map/all_to_all | solution.py:59
  136.8 42.0 %all-reduce.11.cloned.1.call-start = ((), (), s32[]{:S(2)}) async-start(), calls=%async_computation.4 | async-start | bytes 1572864 | tf_op jit(solution)/shard_map/psum | solution.py:31
  144.2 2.7 copy-start.14
  149.8 0.8 copy-start.17
  149.8 13.7 %copy-start.10 = (bf16[1,2,128,256]{3,2,1,0:T(8,128)(2,1)S(1)}, bf16[1,2,128,256]{3,2,1,0:T(8,128)(2,1)}, u32[]{:S(2)}) copy-start(bf16[1,2,128,256]{3,2,1,0:T(8,128)(2,1)} %get-tuple-element.22) | copy-start | bytes 393220
  149.9 62.3 %all-reduce.13.cloned.1.call-start = ((), (), s32[]{:S(2)}) async-start(), calls=%async_computation.5 | async-start | bytes 655360 | tf_op jit(solution)/shard_map/psum | solution.py:31
  178.4 1.8 copy-start.30
  178.7 1.5 copy-start.3
  181.0 1.0 copy-start.16
  181.0 15.5 %copy-start.6 = (bf16[1,3,128,256]{3,2,1,0:T(8,128)(2,1)S(1)}, bf16[1,3,128,256]{3,2,1,0:T(8,128)(2,1)}, u32[]{:S(2)}) copy-start(bf16[1,3,128,256]{3,2,1,0:T(8,128)(2,1)} %get-tuple-element.17) | copy-start | bytes 589828
  215.9 10.5 %all-to-all-start.1 = ((bf16[8,8,512]{2,1,0:T(8,128)(2,1)}), bf16[8,8,512]{2,1,0:T(8,128)(2,1)S(1)}, u32[]{:S(2)}, u32[]{:S(2)}) async-start(bf16[8,8,512]{2,1,0:T(8,128)(2,1)} %bitcast_select_fusion), calls=%async_computation.1 | async-start | bytes 131072 | tf_op jit(solution)/shard_map/all_to_all | solution.py:59
  219.3 41.9 %all-reduce.15.cloned.1.call-start = ((), (), s32[]{:S(2)}) async-start(), calls=%async_computation.6 | async-start | bytes 1572864 | tf_op jit(solution)/shard_map/psum | solution.py:31
  226.6 2.7 copy-start.13
  232.5 0.8 copy-start.15
  232.5 13.7 %copy-start.9 = (bf16[1,2,128,256]{3,2,1,0:T(8,128)(2,1)S(1)}, bf16[1,2,128,256]{3,2,1,0:T(8,128)(2,1)}, u32[]{:S(2)}) copy-start(bf16[1,2,128,256]{3,2,1,0:T(8,128)(2,1)} %get-tuple-element.20) | copy-start | bytes 393220
  232.6 48.0 %all-reduce.17.cloned.1.call-start = ((), (), s32[]{:S(2)}) async-start(), calls=%async_computation.7 | async-start | bytes 655360 | tf_op jit(solution)/shard_map/psum | solution.py:31
  261.2 1.5 copy-start.5
Sparse Core Ops, SparseCore 0:
  67.2 17.5 all-reduce.6
  99.6 16.5 all-reduce.8
  150.0 16.6 all-reduce.10
  182.2 15.8 all-reduce.12
  232.7 16.7 all-reduce.14
  264.6 15.8 all-reduce.16
where the time goes:
time: 292 us; the launch traced here: 291 us
  blocking collectives  179 us (61%)
  waiting for transfers between devices  25.6 us (9%)
  local copies, waits for them, and re-layouts  24.8 us (8%)
  matrix products  17.3 us (6%)
  other arithmetic  16.5 us (6%)
  between operations  14 us (5%)
  starting transfers between devices  13.8 us (5%)
    all_gather x3, blocking collectives, on_device(): lax.all_gather(edge_mats[block_id], 'mesh', axis=1, tiled=True)  52.7 us
    all_gather x3, blocking collectives, on_device(): lax.all_gather(node_mats[block_id], 'mesh', axis=1, tiled=True)  44.5 us
    all_gather x3, blocking collectives, on_device(): lax.all_gather(edge_back[block_id], 'mesh', axis=1, tiled=True)  42.7 us
    all_gather x3, blocking collectives, on_device(): lax.all_gather(node_back[block_id], 'mesh', axis=1, tiled=True)  38.8 us
    psum x6, waiting for transfers between devices, finish(): lax.psum(partial_value.astype(jnp.bfloat16), 'width').astype(jnp.float32)  16.1 us
    all_to_all x2, waiting for transfers between devices, mesh_table(): lax.all_to_all(packed, ('mesh', 'band'), split_axis=0, concat_axis=0, til...  9.36 us
    dot_general x3, matrix products, edge_update(): jnp.dot(edge_hidden, edge_back, preferred_element_type=jnp.float32)  9 us
    reduce_sum x6, other arithmetic, normalize(): row_mean = jnp.mean(total, axis=1, keepdims=True)  8.01 us
  transfers between devices with their start and end apart: 10, of which 3 were waited for; matrix products, arithmetic and copies ran while one was open for 5% of the time, Pallas kernels for 0%

commit v1 on v0

v1 whole, which is shorter than its diff:
```python
import functools

import jax
import jax.numpy as jnp
from jax import lax
from jax.experimental import pallas as pl
from jax.experimental.pallas import tpu as pltpu
from jax.sharding import PartitionSpec as P

BF = jnp.bfloat16
F32 = jnp.float32
ROWS = 256
SWAP = [(0, 1), (1, 0)]
PARAMS = pltpu.CompilerParams(vmem_limit_bytes=32 * 2**20)


def dot(a, b):
    return jnp.dot(a, b, preferred_element_type=F32)


def silu(v):
    return v / (1.0 + jnp.exp(-v))


def normalize(total):
    mean = jnp.mean(total, axis=1, keepdims=True)
    meansq = jnp.mean(total * total, axis=1, keepdims=True)
    return (total - mean) * lax.rsqrt(meansq - mean * mean + 1e-05)


def hot_columns(ids, count):
    spots = lax.broadcasted_iota(jnp.int32, (ids.shape[0], count), 1)
    return jnp.where(spots == ids, 1.0, 0.0).astype(BF)


def hot_rows(ids, count):
    spots = lax.broadcasted_iota(jnp.int32, (count, ids.shape[1]), 0)
    return jnp.where(spots == ids, 1.0, 0.0).astype(BF)


def call(body, outs, scratch, *args):
    return pl.pallas_call(
        body,
        out_shape=outs,
        scratch_shapes=scratch,
        compiler_params=PARAMS,
    )(*args)


def shaped(*dims):
    return jax.ShapeDtypeStruct(dims, BF)


def cut_body(plan, em, nm, eb, nb, *outs):
    index = {"quarter": 2 * lax.axis_index("groups") + lax.axis_index("band"), "x": lax.axis_index("band"), "y": lax.axis_index("groups")}
    for (block, kind, split, rows), out in zip(plan, outs):
        part = index[split]
        first = pl.ds(pl.multiple_of(part * rows, rows), rows)
        low = pl.ds(pl.multiple_of(part * 2 * rows, rows), rows)
        high = pl.ds(pl.multiple_of(part * 2 * rows + rows, rows), rows)
        spot = 0
        for letter, mats, back in (("e", em, eb), ("n", nm, nb)):
            if letter not in kind:
                continue
            for m in range(mats.shape[1]):
                out[spot] = mats[block, m, first, :]
                spot += 1
            width = back.shape[2]
            out[spot, :, 0:width] = back[block, low, :]
            out[spot, :, width:] = back[block, high, :]
            spot += 1


def put(src, zs, part, rows, half, kind, weights):
    for k, z in enumerate(zs):
        spot = 0
        for letter, mats, back in (("e", weights.get("em"), weights.get("eb")), ("n", weights.get("nm"), weights.get("nb"))):
            if letter not in kind:
                continue
            count = mats.shape[0] // mats.shape[1]
            depth = mats.shape[1]
            cols = src.shape[-1]
            lanes = cols // 2
            for m in range(count):
                at = pl.multiple_of(m * depth + z * lanes + part * rows, rows)
                mats[pl.ds(at, rows), half * cols : (half + 1) * cols] = src[k, spot]
                spot += 1
            for j in range(2):
                at = pl.multiple_of(half * cols + part * 2 * rows + j * rows, rows)
                back[pl.ds(at, rows), pl.ds(pl.multiple_of(z * lanes, lanes), lanes)] = src[
                    k, spot, :, j * lanes : (j + 1) * lanes
                ]
            spot += 1


def put_own(block, raws, half, kind, weights):
    z = lax.axis_index("mesh")
    for letter, mats, back in (("e", weights.get("em"), weights.get("eb")), ("n", weights.get("nm"), weights.get("nb"))):
        if letter not in kind:
            continue
        raw_mats, raw_back = raws[letter]
        depth, cols = raw_mats.shape[2:]
        for m in range(raw_mats.shape[1]):
            at = pl.multiple_of(m * mats.shape[1] + z * depth, depth)
            mats[pl.ds(at, depth), half * cols : (half + 1) * cols] = raw_mats[block, m]
        back[half * cols : (half + 1) * cols, pl.ds(pl.multiple_of(z * depth, depth), depth)] = raw_back[block]


def assemble(block, kind, split, rows, refs, weights):
    count = lax.axis_size("mesh")
    z = lax.axis_index("mesh")
    zs = [lax.rem(z + count - k, count) for k in range(1, count)]
    x, y = lax.axis_index("band"), lax.axis_index("groups")
    parts = {
        "quarter": [2 * y + x, 2 * y + 1 - x, 2 * (1 - y) + x, 2 * (1 - y) + 1 - x],
        "x": [x, 1 - x],
        "y": [y, 1 - y],
    }[split]
    for half, (raws, arrays) in enumerate(refs):
        put_own(block, raws, half, kind, weights)
        for part, src in zip(parts, arrays):
            put(src, zs, part, rows, half, kind, weights)


class Parts:
    def __init__(self, block, kind, split, rows, own, other, arrays, swapped):
        self.block, self.kind, self.split, self.rows = block, kind, split, rows
        self.operands = []
        for raws, got in ((own, arrays), (other, swapped)):
            for letter in kind:
                self.operands += list(raws[letter])
            self.operands += got

    def scratch(self, hidden, depth):
        found = []
        if "e" in self.kind:
            found += [pltpu.VMEM((3 * depth, hidden), BF), pltpu.VMEM((hidden, depth), BF)]
        if "n" in self.kind:
            found += [pltpu.VMEM((2 * depth, hidden), BF), pltpu.VMEM((hidden, depth), BF)]
        return found

    def load(self, operands, scratch):
        weights = dict(zip([name for letter in self.kind for name in (letter + "m", letter + "b")], scratch))
        each = len(operands) // 2
        refs = []
        for half in range(2):
            mine = list(operands[half * each : (half + 1) * each])
            raws = {}
            for letter in self.kind:
                raws[letter] = (mine.pop(0), mine.pop(0))
            refs.append((raws, mine))
        assemble(self.block, self.kind, self.split, self.rows, refs, weights)
        return weights


class Whole:
    def __init__(self, kind, arrays):
        self.kind = kind
        self.operands = arrays

    def scratch(self, hidden, depth):
        return []

    def load(self, operands, scratch):
        return dict(zip([name for letter in self.kind for name in (letter + "m", letter + "b")], operands))


def pack_body(rows, ids, out):
    out[...] = dot(hot_columns(ids[...], rows.shape[0]), rows[...]).astype(BF)


def sender_body(grid, low, high, nodes, slots, targets, out):
    table = jnp.concatenate([grid[...], low[...], high[...]], axis=0)
    depth = grid.shape[1]
    for at in range(0, out.shape[0], ROWS):
        rows = slice(at, at + ROWS)
        out[rows, 0:depth] = dot(hot_columns(slots[rows, :], table.shape[0]), table).astype(BF)
        out[rows, depth:] = dot(hot_columns(targets[rows, :], nodes.shape[0]), nodes[...]).astype(BF)


def edge_tail(pre, back, message, rows):
    total = dot(silu(pre).astype(BF), back[...])
    normed = normalize(total)
    message[rows, :] = normed.astype(BF)
    return normed


def node_tail(nodes, incoming, weights):
    depth = nodes.shape[1]
    pre = dot(nodes[...], weights["nm"][0:depth, :]) + dot(incoming, weights["nm"][depth:, :])
    total = dot(silu(pre).astype(BF), weights["nb"][...])
    return (nodes[...].astype(F32) + normalize(total)).astype(BF)


def first_edges_body(pack, count, gathered, edges, ids, *refs):
    operands, rest = refs[:count], refs[count:]
    out, message, scratch = rest[0], rest[1], rest[2:]
    weights = pack.load(operands, scratch)
    both = gathered.shape[1]
    for at in range(0, edges.shape[0], ROWS):
        rows = slice(at, at + ROWS)
        pre = dot(gathered[rows, :], weights["em"][0:both, :]) + dot(edges[rows, :], weights["em"][both:, :])
        edge_tail(pre, weights["eb"], message, rows)
    out[...] = dot(hot_rows(ids[...], out.shape[0]), message[...]).astype(BF)


def nodes_body(pack, count, nodes, incoming, lists, *refs):
    operands, rest = refs[:count], refs[count:]
    out, packed, scratch = rest[0], rest[1], rest[2:]
    weights = pack.load(operands, scratch)
    out[...] = node_tail(nodes, incoming[...], weights)
    packed[...] = dot(hot_columns(lists[...], nodes.shape[0]), out[...]).astype(BF)


def block_body(pack, count, last, senders, nodes, edges, slots, targets, ids, lists, *refs):
    operands, rest = refs[:count], refs[count:]
    if last:
        out, rest = rest[0], rest[1:]
    else:
        out, packed, edge_next, rest = rest[0], rest[1], rest[2], rest[3:]
    message, table, scratch = rest[0], rest[1], rest[2:]
    weights = pack.load(operands, scratch)
    depth = nodes.shape[1]
    sent = senders.shape[0]
    em = weights["em"]
    table[0:sent, :] = dot(senders[...], em[0:depth, :]).astype(BF)
    table[sent:, :] = dot(nodes[...], em[depth : 2 * depth, :]).astype(BF)
    for at in range(0, edges.shape[0], ROWS):
        rows = slice(at, at + ROWS)
        pre = dot(edges[rows, :], em[2 * depth :, :])
        pre = pre + dot(hot_columns(slots[rows, :], sent), table[0:sent, :])
        pre = pre + dot(hot_columns(targets[rows, :], nodes.shape[0]), table[sent:, :])
        normed = edge_tail(pre, weights["eb"], message, rows)
        if not last:
            edge_next[rows, :] = (edges[rows, :].astype(F32) + normed).astype(BF)
    incoming = dot(hot_rows(ids[...], nodes.shape[0]), message[...]).astype(BF)
    out[...] = node_tail(nodes, incoming, weights)
    if not last:
        packed[...] = dot(hot_columns(lists[...], nodes.shape[0]), out[...]).astype(BF)


def spread(chunk, split):
    count = lax.axis_size("mesh")
    turned = [lax.ppermute(chunk, "mesh", [(i, (i + k) % count) for i in range(count)]) for k in range(1, count)]
    own = jnp.stack(turned)
    if split == "x":
        return [own, lax.ppermute(own, "band", SWAP)]
    if split == "y":
        return [own, lax.ppermute(own, "groups", SWAP)]
    return [
        own,
        lax.ppermute(own, "band", SWAP),
        lax.ppermute(own, "groups", SWAP),
        lax.ppermute(own, ("groups", "band"), [(0, 3), (3, 0), (1, 2), (2, 1)]),
    ]


def swap_width(array):
    return lax.ppermute(array, "width", SWAP)


def weights_by_parts(edge_mats, node_mats, edge_back, node_back):
    depth = edge_mats.shape[2]
    quarter, halved = depth // 4, depth // 2
    plan = [(0, "e", "quarter", quarter), (0, "n", "quarter", quarter), (1, "en", "x", halved), (2, "en", "y", halved)]
    counts = {"e": 4, "n": 3, "en": 7}
    chunks = call(
        functools.partial(cut_body, plan),
        [shaped(counts[kind], rows, edge_mats.shape[3]) for _, kind, _, rows in plan],
        [],
        edge_mats,
        node_mats,
        edge_back,
        node_back,
    )
    own = {"e": (edge_mats, edge_back), "n": (node_mats, node_back)}
    other = {letter: tuple(swap_width(a) for a in pair) for letter, pair in own.items()}
    found = []
    for (block, kind, split, rows), chunk in zip(plan, chunks):
        arrays = spread(chunk, split)
        found.append(Parts(block, kind, split, rows, own, other, arrays, [swap_width(a) for a in arrays]))
    return found


def weights_whole(edge_mats, node_mats, edge_back, node_back):
    def joined(array, rows, cols):
        axis = {rows: array.ndim - 2, cols: array.ndim - 1}
        for name in ("mesh", "width"):
            array = lax.all_gather(array, name, axis=axis[name], tiled=True)
        return array

    em, nm = joined(edge_mats, "mesh", "width"), joined(node_mats, "mesh", "width")
    eb, nb = joined(edge_back, "width", "mesh"), joined(node_back, "width", "mesh")
    em = em.reshape(em.shape[0], -1, em.shape[3])
    nm = nm.reshape(nm.shape[0], -1, nm.shape[3])
    found = [Whole("e", [em[0], eb[0]]), Whole("n", [nm[0], nb[0]])]
    for block in range(1, em.shape[0]):
        found.append(Whole("en", [em[block], eb[block], nm[block], nb[block]]))
    return found


def on_device(
    grid_latent,
    mesh_latent,
    grid_edge,
    mesh_edge,
    encoder_slot,
    encoder_target,
    halo_down,
    halo_up,
    send_lists,
    mesh_slot,
    mesh_target,
    edge_mats,
    node_mats,
    edge_back,
    node_back,
):
    depth = grid_latent.shape[1]
    hidden = edge_mats.shape[3] * lax.axis_size("width")
    nodes = mesh_latent.shape[0]
    sizes = [lax.axis_size(name) for name in ("groups", "mesh", "band", "width")]
    by_parts = sizes == [2, 4, 2, 2] and edge_mats.shape[0] == 3
    halo = halo_down.shape[0]
    line = sizes[1] * sizes[2]
    packs = (weights_by_parts if by_parts else weights_whole)(edge_mats, node_mats, edge_back, node_back)

    lent = call(pack_body, shaped(2 * halo, depth), [], grid_latent, jnp.concatenate([halo_down, halo_up])[:, None])
    from_upper = lax.ppermute(lent[:halo], ("mesh", "band"), [((i + 1) % line, i) for i in range(line)])
    from_lower = lax.ppermute(lent[halo:], ("mesh", "band"), [(i, (i + 1) % line) for i in range(line)])
    gathered = call(
        sender_body,
        shaped(grid_edge.shape[0], 2 * depth),
        [],
        grid_latent,
        from_lower,
        from_upper,
        mesh_latent,
        encoder_slot[:, None],
        encoder_target[:, None],
    )
    pack = packs[0]
    incoming = call(
        functools.partial(first_edges_body, pack, len(pack.operands)),
        shaped(nodes, depth),
        [pltpu.VMEM(grid_edge.shape, BF)] + pack.scratch(hidden, depth),
        gathered,
        grid_edge,
        encoder_target[None, :],
        *pack.operands,
    )
    pack = packs[1]
    lists = send_lists.reshape(-1, 1)
    rows, packed = call(
        functools.partial(nodes_body, pack, len(pack.operands)),
        [shaped(nodes, depth), shaped(lists.shape[0], depth)],
        pack.scratch(hidden, depth),
        mesh_latent,
        incoming,
        lists,
        *pack.operands,
    )
    edges = mesh_edge
    slots, targets, ids = mesh_slot[:, None], mesh_target[:, None], mesh_target[None, :]
    for pack in packs[2:]:
        last = pack is packs[-1]
        cut = packed.reshape(send_lists.shape[1:] + (depth,))
        senders = lax.all_to_all(cut, ("mesh", "band"), split_axis=0, concat_axis=0, tiled=True).reshape(-1, depth)
        outs = [shaped(nodes, depth)]
        if not last:
            outs += [shaped(lists.shape[0], depth), shaped(*edges.shape)]
        got = call(
            functools.partial(block_body, pack, len(pack.operands), last),
            outs,
            [pltpu.VMEM(edges.shape, BF), pltpu.VMEM((senders.shape[0] + nodes, hidden), BF)] + pack.scratch(hidden, depth),
            senders,
            rows,
            edges,
            slots,
            targets,
            ids,
            lists,
            *pack.operands,
        )
        if last:
            rows = got[0]
        else:
            rows, packed, edges = got
    return rows


def solution(mesh):
    return jax.shard_map(
        on_device,
        mesh=mesh,
        in_specs=(
            P(("groups", "mesh", "band"), None),
            P(("groups", "mesh", "band"), None),
            P(("groups", "mesh", "band"), None),
            P(("groups", "mesh", "band"), None),
            P(("groups", "mesh", "band")),
            P(("groups", "mesh", "band")),
            P(("groups", "mesh", "band")),
            P(("groups", "mesh", "band")),
            P(("groups", "mesh", "band"), None, None),
            P(("groups", "mesh", "band")),
            P(("groups", "mesh", "band")),
            P(None, None, "mesh", "width"),
            P(None, None, "mesh", "width"),
            P(None, "width", "mesh"),
            P(None, "width", "mesh"),
        ),
        out_specs=P(("groups", "mesh", "band"), None),
        check_vma=False,
    )
```

time: 292 us -> 147 us (0.50)
  blocking collectives: 179 us -> 0 us
  starting transfers between devices: 13.8 us -> 46.8 us
  waiting for transfers between devices: 25.6 us -> 48.2 us
  Pallas kernels: 0 us -> 17.9 us
  matrix products: 17.3 us -> 0 us
  other arithmetic: 16.5 us -> 2.66 us
  between operations: 14 us -> 0.49 us
  local copies, waits for them, and re-layouts: 24.8 us -> 29.8 us
    all_gather x12 -> x0, blocking collectives: 179 us -> none  [the longest x3 52.7 us: on_device(): lax.all_gather(edge_mats[block_id], 'mesh', axis=1, tiled=True)]
    ppermute x2 -> x38, waiting for transfers between devices: 0.01 us -> 34.7 us  [the longest x12 26.2 us: spread(): lax.ppermute(chunk, 'mesh', [(i, (i + k) % count) for i in range(count)])]
    ppermute x2 -> x38, starting transfers between devices: 6.73 us -> 38.4 us  [the longest x12 15 us: spread(): lax.ppermute(chunk, 'mesh', [(i, (i + k) % count) for i in range(count)])]
    unnamed x62 -> x126, local copies, waits for them, and re-layouts: 2.4 us -> 27.5 us
    gather x10 -> x0, local copies, waits for them, and re-layouts: 19.5 us -> none  [the longest x3 7.97 us: edge_update(): send_table[send_slot].astype(jnp.float32)]
    pallas_call x0 -> x7, Pallas kernels: none -> 17.9 us  [call(): pl.pallas_call(body, out_shape=outs, scratch_shapes=scratch, compiler_par...]
    dot_general x18 -> x0, matrix products: 17.3 us -> none  [the longest x3 9 us: edge_update(): jnp.dot(edge_hidden, edge_back, preferred_element_type=jnp.float32)]
    psum x6 -> x0, waiting for transfers between devices: 16.1 us -> none  [finish(): lax.psum(partial_value.astype(jnp.bfloat16), 'width').astype(jnp.float32)]
  transfers between devices with their start and end apart: 10 -> 40, of which waited for: 3 -> 12; matrix products, arithmetic and copies ran while one was open for 5% -> 3% of each run, Pallas kernels for 0% -> 8%
where the time goes in v1:
time: 147 us; the launch traced here: 146 us
  waiting for transfers between devices  48.2 us (33%)
  starting transfers between devices  46.8 us (32%)
  local copies, waits for them, and re-layouts  29.8 us (20%)
  Pallas kernels  17.9 us (12%)
  other arithmetic  2.66 us (2%)
    unnamed x126, local copies, waits for them, and re-layouts  27.5 us
    ppermute x12, waiting for transfers between devices, spread(): lax.ppermute(chunk, 'mesh', [(i, (i + k) % count) for i in range(count)])  26.2 us
    pallas_call x7, Pallas kernels, call(): pl.pallas_call(body, out_shape=outs, scratch_shapes=scratch, compiler_par...  17.9 us
    ppermute x12, starting transfers between devices, spread(): lax.ppermute(chunk, 'mesh', [(i, (i + k) % count) for i in range(count)])  15 us
    all_to_all x2, waiting for transfers between devices, on_device(): lax.all_to_all(cut, ('mesh', 'band'), split_axis=0, concat_axis=0, tiled=...  13.6 us
    all_to_all x2, starting transfers between devices, on_device(): lax.all_to_all(cut, ('mesh', 'band'), split_axis=0, concat_axis=0, tiled=...  8.35 us
    ppermute x2, starting transfers between devices, spread(): lax.ppermute(own, 'band', SWAP)  4.85 us
    ppermute x1, waiting for transfers between devices, spread(): return [own, lax.ppermute(own, 'band', SWAP)]  4.65 us
  transfers between devices with their start and end apart: 40, of which 12 were waited for; matrix products, arithmetic and copies ran while one was open for 3% of the time, Pallas kernels for 8%

profile of v1, /device:TPU:0, one launch (start us, length us, event | category | flops | bytes accessed | tf_op | source)
XLA Modules:
  0.0 145.9 jit_solution(2523873588571333759)
XLA Ops:
  0.0 1.1 copy-done
  1.1 1.0 copy-done.2
  2.1 0.9 copy-done.4
  3.0 0.9 copy-done.6
  4.0 3.1 %collective-permute-start.2 = (bf16[4,32,256]{2,1,0:T(8,128)(2,1)S(1)}, bf16[4,32,256]{2,1,0:T(8,128)(2,1)S(1)}, u32[]{:S(2)}, u32[]{:S(2)}) collective-permute-start(bf16[4,32,256]{2,1,0:T(8,128)(2,1)S(1)} %get-tuple-element.14), channel_id=1, source_target_pairs={{0,4},{4,8},{8,12},{12,0},{1,5},{5,9},{9,13},{13,1},{2,6},{6,10},{... | collective-permute-start | bytes 196616 | tf_op jit(solution)/shard_map/ppermute | solution.py:244
  7.1 2.6 %collective-permute-start.3 = (bf16[4,32,256]{2,1,0:T(8,128)(2,1)S(1)}, bf16[4,32,256]{2,1,0:T(8,128)(2,1)S(1)}, u32[]{:S(2)}, u32[]{:S(2)}) collective-permute-start(bf16[4,32,256]{2,1,0:T(8,128)(2,1)S(1)} %get-tuple-element.14), channel_id=1, source_target_pairs={{0,8},{4,12},{8,0},{12,4},{1,9},{5,13},{9,1},{13,5},{2,10},{6,14},... | collective-permute-start | bytes 196616 | tf_op jit(solution)/shard_map/ppermute | solution.py:244
  9.7 1.8 %collective-permute-start.15 = (bf16[3,32,256]{2,1,0:T(8,128)(2,1)S(1)}, bf16[3,32,256]{2,1,0:T(8,128)(2,1)S(1)}, u32[]{:S(2)}, u32[]{:S(2)}) collective-permute-start(bf16[3,32,256]{2,1,0:T(8,128)(2,1)S(1)} %get-tuple-element.15), channel_id=1, source_target_pairs={{0,8},{4,12},{8,0},{12,4},{1,9},{5,13},{9,1},{13,5},{2,10},{6,14},... | collective-permute-start | bytes 147464 | tf_op jit(solution)/shard_map/ppermute | solution.py:244
  11.6 1.9 %collective-permute-start.16 = (bf16[3,32,256]{2,1,0:T(8,128)(2,1)S(1)}, bf16[3,32,256]{2,1,0:T(8,128)(2,1)S(1)}, u32[]{:S(2)}, u32[]{:S(2)}) collective-permute-start(bf16[3,32,256]{2,1,0:T(8,128)(2,1)S(1)} %get-tuple-element.15), channel_id=1, source_target_pairs={{0,12},{4,0},{8,4},{12,8},{1,13},{5,1},{9,5},{13,9},{2,14},{6,2},{... | collective-permute-start | bytes 147464 | tf_op jit(solution)/shard_map/ppermute | solution.py:244
  13.5 0.7 add_bitcast_fusion
  14.6 1.0 collective-permute-done.14
  15.6 1.7 %collective-permute-done.15 = bf16[3,32,256]{2,1,0:T(8,128)(2,1)S(1)} collective-permute-done((bf16[3,32,256]{2,1,0:T(8,128)(2,1)S(1)}, bf16[3,32,256]{2,1,0:T(8,128)(2,1)S(1)}, u32[]{:S(2)}, u32[]{:S(2)}) %collective-permute-start.15) | collective-permute-done | bytes 49184 | tf_op jit(solution)/shard_map/ppermute | solution.py:244
  17.3 1.8 %collective-permute-start.17 = (bf16[3,3,32,256]{3,2,1,0:T(8,128)(2,1)S(1)}, bf16[3,3,32,256]{3,2,1,0:T(8,128)(2,1)S(1)}, u32[]{:S(2)}, u32[]{:S(2)}) collective-permute-start(bf16[3,3,32,256]{3,2,1,0:T(8,128)(2,1)S(1)} %pad_maximum_fusion.3.refs_2_), channel_id=1, source_target_pairs={{0,2},{2,0},{1,3},{3,1},{4,6},{6,4},{5,7},{7,5},{8,10},{10,8},{9,1... | collective-permute-start | bytes 442376 | tf_op jit(solution)/shard_map/ppermute | solution.py:252
  19.4 4.5 %collective-permute-start.1 = (bf16[64,512]{1,0:T(8,128)(2,1)S(1)}, bf16[64,512]{1,0:T(8,128)(2,1)S(1)}, u32[]{:S(2)}, u32[]{:S(2)}) collective-permute-start(bf16[64,512]{1,0:T(8,128)(2,1)S(1)} %get-tuple-element.23), channel_id=1, source_target_pairs={{2,0},{4,2},{6,4},{8,6},{10,8},{12,10},{14,12},{0,14},{3,1},{5,3},... | collective-permute-start | bytes 196616 | tf_op jit(solution)/shard_map/ppermute | solution.py:329
  23.9 1.5 %collective-permute-start.18 = (bf16[3,3,32,256]{3,2,1,0:T(8,128)(2,1)S(1)}, bf16[3,3,32,256]{3,2,1,0:T(8,128)(2,1)S(1)}, u32[]{:S(2)}, u32[]{:S(2)}) collective-permute-start(bf16[3,3,32,256]{3,2,1,0:T(8,128)(2,1)S(1)} %pad_maximum_fusion.3.refs_2_), channel_id=1, source_target_pairs={{0,16},{16,0},{1,17},{17,1},{2,18},{18,2},{3,19},{19,3},{4,20},{20... | collective-permute-start | bytes 442376 | tf_op jit(solution)/shard_map/ppermute | solution.py:253
  25.4 0.8 collective-permute-done.low
  26.8 1.6 %collective-permute-start.27 = (bf16[7,64,256]{2,1,0:T(8,128)(2,1)S(1)}, bf16[7,64,256]{2,1,0:T(8,128)(2,1)S(1)}, u32[]{:S(2)}, u32[]{:S(2)}) collective-permute-start(bf16[7,64,256]{2,1,0:T(8,128)(2,1)S(1)} %get-tuple-element.18), channel_id=1, source_target_pairs={{0,8},{4,12},{8,0},{12,4},{1,9},{5,13},{9,1},{13,5},{2,10},{6,14},... | collective-permute-start | bytes 688136 | tf_op jit(solution)/shard_map/ppermute | solution.py:244
  29.0 1.7 %collective-permute-start.28 = (bf16[7,64,256]{2,1,0:T(8,128)(2,1)S(1)}, bf16[7,64,256]{2,1,0:T(8,128)(2,1)S(1)}, u32[]{:S(2)}, u32[]{:S(2)}) collective-permute-start(bf16[7,64,256]{2,1,0:T(8,128)(2,1)S(1)} %get-tuple-element.18), channel_id=1, source_target_pairs={{0,12},{4,0},{8,4},{12,8},{1,13},{5,1},{9,5},{13,9},{2,14},{6,2},{... | collective-permute-start | bytes 688136 | tf_op jit(solution)/shard_map/ppermute | solution.py:244
  30.7 3.1 %collective-permute-start.19 = (bf16[3,3,32,256]{3,2,1,0:T(8,128)(2,1)S(1)}, bf16[3,3,32,256]{3,2,1,0:T(8,128)(2,1)S(1)}, u32[]{:S(2)}, u32[]{:S(2)}) collective-permute-start(bf16[3,3,32,256]{3,2,1,0:T(8,128)(2,1)S(1)} %pad_maximum_fusion.3.refs_2_), channel_id=1, source_target_pairs={{0,18},{18,0},{2,16},{16,2},{1,19},{19,1},{3,17},{17,3},{4,22},{22... | collective-permute-start | bytes 442376 | tf_op jit(solution)/shard_map/ppermute | solution.py:254
  35.1 1.8 %collective-permute-done.19.refs_5_ = bf16[3,3,32,256]{3,2,1,0:T(8,128)(2,1)S(1)} collective-permute-done((bf16[3,3,32,256]{3,2,1,0:T(8,128)(2,1)S(1)}, bf16[3,3,32,256]{3,2,1,0:T(8,128)(2,1)S(1)}, u32[]{:S(2)}, u32[]{:S(2)}) %collective-permute-start.19) | collective-permute-done | bytes 147488 | tf_op jit(solution)/shard_map/ppermute | solution.py:254
  37.0 0.7 copy-done.45
  38.9 1.0 collective-permute-start.33
  39.9 9.3 %collective-permute-done.28 = bf16[7,64,256]{2,1,0:T(8,128)(2,1)S(1)} collective-permute-done((bf16[7,64,256]{2,1,0:T(8,128)(2,1)S(1)}, bf16[7,64,256]{2,1,0:T(8,128)(2,1)S(1)}, u32[]{:S(2)}, u32[]{:S(2)}) %collective-permute-start.28) | collective-permute-done | bytes 229408 | tf_op jit(solution)/shard_map/ppermute | solution.py:244
  49.3 3.0 %collective-permute-start.5 = (bf16[3,4,32,256]{3,2,1,0:T(8,128)(2,1)S(1)}, bf16[3,4,32,256]{3,2,1,0:T(8,128)(2,1)S(1)}, u32[]{:S(2)}, u32[]{:S(2)}) collective-permute-start(bf16[3,4,32,256]{3,2,1,0:T(8,128)(2,1)S(1)} %pad_maximum_fusion.2.refs_2_), channel_id=1, source_target_pairs={{0,2},{2,0},{1,3},{3,1},{4,6},{6,4},{5,7},{7,5},{8,10},{10,8},{9,1... | collective-permute-start | bytes 589832 | tf_op jit(solution)/shard_map/ppermute | solution.py:252
  52.3 0.9 pad_maximum_fusion.refs_4_
  53.2 1.5 %collective-permute-start.6 = (bf16[3,4,32,256]{3,2,1,0:T(8,128)(2,1)S(1)}, bf16[3,4,32,256]{3,2,1,0:T(8,128)(2,1)S(1)}, u32[]{:S(2)}, u32[]{:S(2)}) collective-permute-start(bf16[3,4,32,256]{3,2,1,0:T(8,128)(2,1)S(1)} %pad_maximum_fusion.2.refs_2_), channel_id=1, source_target_pairs={{0,16},{16,0},{1,17},{17,1},{2,18},{18,2},{3,19},{19,3},{4,20},{20... | collective-permute-start | bytes 589832 | tf_op jit(solution)/shard_map/ppermute | solution.py:253
  54.7 8.8 %collective-permute-done.33 = bf16[7,64,256]{2,1,0:T(8,128)(2,1)S(1)} collective-permute-done((bf16[7,64,256]{2,1,0:T(8,128)(2,1)S(1)}, bf16[7,64,256]{2,1,0:T(8,128)(2,1)S(1)}, u32[]{:S(2)}, u32[]{:S(2)}) %collective-permute-start.33) | collective-permute-done | bytes 229408 | tf_op jit(solution)/shard_map/ppermute | solution.py:244
  63.5 4.8 %collective-permute-done.34 = bf16[7,64,256]{2,1,0:T(8,128)(2,1)S(1)} collective-permute-done((bf16[7,64,256]{2,1,0:T(8,128)(2,1)S(1)}, bf16[7,64,256]{2,1,0:T(8,128)(2,1)S(1)}, u32[]{:S(2)}, u32[]{:S(2)}) %collective-permute-start.34) | collective-permute-done | bytes 229408 | tf_op jit(solution)/shard_map/ppermute | solution.py:244
  68.3 3.1 %collective-permute-start.29 = (bf16[3,7,64,256]{3,2,1,0:T(8,128)(2,1)}, bf16[3,7,64,256]{3,2,1,0:T(8,128)(2,1)}, u32[]{:S(2)}, u32[]{:S(2)}) collective-permute-start(bf16[3,7,64,256]{3,2,1,0:T(8,128)(2,1)} %pad_maximum_fusion.refs_4_), channel_id=1, source_target_pairs={{0,2},{2,0},{1,3},{3,1},{4,6},{6,4},{5,7},{7,5},{8,10},{10,8},{9,1... | collective-permute-start | bytes 2064392 | tf_op jit(solution)/shard_map/ppermute | solution.py:247
  71.4 0.9 pad_maximum_fusion.1.refs_4_
  72.4 1.5 %collective-permute-start.35 = (bf16[3,7,64,256]{3,2,1,0:T(8,128)(2,1)}, bf16[3,7,64,256]{3,2,1,0:T(8,128)(2,1)}, u32[]{:S(2)}, u32[]{:S(2)}) collective-permute-start(bf16[3,7,64,256]{3,2,1,0:T(8,128)(2,1)} %pad_maximum_fusion.1.refs_4_), channel_id=1, source_target_pairs={{0,16},{16,0},{1,17},{17,1},{2,18},{18,2},{3,19},{19,3},{4,20},{20... | collective-permute-start | bytes 2064392 | tf_op jit(solution)/shard_map/ppermute | solution.py:249
  73.9 0.7 copy-done.39
  75.1 0.7 copy-done.31
  77.6 0.7 copy-done.25
  79.5 0.7 copy-done.27
  80.2 0.7 copy-done.33
  80.9 0.7 copy-done.29
  82.7 4.7 %collective-permute-done.29.refs_5_ = bf16[3,7,64,256]{3,2,1,0:T(8,128)(2,1)} collective-permute-done((bf16[3,7,64,256]{3,2,1,0:T(8,128)(2,1)}, bf16[3,7,64,256]{3,2,1,0:T(8,128)(2,1)}, u32[]{:S(2)}, u32[]{:S(2)}) %collective-permute-start.29) | collective-permute-done | bytes 688160 | tf_op jit(solution)/shard_map/ppermute | solution.py:247
  87.4 0.7 copy-done.37
  88.6 1.2 collective-permute-done.35.refs_5_
  90.3 0.9 broadcast_in_dim.29.targets
  91.2 0.9 broadcast_in_dim.28.slots
  92.2 1.0 copy-done.9
  93.2 1.0 copy-done.10
  94.2 1.0 copy-done.11
  95.2 0.8 copy-done.54
  96.0 0.8 copy-done.56
  96.9 1.3 shard_map.146.gathered
  98.5 2.7 %shard_map.148.incoming = bf16[320,512]{1,0:T(8,128)(2,1)S(1)} custom-call(bf16[768,1024]{1,0:T(8,128)(2,1)S(1)} %shard_map.146.gathered, bf16[768,512]{1,0:T(8,128)(2,1)S(1)} %copy-done.15, s32[1,768]{1,0:T(1,128)S(1)} %broadcast_in_dim.24.ids, bf16[3,3,128,256]{3,2,1,0:T(8,128)(2,1)S(1)} %copy-done.1, bf16[3,256,128]{2,1,0:T(8,128)(2,1)S(1)} %copy-done.5, ...), custom_call_target="tpu_custom_call" | custom-call | tf_op jit(solution)/shard_map/pallas_call | solution.py:42
  101.3 1.9 %shard_map.149 = (bf16[320,512]{1,0:T(8,128)(2,1)S(1)}, bf16[64,512]{1,0:T(8,128)(2,1)}) custom-call(bf16[320,512]{1,0:T(8,128)(2,1)S(1)} %copy-done.11, bf16[320,512]{1,0:T(8,128)(2,1)S(1)} %shard_map.148.incoming, s32[64,1]{1,0:T(8,128)S(1)} %reshape.20.lists, bf16[3,2,128,256]{3,2,1,0:T(8,128)(2,1)S(1)} %copy-done.3, bf16[3,256,128]{2,1,0:T(8,128)(2,1)S(1)} %copy-done.7, ...), custom_call_target="tpu_custom_call" | custom-call | tf_op jit(solution)/shard_map/pallas_call | solution.py:42
  103.2 0.7 copy-done.21
  103.9 4.4 %all-to-all-start = ((bf16[8,8,512]{2,1,0:T(8,128)(2,1)}), bf16[8,8,512]{2,1,0:T(8,128)(2,1)}, u32[]{:S(2)}, u32[]{:S(2)}) async-start(bf16[8,8,512]{2,1,0:T(8,128)(2,1)} %bitcast.7), calls=%async_computation | async-start | bytes 131072 | tf_op jit(solution)/shard_map/all_to_all | solution.py:368
  108.7 6.7 %all-to-all-done = bf16[8,8,512]{2,1,0:T(8,128)(2,1)} async-done(((bf16[8,8,512]{2,1,0:T(8,128)(2,1)}), bf16[8,8,512]{2,1,0:T(8,128)(2,1)}, u32[]{:S(2)}, u32[]{:S(2)}) %all-to-all-start) | async-done | bytes 65568 | tf_op jit(solution)/shard_map/all_to_all | solution.py:368
  115.3 1.1 copy-done.12
  116.5 0.8 copy-done.19
  117.2 1.0 copy-done.22
  118.2 5.6 %shard_map.150 = (bf16[320,512]{1,0:T(8,128)(2,1)S(1)}, bf16[64,512]{1,0:T(8,128)(2,1)S(1)}, bf16[768,512]{1,0:T(8,128)(2,1)S(1)}) custom-call(bf16[64,512]{1,0:T(8,128)(2,1)} %bitcast.8.senders, bf16[320,512]{1,0:T(8,128)(2,1)S(1)} %copy-done.22, bf16[768,512]{1,0:T(8,128)(2,1)S(1)} %copy-done.12, s32[768,1]{1,0:T(8,128)S(1)} %broadcast_in_dim.30.slots, ...), custom_call_target="tpu_custom_call" | custom-call | tf_op jit(solution)/shard_map/pallas_call | solution.py:42
  123.8 0.9 copy-done.13
  124.7 0.7 copy-done.23
  126.0 4.0 %all-to-all-start.1 = ((bf16[8,8,512]{2,1,0:T(8,128)(2,1)}), bf16[8,8,512]{2,1,0:T(8,128)(2,1)}, u32[]{:S(2)}, u32[]{:S(2)}) async-start(bf16[8,8,512]{2,1,0:T(8,128)(2,1)} %bitcast.18), calls=%async_computation.1 | async-start | bytes 131072 | tf_op jit(solution)/shard_map/all_to_all | solution.py:368
  130.0 6.9 %all-to-all-done.1 = bf16[8,8,512]{2,1,0:T(8,128)(2,1)} async-done(((bf16[8,8,512]{2,1,0:T(8,128)(2,1)}), bf16[8,8,512]{2,1,0:T(8,128)(2,1)}, u32[]{:S(2)}, u32[]{:S(2)}) %all-to-all-start.1) | async-done | bytes 65568 | tf_op jit(solution)/shard_map/all_to_all | solution.py:368
  136.9 1.1 copy-done.14
  138.0 0.8 copy-done.20
  138.8 1.0 copy-done.24
  139.8 6.1 %shard_map.151 = bf16[320,512]{1,0:T(8,128)(2,1)} custom-call(bf16[64,512]{1,0:T(8,128)(2,1)} %bitcast.13.senders, bf16[320,512]{1,0:T(8,128)(2,1)S(1)} %copy-done.24, bf16[768,512]{1,0:T(8,128)(2,1)S(1)} %copy-done.14, s32[768,1]{1,0:T(8,128)S(1)} %broadcast_in_dim.30.slots, s32[768,1]{1,0:T(8,128)S(1)} %broadcast_in_dim.31.targets, ...), custom_call_target="tpu_custom_call" | custom-call | tf_op jit(solution)/shard_map/pallas_call | solution.py:42
  (163 shorter events, 11.7 us)
Async XLA Ops:
  3.9 10.4 %copy-start.8 = (bf16[512,512]{1,0:T(8,128)(2,1)S(1)}, bf16[512,512]{1,0:T(8,128)(2,1)}, u32[]{:S(2)}) copy-start(bf16[512,512]{1,0:T(8,128)(2,1)} %grid.1) | copy-start | bytes 1572868
  3.9 13.4 %copy-start.5 = (bf16[3,256,128]{2,1,0:T(8,128)(2,1)S(1)}, bf16[3,256,128]{2,1,0:T(8,128)(2,1)}, u32[]{:S(2)}) copy-start(bf16[3,256,128]{2,1,0:T(8,128)(2,1)} %refs_1_.7) | copy-start | bytes 589828
  3.9 33.0 %copy-start.7 = (bf16[3,256,128]{2,1,0:T(8,128)(2,1)S(1)}, bf16[3,256,128]{2,1,0:T(8,128)(2,1)}, u32[]{:S(2)}) copy-start(bf16[3,256,128]{2,1,0:T(8,128)(2,1)} %refs_3_.3) | copy-start | bytes 589828
  4.0 15.2 %collective-permute-start.2 = (bf16[4,32,256]{2,1,0:T(8,128)(2,1)S(1)}, bf16[4,32,256]{2,1,0:T(8,128)(2,1)S(1)}, u32[]{:S(2)}, u32[]{:S(2)}) collective-permute-start(bf16[4,32,256]{2,1,0:T(8,128)(2,1)S(1)} %get-tuple-element.14), channel_id=1, source_target_pairs={{0,4},{4,8},{8,12},{12,0},{1,5},{5,9},{9,13},{13,1},{2,6},{6,10},{... | collective-permute-start | bytes 196616 | tf_op jit(solution)/shard_map/ppermute | solution.py:244
  7.1 12.4 %collective-permute-start.3 = (bf16[4,32,256]{2,1,0:T(8,128)(2,1)S(1)}, bf16[4,32,256]{2,1,0:T(8,128)(2,1)S(1)}, u32[]{:S(2)}, u32[]{:S(2)}) collective-permute-start(bf16[4,32,256]{2,1,0:T(8,128)(2,1)S(1)} %get-tuple-element.14), channel_id=1, source_target_pairs={{0,8},{4,12},{8,0},{12,4},{1,9},{5,13},{9,1},{13,5},{2,10},{6,14},... | collective-permute-start | bytes 196616 | tf_op jit(solution)/shard_map/ppermute | solution.py:244
  9.6 6.0 %collective-permute-start.14 = (bf16[3,32,256]{2,1,0:T(8,128)(2,1)S(1)}, bf16[3,32,256]{2,1,0:T(8,128)(2,1)S(1)}, u32[]{:S(2)}, u32[]{:S(2)}) collective-permute-start(bf16[3,32,256]{2,1,0:T(8,128)(2,1)S(1)} %get-tuple-element.15), channel_id=1, source_target_pairs={{0,4},{4,8},{8,12},{12,0},{1,5},{5,9},{9,13},{13,1},{2,6},{6,10},{... | collective-permute-start | bytes 147464 | tf_op jit(solution)/shard_map/ppermute | solution.py:244
  9.7 7.6 %collective-permute-start.15 = (bf16[3,32,256]{2,1,0:T(8,128)(2,1)S(1)}, bf16[3,32,256]{2,1,0:T(8,128)(2,1)S(1)}, u32[]{:S(2)}, u32[]{:S(2)}) collective-permute-start(bf16[3,32,256]{2,1,0:T(8,128)(2,1)S(1)} %get-tuple-element.15), channel_id=1, source_target_pairs={{0,8},{4,12},{8,0},{12,4},{1,9},{5,13},{9,1},{13,5},{2,10},{6,14},... | collective-permute-start | bytes 147464 | tf_op jit(solution)/shard_map/ppermute | solution.py:244
  11.6 5.7 %collective-permute-start.16 = (bf16[3,32,256]{2,1,0:T(8,128)(2,1)S(1)}, bf16[3,32,256]{2,1,0:T(8,128)(2,1)S(1)}, u32[]{:S(2)}, u32[]{:S(2)}) collective-permute-start(bf16[3,32,256]{2,1,0:T(8,128)(2,1)S(1)} %get-tuple-element.15), channel_id=1, source_target_pairs={{0,12},{4,0},{8,4},{12,8},{1,13},{5,1},{9,5},{13,9},{2,14},{6,2},{... | collective-permute-start | bytes 147464 | tf_op jit(solution)/shard_map/ppermute | solution.py:244
  15.6 8.3 %collective-permute-start.4 = (bf16[4,32,256]{2,1,0:T(8,128)(2,1)S(1)}, bf16[4,32,256]{2,1,0:T(8,128)(2,1)S(1)}, u32[]{:S(2)}, u32[]{:S(2)}) collective-permute-start(bf16[4,32,256]{2,1,0:T(8,128)(2,1)S(1)} %get-tuple-element.14), channel_id=1, source_target_pairs={{0,12},{4,0},{8,4},{12,8},{1,13},{5,1},{9,5},{13,9},{2,14},{6,2},{... | collective-permute-start | bytes 196616 | tf_op jit(solution)/shard_map/ppermute | solution.py:244
  17.3 13.5 %collective-permute-start.9 = (bf16[3,256,128]{2,1,0:T(8,128)(2,1)S(1)}, bf16[3,256,128]{2,1,0:T(8,128)(2,1)S(1)}, u32[]{:S(2)}, u32[]{:S(2)}) collective-permute-start(bf16[3,256,128]{2,1,0:T(8,128)(2,1)S(1)} %copy-done.5), channel_id=1, source_target_pairs={{0,1},{1,0},{2,3},{3,2},{4,5},{5,4},{6,7},{7,6},{8,9},{9,8},{10,11... | collective-permute-start | bytes 589832 | tf_op jit(solution)/shard_map/ppermute | solution.py:259
  17.3 16.5 %collective-permute-start.17 = (bf16[3,3,32,256]{3,2,1,0:T(8,128)(2,1)S(1)}, bf16[3,3,32,256]{3,2,1,0:T(8,128)(2,1)S(1)}, u32[]{:S(2)}, u32[]{:S(2)}) collective-permute-start(bf16[3,3,32,256]{3,2,1,0:T(8,128)(2,1)S(1)} %pad_maximum_fusion.3.refs_2_), channel_id=1, source_target_pairs={{0,2},{2,0},{1,3},{3,1},{4,6},{6,4},{5,7},{7,5},{8,10},{10,8},{9,1... | collective-permute-start | bytes 442376 | tf_op jit(solution)/shard_map/ppermute | solution.py:252
  19.2 7.0 %collective-permute-start = (bf16[64,512]{1,0:T(8,128)(2,1)S(1)}, bf16[64,512]{1,0:T(8,128)(2,1)S(1)}, u32[]{:S(2)}, u32[]{:S(2)}) collective-permute-start(bf16[64,512]{1,0:T(8,128)(2,1)S(1)} %get-tuple-element.24), channel_id=1, source_target_pairs={{0,2},{2,4},{4,6},{6,8},{8,10},{10,12},{12,14},{14,0},{1,3},{3,5},... | collective-permute-start | bytes 196616 | tf_op jit(solution)/shard_map/ppermute | solution.py:330
  19.4 9.0 %collective-permute-start.1 = (bf16[64,512]{1,0:T(8,128)(2,1)S(1)}, bf16[64,512]{1,0:T(8,128)(2,1)S(1)}, u32[]{:S(2)}, u32[]{:S(2)}) collective-permute-start(bf16[64,512]{1,0:T(8,128)(2,1)S(1)} %get-tuple-element.23), channel_id=1, source_target_pairs={{2,0},{4,2},{6,4},{8,6},{10,8},{12,10},{14,12},{0,14},{3,1},{5,3},... | collective-permute-start | bytes 196616 | tf_op jit(solution)/shard_map/ppermute | solution.py:329
  23.9 10.6 %collective-permute-start.18 = (bf16[3,3,32,256]{3,2,1,0:T(8,128)(2,1)S(1)}, bf16[3,3,32,256]{3,2,1,0:T(8,128)(2,1)S(1)}, u32[]{:S(2)}, u32[]{:S(2)}) collective-permute-start(bf16[3,3,32,256]{3,2,1,0:T(8,128)(2,1)S(1)} %pad_maximum_fusion.3.refs_2_), channel_id=1, source_target_pairs={{0,16},{16,0},{1,17},{17,1},{2,18},{18,2},{3,19},{19,3},{4,20},{20... | collective-permute-start | bytes 442376 | tf_op jit(solution)/shard_map/ppermute | solution.py:253
  26.8 12.1 %collective-permute-start.27 = (bf16[7,64,256]{2,1,0:T(8,128)(2,1)S(1)}, bf16[7,64,256]{2,1,0:T(8,128)(2,1)S(1)}, u32[]{:S(2)}, u32[]{:S(2)}) collective-permute-start(bf16[7,64,256]{2,1,0:T(8,128)(2,1)S(1)} %get-tuple-element.18), channel_id=1, source_target_pairs={{0,8},{4,12},{8,0},{12,4},{1,9},{5,13},{9,1},{13,5},{2,10},{6,14},... | collective-permute-start | bytes 688136 | tf_op jit(solution)/shard_map/ppermute | solution.py:244
  29.0 20.2 %collective-permute-start.28 = (bf16[7,64,256]{2,1,0:T(8,128)(2,1)S(1)}, bf16[7,64,256]{2,1,0:T(8,128)(2,1)S(1)}, u32[]{:S(2)}, u32[]{:S(2)}) collective-permute-start(bf16[7,64,256]{2,1,0:T(8,128)(2,1)S(1)} %get-tuple-element.18), channel_id=1, source_target_pairs={{0,12},{4,0},{8,4},{12,8},{1,13},{5,1},{9,5},{13,9},{2,14},{6,2},{... | collective-permute-start | bytes 688136 | tf_op jit(solution)/shard_map/ppermute | solution.py:244
  30.7 6.2 %collective-permute-start.19 = (bf16[3,3,32,256]{3,2,1,0:T(8,128)(2,1)S(1)}, bf16[3,3,32,256]{3,2,1,0:T(8,128)(2,1)S(1)}, u32[]{:S(2)}, u32[]{:S(2)}) collective-permute-start(bf16[3,3,32,256]{3,2,1,0:T(8,128)(2,1)S(1)} %pad_maximum_fusion.3.refs_2_), channel_id=1, source_target_pairs={{0,18},{18,0},{2,16},{16,2},{1,19},{19,1},{3,17},{17,3},{4,22},{22... | collective-permute-start | bytes 442376 | tf_op jit(solution)/shard_map/ppermute | solution.py:254
  33.8 3.1 %collective-permute-start.22 = (bf16[3,3,32,256]{3,2,1,0:T(8,128)(2,1)S(1)}, bf16[3,3,32,256]{3,2,1,0:T(8,128)(2,1)S(1)}, u32[]{:S(2)}, u32[]{:S(2)}) collective-permute-start(bf16[3,3,32,256]{3,2,1,0:T(8,128)(2,1)S(1)} %pad_maximum_fusion.3.refs_2_), channel_id=1, source_target_pairs={{0,1},{1,0},{2,3},{3,2},{4,5},{5,4},{6,7},{7,6},{8,9},{9,8},{10,11... | collective-permute-start | bytes 442376 | tf_op jit(solution)/shard_map/ppermute | solution.py:259
  34.5 40.1 %copy-start.41 = (bf16[3,3,32,256]{3,2,1,0:T(8,128)(2,1)}, bf16[3,3,32,256]{3,2,1,0:T(8,128)(2,1)S(1)}, u32[]{:S(2)}) copy-start(bf16[3,3,32,256]{3,2,1,0:T(8,128)(2,1)S(1)} %collective-permute-done.18.refs_4_) | copy-start | bytes 442372
  34.5 14.7 %collective-permute-start.26 = (bf16[7,64,256]{2,1,0:T(8,128)(2,1)S(1)}, bf16[7,64,256]{2,1,0:T(8,128)(2,1)S(1)}, u32[]{:S(2)}, u32[]{:S(2)}) collective-permute-start(bf16[7,64,256]{2,1,0:T(8,128)(2,1)S(1)} %get-tuple-element.18), channel_id=1, source_target_pairs={{0,4},{4,8},{8,12},{12,0},{1,5},{5,9},{9,13},{13,1},{2,6},{6,10},{... | collective-permute-start | bytes 688136 | tf_op jit(solution)/shard_map/ppermute | solution.py:244
  37.0 38.9 %copy-start.43 = (bf16[3,3,32,256]{3,2,1,0:T(8,128)(2,1)}, bf16[3,3,32,256]{3,2,1,0:T(8,128)(2,1)S(1)}, u32[]{:S(2)}) copy-start(bf16[3,3,32,256]{3,2,1,0:T(8,128)(2,1)S(1)} %collective-permute-done.19.refs_5_) | copy-start | bytes 442372
  37.0 16.3 %collective-permute-start.21 = (bf16[3,256,128]{2,1,0:T(8,128)(2,1)S(1)}, bf16[3,256,128]{2,1,0:T(8,128)(2,1)S(1)}, u32[]{:S(2)}, u32[]{:S(2)}) collective-permute-start(bf16[3,256,128]{2,1,0:T(8,128)(2,1)S(1)} %copy-done.7), channel_id=1, source_target_pairs={{0,1},{1,0},{2,3},{3,2},{4,5},{5,4},{6,7},{7,6},{8,9},{9,8},{10,11... | collective-permute-start | bytes 589832 | tf_op jit(solution)/shard_map/ppermute | solution.py:259
  37.7 17.1 %collective-permute-start.32 = (bf16[7,64,256]{2,1,0:T(8,128)(2,1)S(1)}, bf16[7,64,256]{2,1,0:T(8,128)(2,1)S(1)}, u32[]{:S(2)}, u32[]{:S(2)}) collective-permute-start(bf16[7,64,256]{2,1,0:T(8,128)(2,1)S(1)} %get-tuple-element.22), channel_id=1, source_target_pairs={{0,4},{4,8},{8,12},{12,0},{1,5},{5,9},{9,13},{13,1},{2,6},{6,10},{... | collective-permute-start | bytes 688136 | tf_op jit(solution)/shard_map/ppermute | solution.py:244
  38.9 24.6 %collective-permute-start.33 = (bf16[7,64,256]{2,1,0:T(8,128)(2,1)S(1)}, bf16[7,64,256]{2,1,0:T(8,128)(2,1)S(1)}, u32[]{:S(2)}, u32[]{:S(2)}) collective-permute-start(bf16[7,64,256]{2,1,0:T(8,128)(2,1)S(1)} %get-tuple-element.22), channel_id=1, source_target_pairs={{0,8},{4,12},{8,0},{12,4},{1,9},{5,13},{9,1},{13,5},{2,10},{6,14},... | collective-permute-start | bytes 688136 | tf_op jit(solution)/shard_map/ppermute | solution.py:244
  49.2 19.1 %collective-permute-start.34 = (bf16[7,64,256]{2,1,0:T(8,128)(2,1)S(1)}, bf16[7,64,256]{2,1,0:T(8,128)(2,1)S(1)}, u32[]{:S(2)}, u32[]{:S(2)}) collective-permute-start(bf16[7,64,256]{2,1,0:T(8,128)(2,1)S(1)} %get-tuple-element.22), channel_id=1, source_target_pairs={{0,12},{4,0},{8,4},{12,8},{1,13},{5,1},{9,5},{13,9},{2,14},{6,2},{... | collective-permute-start | bytes 688136 | tf_op jit(solution)/shard_map/ppermute | solution.py:244
  49.2 26.6 %copy-start.1 = (bf16[3,3,128,256]{3,2,1,0:T(8,128)(2,1)S(1)}, bf16[3,3,128,256]{3,2,1,0:T(8,128)(2,1)}, u32[]{:S(2)}) copy-start(bf16[3,3,128,256]{3,2,1,0:T(8,128)(2,1)} %refs_0_.7) | copy-start | bytes 1769476
  49.2 40.6 %copy-start.3 = (bf16[3,2,128,256]{3,2,1,0:T(8,128)(2,1)S(1)}, bf16[3,2,128,256]{3,2,1,0:T(8,128)(2,1)}, u32[]{:S(2)}) copy-start(bf16[3,2,128,256]{3,2,1,0:T(8,128)(2,1)} %refs_2_.3) | copy-start | bytes 1179652
  49.2 41.1 %copy-start.58 = (s32[768]{0:T(1024)S(1)}, s32[768]{0:T(1024)}, u32[]{:S(2)}) copy-start(s32[768]{0:T(1024)} %param.20) | copy-start | bytes 9220
  49.3 23.1 %collective-permute-start.5 = (bf16[3,4,32,256]{3,2,1,0:T(8,128)(2,1)S(1)}, bf16[3,4,32,256]{3,2,1,0:T(8,128)(2,1)S(1)}, u32[]{:S(2)}, u32[]{:S(2)}) collective-permute-start(bf16[3,4,32,256]{3,2,1,0:T(8,128)(2,1)S(1)} %pad_maximum_fusion.2.refs_2_), channel_id=1, source_target_pairs={{0,2},{2,0},{1,3},{3,1},{4,6},{6,4},{5,7},{7,5},{8,10},{10,8},{9,1... | collective-permute-start | bytes 589832 | tf_op jit(solution)/shard_map/ppermute | solution.py:252
  52.3 38.9 %copy-start.60 = (s32[768]{0:T(1024)S(1)}, s32[768]{0:T(1024)}, u32[]{:S(2)}) copy-start(s32[768]{0:T(1024)} %param.19) | copy-start | bytes 9220
  52.3 39.9 %copy-start.62 = (s32[1,8,8]{2,1,0:T(8,128)S(1)}, s32[1,8,8]{2,1,0:T(8,128)}, u32[]{:S(2)}) copy-start(s32[1,8,8]{2,1,0:T(8,128)} %param.23) | copy-start | bytes 772
  53.2 20.7 %collective-permute-start.6 = (bf16[3,4,32,256]{3,2,1,0:T(8,128)(2,1)S(1)}, bf16[3,4,32,256]{3,2,1,0:T(8,128)(2,1)S(1)}, u32[]{:S(2)}, u32[]{:S(2)}) collective-permute-start(bf16[3,4,32,256]{3,2,1,0:T(8,128)(2,1)S(1)} %pad_maximum_fusion.2.refs_2_), channel_id=1, source_target_pairs={{0,16},{16,0},{1,17},{17,1},{2,18},{18,2},{3,19},{19,3},{4,20},{20... | collective-permute-start | bytes 589832 | tf_op jit(solution)/shard_map/ppermute | solution.py:253
  54.7 19.9 %collective-permute-start.7 = (bf16[3,4,32,256]{3,2,1,0:T(8,128)(2,1)S(1)}, bf16[3,4,32,256]{3,2,1,0:T(8,128)(2,1)S(1)}, u32[]{:S(2)}, u32[]{:S(2)}) collective-permute-start(bf16[3,4,32,256]{3,2,1,0:T(8,128)(2,1)S(1)} %pad_maximum_fusion.2.refs_2_), channel_id=1, source_target_pairs={{0,18},{18,0},{2,16},{16,2},{1,19},{19,1},{3,17},{17,3},{4,22},{22... | collective-permute-start | bytes 589832 | tf_op jit(solution)/shard_map/ppermute | solution.py:254
  63.5 11.6 %collective-permute-start.10 = (bf16[3,4,32,256]{3,2,1,0:T(8,128)(2,1)S(1)}, bf16[3,4,32,256]{3,2,1,0:T(8,128)(2,1)S(1)}, u32[]{:S(2)}, u32[]{:S(2)}) collective-permute-start(bf16[3,4,32,256]{3,2,1,0:T(8,128)(2,1)S(1)} %pad_maximum_fusion.2.refs_2_), channel_id=1, source_target_pairs={{0,1},{1,0},{2,3},{3,2},{4,5},{5,4},{6,7},{7,6},{8,9},{9,8},{10,11... | collective-permute-start | bytes 589832 | tf_op jit(solution)/shard_map/ppermute | solution.py:259
  68.3 19.1 %collective-permute-start.29 = (bf16[3,7,64,256]{3,2,1,0:T(8,128)(2,1)}, bf16[3,7,64,256]{3,2,1,0:T(8,128)(2,1)}, u32[]{:S(2)}, u32[]{:S(2)}) collective-permute-start(bf16[3,7,64,256]{3,2,1,0:T(8,128)(2,1)} %pad_maximum_fusion.refs_4_), channel_id=1, source_target_pairs={{0,2},{2,0},{1,3},{3,1},{4,6},{6,4},{5,7},{7,5},{8,10},{10,8},{9,1... | collective-permute-start | bytes 2064392 | tf_op jit(solution)/shard_map/ppermute | solution.py:247
  72.4 17.4 %collective-permute-start.35 = (bf16[3,7,64,256]{3,2,1,0:T(8,128)(2,1)}, bf16[3,7,64,256]{3,2,1,0:T(8,128)(2,1)}, u32[]{:S(2)}, u32[]{:S(2)}) collective-permute-start(bf16[3,7,64,256]{3,2,1,0:T(8,128)(2,1)} %pad_maximum_fusion.1.refs_4_), channel_id=1, source_target_pairs={{0,16},{16,0},{1,17},{17,1},{2,18},{18,2},{3,19},{19,3},{4,20},{20... | collective-permute-start | bytes 2064392 | tf_op jit(solution)/shard_map/ppermute | solution.py:249
  73.9 1.9 %collective-permute-start.23 = (bf16[3,3,32,256]{3,2,1,0:T(8,128)(2,1)S(1)}, bf16[3,3,32,256]{3,2,1,0:T(8,128)(2,1)S(1)}, u32[]{:S(2)}, u32[]{:S(2)}) collective-permute-start(bf16[3,3,32,256]{3,2,1,0:T(8,128)(2,1)S(1)} %collective-permute-done.17.refs_3_), channel_id=1, source_target_pairs={{0,1},{1,0},{2,3},{3,2},{4,5},{5,4},{6,7},{7,6},{8,9},{9,8},{10,11... | collective-permute-start | bytes 442376 | tf_op jit(solution)/shard_map/ppermute | solution.py:259
  74.6 2.4 %collective-permute-start.24 = (bf16[3,3,32,256]{3,2,1,0:T(8,128)(2,1)S(1)}, bf16[3,3,32,256]{3,2,1,0:T(8,128)(2,1)S(1)}, u32[]{:S(2)}, u32[]{:S(2)}) collective-permute-start(bf16[3,3,32,256]{3,2,1,0:T(8,128)(2,1)S(1)} %collective-permute-done.18.refs_4_), channel_id=1, source_target_pairs={{0,1},{1,0},{2,3},{3,2},{4,5},{5,4},{6,7},{7,6},{8,9},{9,8},{10,11... | collective-permute-start | bytes 442376 | tf_op jit(solution)/shard_map/ppermute | solution.py:259
  75.8 14.0 %collective-permute-start.8 = (bf16[3,3,128,256]{3,2,1,0:T(8,128)(2,1)S(1)}, bf16[3,3,128,256]{3,2,1,0:T(8,128)(2,1)S(1)}, u32[]{:S(2)}, u32[]{:S(2)}) collective-permute-start(bf16[3,3,128,256]{3,2,1,0:T(8,128)(2,1)S(1)} %copy-done.1), channel_id=1, source_target_pairs={{0,1},{1,0},{2,3},{3,2},{4,5},{5,4},{6,7},{7,6},{8,9},{9,8},{10,11... | collective-permute-start | bytes 1769480 | tf_op jit(solution)/shard_map/ppermute | solution.py:259
  76.5 1.9 %collective-permute-start.25 = (bf16[3,3,32,256]{3,2,1,0:T(8,128)(2,1)S(1)}, bf16[3,3,32,256]{3,2,1,0:T(8,128)(2,1)S(1)}, u32[]{:S(2)}, u32[]{:S(2)}) collective-permute-start(bf16[3,3,32,256]{3,2,1,0:T(8,128)(2,1)S(1)} %collective-permute-done.19.refs_5_), channel_id=1, source_target_pairs={{0,1},{1,0},{2,3},{3,2},{4,5},{5,4},{6,7},{7,6},{8,9},{9,8},{10,11... | collective-permute-start | bytes 442376 | tf_op jit(solution)/shard_map/ppermute | solution.py:259
  77.6 2.5 %collective-permute-start.11 = (bf16[3,4,32,256]{3,2,1,0:T(8,128)(2,1)S(1)}, bf16[3,4,32,256]{3,2,1,0:T(8,128)(2,1)S(1)}, u32[]{:S(2)}, u32[]{:S(2)}) collective-permute-start(bf16[3,4,32,256]{3,2,1,0:T(8,128)(2,1)S(1)} %collective-permute-done.5.refs_3_), channel_id=1, source_target_pairs={{0,1},{1,0},{2,3},{3,2},{4,5},{5,4},{6,7},{7,6},{8,9},{9,8},{10,11... | collective-permute-start | bytes 589832 | tf_op jit(solution)/shard_map/ppermute | solution.py:259
  79.0 2.6 %collective-permute-start.12 = (bf16[3,4,32,256]{3,2,1,0:T(8,128)(2,1)S(1)}, bf16[3,4,32,256]{3,2,1,0:T(8,128)(2,1)S(1)}, u32[]{:S(2)}, u32[]{:S(2)}) collective-permute-start(bf16[3,4,32,256]{3,2,1,0:T(8,128)(2,1)S(1)} %collective-permute-done.6.refs_4_), channel_id=1, source_target_pairs={{0,1},{1,0},{2,3},{3,2},{4,5},{5,4},{6,7},{7,6},{8,9},{9,8},{10,11... | collective-permute-start | bytes 589832 | tf_op jit(solution)/shard_map/ppermute | solution.py:259
  80.9 6.5 %collective-permute-start.13 = (bf16[3,4,32,256]{3,2,1,0:T(8,128)(2,1)S(1)}, bf16[3,4,32,256]{3,2,1,0:T(8,128)(2,1)S(1)}, u32[]{:S(2)}, u32[]{:S(2)}) collective-permute-start(bf16[3,4,32,256]{3,2,1,0:T(8,128)(2,1)S(1)} %collective-permute-done.7.refs_5_), channel_id=1, source_target_pairs={{0,1},{1,0},{2,3},{3,2},{4,5},{5,4},{6,7},{7,6},{8,9},{9,8},{10,11... | collective-permute-start | bytes 589832 | tf_op jit(solution)/shard_map/ppermute | solution.py:259
  82.2 33.1 %collective-permute-start.30 = (bf16[3,7,64,256]{3,2,1,0:T(8,128)(2,1)}, bf16[3,7,64,256]{3,2,1,0:T(8,128)(2,1)}, u32[]{:S(2)}, u32[]{:S(2)}) collective-permute-start(bf16[3,7,64,256]{3,2,1,0:T(8,128)(2,1)} %pad_maximum_fusion.refs_4_), channel_id=1, source_target_pairs={{0,1},{1,0},{2,3},{3,2},{4,5},{5,4},{6,7},{7,6},{8,9},{9,8},{10,11... | collective-permute-start | bytes 2064392 | tf_op jit(solution)/shard_map/ppermute | solution.py:259
  87.4 28.0 %collective-permute-start.31 = (bf16[3,7,64,256]{3,2,1,0:T(8,128)(2,1)}, bf16[3,7,64,256]{3,2,1,0:T(8,128)(2,1)}, u32[]{:S(2)}, u32[]{:S(2)}) collective-permute-start(bf16[3,7,64,256]{3,2,1,0:T(8,128)(2,1)} %collective-permute-done.29.refs_5_), channel_id=1, source_target_pairs={{0,1},{1,0},{2,3},{3,2},{4,5},{5,4},{6,7},{7,6},{8,9},{9,8},{10,11... | collective-permute-start | bytes 2064392 | tf_op jit(solution)/shard_map/ppermute | solution.py:259
  88.1 41.9 %collective-permute-start.36 = (bf16[3,7,64,256]{3,2,1,0:T(8,128)(2,1)}, bf16[3,7,64,256]{3,2,1,0:T(8,128)(2,1)}, u32[]{:S(2)}, u32[]{:S(2)}) collective-permute-start(bf16[3,7,64,256]{3,2,1,0:T(8,128)(2,1)} %pad_maximum_fusion.1.refs_4_), channel_id=1, source_target_pairs={{0,1},{1,0},{2,3},{3,2},{4,5},{5,4},{6,7},{7,6},{8,9},{9,8},{10,11... | collective-permute-start | bytes 2064392 | tf_op jit(solution)/shard_map/ppermute | solution.py:259
  89.8 40.2 %collective-permute-start.37 = (bf16[3,7,64,256]{3,2,1,0:T(8,128)(2,1)}, bf16[3,7,64,256]{3,2,1,0:T(8,128)(2,1)}, u32[]{:S(2)}, u32[]{:S(2)}) collective-permute-start(bf16[3,7,64,256]{3,2,1,0:T(8,128)(2,1)} %collective-permute-done.35.refs_5_), channel_id=1, source_target_pairs={{0,1},{1,0},{2,3},{3,2},{4,5},{5,4},{6,7},{7,6},{8,9},{9,8},{10,11... | collective-permute-start | bytes 2064392 | tf_op jit(solution)/shard_map/ppermute | solution.py:259
  89.8 11.4 %collective-permute-start.20 = (bf16[3,2,128,256]{3,2,1,0:T(8,128)(2,1)S(1)}, bf16[3,2,128,256]{3,2,1,0:T(8,128)(2,1)S(1)}, u32[]{:S(2)}, u32[]{:S(2)}) collective-permute-start(bf16[3,2,128,256]{3,2,1,0:T(8,128)(2,1)S(1)} %copy-done.3), channel_id=1, source_target_pairs={{0,1},{1,0},{2,3},{3,2},{4,5},{5,4},{6,7},{7,6},{8,9},{9,8},{10,11... | collective-permute-start | bytes 1179656 | tf_op jit(solution)/shard_map/ppermute | solution.py:259
  96.9 4.3 %copy-start.18 = (s32[64,1]{1,0:T(8,128)}, s32[64,1]{1,0:T(8,128)S(1)}, u32[]{:S(2)}) copy-start(s32[64,1]{1,0:T(8,128)S(1)} %reshape.20.lists) | copy-start | bytes 772
  96.9 1.4 copy-start.34
  96.9 1.4 copy-start.36
  96.9 1.5 %copy-start.38 = (bf16[3,4,32,256]{3,2,1,0:T(8,128)(2,1)S(1)}, bf16[3,4,32,256]{3,2,1,0:T(8,128)(2,1)}, u32[]{:S(2)}) copy-start(bf16[3,4,32,256]{3,2,1,0:T(8,128)(2,1)} %copy-done.37) | copy-start | bytes 589828
  98.4 2.8 %copy-start.17 = (bf16[3,3,32,256]{3,2,1,0:T(8,128)(2,1)S(1)}, bf16[3,3,32,256]{3,2,1,0:T(8,128)(2,1)}, u32[]{:S(2)}) copy-start(bf16[3,3,32,256]{3,2,1,0:T(8,128)(2,1)} %copy-done.16) | copy-start | bytes 442372
  98.4 2.8 %copy-start.40 = (bf16[3,3,32,256]{3,2,1,0:T(8,128)(2,1)S(1)}, bf16[3,3,32,256]{3,2,1,0:T(8,128)(2,1)}, u32[]{:S(2)}) copy-start(bf16[3,3,32,256]{3,2,1,0:T(8,128)(2,1)} %copy-done.39) | copy-start | bytes 442372
  98.4 2.8 %copy-start.42 = (bf16[3,3,32,256]{3,2,1,0:T(8,128)(2,1)S(1)}, bf16[3,3,32,256]{3,2,1,0:T(8,128)(2,1)}, u32[]{:S(2)}) copy-start(bf16[3,3,32,256]{3,2,1,0:T(8,128)(2,1)} %copy-done.41) | copy-start | bytes 442372
  98.4 2.8 %copy-start.44 = (bf16[3,3,32,256]{3,2,1,0:T(8,128)(2,1)S(1)}, bf16[3,3,32,256]{3,2,1,0:T(8,128)(2,1)}, u32[]{:S(2)}) copy-start(bf16[3,3,32,256]{3,2,1,0:T(8,128)(2,1)} %copy-done.43) | copy-start | bytes 442372
  98.4 2.9 %copy-start.46 = (bf16[3,3,32,256]{3,2,1,0:T(8,128)(2,1)S(1)}, bf16[3,3,32,256]{3,2,1,0:T(8,128)(2,1)}, u32[]{:S(2)}) copy-start(bf16[3,3,32,256]{3,2,1,0:T(8,128)(2,1)} %copy-done.45) | copy-start | bytes 442372
  98.4 2.9 %copy-start.48 = (bf16[3,3,32,256]{3,2,1,0:T(8,128)(2,1)S(1)}, bf16[3,3,32,256]{3,2,1,0:T(8,128)(2,1)}, u32[]{:S(2)}) copy-start(bf16[3,3,32,256]{3,2,1,0:T(8,128)(2,1)} %copy-done.47) | copy-start | bytes 442372
  98.5 2.9 %copy-start.50 = (bf16[3,3,32,256]{3,2,1,0:T(8,128)(2,1)S(1)}, bf16[3,3,32,256]{3,2,1,0:T(8,128)(2,1)}, u32[]{:S(2)}) copy-start(bf16[3,3,32,256]{3,2,1,0:T(8,128)(2,1)} %copy-done.49) | copy-start | bytes 442372
  98.5 2.9 %copy-start.52 = (bf16[3,3,32,256]{3,2,1,0:T(8,128)(2,1)S(1)}, bf16[3,3,32,256]{3,2,1,0:T(8,128)(2,1)}, u32[]{:S(2)}) copy-start(bf16[3,3,32,256]{3,2,1,0:T(8,128)(2,1)} %copy-done.51) | copy-start | bytes 442372
  101.2 7.1 %copy-start.59 = (s32[768]{0:T(1024)S(1)}, s32[768]{0:T(1024)}, u32[]{:S(2)}) copy-start(s32[768]{0:T(1024)} %param.25) | copy-start | bytes 9220
  101.2 7.3 %copy-start.61 = (s32[768]{0:T(1024)S(1)}, s32[768]{0:T(1024)}, u32[]{:S(2)}) copy-start(s32[768]{0:T(1024)} %param.24) | copy-start | bytes 9220
  103.9 11.4 %all-to-all-start = ((bf16[8,8,512]{2,1,0:T(8,128)(2,1)}), bf16[8,8,512]{2,1,0:T(8,128)(2,1)}, u32[]{:S(2)}, u32[]{:S(2)}) async-start(bf16[8,8,512]{2,1,0:T(8,128)(2,1)} %bitcast.7), calls=%async_computation | async-start | bytes 131072 | tf_op jit(solution)/shard_map/all_to_all | solution.py:368
  126.0 10.9 %all-to-all-start.1 = ((bf16[8,8,512]{2,1,0:T(8,128)(2,1)}), bf16[8,8,512]{2,1,0:T(8,128)(2,1)}, u32[]{:S(2)}, u32[]{:S(2)}) async-start(bf16[8,8,512]{2,1,0:T(8,128)(2,1)} %bitcast.18), calls=%async_computation.1 | async-start | bytes 131072 | tf_op jit(solution)/shard_map/all_to_all | solution.py:368
  (39 other events, 34.0 us)

commit v2 on v0

v2 whole, which is shorter than its diff:
```python
import functools

import jax
import jax.numpy as jnp
from jax import lax
from jax.experimental import pallas as pl
from jax.experimental.pallas import tpu as pltpu
from jax.sharding import PartitionSpec as P

BF = jnp.bfloat16
F32 = jnp.float32
ROWS = 256
SWAP = [(0, 1), (1, 0)]
DIAGONAL = [(0, 3), (3, 0), (1, 2), (2, 1)]
LIMIT = 28 * 2**20


def dot(a, b):
    return jnp.dot(a, b, preferred_element_type=F32)


def silu(v):
    return v / (1.0 + jnp.exp(-v))


def normalize(total):
    mean = jnp.mean(total, axis=1, keepdims=True)
    meansq = jnp.mean(total * total, axis=1, keepdims=True)
    return (total - mean) * lax.rsqrt(meansq - mean * mean + 1e-05)


def columns_of(ids):
    return jnp.broadcast_to(ids, (128, ids.shape[1])).T


def one_hot(ids, count):
    spread_ids = columns_of(ids)
    pieces = []
    for at in range(0, count, 128):
        width = min(128, count - at)
        spots = lax.broadcasted_iota(jnp.int32, (ids.shape[1], width), 1) + at
        pieces.append(jnp.where(spots == spread_ids[:, :width], 1.0, 0.0).astype(BF))
    return jnp.concatenate(pieces, axis=1) if len(pieces) > 1 else pieces[0]


def one_hot_rows(ids, count):
    spots = lax.broadcasted_iota(jnp.int32, (count, ids.shape[1]), 0)
    return jnp.where(spots == ids, 1.0, 0.0).astype(BF)


def call(body, outs, scratch, fast, slow=(), cost=0.5, far=0, keep=True):
    many = isinstance(outs, list)
    full = [(o if isinstance(o[1], tuple) or not isinstance(o[0], int) else (o, BF)) for o in (outs if many else [outs])]
    places = [pltpu.VMEM] * (len(full) - far) + [pltpu.HBM] * far
    shapes = [(place if keep else jax.ShapeDtypeStruct)(shape, dtype) for place, (shape, dtype) in zip(places, full)]
    operands = [pltpu.with_memory_space_constraint(a, pltpu.VMEM) for a in fast]
    operands += [pltpu.with_memory_space_constraint(a, pltpu.HBM) for a in slow]
    specs = [pl.BlockSpec(memory_space=pltpu.VMEM)] * len(fast) + [pl.BlockSpec(memory_space=pltpu.HBM)] * len(slow)
    return pl.pallas_call(
        body,
        out_shape=shapes if many else shapes[0],
        in_specs=specs,
        out_specs=[pl.BlockSpec(memory_space=place) for place in places] if many else pl.BlockSpec(memory_space=places[0]),
        scratch_shapes=scratch,
        compiler_params=pltpu.CompilerParams(vmem_limit_bytes=LIMIT),
        cost_estimate=pl.CostEstimate(flops=int(cost * 1e9), bytes_accessed=0, transcendentals=0),
    )(*operands)


def after(array, *others):
    return lax.optimization_barrier((array,) + others)[0]


MATS = {"e": 3, "n": 2}


def arrays_in(kind):
    return sum(MATS[letter] + 1 for letter in kind)


def weight_shapes(kind, hidden, depth):
    found = []
    for letter in kind:
        found += [(MATS[letter] * depth, hidden), (hidden, depth)]
    return found


def named(kind, refs):
    return dict(zip([letter + name for letter in kind for name in "mb"], refs))


def cut_body(plan, *refs):
    raws = (refs[0], refs[1]), (refs[2], refs[3])
    outs, sem = refs[4:-1], refs[-1]
    part = {"quarter": 2 * lax.axis_index("groups") + lax.axis_index("band"), "whole": 0}
    copies = []
    for (blocks, split, rows), out in zip(plan, outs):
        spot = 0
        for block in blocks:
            for mats, back in raws:
                lanes, count = back.shape[2], mats.shape[1]
                first = pl.ds(pl.multiple_of(part[split] * rows, rows), rows)
                copies.append((mats.at[block, :, first, :], out.at[spot : spot + count]))
                spot += count
                for j in range(2):
                    at = pl.ds(pl.multiple_of(part[split] * 2 * rows + j * rows, rows), rows)
                    copies.append((back.at[block, at, :], out.at[spot, :, j * lanes : (j + 1) * lanes]))
                spot += 1
    started = [pltpu.make_async_copy(src, dst, sem.at[i]) for i, (src, dst) in enumerate(copies)]
    for copy in started:
        copy.start()
    for copy in started:
        copy.wait()


def cut(plan, raws):
    shapes = [(arrays_in("en") * len(blocks), rows, raws[0].shape[3]) for blocks, _, rows in plan]
    copies = sum(6 * len(blocks) for blocks, _, _ in plan)
    return call(functools.partial(cut_body, plan), shapes, [pltpu.SemaphoreType.DMA((copies,))], [], raws)


def put(src, zs, part, half, kind, weights):
    def piece(k, spot):
        return src.at[spot] if len(src.shape) == 3 else src.at[k, spot]

    rows, cols = src.shape[-2:]
    lanes = cols // 2
    spot = 0
    for letter in "en":
        if letter in kind:
            mats, back = weights[letter + "m"], weights[letter + "b"]
            depth = back.shape[1]
            for k, z in enumerate(zs):
                for m in range(MATS[letter]):
                    at = pl.multiple_of(m * depth + z * lanes + part * rows, rows)
                    mats[pl.ds(at, rows), half * cols : (half + 1) * cols] = piece(k, spot + m)[...]
                for j in range(2):
                    at = pl.multiple_of(half * cols + part * 2 * rows + j * rows, rows)
                    into = pl.ds(pl.multiple_of(z * lanes, lanes), lanes)
                    back[pl.ds(at, rows), into] = piece(k, spot + MATS[letter])[:, j * lanes : (j + 1) * lanes]
        spot += MATS[letter] + 1


class Parts:
    def __init__(self, kind, sides, far):
        self.kind, self.sides, self.far = kind, len(sides), far
        self.operands = [array for side in sides for array in side]

    def scratch(self, hidden, depth):
        found = [pltpu.VMEM(shape, BF) for shape in weight_shapes(self.kind, hidden, depth)]
        if self.far:
            found += [pltpu.VMEM(array.shape, BF) for array in self.operands]
            found += [pltpu.SemaphoreType.DMA((len(self.operands),))]
        return found

    def start(self, operands, scratch):
        if not self.far:
            return []
        *places, sems = scratch[2 * len(self.kind) :]
        copies = [pltpu.make_async_copy(src, dst, sems.at[i]) for i, (src, dst) in enumerate(zip(operands, places))]
        for copy in copies:
            copy.start()
        return copies

    def finish(self, operands, scratch, copies):
        weights = named(self.kind, scratch)
        if self.far:
            operands = scratch[2 * len(self.kind) : -1]
        count = lax.axis_size("mesh")
        z = lax.axis_index("mesh")
        x, y = lax.axis_index("band"), lax.axis_index("groups")
        quarters = [2 * y + x, 2 * y + 1 - x, 2 * (1 - y) + x, 2 * (1 - y) + 1 - x]
        each = len(operands) // self.sides
        for half in range(self.sides):
            for copy in copies[half * each : (half + 1) * each]:
                copy.wait()
            own, *arrays = operands[half * each : (half + 1) * each]
            put(own, [z], 0, half, self.kind, weights)
            for part, src in zip(quarters, arrays):
                put(src, [z ^ k for k in range(1, count)], part, half, self.kind, weights)
        return weights


class Whole:
    far = False

    def __init__(self, kind, arrays):
        self.kind, self.operands = kind, arrays

    def scratch(self, hidden, depth):
        return []

    def start(self, operands, scratch):
        return []

    def finish(self, operands, scratch, copies):
        return named(self.kind, operands)


def join_body(*refs):
    blocks = [ref for ref in refs if len(ref.shape) == 4]
    for k, ref in enumerate(refs[: -len(blocks)]):
        for i, block in enumerate(blocks):
            block[k] = ref[i * block.shape[1] : (i + 1) * block.shape[1]]


def join(arrays, blocks):
    count, rows, cols = arrays[0].shape
    return call(join_body, [(len(arrays), count // blocks, rows, cols)] * blocks, [], arrays)


def lend_body(grid, down, up, low, high):
    low[...] = dot(one_hot(down[...], grid.shape[0]), grid[...]).astype(BF)
    high[...] = dot(one_hot(up[...], grid.shape[0]), grid[...]).astype(BF)


def gather_body(grid, low, high, nodes, slots, targets, out):
    table = jnp.concatenate([grid[...], low[...], high[...]], axis=0)
    depth = grid.shape[1]
    for at in range(0, out.shape[0], ROWS):
        rows = slice(at, at + ROWS)
        out[rows, 0:depth] = dot(one_hot(slots[:, rows], table.shape[0]), table).astype(BF)
        out[rows, depth:] = dot(one_hot(targets[:, rows], nodes.shape[0]), nodes[...]).astype(BF)


def edge_tail(weights, pre):
    return normalize(dot(silu(pre).astype(BF), weights["eb"][...]))


def node_pre(weights, nodes, incoming):
    depth = nodes.shape[1]
    return dot(nodes, weights["nm"][0:depth, :]) + dot(incoming, weights["nm"][depth:, :])


def node_tail(weights, nodes, incoming):
    pre = node_pre(weights, nodes, incoming)
    return (nodes.astype(F32) + normalize(dot(silu(pre).astype(BF), weights["nb"][...]))).astype(BF)


def sum_of(terms, rows=slice(None)):
    total = terms[0][rows, :].astype(F32)
    for term in terms[1:]:
        total = total + term[rows, :].astype(F32)
    return total


def first_edges_body(pack, gathered, *refs):
    count = len(pack.operands)
    edges, out, buffer, sem, scratch = refs[count], refs[count + 1], refs[count + 2], refs[count + 3], refs[count + 4 :]
    fetch = pltpu.make_async_copy(edges, buffer, sem)
    fetch.start()
    weights = pack.finish(refs[:count], scratch, [])
    for at in range(0, edges.shape[0], ROWS):
        rows = slice(at, at + ROWS)
        both = gathered.shape[1]
        pre = dot(gathered[rows, :], weights["em"][0:both, :])
        if at == 0:
            fetch.wait()
        pre = pre + dot(buffer[rows, :], weights["em"][both:, :])
        out[rows, :] = dot(silu(pre).astype(BF), weights["eb"][...]).astype(BF)


def first_sums_body(targets, *refs):
    terms, out, message = refs[:-2], refs[-2], refs[-1]
    for at in range(0, message.shape[0], ROWS):
        rows = slice(at, at + ROWS)
        message[rows, :] = normalize(sum_of(terms, rows)).astype(BF)
    out[...] = dot(one_hot_rows(targets[...], out.shape[0]), message[...]).astype(BF)


def first_nodes_body(pack, nodes, incoming, *refs):
    count = len(pack.operands)
    out, scratch = refs[count], refs[count + 1 :]
    weights = pack.finish(refs[:count], scratch, [])
    pre = node_pre(weights, nodes[...], incoming[...])
    out[...] = dot(silu(pre).astype(BF), weights["nb"][...]).astype(BF)


def first_next_body(nodes, lists, *refs):
    terms, packed, out, buffer, sem = refs[:-4], refs[-4], refs[-3], refs[-2], refs[-1]
    buffer[...] = (nodes[...].astype(F32) + normalize(sum_of(terms))).astype(BF)
    save = pltpu.make_async_copy(buffer, out, sem)
    save.start()
    packed[...] = dot(one_hot(lists[...], nodes.shape[0]), buffer[...]).astype(BF)
    save.wait()


def block_body(pack, last, sent, slots, targets, lists, *refs):
    count = len(pack.operands)
    refs, operands = refs[count:], refs[:count]
    if pack.far:
        nodes, edges, operands, refs = operands[0], operands[1], operands[2:] + refs[:2], refs[2:]
    else:
        nodes, edges, refs = refs[0], refs[1], refs[2:]
    if last:
        (out, *refs) = refs
    else:
        (packed, saved, edges_saved, *refs) = refs
    message, sent_table, node_table, node_buffer, edge_buffer, sems, *scratch = refs
    get_nodes = pltpu.make_async_copy(nodes, node_buffer, sems.at[0])
    get_edges = pltpu.make_async_copy(edges, edge_buffer, sems.at[1])
    get_nodes.start()
    get_edges.start()
    weights = pack.finish(operands, scratch, pack.start(operands, scratch))
    em, depth = weights["em"], sent.shape[1]
    sent_table[...] = dot(sent[...], em[0:depth, :]).astype(BF)
    get_nodes.wait()
    node_table[...] = dot(node_buffer[...], em[depth : 2 * depth, :]).astype(BF)
    get_edges.wait()
    for at in range(0, message.shape[0], ROWS):
        rows = slice(at, at + ROWS)
        pre = dot(edge_buffer[rows, :], em[2 * depth :, :])
        pre = pre + dot(one_hot(targets[:, rows], nodes.shape[0]), node_table[...])
        pre = pre + dot(one_hot(slots[:, rows], sent.shape[0]), sent_table[...])
        normed = edge_tail(weights, pre)
        message[rows, :] = normed.astype(BF)
        if not last:
            edge_buffer[rows, :] = (edge_buffer[rows, :].astype(F32) + normed).astype(BF)
    if not last:
        save_edges = pltpu.make_async_copy(edge_buffer, edges_saved, sems.at[2])
        save_edges.start()
    incoming = dot(one_hot_rows(targets[...], nodes.shape[0]), message[...]).astype(BF)
    new = node_tail(weights, node_buffer[...], incoming)
    if last:
        out[...] = new
        return
    node_buffer[...] = new
    save_nodes = pltpu.make_async_copy(node_buffer, saved, sems.at[3])
    save_nodes.start()
    packed[...] = dot(one_hot(lists[...], nodes.shape[0]), new).astype(BF)
    save_edges.wait()
    save_nodes.wait()


def over_slices(chunk):
    count = lax.axis_size("mesh")
    return [lax.ppermute(chunk, "mesh", [(i, i ^ k) for i in range(count)]) for k in range(1, count)]


def over_plane(own):
    return [
        lax.ppermute(own, "band", SWAP),
        lax.ppermute(own, "groups", SWAP),
        lax.ppermute(own, ("groups", "band"), DIAGONAL),
    ]


def swap_width(array):
    return lax.ppermute(array, "width", SWAP)


def weights_whole(edge_mats, node_mats, edge_back, node_back):
    def joined(array, rows, cols):
        axis = {rows: array.ndim - 2, cols: array.ndim - 1}
        for name in ("mesh", "width"):
            array = lax.all_gather(array, name, axis=axis[name], tiled=True)
        return array

    em, nm = joined(edge_mats, "mesh", "width"), joined(node_mats, "mesh", "width")
    eb, nb = joined(edge_back, "width", "mesh"), joined(node_back, "width", "mesh")
    em = em.reshape(em.shape[0], -1, em.shape[3])
    nm = nm.reshape(nm.shape[0], -1, nm.shape[3])
    found = []
    cols = edge_mats.shape[3]
    at = lax.axis_index("width") * cols
    for kind, mats, back in (("e", em[0], eb[0]), ("n", nm[0], nb[0])):
        mine = [lax.dynamic_slice_in_dim(mats, at, cols, 1), lax.dynamic_slice_in_dim(back, at, cols, 0)]
        found.append(Whole(kind, mine))
    for block in range(1, em.shape[0]):
        found.append(Whole("en", [em[block], eb[block], nm[block], nb[block]]))
    return found


def on_device(
    grid_latent,
    mesh_latent,
    grid_edge,
    mesh_edge,
    encoder_slot,
    encoder_target,
    halo_down,
    halo_up,
    send_lists,
    mesh_slot,
    mesh_target,
    edge_mats,
    node_mats,
    edge_back,
    node_back,
):
    depth = grid_latent.shape[1]
    nodes = mesh_latent.shape[0]
    grid_edges, mesh_edges = grid_edge.shape[0], mesh_edge.shape[0]
    sizes = [lax.axis_size(name) for name in ("groups", "mesh", "band", "width")]
    by_parts = sizes == [2, 4, 2, 2] and edge_mats.shape[0] == 3
    halo = halo_down.shape[0]
    line = sizes[1] * sizes[2]
    sent_rows = send_lists.shape[1] * send_lists.shape[2]
    hidden = edge_mats.shape[3] * sizes[3]
    lists = send_lists.reshape(1, -1)
    node_buffer, edge_buffer = pltpu.VMEM((nodes, depth), BF), pltpu.VMEM((mesh_edges, depth), BF)

    lent_down, lent_up = call(
        lend_body, [(halo, depth), (halo, depth)], [], [grid_latent, halo_down[None, :], halo_up[None, :]]
    )
    if by_parts:
        raws = [edge_mats, edge_back, node_mats, node_back]
        slab = edge_mats.shape[2]
        quarter = slab // 4
        [cut0] = cut([((0,), "quarter", quarter)], raws)
        cut12, own0, own1, own2 = cut([((1, 2), "quarter", quarter)] + [((block,), "whole", slab) for block in range(3)], raws)
        turned0 = over_slices(cut0)
        lent_down, lent_up = after(lent_down, turned0[0]), after(lent_up, turned0[0])
    from_upper = lax.ppermute(lent_down, ("mesh", "band"), [(i + 1, i) for i in range(line - 1)])
    from_lower = lax.ppermute(lent_up, ("mesh", "band"), [(i, i + 1) for i in range(line - 1)])
    if by_parts:
        [joined0] = join(turned0[:-1] + [after(turned0[-1], from_upper, from_lower, cut12)], 1)
        plane0 = over_plane(joined0)
        side0 = [own0, joined0] + plane0
        packs = [Parts("e", [side0], False), Parts("n", [side0], False), None, None]
        joined1, joined2 = join(over_slices(after(cut12, joined0)), 2)
        from_lower = after(from_lower, joined1)
    else:
        packs = weights_whole(edge_mats, node_mats, edge_back, node_back)
    gathered = call(
        gather_body,
        (grid_edges, 2 * depth),
        [],
        [grid_latent, from_lower, from_upper, mesh_latent, encoder_slot[None, :], encoder_target[None, :]],
        cost=1.2,
    )
    pack = packs[0]
    term = call(
        functools.partial(first_edges_body, pack),
        (grid_edges, depth),
        [pltpu.VMEM((grid_edges, depth), BF), pltpu.SemaphoreType.DMA(())] + pack.scratch(hidden // 2, depth),
        [gathered] + pack.operands,
        [grid_edge],
        cost=3.0,
    )
    if by_parts:
        plane1 = over_plane(after(joined1, term))
    incoming = call(
        first_sums_body,
        (nodes, depth),
        [pltpu.VMEM((grid_edges, depth), BF)],
        [encoder_target[None, :], term, swap_width(term)],
        cost=0.8,
    )
    pack = packs[1]
    term = call(
        functools.partial(first_nodes_body, pack),
        (nodes, depth),
        pack.scratch(hidden // 2, depth),
        [mesh_latent, incoming] + pack.operands,
        cost=0.8,
    )
    packed, rows = call(
        first_next_body,
        [(sent_rows, depth), (nodes, depth)],
        [node_buffer, pltpu.SemaphoreType.DMA(())],
        [mesh_latent, lists, term, swap_width(term)],
        cost=1.6,
        far=1,
    )
    edges = mesh_edge
    slots, targets = mesh_slot[None, :], mesh_target[None, :]
    early = incoming
    for block in range(1, edge_mats.shape[0]):
        last = block == edge_mats.shape[0] - 1
        pack = packs[block + 1]
        cut_rows = packed.reshape(send_lists.shape[1:] + (depth,))
        sent = lax.all_to_all(cut_rows, ("mesh", "band"), split_axis=0, concat_axis=0, tiled=True).reshape(-1, depth)
        if by_parts:
            if not last:
                plane2 = over_plane(after(joined2, sent, *plane1))
                side = [own1, joined1] + plane1
            else:
                side = [own2, joined2] + plane2
            other = [swap_width(after(a, early)) for a in side[:2]] + [swap_width(after(a, sent)) for a in side[2:]]
            pack = Parts("en", [side, other], True)
            early = sent
        near = [sent, slots, targets, lists]
        got = call(
            functools.partial(block_body, pack, last),
            (nodes, depth) if last else [(sent_rows, depth), (nodes, depth), (mesh_edges, depth)],
            [edge_buffer, pltpu.VMEM((sent_rows, hidden), BF), pltpu.VMEM((nodes, hidden), BF), node_buffer, edge_buffer]
            + [pltpu.SemaphoreType.DMA((4,))]
            + pack.scratch(hidden, depth),
            near if pack.far else near + pack.operands,
            [rows, edges] + (pack.operands if pack.far else []),
            cost=6.5,
            far=0 if last else 2,
            keep=not last,
        )
        if last:
            rows = got
        else:
            packed, rows, edges = got
    return rows


def solution(mesh):
    return jax.shard_map(
        on_device,
        mesh=mesh,
        in_specs=(
            P(("groups", "mesh", "band"), None),
            P(("groups", "mesh", "band"), None),
            P(("groups", "mesh", "band"), None),
            P(("groups", "mesh", "band"), None),
            P(("groups", "mesh", "band")),
            P(("groups", "mesh", "band")),
            P(("groups", "mesh", "band")),
            P(("groups", "mesh", "band")),
            P(("groups", "mesh", "band"), None, None),
            P(("groups", "mesh", "band")),
            P(("groups", "mesh", "band")),
            P(None, None, "mesh", "width"),
            P(None, None, "mesh", "width"),
            P(None, "width", "mesh"),
            P(None, "width", "mesh"),
        ),
        out_specs=P(("groups", "mesh", "band"), None),
        check_vma=False,
    )
```

time: 292 us -> 103 us (0.35)
  blocking collectives: 179 us -> 0 us
  starting transfers between devices: 13.8 us -> 47.5 us
  Pallas kernels: 0 us -> 25.4 us
  local copies, waits for them, and re-layouts: 24.8 us -> 1.68 us
  matrix products: 17.3 us -> 0 us
  other arithmetic: 16.5 us -> 0 us
  between operations: 14 us -> 0.57 us
    all_gather x12 -> x0, blocking collectives: 179 us -> none  [the longest x3 52.7 us: on_device(): lax.all_gather(edge_mats[block_id], 'mesh', axis=1, tiled=True)]
    ppermute x2 -> x29, starting transfers between devices: 6.73 us -> 35.1 us  [the longest x6 11 us: over_slices(): lax.ppermute(chunk, 'mesh', [(i, i ^ k) for i in range(count)])]
    pallas_call x0 -> x12, Pallas kernels: none -> 25.4 us  [call(): pl.pallas_call(body, out_shape=shapes if many else shapes[0], in_specs=sp...]
    gather x10 -> x0, local copies, waits for them, and re-layouts: 19.5 us -> none  [the longest x3 7.97 us: edge_update(): send_table[send_slot].astype(jnp.float32)]
    dot_general x18 -> x0, matrix products: 17.3 us -> none  [the longest x3 9 us: edge_update(): jnp.dot(edge_hidden, edge_back, preferred_element_type=jnp.float32)]
    psum x6 -> x0, waiting for transfers between devices: 16.1 us -> none  [finish(): lax.psum(partial_value.astype(jnp.bfloat16), 'width').astype(jnp.float32)]
    ppermute x2 -> x29, waiting for transfers between devices: 0.01 us -> 14.2 us  [the longest x6 6.17 us: over_slices(): lax.ppermute(chunk, 'mesh', [(i, i ^ k) for i in range(count)])]
    reduce_sum x6 -> x0, other arithmetic: 8.01 us -> none  [normalize(): row_mean = jnp.mean(total, axis=1, keepdims=True)]
  transfers between devices with their start and end apart: 10 -> 31, of which waited for: 3 -> 13; matrix products, arithmetic and copies ran while one was open for 5% -> 0% of each run, Pallas kernels for 0% -> 13%
where the time goes in v2:
time: 103 us; the launch traced here: 102 us
  starting transfers between devices  47.5 us (46%)
  waiting for transfers between devices  27 us (26%)
  Pallas kernels  25.4 us (25%)
  local copies, waits for them, and re-layouts  1.68 us (2%)
    pallas_call x12, Pallas kernels, call(): pl.pallas_call(body, out_shape=shapes if many else shapes[0], in_specs=sp...  25.4 us
    all_to_all x2, waiting for transfers between devices, on_device(): lax.all_to_all(cut_rows, ('mesh', 'band'), split_axis=0, concat_axis=0, t...  12.8 us
    all_to_all x2, starting transfers between devices, on_device(): lax.all_to_all(cut_rows, ('mesh', 'band'), split_axis=0, concat_axis=0, t...  12.4 us
    ppermute x6, starting transfers between devices, over_slices(): lax.ppermute(chunk, 'mesh', [(i, i ^ k) for i in range(count)])  11 us
    ppermute x3, starting transfers between devices, over_plane(): lax.ppermute(own, ('groups', 'band'), DIAGONAL)  8.44 us
    ppermute x6, waiting for transfers between devices, over_slices(): lax.ppermute(chunk, 'mesh', [(i, i ^ k) for i in range(count)])  6.17 us
    ppermute x12, waiting for transfers between devices, swap_width(): return lax.ppermute(array, 'width', SWAP)  4.52 us
    ppermute x3, starting transfers between devices, over_plane(): lax.ppermute(own, 'band', SWAP)  4.2 us
  transfers between devices with their start and end apart: 31, of which 13 were waited for; matrix products, arithmetic and copies ran while one was open for 0% of the time, Pallas kernels for 13%

profile of v2, /device:TPU:0, one launch (start us, length us, event | category | flops | bytes accessed | tf_op | source)
XLA Modules:
  0.0 102.1 jit_solution(6492845130985408888)
XLA Ops:
  0.0 0.9 shard_map.146
  0.9 3.1 %collective-permute-start = (bf16[7,32,256]{2,1,0:T(8,128)(2,1)S(1)}, bf16[7,32,256]{2,1,0:T(8,128)(2,1)S(1)}, u32[]{:S(2)}, u32[]{:S(2)}) collective-permute-start(bf16[7,32,256]{2,1,0:T(8,128)(2,1)S(1)} %shard_map.146), channel_id=1, source_target_pairs={{0,4},{4,0},{8,12},{12,8},{1,5},{5,1},{9,13},{13,9},{2,6},{6,2},{1... | collective-permute-start | bytes 344072 | tf_op jit(solution)/shard_map/ppermute | solution.py:337
  4.0 2.5 %collective-permute-start.3 = (bf16[7,32,256]{2,1,0:T(8,128)(2,1)S(1)}, bf16[7,32,256]{2,1,0:T(8,128)(2,1)S(1)}, u32[]{:S(2)}, u32[]{:S(2)}) collective-permute-start(bf16[7,32,256]{2,1,0:T(8,128)(2,1)S(1)} %shard_map.146), channel_id=1, source_target_pairs={{0,12},{4,8},{8,4},{12,0},{1,13},{5,9},{9,5},{13,1},{2,14},{6,10},... | collective-permute-start | bytes 344072 | tf_op jit(solution)/shard_map/ppermute | solution.py:337
  6.5 0.1 collective-permute-start.2
  6.6 0.3 shard_map.145
  7.0 0.2 collective-permute-done.refs_0_
  7.2 3.6 %collective-permute-start.1 = (bf16[64,512]{1,0:T(8,128)(2,1)S(1)}, bf16[64,512]{1,0:T(8,128)(2,1)S(1)}, u32[]{:S(2)}, u32[]{:S(2)}) collective-permute-start(bf16[64,512]{1,0:T(8,128)(2,1)S(1)} %get-tuple-element.36), channel_id=1, source_target_pairs={{0,2},{2,4},{4,6},{6,8},{8,10},{10,12},{12,14},{1,3},{3,5},{5,7},{... | collective-permute-start | bytes 196616 | tf_op jit(solution)/shard_map/ppermute | solution.py:415
  10.8 0.0 copy-start.8
  10.8 0.0 copy-start.9
  10.8 1.3 %collective-permute-start.4 = (bf16[64,512]{1,0:T(8,128)(2,1)S(1)}, bf16[64,512]{1,0:T(8,128)(2,1)S(1)}, u32[]{:S(2)}, u32[]{:S(2)}) collective-permute-start(bf16[64,512]{1,0:T(8,128)(2,1)S(1)} %get-tuple-element.39), channel_id=1, source_target_pairs={{2,0},{4,2},{6,4},{8,6},{10,8},{12,10},{14,12},{3,1},{5,3},{7,5},{... | collective-permute-start | bytes 196616 | tf_op jit(solution)/shard_map/ppermute | solution.py:414
  12.1 1.8 %shard_map.147 = (bf16[14,32,256]{2,1,0:T(8,128)(2,1)S(1)}, bf16[7,128,256]{2,1,0:T(8,128)(2,1)S(1)}, bf16[7,128,256]{2,1,0:T(8,128)(2,1)S(1)}, bf16[7,128,256]{2,1,0:T(8,128)(2,1)S(1)}) custom-call(bf16[3,3,128,256]{3,2,1,0:T(8,128)(2,1)} %refs_0_.3, bf16[3,256,128]{2,1,0:T(8,128)(2,1)} %refs_1_.4, bf16[3,2,128,256]{3,2,1,0:T(8,128)(2,1)} %refs_2_.3, ...), custom_call_target="tpu_custom_call" | custom-call | flops 500000000 | tf_op jit(solution)/shard_map/pallas_call | solution.py:59
  13.9 0.0 collective-permute-done.3.refs_2_
  13.9 3.0 %collective-permute-done.4.high = bf16[64,512]{1,0:T(8,128)(2,1)S(1)} collective-permute-done((bf16[64,512]{1,0:T(8,128)(2,1)S(1)}, bf16[64,512]{1,0:T(8,128)(2,1)S(1)}, u32[]{:S(2)}, u32[]{:S(2)}) %collective-permute-start.4) | collective-permute-done | bytes 65568 | tf_op jit(solution)/shard_map/ppermute | solution.py:414
  16.9 0.7 collective-permute-done.2.refs_1_
  17.6 1.6 %collective-permute-start.5 = (bf16[14,32,256]{2,1,0:T(8,128)(2,1)S(1)}, bf16[14,32,256]{2,1,0:T(8,128)(2,1)S(1)}, u32[]{:S(2)}, u32[]{:S(2)}) collective-permute-start(bf16[14,32,256]{2,1,0:T(8,128)(2,1)S(1)} %get-tuple-element.41), channel_id=1, source_target_pairs={{0,4},{4,0},{8,12},{12,8},{1,5},{5,1},{9,13},{13,9},{2,6},{6,2},{1... | collective-permute-start | bytes 688136 | tf_op jit(solution)/shard_map/ppermute | solution.py:337
  19.3 3.3 %collective-permute-start.6 = (bf16[14,32,256]{2,1,0:T(8,128)(2,1)S(1)}, bf16[14,32,256]{2,1,0:T(8,128)(2,1)S(1)}, u32[]{:S(2)}, u32[]{:S(2)}) collective-permute-start(bf16[14,32,256]{2,1,0:T(8,128)(2,1)S(1)} %get-tuple-element.41), channel_id=1, source_target_pairs={{0,8},{4,12},{8,0},{12,4},{1,9},{5,13},{9,1},{13,5},{2,10},{6,14},... | collective-permute-start | bytes 688136 | tf_op jit(solution)/shard_map/ppermute | solution.py:337
  22.6 0.4 collective-permute-start.7
  22.9 2.0 %collective-permute-start.8 = (bf16[3,7,32,256]{3,2,1,0:T(8,128)(2,1)S(1)}, bf16[3,7,32,256]{3,2,1,0:T(8,128)(2,1)S(1)}, u32[]{:S(2)}, u32[]{:S(2)}) collective-permute-start(bf16[3,7,32,256]{3,2,1,0:T(8,128)(2,1)S(1)} %shard_map.148.refs_1_), channel_id=1, source_target_pairs={{0,2},{2,0},{1,3},{3,1},{4,6},{6,4},{5,7},{7,5},{8,10},{10,8},{9,1... | collective-permute-start | bytes 1032200 | tf_op jit(solution)/shard_map/ppermute | solution.py:342
  24.9 1.5 %collective-permute-start.9 = (bf16[3,7,32,256]{3,2,1,0:T(8,128)(2,1)S(1)}, bf16[3,7,32,256]{3,2,1,0:T(8,128)(2,1)S(1)}, u32[]{:S(2)}, u32[]{:S(2)}) collective-permute-start(bf16[3,7,32,256]{3,2,1,0:T(8,128)(2,1)S(1)} %shard_map.148.refs_1_), channel_id=1, source_target_pairs={{0,16},{16,0},{1,17},{17,1},{2,18},{18,2},{3,19},{19,3},{4,20},{20... | collective-permute-start | bytes 1032200 | tf_op jit(solution)/shard_map/ppermute | solution.py:343
  26.4 0.6 collective-permute-done.5.refs_0_
  27.0 6.2 %collective-permute-start.10 = (bf16[3,7,32,256]{3,2,1,0:T(8,128)(2,1)S(1)}, bf16[3,7,32,256]{3,2,1,0:T(8,128)(2,1)S(1)}, u32[]{:S(2)}, u32[]{:S(2)}) collective-permute-start(bf16[3,7,32,256]{3,2,1,0:T(8,128)(2,1)S(1)} %shard_map.148.refs_1_), channel_id=1, source_target_pairs={{0,18},{18,0},{2,16},{16,2},{1,19},{19,1},{3,17},{17,3},{4,22},{22... | collective-permute-start | bytes 1032200 | tf_op jit(solution)/shard_map/ppermute | solution.py:344
  33.2 4.7 %collective-permute-done.6.refs_1_ = bf16[14,32,256]{2,1,0:T(8,128)(2,1)S(1)} collective-permute-done((bf16[14,32,256]{2,1,0:T(8,128)(2,1)S(1)}, bf16[14,32,256]{2,1,0:T(8,128)(2,1)S(1)}, u32[]{:S(2)}, u32[]{:S(2)}) %collective-permute-start.6) | collective-permute-done | bytes 229408 | tf_op jit(solution)/shard_map/ppermute | solution.py:337
  38.0 1.2 %shard_map.150.gathered = bf16[768,1024]{1,0:T(8,128)(2,1)S(1)} custom-call(bf16[512,512]{1,0:T(8,128)(2,1)S(1)} %copy-done, bf16[64,512]{1,0:T(8,128)(2,1)S(1)} %collective-permute-done.1.low, bf16[64,512]{1,0:T(8,128)(2,1)S(1)} %collective-permute-done.4.high, bf16[320,512]{1,0:T(8,128)(2,1)S(1)} %copy-done.5, s32[1,768]{1,0:T(1,128)S(1)} %broadcast_in_dim.22.slots, ...), custom_call_target="tpu_custom_call" | custom-call | flops 1200000000 | tf_op jit(solution)/shard_map/pallas_call | solution.py:59
  39.3 0.2 collective-permute-done.9.refs_3_
  39.4 0.0 collective-permute-done.10.refs_4_
  39.4 3.0 %shard_map.151.refs_0_ = bf16[768,512]{1,0:T(8,128)(2,1)S(1)} custom-call(bf16[768,1024]{1,0:T(8,128)(2,1)S(1)} %shard_map.150.gathered, bf16[7,128,256]{2,1,0:T(8,128)(2,1)S(1)} %get-tuple-element.44.refs_0_, bf16[3,7,32,256]{3,2,1,0:T(8,128)(2,1)S(1)} %shard_map.148.refs_1_, bf16[3,7,32,256]{3,2,1,0:T(8,128)(2,1)S(1)} %collective-permute-done.8.refs_2_, ...), custom_call_target="tpu_custom_call" | custom-call | flops 3000000000 | tf_op jit(solution)/shard_map/pallas_call | solution.py:59
  42.4 0.1 collective-permute-start.11
  42.5 2.3 %collective-permute-done.11.refs_1_ = bf16[768,512]{1,0:T(8,128)(2,1)S(1)} collective-permute-done((bf16[768,512]{1,0:T(8,128)(2,1)S(1)}, bf16[768,512]{1,0:T(8,128)(2,1)S(1)}, u32[]{:S(2)}, u32[]{:S(2)}) %collective-permute-start.11) | collective-permute-done | bytes 786464 | tf_op jit(solution)/shard_map/ppermute | solution.py:349
  44.8 0.8 shard_map.152.incoming
  45.6 0.0 copy-start.12
  45.6 0.7 shard_map.153.refs_0_
  46.3 0.2 collective-permute-start.12
  46.5 1.1 %collective-permute-start.13 = (bf16[3,7,32,256]{3,2,1,0:T(8,128)(2,1)S(1)}, bf16[3,7,32,256]{3,2,1,0:T(8,128)(2,1)S(1)}, u32[]{:S(2)}, u32[]{:S(2)}) collective-permute-start(bf16[3,7,32,256]{3,2,1,0:T(8,128)(2,1)S(1)} %get-tuple-element.50.refs_3_), channel_id=1, source_target_pairs={{0,2},{2,0},{1,3},{3,1},{4,6},{6,4},{5,7},{7,5},{8,10},{10,8},{9,1... | collective-permute-start | bytes 1032200 | tf_op jit(solution)/shard_map/ppermute | solution.py:342
  47.6 1.4 %collective-permute-start.14 = (bf16[3,7,32,256]{3,2,1,0:T(8,128)(2,1)S(1)}, bf16[3,7,32,256]{3,2,1,0:T(8,128)(2,1)S(1)}, u32[]{:S(2)}, u32[]{:S(2)}) collective-permute-start(bf16[3,7,32,256]{3,2,1,0:T(8,128)(2,1)S(1)} %get-tuple-element.50.refs_3_), channel_id=1, source_target_pairs={{0,16},{16,0},{1,17},{17,1},{2,18},{18,2},{3,19},{19,3},{4,20},{20... | collective-permute-start | bytes 1032200 | tf_op jit(solution)/shard_map/ppermute | solution.py:343
  49.0 1.0 collective-permute-start.15
  50.0 0.1 reshape.15.lists
  50.1 1.6 %shard_map.154 = (bf16[64,512]{1,0:T(8,128)(2,1)}, bf16[320,512]{1,0:T(8,128)(2,1)}) custom-call(bf16[320,512]{1,0:T(8,128)(2,1)S(1)} %copy-done.5, s32[1,64]{1,0:T(1,128)S(1)} %reshape.15.lists, bf16[320,512]{1,0:T(8,128)(2,1)S(1)} %shard_map.153.refs_0_, bf16[320,512]{1,0:T(8,128)(2,1)S(1)} %collective-permute-done.12.refs_1_), custom_call_target="tpu_custom_call" | custom-call | flops 1600000000 | tf_op jit(solution)/shard_map/pallas_call | solution.py:59
  51.7 6.1 %all-to-all-start = ((bf16[8,8,512]{2,1,0:T(8,128)(2,1)}), bf16[8,8,512]{2,1,0:T(8,128)(2,1)S(1)}, u32[]{:S(2)}, u32[]{:S(2)}) async-start(bf16[8,8,512]{2,1,0:T(8,128)(2,1)} %bitcast.2), calls=%async_computation | async-start | bytes 131072 | tf_op jit(solution)/shard_map/all_to_all | solution.py:473
  57.9 0.1 collective-permute-start.16
  57.9 0.5 collective-permute-start.17
  58.4 0.0 collective-permute-done.13.refs_4_
  58.4 6.5 %all-to-all-done = bf16[8,8,512]{2,1,0:T(8,128)(2,1)S(1)} async-done(((bf16[8,8,512]{2,1,0:T(8,128)(2,1)}), bf16[8,8,512]{2,1,0:T(8,128)(2,1)S(1)}, u32[]{:S(2)}, u32[]{:S(2)}) %all-to-all-start) | async-done | bytes 65568 | tf_op jit(solution)/shard_map/all_to_all | solution.py:473
  64.9 0.0 collective-permute-start.18
  64.9 0.0 collective-permute-done.14.refs_5_
  65.0 0.5 collective-permute-start.19
  65.5 0.4 collective-permute-done.15.refs_6_
  65.9 1.1 %collective-permute-start.21 = (bf16[3,7,32,256]{3,2,1,0:T(8,128)(2,1)S(1)}, bf16[3,7,32,256]{3,2,1,0:T(8,128)(2,1)S(1)}, u32[]{:S(2)}, u32[]{:S(2)}) collective-permute-start(bf16[3,7,32,256]{3,2,1,0:T(8,128)(2,1)S(1)} %get-tuple-element.61.refs_3_), channel_id=1, source_target_pairs={{0,2},{2,0},{1,3},{3,1},{4,6},{6,4},{5,7},{7,5},{8,10},{10,8},{9,1... | collective-permute-start | bytes 1032200 | tf_op jit(solution)/shard_map/ppermute | solution.py:342
  67.0 1.2 %collective-permute-start.22 = (bf16[3,7,32,256]{3,2,1,0:T(8,128)(2,1)S(1)}, bf16[3,7,32,256]{3,2,1,0:T(8,128)(2,1)S(1)}, u32[]{:S(2)}, u32[]{:S(2)}) collective-permute-start(bf16[3,7,32,256]{3,2,1,0:T(8,128)(2,1)S(1)} %get-tuple-element.61.refs_3_), channel_id=1, source_target_pairs={{0,16},{16,0},{1,17},{17,1},{2,18},{18,2},{3,19},{19,3},{4,20},{20... | collective-permute-start | bytes 1032200 | tf_op jit(solution)/shard_map/ppermute | solution.py:343
  68.2 1.3 %collective-permute-start.23 = (bf16[3,7,32,256]{3,2,1,0:T(8,128)(2,1)S(1)}, bf16[3,7,32,256]{3,2,1,0:T(8,128)(2,1)}, u32[]{:S(2)}, u32[]{:S(2)}) collective-permute-start(bf16[3,7,32,256]{3,2,1,0:T(8,128)(2,1)S(1)} %get-tuple-element.61.refs_3_), channel_id=1, source_target_pairs={{0,18},{18,0},{2,16},{16,2},{1,19},{19,1},{3,17},{17,3},{4,22},{22... | collective-permute-start | bytes 1032200 | tf_op jit(solution)/shard_map/ppermute | solution.py:344
  69.6 0.7 copy-done.22
  70.3 0.1 copy-done.23
  70.4 7.8 %shard_map.155 = (bf16[64,512]{1,0:T(8,128)(2,1)}, bf16[320,512]{1,0:T(8,128)(2,1)}, bf16[768,512]{1,0:T(8,128)(2,1)}) custom-call(bf16[64,512]{1,0:T(8,128)(2,1)S(1)} %bitcast.6, s32[1,768]{1,0:T(1,128)S(1)} %broadcast_in_dim.23.slots, s32[1,768]{1,0:T(1,128)S(1)} %broadcast_in_dim.24.targets, s32[1,64]{1,0:T(1,128)S(1)} %reshape.15.lists, ...), custom_call_target="tpu_custom_call" | custom-call | flops 6499999744 | tf_op jit(solution)/shard_map/pallas_call | solution.py:59
  78.2 6.2 %all-to-all-start.1 = ((bf16[8,8,512]{2,1,0:T(8,128)(2,1)}), bf16[8,8,512]{2,1,0:T(8,128)(2,1)S(1)}, u32[]{:S(2)}, u32[]{:S(2)}) async-start(bf16[8,8,512]{2,1,0:T(8,128)(2,1)} %bitcast.4), calls=%async_computation.1 | async-start | bytes 131072 | tf_op jit(solution)/shard_map/all_to_all | solution.py:473
  84.4 0.1 collective-permute-start.24
  84.5 0.5 collective-permute-start.25
  85.0 6.3 %all-to-all-done.1 = bf16[8,8,512]{2,1,0:T(8,128)(2,1)S(1)} async-done(((bf16[8,8,512]{2,1,0:T(8,128)(2,1)}), bf16[8,8,512]{2,1,0:T(8,128)(2,1)S(1)}, u32[]{:S(2)}, u32[]{:S(2)}) %all-to-all-start.1) | async-done | bytes 65568 | tf_op jit(solution)/shard_map/all_to_all | solution.py:473
  91.3 0.5 collective-permute-start.27
  91.8 0.1 collective-permute-start.28
  91.9 1.0 %collective-permute-done.26.refs_9_ = bf16[3,7,32,256]{3,2,1,0:T(8,128)(2,1)S(1)} collective-permute-done((bf16[3,7,32,256]{3,2,1,0:T(8,128)(2,1)S(1)}, bf16[3,7,32,256]{3,2,1,0:T(8,128)(2,1)S(1)}, u32[]{:S(2)}, u32[]{:S(2)}) %collective-permute-start.26) | collective-permute-done | bytes 344096 | tf_op jit(solution)/shard_map/ppermute | solution.py:349
  93.0 0.5 collective-permute-done.27.refs_10_
  93.4 0.7 collective-permute-done.28.refs_11_
  94.2 0.0 copy-done.25
  94.2 0.7 copy-done.26
  94.9 7.1 %shard_map.156 = bf16[320,512]{1,0:T(8,128)(2,1)} custom-call(bf16[64,512]{1,0:T(8,128)(2,1)S(1)} %bitcast.7, s32[1,768]{1,0:T(1,128)S(1)} %broadcast_in_dim.23.slots, s32[1,768]{1,0:T(1,128)S(1)} %broadcast_in_dim.24.targets, s32[1,64]{1,0:T(1,128)S(1)} %reshape.15.lists, bf16[320,512]{1,0:T(8,128)(2,1)} %get-tuple-element.55.refs_0_, ...), custom_call_target="tpu_custom_call" | custom-call | flops 6499999744 | tf_op jit(solution)/shard_map/pallas_call | solution.py:59
  (69 shorter events, 0.2 us)
Async XLA Ops:
  0.0 6.6 %copy-start = (bf16[512,512]{1,0:T(8,128)(2,1)S(1)}, bf16[512,512]{1,0:T(8,128)(2,1)}, u32[]{:S(2)}) copy-start(bf16[512,512]{1,0:T(8,128)(2,1)} %grid.3) | copy-start | bytes 1572868
  0.0 6.6 %copy-start.6 = (s32[64]{0:T(128)S(1)}, s32[64]{0:T(128)}, u32[]{:S(2)}) copy-start(s32[64]{0:T(128)} %param.21) | copy-start | bytes 772
  0.0 6.6 %copy-start.7 = (s32[64]{0:T(128)S(1)}, s32[64]{0:T(128)}, u32[]{:S(2)}) copy-start(s32[64]{0:T(128)} %param.22) | copy-start | bytes 772
  0.9 6.2 %collective-permute-start = (bf16[7,32,256]{2,1,0:T(8,128)(2,1)S(1)}, bf16[7,32,256]{2,1,0:T(8,128)(2,1)S(1)}, u32[]{:S(2)}, u32[]{:S(2)}) collective-permute-start(bf16[7,32,256]{2,1,0:T(8,128)(2,1)S(1)} %shard_map.146), channel_id=1, source_target_pairs={{0,4},{4,0},{8,12},{12,8},{1,5},{5,1},{9,13},{13,9},{2,6},{6,2},{1... | collective-permute-start | bytes 344072 | tf_op jit(solution)/shard_map/ppermute | solution.py:337
  4.0 9.9 %collective-permute-start.3 = (bf16[7,32,256]{2,1,0:T(8,128)(2,1)S(1)}, bf16[7,32,256]{2,1,0:T(8,128)(2,1)S(1)}, u32[]{:S(2)}, u32[]{:S(2)}) collective-permute-start(bf16[7,32,256]{2,1,0:T(8,128)(2,1)S(1)} %shard_map.146), channel_id=1, source_target_pairs={{0,12},{4,8},{8,4},{12,0},{1,13},{5,9},{9,5},{13,1},{2,14},{6,10},... | collective-permute-start | bytes 344072 | tf_op jit(solution)/shard_map/ppermute | solution.py:337
  6.5 11.1 %collective-permute-start.2 = (bf16[7,32,256]{2,1,0:T(8,128)(2,1)S(1)}, bf16[7,32,256]{2,1,0:T(8,128)(2,1)S(1)}, u32[]{:S(2)}, u32[]{:S(2)}) collective-permute-start(bf16[7,32,256]{2,1,0:T(8,128)(2,1)S(1)} %shard_map.146), channel_id=1, source_target_pairs={{0,8},{4,12},{8,0},{12,4},{1,9},{5,13},{9,1},{13,5},{2,10},{6,14},... | collective-permute-start | bytes 344072 | tf_op jit(solution)/shard_map/ppermute | solution.py:337
  7.2 6.7 %collective-permute-start.1 = (bf16[64,512]{1,0:T(8,128)(2,1)S(1)}, bf16[64,512]{1,0:T(8,128)(2,1)S(1)}, u32[]{:S(2)}, u32[]{:S(2)}) collective-permute-start(bf16[64,512]{1,0:T(8,128)(2,1)S(1)} %get-tuple-element.36), channel_id=1, source_target_pairs={{0,2},{2,4},{4,6},{6,8},{8,10},{10,12},{12,14},{1,3},{3,5},{5,7},{... | collective-permute-start | bytes 196616 | tf_op jit(solution)/shard_map/ppermute | solution.py:415
  10.8 22.4 %copy-start.8 = (s32[768]{0:T(1024)S(1)}, s32[768]{0:T(1024)}, u32[]{:S(2)}) copy-start(s32[768]{0:T(1024)} %param.20) | copy-start | bytes 9220
  10.8 22.4 %copy-start.9 = (s32[768]{0:T(1024)S(1)}, s32[768]{0:T(1024)}, u32[]{:S(2)}) copy-start(s32[768]{0:T(1024)} %param.19) | copy-start | bytes 9220
  10.8 6.2 %collective-permute-start.4 = (bf16[64,512]{1,0:T(8,128)(2,1)S(1)}, bf16[64,512]{1,0:T(8,128)(2,1)S(1)}, u32[]{:S(2)}, u32[]{:S(2)}) collective-permute-start(bf16[64,512]{1,0:T(8,128)(2,1)S(1)} %get-tuple-element.39), channel_id=1, source_target_pairs={{2,0},{4,2},{6,4},{8,6},{10,8},{12,10},{14,12},{3,1},{5,3},{7,5},{... | collective-permute-start | bytes 196616 | tf_op jit(solution)/shard_map/ppermute | solution.py:414
  13.9 44.0 %copy-start.2 = (bf16[7,128,256]{2,1,0:T(8,128)(2,1)}, bf16[7,128,256]{2,1,0:T(8,128)(2,1)S(1)}, u32[]{:S(2)}) copy-start(bf16[7,128,256]{2,1,0:T(8,128)(2,1)S(1)} %get-tuple-element.49.refs_2_) | copy-start | bytes 1376260
  13.9 70.5 %copy-start.1 = (bf16[7,128,256]{2,1,0:T(8,128)(2,1)}, bf16[7,128,256]{2,1,0:T(8,128)(2,1)S(1)}, u32[]{:S(2)}) copy-start(bf16[7,128,256]{2,1,0:T(8,128)(2,1)S(1)} %get-tuple-element.60.refs_2_) | copy-start | bytes 1376260
  16.9 21.1 %copy-start.5 = (bf16[320,512]{1,0:T(8,128)(2,1)S(1)}, bf16[320,512]{1,0:T(8,128)(2,1)}, u32[]{:S(2)}) copy-start(bf16[320,512]{1,0:T(8,128)(2,1)} %nodes.5) | copy-start | bytes 983044
  17.6 9.4 %collective-permute-start.5 = (bf16[14,32,256]{2,1,0:T(8,128)(2,1)S(1)}, bf16[14,32,256]{2,1,0:T(8,128)(2,1)S(1)}, u32[]{:S(2)}, u32[]{:S(2)}) collective-permute-start(bf16[14,32,256]{2,1,0:T(8,128)(2,1)S(1)} %get-tuple-element.41), channel_id=1, source_target_pairs={{0,4},{4,0},{8,12},{12,8},{1,5},{5,1},{9,13},{13,9},{2,6},{6,2},{1... | collective-permute-start | bytes 688136 | tf_op jit(solution)/shard_map/ppermute | solution.py:337
  19.3 18.6 %collective-permute-start.6 = (bf16[14,32,256]{2,1,0:T(8,128)(2,1)S(1)}, bf16[14,32,256]{2,1,0:T(8,128)(2,1)S(1)}, u32[]{:S(2)}, u32[]{:S(2)}) collective-permute-start(bf16[14,32,256]{2,1,0:T(8,128)(2,1)S(1)} %get-tuple-element.41), channel_id=1, source_target_pairs={{0,8},{4,12},{8,0},{12,4},{1,9},{5,13},{9,1},{13,5},{2,10},{6,14},... | collective-permute-start | bytes 688136 | tf_op jit(solution)/shard_map/ppermute | solution.py:337
  22.6 15.3 %collective-permute-start.7 = (bf16[14,32,256]{2,1,0:T(8,128)(2,1)S(1)}, bf16[14,32,256]{2,1,0:T(8,128)(2,1)S(1)}, u32[]{:S(2)}, u32[]{:S(2)}) collective-permute-start(bf16[14,32,256]{2,1,0:T(8,128)(2,1)S(1)} %get-tuple-element.41), channel_id=1, source_target_pairs={{0,12},{4,8},{8,4},{12,0},{1,13},{5,9},{9,5},{13,1},{2,14},{6,10},... | collective-permute-start | bytes 688136 | tf_op jit(solution)/shard_map/ppermute | solution.py:337
  22.9 16.3 %collective-permute-start.8 = (bf16[3,7,32,256]{3,2,1,0:T(8,128)(2,1)S(1)}, bf16[3,7,32,256]{3,2,1,0:T(8,128)(2,1)S(1)}, u32[]{:S(2)}, u32[]{:S(2)}) collective-permute-start(bf16[3,7,32,256]{3,2,1,0:T(8,128)(2,1)S(1)} %shard_map.148.refs_1_), channel_id=1, source_target_pairs={{0,2},{2,0},{1,3},{3,1},{4,6},{6,4},{5,7},{7,5},{8,10},{10,8},{9,1... | collective-permute-start | bytes 1032200 | tf_op jit(solution)/shard_map/ppermute | solution.py:342
  24.9 14.5 %collective-permute-start.9 = (bf16[3,7,32,256]{3,2,1,0:T(8,128)(2,1)S(1)}, bf16[3,7,32,256]{3,2,1,0:T(8,128)(2,1)S(1)}, u32[]{:S(2)}, u32[]{:S(2)}) collective-permute-start(bf16[3,7,32,256]{3,2,1,0:T(8,128)(2,1)S(1)} %shard_map.148.refs_1_), channel_id=1, source_target_pairs={{0,16},{16,0},{1,17},{17,1},{2,18},{18,2},{3,19},{19,3},{4,20},{20... | collective-permute-start | bytes 1032200 | tf_op jit(solution)/shard_map/ppermute | solution.py:343
  27.0 12.4 %collective-permute-start.10 = (bf16[3,7,32,256]{3,2,1,0:T(8,128)(2,1)S(1)}, bf16[3,7,32,256]{3,2,1,0:T(8,128)(2,1)S(1)}, u32[]{:S(2)}, u32[]{:S(2)}) collective-permute-start(bf16[3,7,32,256]{3,2,1,0:T(8,128)(2,1)S(1)} %shard_map.148.refs_1_), channel_id=1, source_target_pairs={{0,18},{18,0},{2,16},{16,2},{1,19},{19,1},{3,17},{17,3},{4,22},{22... | collective-permute-start | bytes 1032200 | tf_op jit(solution)/shard_map/ppermute | solution.py:344
  38.0 20.0 %copy-start.4 = (bf16[3,7,32,256]{3,2,1,0:T(8,128)(2,1)}, bf16[3,7,32,256]{3,2,1,0:T(8,128)(2,1)S(1)}, u32[]{:S(2)}) copy-start(bf16[3,7,32,256]{3,2,1,0:T(8,128)(2,1)S(1)} %get-tuple-element.50.refs_3_) | copy-start | bytes 1032196
  38.0 46.5 %copy-start.3 = (bf16[3,7,32,256]{3,2,1,0:T(8,128)(2,1)}, bf16[3,7,32,256]{3,2,1,0:T(8,128)(2,1)S(1)}, u32[]{:S(2)}) copy-start(bf16[3,7,32,256]{3,2,1,0:T(8,128)(2,1)S(1)} %get-tuple-element.61.refs_3_) | copy-start | bytes 1032196
  42.4 2.4 %collective-permute-start.11 = (bf16[768,512]{1,0:T(8,128)(2,1)S(1)}, bf16[768,512]{1,0:T(8,128)(2,1)S(1)}, u32[]{:S(2)}, u32[]{:S(2)}) collective-permute-start(bf16[768,512]{1,0:T(8,128)(2,1)S(1)} %shard_map.151.refs_0_), channel_id=1, source_target_pairs={{0,1},{1,0},{2,3},{3,2},{4,5},{5,4},{6,7},{7,6},{8,9},{9,8},{10,11... | collective-permute-start | bytes 2359304 | tf_op jit(solution)/shard_map/ppermute | solution.py:349
  45.6 4.4 %copy-start.12 = (s32[1,8,8]{2,1,0:T(8,128)S(1)}, s32[1,8,8]{2,1,0:T(8,128)}, u32[]{:S(2)}) copy-start(s32[1,8,8]{2,1,0:T(8,128)} %param.23) | copy-start | bytes 772
  46.3 3.8 %collective-permute-start.12 = (bf16[320,512]{1,0:T(8,128)(2,1)S(1)}, bf16[320,512]{1,0:T(8,128)(2,1)S(1)}, u32[]{:S(2)}, u32[]{:S(2)}) collective-permute-start(bf16[320,512]{1,0:T(8,128)(2,1)S(1)} %shard_map.153.refs_0_), channel_id=1, source_target_pairs={{0,1},{1,0},{2,3},{3,2},{4,5},{5,4},{6,7},{7,6},{8,9},{9,8},{10,11... | collective-permute-start | bytes 983048 | tf_op jit(solution)/shard_map/ppermute | solution.py:349
  46.5 12.0 %collective-permute-start.13 = (bf16[3,7,32,256]{3,2,1,0:T(8,128)(2,1)S(1)}, bf16[3,7,32,256]{3,2,1,0:T(8,128)(2,1)S(1)}, u32[]{:S(2)}, u32[]{:S(2)}) collective-permute-start(bf16[3,7,32,256]{3,2,1,0:T(8,128)(2,1)S(1)} %get-tuple-element.50.refs_3_), channel_id=1, source_target_pairs={{0,2},{2,0},{1,3},{3,1},{4,6},{6,4},{5,7},{7,5},{8,10},{10,8},{9,1... | collective-permute-start | bytes 1032200 | tf_op jit(solution)/shard_map/ppermute | solution.py:342
  47.6 17.4 %collective-permute-start.14 = (bf16[3,7,32,256]{3,2,1,0:T(8,128)(2,1)S(1)}, bf16[3,7,32,256]{3,2,1,0:T(8,128)(2,1)S(1)}, u32[]{:S(2)}, u32[]{:S(2)}) collective-permute-start(bf16[3,7,32,256]{3,2,1,0:T(8,128)(2,1)S(1)} %get-tuple-element.50.refs_3_), channel_id=1, source_target_pairs={{0,16},{16,0},{1,17},{17,1},{2,18},{18,2},{3,19},{19,3},{4,20},{20... | collective-permute-start | bytes 1032200 | tf_op jit(solution)/shard_map/ppermute | solution.py:343
  49.0 16.8 %collective-permute-start.15 = (bf16[3,7,32,256]{3,2,1,0:T(8,128)(2,1)S(1)}, bf16[3,7,32,256]{3,2,1,0:T(8,128)(2,1)}, u32[]{:S(2)}, u32[]{:S(2)}) collective-permute-start(bf16[3,7,32,256]{3,2,1,0:T(8,128)(2,1)S(1)} %get-tuple-element.50.refs_3_), channel_id=1, source_target_pairs={{0,18},{18,0},{2,16},{16,2},{1,19},{19,1},{3,17},{17,3},{4,22},{22... | collective-permute-start | bytes 1032200 | tf_op jit(solution)/shard_map/ppermute | solution.py:344
  50.1 15.8 %copy-start.10 = (s32[768]{0:T(1024)S(1)}, s32[768]{0:T(1024)}, u32[]{:S(2)}) copy-start(s32[768]{0:T(1024)} %param.24) | copy-start | bytes 9220
  50.1 15.8 %copy-start.11 = (s32[768]{0:T(1024)S(1)}, s32[768]{0:T(1024)}, u32[]{:S(2)}) copy-start(s32[768]{0:T(1024)} %param.25) | copy-start | bytes 9220
  51.7 13.2 %all-to-all-start = ((bf16[8,8,512]{2,1,0:T(8,128)(2,1)}), bf16[8,8,512]{2,1,0:T(8,128)(2,1)S(1)}, u32[]{:S(2)}, u32[]{:S(2)}) async-start(bf16[8,8,512]{2,1,0:T(8,128)(2,1)} %bitcast.2), calls=%async_computation | async-start | bytes 131072 | tf_op jit(solution)/shard_map/all_to_all | solution.py:473
  57.9 9.1 %collective-permute-start.16 = (bf16[7,128,256]{2,1,0:T(8,128)(2,1)S(1)}, bf16[7,128,256]{2,1,0:T(8,128)(2,1)S(1)}, u32[]{:S(2)}, u32[]{:S(2)}) collective-permute-start(bf16[7,128,256]{2,1,0:T(8,128)(2,1)S(1)} %get-tuple-element.49.refs_2_), channel_id=1, source_target_pairs={{0,1},{1,0},{2,3},{3,2},{4,5},{5,4},{6,7},{7,6},{8,9},{9,8},{10,11... | collective-permute-start | bytes 1376264 | tf_op jit(solution)/shard_map/ppermute | solution.py:349
  57.9 7.9 %collective-permute-start.17 = (bf16[3,7,32,256]{3,2,1,0:T(8,128)(2,1)S(1)}, bf16[3,7,32,256]{3,2,1,0:T(8,128)(2,1)S(1)}, u32[]{:S(2)}, u32[]{:S(2)}) collective-permute-start(bf16[3,7,32,256]{3,2,1,0:T(8,128)(2,1)S(1)} %get-tuple-element.50.refs_3_), channel_id=1, source_target_pairs={{0,1},{1,0},{2,3},{3,2},{4,5},{5,4},{6,7},{7,6},{8,9},{9,8},{10,11... | collective-permute-start | bytes 1032200 | tf_op jit(solution)/shard_map/ppermute | solution.py:349
  58.4 11.1 %copy-start.16 = (bf16[3,7,32,256]{3,2,1,0:T(8,128)(2,1)}, bf16[3,7,32,256]{3,2,1,0:T(8,128)(2,1)S(1)}, u32[]{:S(2)}) copy-start(bf16[3,7,32,256]{3,2,1,0:T(8,128)(2,1)S(1)} %collective-permute-done.13.refs_4_) | copy-start | bytes 1032196
  64.9 3.3 %collective-permute-start.18 = (bf16[3,7,32,256]{3,2,1,0:T(8,128)(2,1)S(1)}, bf16[3,7,32,256]{3,2,1,0:T(8,128)(2,1)S(1)}, u32[]{:S(2)}, u32[]{:S(2)}) collective-permute-start(bf16[3,7,32,256]{3,2,1,0:T(8,128)(2,1)S(1)} %collective-permute-done.13.refs_4_), channel_id=1, source_target_pairs={{0,1},{1,0},{2,3},{3,2},{4,5},{5,4},{6,7},{7,6},{8,9},{9,8},{10,11... | collective-permute-start | bytes 1032200 | tf_op jit(solution)/shard_map/ppermute | solution.py:349
  64.9 4.6 %copy-start.18 = (bf16[3,7,32,256]{3,2,1,0:T(8,128)(2,1)}, bf16[3,7,32,256]{3,2,1,0:T(8,128)(2,1)S(1)}, u32[]{:S(2)}) copy-start(bf16[3,7,32,256]{3,2,1,0:T(8,128)(2,1)S(1)} %collective-permute-done.14.refs_5_) | copy-start | bytes 1032196
  65.0 4.6 %collective-permute-start.19 = (bf16[3,7,32,256]{3,2,1,0:T(8,128)(2,1)S(1)}, bf16[3,7,32,256]{3,2,1,0:T(8,128)(2,1)S(1)}, u32[]{:S(2)}, u32[]{:S(2)}) collective-permute-start(bf16[3,7,32,256]{3,2,1,0:T(8,128)(2,1)S(1)} %collective-permute-done.14.refs_5_), channel_id=1, source_target_pairs={{0,1},{1,0},{2,3},{3,2},{4,5},{5,4},{6,7},{7,6},{8,9},{9,8},{10,11... | collective-permute-start | bytes 1032200 | tf_op jit(solution)/shard_map/ppermute | solution.py:349
  65.8 3.7 %collective-permute-start.20 = (bf16[3,7,32,256]{3,2,1,0:T(8,128)(2,1)}, bf16[3,7,32,256]{3,2,1,0:T(8,128)(2,1)S(1)}, u32[]{:S(2)}, u32[]{:S(2)}) collective-permute-start(bf16[3,7,32,256]{3,2,1,0:T(8,128)(2,1)} %collective-permute-done.15.refs_6_), channel_id=1, source_target_pairs={{0,1},{1,0},{2,3},{3,2},{4,5},{5,4},{6,7},{7,6},{8,9},{9,8},{10,11... | collective-permute-start | bytes 1032200 | tf_op jit(solution)/shard_map/ppermute | solution.py:349
  65.9 1.1 %copy-start.19 = (bf16[3,7,32,256]{3,2,1,0:T(8,128)(2,1)}, bf16[3,7,32,256]{3,2,1,0:T(8,128)(2,1)S(1)}, u32[]{:S(2)}) copy-start(bf16[3,7,32,256]{3,2,1,0:T(8,128)(2,1)S(1)} %collective-permute-done.17.refs_8_) | copy-start | bytes 1032196
  65.9 19.1 %collective-permute-start.21 = (bf16[3,7,32,256]{3,2,1,0:T(8,128)(2,1)S(1)}, bf16[3,7,32,256]{3,2,1,0:T(8,128)(2,1)S(1)}, u32[]{:S(2)}, u32[]{:S(2)}) collective-permute-start(bf16[3,7,32,256]{3,2,1,0:T(8,128)(2,1)S(1)} %get-tuple-element.61.refs_3_), channel_id=1, source_target_pairs={{0,2},{2,0},{1,3},{3,1},{4,6},{6,4},{5,7},{7,5},{8,10},{10,8},{9,1... | collective-permute-start | bytes 1032200 | tf_op jit(solution)/shard_map/ppermute | solution.py:342
  67.0 2.5 %copy-start.13 = (bf16[7,128,256]{2,1,0:T(8,128)(2,1)}, bf16[7,128,256]{2,1,0:T(8,128)(2,1)S(1)}, u32[]{:S(2)}) copy-start(bf16[7,128,256]{2,1,0:T(8,128)(2,1)S(1)} %collective-permute-done.16.refs_7_) | copy-start | bytes 1376260
  67.0 24.3 %collective-permute-start.22 = (bf16[3,7,32,256]{3,2,1,0:T(8,128)(2,1)S(1)}, bf16[3,7,32,256]{3,2,1,0:T(8,128)(2,1)S(1)}, u32[]{:S(2)}, u32[]{:S(2)}) collective-permute-start(bf16[3,7,32,256]{3,2,1,0:T(8,128)(2,1)S(1)} %get-tuple-element.61.refs_3_), channel_id=1, source_target_pairs={{0,16},{16,0},{1,17},{17,1},{2,18},{18,2},{3,19},{19,3},{4,20},{20... | collective-permute-start | bytes 1032200 | tf_op jit(solution)/shard_map/ppermute | solution.py:343
  68.2 1.4 %copy-start.20 = (bf16[3,7,32,256]{3,2,1,0:T(8,128)(2,1)}, bf16[3,7,32,256]{3,2,1,0:T(8,128)(2,1)S(1)}, u32[]{:S(2)}) copy-start(bf16[3,7,32,256]{3,2,1,0:T(8,128)(2,1)S(1)} %collective-permute-done.18.refs_9_) | copy-start | bytes 1032196
  68.2 23.6 %collective-permute-start.23 = (bf16[3,7,32,256]{3,2,1,0:T(8,128)(2,1)S(1)}, bf16[3,7,32,256]{3,2,1,0:T(8,128)(2,1)}, u32[]{:S(2)}, u32[]{:S(2)}) collective-permute-start(bf16[3,7,32,256]{3,2,1,0:T(8,128)(2,1)S(1)} %get-tuple-element.61.refs_3_), channel_id=1, source_target_pairs={{0,18},{18,0},{2,16},{16,2},{1,19},{19,1},{3,17},{17,3},{4,22},{22... | collective-permute-start | bytes 1032200 | tf_op jit(solution)/shard_map/ppermute | solution.py:344
  69.5 0.7 copy-start.22
  69.5 0.8 copy-start.23
  78.2 13.1 %all-to-all-start.1 = ((bf16[8,8,512]{2,1,0:T(8,128)(2,1)}), bf16[8,8,512]{2,1,0:T(8,128)(2,1)S(1)}, u32[]{:S(2)}, u32[]{:S(2)}) async-start(bf16[8,8,512]{2,1,0:T(8,128)(2,1)} %bitcast.4), calls=%async_computation.1 | async-start | bytes 131072 | tf_op jit(solution)/shard_map/all_to_all | solution.py:473
  84.4 7.5 %collective-permute-start.24 = (bf16[7,128,256]{2,1,0:T(8,128)(2,1)S(1)}, bf16[7,128,256]{2,1,0:T(8,128)(2,1)S(1)}, u32[]{:S(2)}, u32[]{:S(2)}) collective-permute-start(bf16[7,128,256]{2,1,0:T(8,128)(2,1)S(1)} %get-tuple-element.60.refs_2_), channel_id=1, source_target_pairs={{0,1},{1,0},{2,3},{3,2},{4,5},{5,4},{6,7},{7,6},{8,9},{9,8},{10,11... | collective-permute-start | bytes 1376264 | tf_op jit(solution)/shard_map/ppermute | solution.py:349
  84.5 7.4 %collective-permute-start.25 = (bf16[3,7,32,256]{3,2,1,0:T(8,128)(2,1)S(1)}, bf16[3,7,32,256]{3,2,1,0:T(8,128)(2,1)S(1)}, u32[]{:S(2)}, u32[]{:S(2)}) collective-permute-start(bf16[3,7,32,256]{3,2,1,0:T(8,128)(2,1)S(1)} %get-tuple-element.61.refs_3_), channel_id=1, source_target_pairs={{0,1},{1,0},{2,3},{3,2},{4,5},{5,4},{6,7},{7,6},{8,9},{9,8},{10,11... | collective-permute-start | bytes 1032200 | tf_op jit(solution)/shard_map/ppermute | solution.py:349
  85.0 9.2 %copy-start.15 = (bf16[3,7,32,256]{3,2,1,0:T(8,128)(2,1)}, bf16[3,7,32,256]{3,2,1,0:T(8,128)(2,1)S(1)}, u32[]{:S(2)}) copy-start(bf16[3,7,32,256]{3,2,1,0:T(8,128)(2,1)S(1)} %collective-permute-done.21.refs_4_) | copy-start | bytes 1032196
  91.3 1.7 %collective-permute-start.26 = (bf16[3,7,32,256]{3,2,1,0:T(8,128)(2,1)S(1)}, bf16[3,7,32,256]{3,2,1,0:T(8,128)(2,1)S(1)}, u32[]{:S(2)}, u32[]{:S(2)}) collective-permute-start(bf16[3,7,32,256]{3,2,1,0:T(8,128)(2,1)S(1)} %collective-permute-done.21.refs_4_), channel_id=1, source_target_pairs={{0,1},{1,0},{2,3},{3,2},{4,5},{5,4},{6,7},{7,6},{8,9},{9,8},{10,11... | collective-permute-start | bytes 1032200 | tf_op jit(solution)/shard_map/ppermute | solution.py:349
  91.3 2.8 %copy-start.17 = (bf16[3,7,32,256]{3,2,1,0:T(8,128)(2,1)}, bf16[3,7,32,256]{3,2,1,0:T(8,128)(2,1)S(1)}, u32[]{:S(2)}) copy-start(bf16[3,7,32,256]{3,2,1,0:T(8,128)(2,1)S(1)} %collective-permute-done.22.refs_5_) | copy-start | bytes 1032196
  91.3 2.1 %collective-permute-start.27 = (bf16[3,7,32,256]{3,2,1,0:T(8,128)(2,1)S(1)}, bf16[3,7,32,256]{3,2,1,0:T(8,128)(2,1)S(1)}, u32[]{:S(2)}, u32[]{:S(2)}) collective-permute-start(bf16[3,7,32,256]{3,2,1,0:T(8,128)(2,1)S(1)} %collective-permute-done.22.refs_5_), channel_id=1, source_target_pairs={{0,1},{1,0},{2,3},{3,2},{4,5},{5,4},{6,7},{7,6},{8,9},{9,8},{10,11... | collective-permute-start | bytes 1032200 | tf_op jit(solution)/shard_map/ppermute | solution.py:349
  91.8 2.3 %collective-permute-start.28 = (bf16[3,7,32,256]{3,2,1,0:T(8,128)(2,1)}, bf16[3,7,32,256]{3,2,1,0:T(8,128)(2,1)S(1)}, u32[]{:S(2)}, u32[]{:S(2)}) collective-permute-start(bf16[3,7,32,256]{3,2,1,0:T(8,128)(2,1)} %collective-permute-done.23.refs_6_), channel_id=1, source_target_pairs={{0,1},{1,0},{2,3},{3,2},{4,5},{5,4},{6,7},{7,6},{8,9},{9,8},{10,11... | collective-permute-start | bytes 1032200 | tf_op jit(solution)/shard_map/ppermute | solution.py:349
  91.9 2.3 %copy-start.21 = (bf16[3,7,32,256]{3,2,1,0:T(8,128)(2,1)}, bf16[3,7,32,256]{3,2,1,0:T(8,128)(2,1)S(1)}, u32[]{:S(2)}) copy-start(bf16[3,7,32,256]{3,2,1,0:T(8,128)(2,1)S(1)} %collective-permute-done.25.refs_8_) | copy-start | bytes 1032196
  91.9 2.3 %copy-start.14 = (bf16[7,128,256]{2,1,0:T(8,128)(2,1)}, bf16[7,128,256]{2,1,0:T(8,128)(2,1)S(1)}, u32[]{:S(2)}) copy-start(bf16[7,128,256]{2,1,0:T(8,128)(2,1)S(1)} %collective-permute-done.24.refs_7_) | copy-start | bytes 1376260
  93.0 1.2 %copy-start.24 = (bf16[3,7,32,256]{3,2,1,0:T(8,128)(2,1)}, bf16[3,7,32,256]{3,2,1,0:T(8,128)(2,1)S(1)}, u32[]{:S(2)}) copy-start(bf16[3,7,32,256]{3,2,1,0:T(8,128)(2,1)S(1)} %collective-permute-done.26.refs_9_) | copy-start | bytes 1032196
  93.4 0.7 copy-start.25
  94.1 0.7 copy-start.26

commit v3 on v2

--- a/solution.py
+++ b/solution.py
@@ -9,7 +9,7 @@
 
 BF = jnp.bfloat16
 F32 = jnp.float32
-ROWS = 256
+ROWS = 384
 SWAP = [(0, 1), (1, 0)]
 DIAGONAL = [(0, 3), (3, 0), (1, 2), (2, 1)]
 LIMIT = 28 * 2**20
@@ -20,7 +20,7 @@
 
 
 def silu(v):
-    return v / (1.0 + jnp.exp(-v))
+    return v * (0.5 * jnp.tanh(0.5 * v) + 0.5)
 
 
 def normalize(total):
@@ -142,59 +142,58 @@
 
 
 class Parts:
-    def __init__(self, kind, sides, far):
-        self.kind, self.sides, self.far = kind, len(sides), far
-        self.operands = [array for side in sides for array in side]
+    def __init__(self, sides, far, kind="en"):
+        arrays = [array for side in sides for array in side]
+        self.kind, self.sides = kind, len(sides)
+        self.far = [i in far for i in range(len(arrays))]
+        self.near_operands = [array for array, far in zip(arrays, self.far) if not far]
+        self.far_operands = [array for array, far in zip(arrays, self.far) if far]
 
     def scratch(self, hidden, depth):
         found = [pltpu.VMEM(shape, BF) for shape in weight_shapes(self.kind, hidden, depth)]
-        if self.far:
-            found += [pltpu.VMEM(array.shape, BF) for array in self.operands]
-            found += [pltpu.SemaphoreType.DMA((len(self.operands),))]
-        return found
-
-    def start(self, operands, scratch):
-        if not self.far:
-            return []
-        *places, sems = scratch[2 * len(self.kind) :]
-        copies = [pltpu.make_async_copy(src, dst, sems.at[i]) for i, (src, dst) in enumerate(zip(operands, places))]
+        found += [pltpu.VMEM(array.shape, BF) for array in self.far_operands]
+        return found + [pltpu.SemaphoreType.DMA((max(len(self.far_operands), 1),))]
+
+    def load(self, near, far, scratch):
+        weights, sems = named(self.kind, scratch), scratch[-1]
+        staged = scratch[2 * len(self.kind) : -1]
+        copies = [pltpu.make_async_copy(src, dst, sems.at[i]) for i, (src, dst) in enumerate(zip(far, staged))]
         for copy in copies:
             copy.start()
-        return copies
-
-    def finish(self, operands, scratch, copies):
-        weights = named(self.kind, scratch)
-        if self.far:
-            operands = scratch[2 * len(self.kind) : -1]
+        sources, near, staged, waits = [], list(near), list(staged), list(copies)
+        for is_far in self.far:
+            sources.append((staged.pop(0), waits.pop(0)) if is_far else (near.pop(0), None))
         count = lax.axis_size("mesh")
         z = lax.axis_index("mesh")
         x, y = lax.axis_index("band"), lax.axis_index("groups")
         quarters = [2 * y + x, 2 * y + 1 - x, 2 * (1 - y) + x, 2 * (1 - y) + 1 - x]
-        each = len(operands) // self.sides
-        for half in range(self.sides):
-            for copy in copies[half * each : (half + 1) * each]:
-                copy.wait()
-            own, *arrays = operands[half * each : (half + 1) * each]
-            put(own, [z], 0, half, self.kind, weights)
-            for part, src in zip(quarters, arrays):
-                put(src, [z ^ k for k in range(1, count)], part, half, self.kind, weights)
-        return weights
+        each = len(sources) // self.sides
+
+        def place(kind):
+            for wanted in (False, True):
+                for i, (src, wait) in enumerate(sources):
+                    if self.far[i] != wanted:
+                        continue
+                    if wait is not None and kind == "e":
+                        wait.wait()
+                    spot = i % each
+                    if spot == 0:
+                        put(src, [z], 0, i // each, kind, weights)
+                    else:
+                        put(src, [z ^ k for k in range(1, count)], quarters[spot - 1], i // each, kind, weights)
+
+        return weights, place
 
 
 class Whole:
-    far = False
-
-    def __init__(self, kind, arrays):
-        self.kind, self.operands = kind, arrays
+    def __init__(self, arrays, kind="en"):
+        self.near_operands, self.far_operands, self.kind = arrays, [], kind
 
     def scratch(self, hidden, depth):
         return []
 
-    def start(self, operands, scratch):
-        return []
-
-    def finish(self, operands, scratch, copies):
-        return named(self.kind, operands)
+    def load(self, near, far, scratch):
+        return named(self.kind, near), lambda kind: None
 
 
 def join_body(*refs):
@@ -223,17 +222,18 @@
         out[rows, depth:] = dot(one_hot(targets[:, rows], nodes.shape[0]), nodes[...]).astype(BF)
 
 
-def edge_tail(weights, pre):
-    return normalize(dot(silu(pre).astype(BF), weights["eb"][...]))
-
-
-def node_pre(weights, nodes, incoming):
-    depth = nodes.shape[1]
-    return dot(nodes, weights["nm"][0:depth, :]) + dot(incoming, weights["nm"][depth:, :])
-
-
-def node_tail(weights, nodes, incoming):
-    pre = node_pre(weights, nodes, incoming)
+def edges_to_nodes(weights, inputs, table, edge_buffer, targets, message, keep):
+    for at in range(0, message.shape[0], ROWS):
+        rows = slice(at, at + ROWS)
+        pre = dot(inputs(rows), table[...])
+        normed = normalize(dot(silu(pre).astype(BF), weights["eb"][...]))
+        message[rows, :] = normed.astype(BF)
+        if keep:
+            edge_buffer[rows, :] = (edge_buffer[rows, :].astype(F32) + normed).astype(BF)
+
+
+def nodes_after(weights, nodes, incoming):
+    pre = dot(jnp.concatenate([nodes, incoming], axis=1), weights["nm"][...])
     return (nodes.astype(F32) + normalize(dot(silu(pre).astype(BF), weights["nb"][...]))).astype(BF)
 
 
@@ -244,41 +244,35 @@
     return total
 
 
-def first_edges_body(pack, gathered, *refs):
-    count = len(pack.operands)
-    edges, out, buffer, sem, scratch = refs[count], refs[count + 1], refs[count + 2], refs[count + 3], refs[count + 4 :]
+def half_edges_body(pack, gathered, *refs):
+    count = len(pack.near_operands)
+    edges, out, buffer, sem, *scratch = refs[count:]
     fetch = pltpu.make_async_copy(edges, buffer, sem)
     fetch.start()
-    weights = pack.finish(refs[:count], scratch, [])
+    weights, place = pack.load(refs[:count], (), scratch)
+    place("e")
+    fetch.wait()
     for at in range(0, edges.shape[0], ROWS):
         rows = slice(at, at + ROWS)
-        both = gathered.shape[1]
-        pre = dot(gathered[rows, :], weights["em"][0:both, :])
-        if at == 0:
-            fetch.wait()
-        pre = pre + dot(buffer[rows, :], weights["em"][both:, :])
+        pre = dot(jnp.concatenate([gathered[rows, :], buffer[rows, :]], axis=1), weights["em"][...])
         out[rows, :] = dot(silu(pre).astype(BF), weights["eb"][...]).astype(BF)
 
 
-def first_sums_body(targets, *refs):
-    terms, out, message = refs[:-2], refs[-2], refs[-1]
+def half_nodes_body(pack, targets, nodes, mine, other, *refs):
+    count = len(pack.near_operands)
+    out, message, *scratch = refs[count:]
+    weights, place = pack.load(refs[:count], (), scratch)
+    place("n")
     for at in range(0, message.shape[0], ROWS):
         rows = slice(at, at + ROWS)
-        message[rows, :] = normalize(sum_of(terms, rows)).astype(BF)
-    out[...] = dot(one_hot_rows(targets[...], out.shape[0]), message[...]).astype(BF)
-
-
-def first_nodes_body(pack, nodes, incoming, *refs):
-    count = len(pack.operands)
-    out, scratch = refs[count], refs[count + 1 :]
-    weights = pack.finish(refs[:count], scratch, [])
-    pre = node_pre(weights, nodes[...], incoming[...])
+        message[rows, :] = normalize(sum_of((mine, other), rows)).astype(BF)
+    incoming = dot(one_hot_rows(targets[...], nodes.shape[0]), message[...]).astype(BF)
+    pre = dot(jnp.concatenate([nodes[...], incoming], axis=1), weights["nm"][...])
     out[...] = dot(silu(pre).astype(BF), weights["nb"][...]).astype(BF)
 
 
-def first_next_body(nodes, lists, *refs):
-    terms, packed, out, buffer, sem = refs[:-4], refs[-4], refs[-3], refs[-2], refs[-1]
-    buffer[...] = (nodes[...].astype(F32) + normalize(sum_of(terms))).astype(BF)
+def first_next_body(nodes, lists, mine, other, packed, out, buffer, sem):
+    buffer[...] = (nodes[...].astype(F32) + normalize(sum_of((mine, other)))).astype(BF)
     save = pltpu.make_async_copy(buffer, out, sem)
     save.start()
     packed[...] = dot(one_hot(lists[...], nodes.shape[0]), buffer[...]).astype(BF)
@@ -286,48 +280,45 @@
 
 
 def block_body(pack, last, sent, slots, targets, lists, *refs):
-    count = len(pack.operands)
-    refs, operands = refs[count:], refs[:count]
-    if pack.far:
-        nodes, edges, operands, refs = operands[0], operands[1], operands[2:] + refs[:2], refs[2:]
-    else:
-        nodes, edges, refs = refs[0], refs[1], refs[2:]
+    near, far = len(pack.near_operands), len(pack.far_operands)
+    near, refs = refs[:near], refs[near:]
+    nodes, edges, far, refs = refs[0], refs[1], refs[2 : 2 + far], refs[2 + far :]
     if last:
         (out, *refs) = refs
     else:
         (packed, saved, edges_saved, *refs) = refs
-    message, sent_table, node_table, node_buffer, edge_buffer, sems, *scratch = refs
+    message, table, node_buffer, edge_buffer, sems, *scratch = refs
     get_nodes = pltpu.make_async_copy(nodes, node_buffer, sems.at[0])
     get_edges = pltpu.make_async_copy(edges, edge_buffer, sems.at[1])
     get_nodes.start()
     get_edges.start()
-    weights = pack.finish(operands, scratch, pack.start(operands, scratch))
-    em, depth = weights["em"], sent.shape[1]
-    sent_table[...] = dot(sent[...], em[0:depth, :]).astype(BF)
+    weights, place = pack.load(near, far, scratch)
+    place("e")
+    em, depth, count = weights["em"], sent.shape[1], nodes.shape[0]
+    table[0:depth, :] = em[2 * depth :, :]
     get_nodes.wait()
-    node_table[...] = dot(node_buffer[...], em[depth : 2 * depth, :]).astype(BF)
+    table[depth : depth + count, :] = dot(node_buffer[...], em[depth : 2 * depth, :]).astype(BF)
+    table[depth + count :, :] = dot(sent[...], em[0:depth, :]).astype(BF)
     get_edges.wait()
-    for at in range(0, message.shape[0], ROWS):
-        rows = slice(at, at + ROWS)
-        pre = dot(edge_buffer[rows, :], em[2 * depth :, :])
-        pre = pre + dot(one_hot(targets[:, rows], nodes.shape[0]), node_table[...])
-        pre = pre + dot(one_hot(slots[:, rows], sent.shape[0]), sent_table[...])
-        normed = edge_tail(weights, pre)
-        message[rows, :] = normed.astype(BF)
-        if not last:
-            edge_buffer[rows, :] = (edge_buffer[rows, :].astype(F32) + normed).astype(BF)
+
+    def inputs(rows):
+        picks = [one_hot(targets[:, rows], count), one_hot(slots[:, rows], sent.shape[0])]
+        return jnp.concatenate([edge_buffer[rows, :]] + picks, axis=1)
+
+    edges_to_nodes(weights, inputs, table, edge_buffer, targets, message, not last)
     if not last:
         save_edges = pltpu.make_async_copy(edge_buffer, edges_saved, sems.at[2])
         save_edges.start()
-    incoming = dot(one_hot_rows(targets[...], nodes.shape[0]), message[...]).astype(BF)
-    new = node_tail(weights, node_buffer[...], incoming)
+    place("n")
+    incoming = dot(one_hot_rows(targets[...], count), message[...]).astype(BF)
+    new = nodes_after(weights, node_buffer[...], incoming)
     if last:
         out[...] = new
         return
     node_buffer[...] = new
     save_nodes = pltpu.make_async_copy(node_buffer, saved, sems.at[3])
     save_nodes.start()
-    packed[...] = dot(one_hot(lists[...], nodes.shape[0]), new).astype(BF)
+    packed[...] = dot(one_hot(lists[...], count), new).astype(BF)
     save_edges.wait()
     save_nodes.wait()
 
@@ -360,15 +351,12 @@
     eb, nb = joined(edge_back, "width", "mesh"), joined(node_back, "width", "mesh")
     em = em.reshape(em.shape[0], -1, em.shape[3])
     nm = nm.reshape(nm.shape[0], -1, nm.shape[3])
-    found = []
     cols = edge_mats.shape[3]
     at = lax.axis_index("width") * cols
+    found = []
     for kind, mats, back in (("e", em[0], eb[0]), ("n", nm[0], nb[0])):
-        mine = [lax.dynamic_slice_in_dim(mats, at, cols, 1), lax.dynamic_slice_in_dim(back, at, cols, 0)]
-        found.append(Whole(kind, mine))
-    for block in range(1, em.shape[0]):
-        found.append(Whole("en", [em[block], eb[block], nm[block], nb[block]]))
-    return found
+        found.append(Whole([lax.dynamic_slice_in_dim(mats, at, cols, 1), lax.dynamic_slice_in_dim(back, at, cols, 0)], kind))
+    return found + [Whole([em[block], eb[block], nm[block], nb[block]]) for block in range(1, em.shape[0])]
 
 
 def on_device(
@@ -417,7 +405,6 @@
         [joined0] = join(turned0[:-1] + [after(turned0[-1], from_upper, from_lower, cut12)], 1)
         plane0 = over_plane(joined0)
         side0 = [own0, joined0] + plane0
-        packs = [Parts("e", [side0], False), Parts("n", [side0], False), None, None]
         joined1, joined2 = join(over_slices(after(cut12, joined0)), 2)
         from_lower = after(from_lower, joined1)
     else:
@@ -429,31 +416,25 @@
         [grid_latent, from_lower, from_upper, mesh_latent, encoder_slot[None, :], encoder_target[None, :]],
         cost=1.2,
     )
-    pack = packs[0]
+    if by_parts:
+        packs = [Parts([side0], [], "e"), Parts([side0], [], "n")]
     term = call(
-        functools.partial(first_edges_body, pack),
+        functools.partial(half_edges_body, packs[0]),
         (grid_edges, depth),
-        [pltpu.VMEM((grid_edges, depth), BF), pltpu.SemaphoreType.DMA(())] + pack.scratch(hidden // 2, depth),
-        [gathered] + pack.operands,
+        [pltpu.VMEM((grid_edges, depth), BF), pltpu.SemaphoreType.DMA(())] + packs[0].scratch(hidden // 2, depth),
+        [gathered] + packs[0].near_operands,
         [grid_edge],
         cost=3.0,
     )
     if by_parts:
         plane1 = over_plane(after(joined1, term))
-    incoming = call(
-        first_sums_body,
+    before = term
+    term = call(
+        functools.partial(half_nodes_body, packs[1]),
         (nodes, depth),
-        [pltpu.VMEM((grid_edges, depth), BF)],
-        [encoder_target[None, :], term, swap_width(term)],
-        cost=0.8,
-    )
-    pack = packs[1]
-    term = call(
-        functools.partial(first_nodes_body, pack),
-        (nodes, depth),
-        pack.scratch(hidden // 2, depth),
-        [mesh_latent, incoming] + pack.operands,
-        cost=0.8,
+        [pltpu.VMEM((grid_edges, depth), BF)] + packs[1].scratch(hidden // 2, depth),
+        [encoder_target[None, :], mesh_latent, term, swap_width(term)] + packs[1].near_operands,
+        cost=1.6,
     )
     packed, rows = call(
         first_next_body,
@@ -465,30 +446,28 @@
     )
     edges = mesh_edge
     slots, targets = mesh_slot[None, :], mesh_target[None, :]
-    early = incoming
     for block in range(1, edge_mats.shape[0]):
         last = block == edge_mats.shape[0] - 1
-        pack = packs[block + 1]
         cut_rows = packed.reshape(send_lists.shape[1:] + (depth,))
         sent = lax.all_to_all(cut_rows, ("mesh", "band"), split_axis=0, concat_axis=0, tiled=True).reshape(-1, depth)
         if by_parts:
             if not last:
-                plane2 = over_plane(after(joined2, sent, *plane1))
+                plane2 = over_plane(after(joined2, sent))
                 side = [own1, joined1] + plane1
             else:
                 side = [own2, joined2] + plane2
-            other = [swap_width(after(a, early)) for a in side[:2]] + [swap_width(after(a, sent)) for a in side[2:]]
-            pack = Parts("en", [side, other], True)
-            early = sent
-        near = [sent, slots, targets, lists]
+            other = [swap_width(after(a, before)) for a in side[:2]] + [swap_width(after(a, sent)) for a in side[2:]]
+            pack = Parts([side, other], range(7))
+            before = sent
+        else:
+            pack = packs[block + 1]
+        table = pltpu.VMEM((depth + nodes + sent_rows, hidden), BF)
         got = call(
             functools.partial(block_body, pack, last),
             (nodes, depth) if last else [(sent_rows, depth), (nodes, depth), (mesh_edges, depth)],
-            [edge_buffer, pltpu.VMEM((sent_rows, hidden), BF), pltpu.VMEM((nodes, hidden), BF), node_buffer, edge_buffer]
-            + [pltpu.SemaphoreType.DMA((4,))]
-            + pack.scratch(hidden, depth),
-            near if pack.far else near + pack.operands,
-            [rows, edges] + (pack.operands if pack.far else []),
+            [edge_buffer, table, node_buffer, edge_buffer, pltpu.SemaphoreType.DMA((4,))] + pack.scratch(hidden, depth),
+            [sent, slots, targets, lists] + pack.near_operands,
+            [rows, edges] + pack.far_operands,
             cost=6.5,
             far=0 if last else 2,
             keep=not last,

time: 103 us -> 98.6 us (0.957)
  Pallas kernels: 25.4 us -> 23.1 us
  local copies, waits for them, and re-layouts: 1.68 us -> 0.17 us
    pallas_call x12 -> x11, Pallas kernels: 25.4 us -> 23.1 us  [call(): pl.pallas_call(body, out_shape=shapes if many else shapes[0], in_specs=sp...]
    unnamed x54 -> x38, local copies, waits for them, and re-layouts: 1.59 us -> 0.08 us
  transfers between devices with their start and end apart: 31 -> 31, of which waited for: 13 -> 13; matrix products, arithmetic and copies ran while one was open for 0% -> 0% of each run, Pallas kernels for 13% -> 12%
where the time goes in v3:
time: 98.6 us; the launch traced here: 98.2 us
  starting transfers between devices  47.4 us (48%)
  waiting for transfers between devices  27 us (27%)
  Pallas kernels  23.1 us (23%)
    pallas_call x11, Pallas kernels, call(): pl.pallas_call(body, out_shape=shapes if many else shapes[0], in_specs=sp...  23.1 us
    all_to_all x2, waiting for transfers between devices, on_device(): lax.all_to_all(cut_rows, ('mesh', 'band'), split_axis=0, concat_axis=0, t...  12.8 us
    all_to_all x2, starting transfers between devices, on_device(): lax.all_to_all(cut_rows, ('mesh', 'band'), split_axis=0, concat_axis=0, t...  12.3 us
    ppermute x6, starting transfers between devices, over_slices(): lax.ppermute(chunk, 'mesh', [(i, i ^ k) for i in range(count)])  11 us
    ppermute x3, starting transfers between devices, over_plane(): lax.ppermute(own, ('groups', 'band'), DIAGONAL)  8.33 us
    ppermute x6, waiting for transfers between devices, over_slices(): lax.ppermute(chunk, 'mesh', [(i, i ^ k) for i in range(count)])  6.17 us
    ppermute x12, waiting for transfers between devices, swap_width(): return lax.ppermute(array, 'width', SWAP)  4.52 us
    ppermute x3, starting transfers between devices, over_plane(): lax.ppermute(own, 'band', SWAP)  4.21 us
  transfers between devices with their start and end apart: 31, of which 13 were waited for; matrix products, arithmetic and copies ran while one was open for 0% of the time, Pallas kernels for 12%

profile of v3, /device:TPU:0, one launch (start us, length us, event | category | flops | bytes accessed | tf_op | source)
XLA Modules:
  0.0 98.2 jit_solution(14685980604990873974)
XLA Ops:
  0.0 0.9 shard_map.146
  0.9 3.1 %collective-permute-start = (bf16[7,32,256]{2,1,0:T(8,128)(2,1)S(1)}, bf16[7,32,256]{2,1,0:T(8,128)(2,1)S(1)}, u32[]{:S(2)}, u32[]{:S(2)}) collective-permute-start(bf16[7,32,256]{2,1,0:T(8,128)(2,1)S(1)} %shard_map.146), channel_id=1, source_target_pairs={{0,4},{4,0},{8,12},{12,8},{1,5},{5,1},{9,13},{13,9},{2,6},{6,2},{1... | collective-permute-start | bytes 344072 | tf_op jit(solution)/shard_map/ppermute | solution.py:328
  4.0 2.5 %collective-permute-start.3 = (bf16[7,32,256]{2,1,0:T(8,128)(2,1)S(1)}, bf16[7,32,256]{2,1,0:T(8,128)(2,1)S(1)}, u32[]{:S(2)}, u32[]{:S(2)}) collective-permute-start(bf16[7,32,256]{2,1,0:T(8,128)(2,1)S(1)} %shard_map.146), channel_id=1, source_target_pairs={{0,12},{4,8},{8,4},{12,0},{1,13},{5,9},{9,5},{13,1},{2,14},{6,10},... | collective-permute-start | bytes 344072 | tf_op jit(solution)/shard_map/ppermute | solution.py:328
  6.5 0.1 collective-permute-start.2
  6.6 0.3 shard_map.145
  7.0 0.2 collective-permute-done.refs_0_
  7.2 3.6 %collective-permute-start.1 = (bf16[64,512]{1,0:T(8,128)(2,1)S(1)}, bf16[64,512]{1,0:T(8,128)(2,1)S(1)}, u32[]{:S(2)}, u32[]{:S(2)}) collective-permute-start(bf16[64,512]{1,0:T(8,128)(2,1)S(1)} %get-tuple-element.34), channel_id=1, source_target_pairs={{0,2},{2,4},{4,6},{6,8},{8,10},{10,12},{12,14},{1,3},{3,5},{5,7},{... | collective-permute-start | bytes 196616 | tf_op jit(solution)/shard_map/ppermute | solution.py:403
  10.8 0.0 copy-start.8
  10.8 0.0 copy-start.9
  10.8 1.3 %collective-permute-start.4 = (bf16[64,512]{1,0:T(8,128)(2,1)S(1)}, bf16[64,512]{1,0:T(8,128)(2,1)S(1)}, u32[]{:S(2)}, u32[]{:S(2)}) collective-permute-start(bf16[64,512]{1,0:T(8,128)(2,1)S(1)} %get-tuple-element.37), channel_id=1, source_target_pairs={{2,0},{4,2},{6,4},{8,6},{10,8},{12,10},{14,12},{3,1},{5,3},{7,5},{... | collective-permute-start | bytes 196616 | tf_op jit(solution)/shard_map/ppermute | solution.py:402
  12.1 1.8 %shard_map.147 = (bf16[14,32,256]{2,1,0:T(8,128)(2,1)S(1)}, bf16[7,128,256]{2,1,0:T(8,128)(2,1)S(1)}, bf16[7,128,256]{2,1,0:T(8,128)(2,1)S(1)}, bf16[7,128,256]{2,1,0:T(8,128)(2,1)S(1)}) custom-call(bf16[3,3,128,256]{3,2,1,0:T(8,128)(2,1)} %refs_0_.3, bf16[3,256,128]{2,1,0:T(8,128)(2,1)} %refs_1_.3, bf16[3,2,128,256]{3,2,1,0:T(8,128)(2,1)} %refs_2_.3, ...), custom_call_target="tpu_custom_call" | custom-call | flops 500000000 | tf_op jit(solution)/shard_map/pallas_call | solution.py:59
  13.9 0.0 collective-permute-done.1.low
  13.9 3.0 %collective-permute-done.4.high = bf16[64,512]{1,0:T(8,128)(2,1)S(1)} collective-permute-done((bf16[64,512]{1,0:T(8,128)(2,1)S(1)}, bf16[64,512]{1,0:T(8,128)(2,1)S(1)}, u32[]{:S(2)}, u32[]{:S(2)}) %collective-permute-start.4) | collective-permute-done | bytes 65568 | tf_op jit(solution)/shard_map/ppermute | solution.py:402
  16.9 0.7 collective-permute-done.2.refs_1_
  17.6 1.6 %collective-permute-start.5 = (bf16[14,32,256]{2,1,0:T(8,128)(2,1)S(1)}, bf16[14,32,256]{2,1,0:T(8,128)(2,1)S(1)}, u32[]{:S(2)}, u32[]{:S(2)}) collective-permute-start(bf16[14,32,256]{2,1,0:T(8,128)(2,1)S(1)} %get-tuple-element.39), channel_id=1, source_target_pairs={{0,4},{4,0},{8,12},{12,8},{1,5},{5,1},{9,13},{13,9},{2,6},{6,2},{1... | collective-permute-start | bytes 688136 | tf_op jit(solution)/shard_map/ppermute | solution.py:328
  19.3 3.3 %collective-permute-start.6 = (bf16[14,32,256]{2,1,0:T(8,128)(2,1)S(1)}, bf16[14,32,256]{2,1,0:T(8,128)(2,1)S(1)}, u32[]{:S(2)}, u32[]{:S(2)}) collective-permute-start(bf16[14,32,256]{2,1,0:T(8,128)(2,1)S(1)} %get-tuple-element.39), channel_id=1, source_target_pairs={{0,8},{4,12},{8,0},{12,4},{1,9},{5,13},{9,1},{13,5},{2,10},{6,14},... | collective-permute-start | bytes 688136 | tf_op jit(solution)/shard_map/ppermute | solution.py:328
  22.6 0.4 collective-permute-start.7
  22.9 2.0 %collective-permute-start.8 = (bf16[3,7,32,256]{3,2,1,0:T(8,128)(2,1)S(1)}, bf16[3,7,32,256]{3,2,1,0:T(8,128)(2,1)S(1)}, u32[]{:S(2)}, u32[]{:S(2)}) collective-permute-start(bf16[3,7,32,256]{3,2,1,0:T(8,128)(2,1)S(1)} %shard_map.148.refs_1_), channel_id=1, source_target_pairs={{0,2},{2,0},{1,3},{3,1},{4,6},{6,4},{5,7},{7,5},{8,10},{10,8},{9,1... | collective-permute-start | bytes 1032200 | tf_op jit(solution)/shard_map/ppermute | solution.py:333
  24.9 1.5 %collective-permute-start.9 = (bf16[3,7,32,256]{3,2,1,0:T(8,128)(2,1)S(1)}, bf16[3,7,32,256]{3,2,1,0:T(8,128)(2,1)S(1)}, u32[]{:S(2)}, u32[]{:S(2)}) collective-permute-start(bf16[3,7,32,256]{3,2,1,0:T(8,128)(2,1)S(1)} %shard_map.148.refs_1_), channel_id=1, source_target_pairs={{0,16},{16,0},{1,17},{17,1},{2,18},{18,2},{3,19},{19,3},{4,20},{20... | collective-permute-start | bytes 1032200 | tf_op jit(solution)/shard_map/ppermute | solution.py:334
  26.4 0.6 collective-permute-done.5.refs_0_
  27.0 6.2 %collective-permute-start.10 = (bf16[3,7,32,256]{3,2,1,0:T(8,128)(2,1)S(1)}, bf16[3,7,32,256]{3,2,1,0:T(8,128)(2,1)S(1)}, u32[]{:S(2)}, u32[]{:S(2)}) collective-permute-start(bf16[3,7,32,256]{3,2,1,0:T(8,128)(2,1)S(1)} %shard_map.148.refs_1_), channel_id=1, source_target_pairs={{0,18},{18,0},{2,16},{16,2},{1,19},{19,1},{3,17},{17,3},{4,22},{22... | collective-permute-start | bytes 1032200 | tf_op jit(solution)/shard_map/ppermute | solution.py:335
  33.2 4.7 %collective-permute-done.6.refs_1_ = bf16[14,32,256]{2,1,0:T(8,128)(2,1)S(1)} collective-permute-done((bf16[14,32,256]{2,1,0:T(8,128)(2,1)S(1)}, bf16[14,32,256]{2,1,0:T(8,128)(2,1)S(1)}, u32[]{:S(2)}, u32[]{:S(2)}) %collective-permute-start.6) | collective-permute-done | bytes 229408 | tf_op jit(solution)/shard_map/ppermute | solution.py:328
  37.9 0.0 collective-permute-done.7.refs_2_
  38.0 1.2 %shard_map.150.gathered = bf16[768,1024]{1,0:T(8,128)(2,1)S(1)} custom-call(bf16[512,512]{1,0:T(8,128)(2,1)S(1)} %copy-done, bf16[64,512]{1,0:T(8,128)(2,1)S(1)} %collective-permute-done.1.low, bf16[64,512]{1,0:T(8,128)(2,1)S(1)} %collective-permute-done.4.high, bf16[320,512]{1,0:T(8,128)(2,1)S(1)} %copy-done.5, s32[1,768]{1,0:T(1,128)S(1)} %broadcast_in_dim.22.slots, ...), custom_call_target="tpu_custom_call" | custom-call | flops 1200000000 | tf_op jit(solution)/shard_map/pallas_call | solution.py:59
  39.2 0.0 collective-permute-done.8.refs_2_
  39.3 0.2 collective-permute-done.9.refs_3_
  39.4 3.1 %shard_map.151.mine = bf16[768,512]{1,0:T(8,128)(2,1)S(1)} custom-call(bf16[768,1024]{1,0:T(8,128)(2,1)S(1)} %shard_map.150.gathered, bf16[7,128,256]{2,1,0:T(8,128)(2,1)S(1)} %get-tuple-element.42.refs_0_, bf16[3,7,32,256]{3,2,1,0:T(8,128)(2,1)S(1)} %shard_map.148.refs_1_, bf16[3,7,32,256]{3,2,1,0:T(8,128)(2,1)S(1)} %collective-permute-done.8.refs_2_, ...), custom_call_target="tpu_custom_call" | custom-call | flops 3000000000 | tf_op jit(solution)/shard_map/pallas_call | solution.py:59
  42.5 0.0 copy-start.12
  42.5 0.1 collective-permute-start.11
  42.6 2.3 %collective-permute-done.11.other = bf16[768,512]{1,0:T(8,128)(2,1)S(1)} collective-permute-done((bf16[768,512]{1,0:T(8,128)(2,1)S(1)}, bf16[768,512]{1,0:T(8,128)(2,1)S(1)}, u32[]{:S(2)}, u32[]{:S(2)}) %collective-permute-start.11) | collective-permute-done | bytes 786464 | tf_op jit(solution)/shard_map/ppermute | solution.py:340
  44.9 1.4 %shard_map.152.mine = bf16[320,512]{1,0:T(8,128)(2,1)S(1)} custom-call(s32[1,768]{1,0:T(1,128)S(1)} %broadcast_in_dim.19.targets, bf16[320,512]{1,0:T(8,128)(2,1)S(1)} %copy-done.5, bf16[768,512]{1,0:T(8,128)(2,1)S(1)} %shard_map.151.mine, bf16[768,512]{1,0:T(8,128)(2,1)S(1)} %collective-permute-done.11.other, ...), custom_call_target="tpu_custom_call" | custom-call | flops 1600000000 | tf_op jit(solution)/shard_map/pallas_call | solution.py:59
  46.2 0.2 collective-permute-start.12
  46.4 1.1 %collective-permute-start.13 = (bf16[3,7,32,256]{3,2,1,0:T(8,128)(2,1)S(1)}, bf16[3,7,32,256]{3,2,1,0:T(8,128)(2,1)S(1)}, u32[]{:S(2)}, u32[]{:S(2)}) collective-permute-start(bf16[3,7,32,256]{3,2,1,0:T(8,128)(2,1)S(1)} %get-tuple-element.44.refs_6_), channel_id=1, source_target_pairs={{0,2},{2,0},{1,3},{3,1},{4,6},{6,4},{5,7},{7,5},{8,10},{10,8},{9,1... | collective-permute-start | bytes 1032200 | tf_op jit(solution)/shard_map/ppermute | solution.py:333
  47.6 1.4 %collective-permute-start.15 = (bf16[3,7,32,256]{3,2,1,0:T(8,128)(2,1)S(1)}, bf16[3,7,32,256]{3,2,1,0:T(8,128)(2,1)}, u32[]{:S(2)}, u32[]{:S(2)}) collective-permute-start(bf16[3,7,32,256]{3,2,1,0:T(8,128)(2,1)S(1)} %get-tuple-element.44.refs_6_), channel_id=1, source_target_pairs={{0,16},{16,0},{1,17},{17,1},{2,18},{18,2},{3,19},{19,3},{4,20},{20... | collective-permute-start | bytes 1032200 | tf_op jit(solution)/shard_map/ppermute | solution.py:334
  49.0 0.9 collective-permute-start.17
  50.0 0.1 reshape.15.lists
  50.1 1.6 %shard_map.153 = (bf16[64,512]{1,0:T(8,128)(2,1)}, bf16[320,512]{1,0:T(8,128)(2,1)}) custom-call(bf16[320,512]{1,0:T(8,128)(2,1)S(1)} %copy-done.5, s32[1,64]{1,0:T(1,128)S(1)} %reshape.15.lists, bf16[320,512]{1,0:T(8,128)(2,1)S(1)} %shard_map.152.mine, bf16[320,512]{1,0:T(8,128)(2,1)S(1)} %collective-permute-done.12.other), custom_call_target="tpu_custom_call" | custom-call | flops 1600000000 | tf_op jit(solution)/shard_map/pallas_call | solution.py:59
  51.7 6.2 %all-to-all-start = ((bf16[8,8,512]{2,1,0:T(8,128)(2,1)}), bf16[8,8,512]{2,1,0:T(8,128)(2,1)S(1)}, u32[]{:S(2)}, u32[]{:S(2)}) async-start(bf16[8,8,512]{2,1,0:T(8,128)(2,1)} %bitcast.2), calls=%async_computation | async-start | bytes 131072 | tf_op jit(solution)/shard_map/all_to_all | solution.py:452
  57.9 0.1 collective-permute-start.19
  57.9 0.5 collective-permute-start.20
  58.4 0.0 collective-permute-done.13.refs_7_
  58.4 6.5 %all-to-all-done = bf16[8,8,512]{2,1,0:T(8,128)(2,1)S(1)} async-done(((bf16[8,8,512]{2,1,0:T(8,128)(2,1)}), bf16[8,8,512]{2,1,0:T(8,128)(2,1)S(1)}, u32[]{:S(2)}, u32[]{:S(2)}) %all-to-all-start) | async-done | bytes 65568 | tf_op jit(solution)/shard_map/all_to_all | solution.py:452
  64.9 0.5 collective-permute-start.16
  65.4 0.4 collective-permute-done.17.refs_9_
  65.8 0.0 collective-permute-start.18
  65.8 0.0 collective-permute-done.20.refs_11_
  65.9 1.1 %collective-permute-start.21 = (bf16[3,7,32,256]{3,2,1,0:T(8,128)(2,1)S(1)}, bf16[3,7,32,256]{3,2,1,0:T(8,128)(2,1)S(1)}, u32[]{:S(2)}, u32[]{:S(2)}) collective-permute-start(bf16[3,7,32,256]{3,2,1,0:T(8,128)(2,1)S(1)} %get-tuple-element.53.refs_6_), channel_id=1, source_target_pairs={{0,2},{2,0},{1,3},{3,1},{4,6},{6,4},{5,7},{7,5},{8,10},{10,8},{9,1... | collective-permute-start | bytes 1032200 | tf_op jit(solution)/shard_map/ppermute | solution.py:333
  67.0 1.2 %collective-permute-start.23 = (bf16[3,7,32,256]{3,2,1,0:T(8,128)(2,1)S(1)}, bf16[3,7,32,256]{3,2,1,0:T(8,128)(2,1)S(1)}, u32[]{:S(2)}, u32[]{:S(2)}) collective-permute-start(bf16[3,7,32,256]{3,2,1,0:T(8,128)(2,1)S(1)} %get-tuple-element.53.refs_6_), channel_id=1, source_target_pairs={{0,16},{16,0},{1,17},{17,1},{2,18},{18,2},{3,19},{19,3},{4,20},{20... | collective-permute-start | bytes 1032200 | tf_op jit(solution)/shard_map/ppermute | solution.py:334
  68.2 1.2 %collective-permute-start.25 = (bf16[3,7,32,256]{3,2,1,0:T(8,128)(2,1)S(1)}, bf16[3,7,32,256]{3,2,1,0:T(8,128)(2,1)}, u32[]{:S(2)}, u32[]{:S(2)}) collective-permute-start(bf16[3,7,32,256]{3,2,1,0:T(8,128)(2,1)S(1)} %get-tuple-element.53.refs_6_), channel_id=1, source_target_pairs={{0,18},{18,0},{2,16},{16,2},{1,19},{19,1},{3,17},{17,3},{4,22},{22... | collective-permute-start | bytes 1032200 | tf_op jit(solution)/shard_map/ppermute | solution.py:335
  69.4 0.0 collective-permute-done.16.refs_1_
  69.4 0.0 collective-permute-done.18.refs_2_
  69.4 6.6 %shard_map.154 = (bf16[64,512]{1,0:T(8,128)(2,1)}, bf16[320,512]{1,0:T(8,128)(2,1)}, bf16[768,512]{1,0:T(8,128)(2,1)}) custom-call(bf16[64,512]{1,0:T(8,128)(2,1)S(1)} %bitcast.6, s32[1,768]{1,0:T(1,128)S(1)} %broadcast_in_dim.23.slots, s32[1,768]{1,0:T(1,128)S(1)} %broadcast_in_dim.24.targets, s32[1,64]{1,0:T(1,128)S(1)} %reshape.15.lists, ...), custom_call_target="tpu_custom_call" | custom-call | flops 6499999744 | tf_op jit(solution)/shard_map/pallas_call | solution.py:59
  76.0 6.2 %all-to-all-start.1 = ((bf16[8,8,512]{2,1,0:T(8,128)(2,1)}), bf16[8,8,512]{2,1,0:T(8,128)(2,1)S(1)}, u32[]{:S(2)}, u32[]{:S(2)}) async-start(bf16[8,8,512]{2,1,0:T(8,128)(2,1)} %bitcast.4), calls=%async_computation.1 | async-start | bytes 131072 | tf_op jit(solution)/shard_map/all_to_all | solution.py:452
  82.2 0.1 collective-permute-start.27
  82.3 0.5 collective-permute-start.28
  82.8 0.0 collective-permute-done.21.refs_7_
  82.8 6.3 %all-to-all-done.1 = bf16[8,8,512]{2,1,0:T(8,128)(2,1)S(1)} async-done(((bf16[8,8,512]{2,1,0:T(8,128)(2,1)}), bf16[8,8,512]{2,1,0:T(8,128)(2,1)S(1)}, u32[]{:S(2)}, u32[]{:S(2)}) %all-to-all-start.1) | async-done | bytes 65568 | tf_op jit(solution)/shard_map/all_to_all | solution.py:452
  89.1 0.5 collective-permute-start.24
  89.6 0.1 collective-permute-start.26
  89.7 0.0 collective-permute-done.28.refs_11_
  89.7 1.0 %collective-permute-done.22.refs_0_ = bf16[3,7,32,256]{3,2,1,0:T(8,128)(2,1)S(1)} collective-permute-done((bf16[3,7,32,256]{3,2,1,0:T(8,128)(2,1)S(1)}, bf16[3,7,32,256]{3,2,1,0:T(8,128)(2,1)S(1)}, u32[]{:S(2)}, u32[]{:S(2)}) %collective-permute-start.22) | collective-permute-done | bytes 344096 | tf_op jit(solution)/shard_map/ppermute | solution.py:340
  90.7 0.5 collective-permute-done.24.refs_1_
  91.2 0.7 collective-permute-done.26.refs_2_
  92.0 6.1 %shard_map.155 = bf16[320,512]{1,0:T(8,128)(2,1)} custom-call(bf16[64,512]{1,0:T(8,128)(2,1)S(1)} %bitcast.7, s32[1,768]{1,0:T(1,128)S(1)} %broadcast_in_dim.23.slots, s32[1,768]{1,0:T(1,128)S(1)} %broadcast_in_dim.24.targets, s32[1,64]{1,0:T(1,128)S(1)} %reshape.15.lists, bf16[3,7,32,256]{3,2,1,0:T(8,128)(2,1)S(1)} %collective-permute-done.22.refs_0_, ...), custom_call_target="tpu_custom_call" | custom-call | flops 6499999744 | tf_op jit(solution)/shard_map/pallas_call | solution.py:59
  (52 shorter events, 0.2 us)
Async XLA Ops:
  0.0 6.6 %copy-start = (bf16[512,512]{1,0:T(8,128)(2,1)S(1)}, bf16[512,512]{1,0:T(8,128)(2,1)}, u32[]{:S(2)}) copy-start(bf16[512,512]{1,0:T(8,128)(2,1)} %grid.3) | copy-start | bytes 1572868
  0.0 6.6 %copy-start.6 = (s32[64]{0:T(128)S(1)}, s32[64]{0:T(128)}, u32[]{:S(2)}) copy-start(s32[64]{0:T(128)} %param.21) | copy-start | bytes 772
  0.0 6.6 %copy-start.7 = (s32[64]{0:T(128)S(1)}, s32[64]{0:T(128)}, u32[]{:S(2)}) copy-start(s32[64]{0:T(128)} %param.22) | copy-start | bytes 772
  0.9 6.2 %collective-permute-start = (bf16[7,32,256]{2,1,0:T(8,128)(2,1)S(1)}, bf16[7,32,256]{2,1,0:T(8,128)(2,1)S(1)}, u32[]{:S(2)}, u32[]{:S(2)}) collective-permute-start(bf16[7,32,256]{2,1,0:T(8,128)(2,1)S(1)} %shard_map.146), channel_id=1, source_target_pairs={{0,4},{4,0},{8,12},{12,8},{1,5},{5,1},{9,13},{13,9},{2,6},{6,2},{1... | collective-permute-start | bytes 344072 | tf_op jit(solution)/shard_map/ppermute | solution.py:328
  4.0 9.9 %collective-permute-start.3 = (bf16[7,32,256]{2,1,0:T(8,128)(2,1)S(1)}, bf16[7,32,256]{2,1,0:T(8,128)(2,1)S(1)}, u32[]{:S(2)}, u32[]{:S(2)}) collective-permute-start(bf16[7,32,256]{2,1,0:T(8,128)(2,1)S(1)} %shard_map.146), channel_id=1, source_target_pairs={{0,12},{4,8},{8,4},{12,0},{1,13},{5,9},{9,5},{13,1},{2,14},{6,10},... | collective-permute-start | bytes 344072 | tf_op jit(solution)/shard_map/ppermute | solution.py:328
  6.5 11.1 %collective-permute-start.2 = (bf16[7,32,256]{2,1,0:T(8,128)(2,1)S(1)}, bf16[7,32,256]{2,1,0:T(8,128)(2,1)S(1)}, u32[]{:S(2)}, u32[]{:S(2)}) collective-permute-start(bf16[7,32,256]{2,1,0:T(8,128)(2,1)S(1)} %shard_map.146), channel_id=1, source_target_pairs={{0,8},{4,12},{8,0},{12,4},{1,9},{5,13},{9,1},{13,5},{2,10},{6,14},... | collective-permute-start | bytes 344072 | tf_op jit(solution)/shard_map/ppermute | solution.py:328
  7.2 6.7 %collective-permute-start.1 = (bf16[64,512]{1,0:T(8,128)(2,1)S(1)}, bf16[64,512]{1,0:T(8,128)(2,1)S(1)}, u32[]{:S(2)}, u32[]{:S(2)}) collective-permute-start(bf16[64,512]{1,0:T(8,128)(2,1)S(1)} %get-tuple-element.34), channel_id=1, source_target_pairs={{0,2},{2,4},{4,6},{6,8},{8,10},{10,12},{12,14},{1,3},{3,5},{5,7},{... | collective-permute-start | bytes 196616 | tf_op jit(solution)/shard_map/ppermute | solution.py:403
  10.8 22.4 %copy-start.8 = (s32[768]{0:T(1024)S(1)}, s32[768]{0:T(1024)}, u32[]{:S(2)}) copy-start(s32[768]{0:T(1024)} %param.20) | copy-start | bytes 9220
  10.8 22.4 %copy-start.9 = (s32[768]{0:T(1024)S(1)}, s32[768]{0:T(1024)}, u32[]{:S(2)}) copy-start(s32[768]{0:T(1024)} %param.19) | copy-start | bytes 9220
  10.8 6.2 %collective-permute-start.4 = (bf16[64,512]{1,0:T(8,128)(2,1)S(1)}, bf16[64,512]{1,0:T(8,128)(2,1)S(1)}, u32[]{:S(2)}, u32[]{:S(2)}) collective-permute-start(bf16[64,512]{1,0:T(8,128)(2,1)S(1)} %get-tuple-element.37), channel_id=1, source_target_pairs={{2,0},{4,2},{6,4},{8,6},{10,8},{12,10},{14,12},{3,1},{5,3},{7,5},{... | collective-permute-start | bytes 196616 | tf_op jit(solution)/shard_map/ppermute | solution.py:402
  13.9 44.0 %copy-start.2 = (bf16[7,128,256]{2,1,0:T(8,128)(2,1)}, bf16[7,128,256]{2,1,0:T(8,128)(2,1)S(1)}, u32[]{:S(2)}) copy-start(bf16[7,128,256]{2,1,0:T(8,128)(2,1)S(1)} %get-tuple-element.50.refs_5_) | copy-start | bytes 1376260
  13.9 68.3 %copy-start.1 = (bf16[7,128,256]{2,1,0:T(8,128)(2,1)}, bf16[7,128,256]{2,1,0:T(8,128)(2,1)S(1)}, u32[]{:S(2)}) copy-start(bf16[7,128,256]{2,1,0:T(8,128)(2,1)S(1)} %get-tuple-element.60.refs_5_) | copy-start | bytes 1376260
  16.9 21.1 %copy-start.5 = (bf16[320,512]{1,0:T(8,128)(2,1)S(1)}, bf16[320,512]{1,0:T(8,128)(2,1)}, u32[]{:S(2)}) copy-start(bf16[320,512]{1,0:T(8,128)(2,1)} %nodes.5) | copy-start | bytes 983044
  17.6 9.4 %collective-permute-start.5 = (bf16[14,32,256]{2,1,0:T(8,128)(2,1)S(1)}, bf16[14,32,256]{2,1,0:T(8,128)(2,1)S(1)}, u32[]{:S(2)}, u32[]{:S(2)}) collective-permute-start(bf16[14,32,256]{2,1,0:T(8,128)(2,1)S(1)} %get-tuple-element.39), channel_id=1, source_target_pairs={{0,4},{4,0},{8,12},{12,8},{1,5},{5,1},{9,13},{13,9},{2,6},{6,2},{1... | collective-permute-start | bytes 688136 | tf_op jit(solution)/shard_map/ppermute | solution.py:328
  19.3 18.6 %collective-permute-start.6 = (bf16[14,32,256]{2,1,0:T(8,128)(2,1)S(1)}, bf16[14,32,256]{2,1,0:T(8,128)(2,1)S(1)}, u32[]{:S(2)}, u32[]{:S(2)}) collective-permute-start(bf16[14,32,256]{2,1,0:T(8,128)(2,1)S(1)} %get-tuple-element.39), channel_id=1, source_target_pairs={{0,8},{4,12},{8,0},{12,4},{1,9},{5,13},{9,1},{13,5},{2,10},{6,14},... | collective-permute-start | bytes 688136 | tf_op jit(solution)/shard_map/ppermute | solution.py:328
  22.6 15.3 %collective-permute-start.7 = (bf16[14,32,256]{2,1,0:T(8,128)(2,1)S(1)}, bf16[14,32,256]{2,1,0:T(8,128)(2,1)S(1)}, u32[]{:S(2)}, u32[]{:S(2)}) collective-permute-start(bf16[14,32,256]{2,1,0:T(8,128)(2,1)S(1)} %get-tuple-element.39), channel_id=1, source_target_pairs={{0,12},{4,8},{8,4},{12,0},{1,13},{5,9},{9,5},{13,1},{2,14},{6,10},... | collective-permute-start | bytes 688136 | tf_op jit(solution)/shard_map/ppermute | solution.py:328
  22.9 16.3 %collective-permute-start.8 = (bf16[3,7,32,256]{3,2,1,0:T(8,128)(2,1)S(1)}, bf16[3,7,32,256]{3,2,1,0:T(8,128)(2,1)S(1)}, u32[]{:S(2)}, u32[]{:S(2)}) collective-permute-start(bf16[3,7,32,256]{3,2,1,0:T(8,128)(2,1)S(1)} %shard_map.148.refs_1_), channel_id=1, source_target_pairs={{0,2},{2,0},{1,3},{3,1},{4,6},{6,4},{5,7},{7,5},{8,10},{10,8},{9,1... | collective-permute-start | bytes 1032200 | tf_op jit(solution)/shard_map/ppermute | solution.py:333
  24.9 14.5 %collective-permute-start.9 = (bf16[3,7,32,256]{3,2,1,0:T(8,128)(2,1)S(1)}, bf16[3,7,32,256]{3,2,1,0:T(8,128)(2,1)S(1)}, u32[]{:S(2)}, u32[]{:S(2)}) collective-permute-start(bf16[3,7,32,256]{3,2,1,0:T(8,128)(2,1)S(1)} %shard_map.148.refs_1_), channel_id=1, source_target_pairs={{0,16},{16,0},{1,17},{17,1},{2,18},{18,2},{3,19},{19,3},{4,20},{20... | collective-permute-start | bytes 1032200 | tf_op jit(solution)/shard_map/ppermute | solution.py:334
  27.0 12.4 %collective-permute-start.10 = (bf16[3,7,32,256]{3,2,1,0:T(8,128)(2,1)S(1)}, bf16[3,7,32,256]{3,2,1,0:T(8,128)(2,1)S(1)}, u32[]{:S(2)}, u32[]{:S(2)}) collective-permute-start(bf16[3,7,32,256]{3,2,1,0:T(8,128)(2,1)S(1)} %shard_map.148.refs_1_), channel_id=1, source_target_pairs={{0,18},{18,0},{2,16},{16,2},{1,19},{19,1},{3,17},{17,3},{4,22},{22... | collective-permute-start | bytes 1032200 | tf_op jit(solution)/shard_map/ppermute | solution.py:335
  38.0 20.0 %copy-start.4 = (bf16[3,7,32,256]{3,2,1,0:T(8,128)(2,1)}, bf16[3,7,32,256]{3,2,1,0:T(8,128)(2,1)S(1)}, u32[]{:S(2)}) copy-start(bf16[3,7,32,256]{3,2,1,0:T(8,128)(2,1)S(1)} %get-tuple-element.44.refs_6_) | copy-start | bytes 1032196
  38.0 44.3 %copy-start.3 = (bf16[3,7,32,256]{3,2,1,0:T(8,128)(2,1)}, bf16[3,7,32,256]{3,2,1,0:T(8,128)(2,1)S(1)}, u32[]{:S(2)}) copy-start(bf16[3,7,32,256]{3,2,1,0:T(8,128)(2,1)S(1)} %get-tuple-element.53.refs_6_) | copy-start | bytes 1032196
  42.5 7.4 %copy-start.12 = (s32[1,8,8]{2,1,0:T(8,128)S(1)}, s32[1,8,8]{2,1,0:T(8,128)}, u32[]{:S(2)}) copy-start(s32[1,8,8]{2,1,0:T(8,128)} %param.23) | copy-start | bytes 772
  42.5 2.4 %collective-permute-start.11 = (bf16[768,512]{1,0:T(8,128)(2,1)S(1)}, bf16[768,512]{1,0:T(8,128)(2,1)S(1)}, u32[]{:S(2)}, u32[]{:S(2)}) collective-permute-start(bf16[768,512]{1,0:T(8,128)(2,1)S(1)} %shard_map.151.mine), channel_id=1, source_target_pairs={{0,1},{1,0},{2,3},{3,2},{4,5},{5,4},{6,7},{7,6},{8,9},{9,8},{10,11... | collective-permute-start | bytes 2359304 | tf_op jit(solution)/shard_map/ppermute | solution.py:340
  46.2 3.8 %collective-permute-start.12 = (bf16[320,512]{1,0:T(8,128)(2,1)S(1)}, bf16[320,512]{1,0:T(8,128)(2,1)S(1)}, u32[]{:S(2)}, u32[]{:S(2)}) collective-permute-start(bf16[320,512]{1,0:T(8,128)(2,1)S(1)} %shard_map.152.mine), channel_id=1, source_target_pairs={{0,1},{1,0},{2,3},{3,2},{4,5},{5,4},{6,7},{7,6},{8,9},{9,8},{10,11... | collective-permute-start | bytes 983048 | tf_op jit(solution)/shard_map/ppermute | solution.py:340
  46.4 12.0 %collective-permute-start.13 = (bf16[3,7,32,256]{3,2,1,0:T(8,128)(2,1)S(1)}, bf16[3,7,32,256]{3,2,1,0:T(8,128)(2,1)S(1)}, u32[]{:S(2)}, u32[]{:S(2)}) collective-permute-start(bf16[3,7,32,256]{3,2,1,0:T(8,128)(2,1)S(1)} %get-tuple-element.44.refs_6_), channel_id=1, source_target_pairs={{0,2},{2,0},{1,3},{3,1},{4,6},{6,4},{5,7},{7,5},{8,10},{10,8},{9,1... | collective-permute-start | bytes 1032200 | tf_op jit(solution)/shard_map/ppermute | solution.py:333
  47.6 17.4 %collective-permute-start.15 = (bf16[3,7,32,256]{3,2,1,0:T(8,128)(2,1)S(1)}, bf16[3,7,32,256]{3,2,1,0:T(8,128)(2,1)}, u32[]{:S(2)}, u32[]{:S(2)}) collective-permute-start(bf16[3,7,32,256]{3,2,1,0:T(8,128)(2,1)S(1)} %get-tuple-element.44.refs_6_), channel_id=1, source_target_pairs={{0,16},{16,0},{1,17},{17,1},{2,18},{18,2},{3,19},{19,3},{4,20},{20... | collective-permute-start | bytes 1032200 | tf_op jit(solution)/shard_map/ppermute | solution.py:334
  49.0 16.8 %collective-permute-start.17 = (bf16[3,7,32,256]{3,2,1,0:T(8,128)(2,1)S(1)}, bf16[3,7,32,256]{3,2,1,0:T(8,128)(2,1)}, u32[]{:S(2)}, u32[]{:S(2)}) collective-permute-start(bf16[3,7,32,256]{3,2,1,0:T(8,128)(2,1)S(1)} %get-tuple-element.44.refs_6_), channel_id=1, source_target_pairs={{0,18},{18,0},{2,16},{16,2},{1,19},{19,1},{3,17},{17,3},{4,22},{22... | collective-permute-start | bytes 1032200 | tf_op jit(solution)/shard_map/ppermute | solution.py:335
  50.0 15.8 %copy-start.10 = (s32[768]{0:T(1024)S(1)}, s32[768]{0:T(1024)}, u32[]{:S(2)}) copy-start(s32[768]{0:T(1024)} %param.24) | copy-start | bytes 9220
  50.0 15.8 %copy-start.11 = (s32[768]{0:T(1024)S(1)}, s32[768]{0:T(1024)}, u32[]{:S(2)}) copy-start(s32[768]{0:T(1024)} %param.25) | copy-start | bytes 9220
  51.7 13.2 %all-to-all-start = ((bf16[8,8,512]{2,1,0:T(8,128)(2,1)}), bf16[8,8,512]{2,1,0:T(8,128)(2,1)S(1)}, u32[]{:S(2)}, u32[]{:S(2)}) async-start(bf16[8,8,512]{2,1,0:T(8,128)(2,1)} %bitcast.2), calls=%async_computation | async-start | bytes 131072 | tf_op jit(solution)/shard_map/all_to_all | solution.py:452
  57.9 9.1 %collective-permute-start.19 = (bf16[7,128,256]{2,1,0:T(8,128)(2,1)S(1)}, bf16[7,128,256]{2,1,0:T(8,128)(2,1)S(1)}, u32[]{:S(2)}, u32[]{:S(2)}) collective-permute-start(bf16[7,128,256]{2,1,0:T(8,128)(2,1)S(1)} %get-tuple-element.50.refs_5_), channel_id=1, source_target_pairs={{0,1},{1,0},{2,3},{3,2},{4,5},{5,4},{6,7},{7,6},{8,9},{9,8},{10,11... | collective-permute-start | bytes 1376264 | tf_op jit(solution)/shard_map/ppermute | solution.py:340
  57.9 7.9 %collective-permute-start.20 = (bf16[3,7,32,256]{3,2,1,0:T(8,128)(2,1)S(1)}, bf16[3,7,32,256]{3,2,1,0:T(8,128)(2,1)}, u32[]{:S(2)}, u32[]{:S(2)}) collective-permute-start(bf16[3,7,32,256]{3,2,1,0:T(8,128)(2,1)S(1)} %get-tuple-element.44.refs_6_), channel_id=1, source_target_pairs={{0,1},{1,0},{2,3},{3,2},{4,5},{5,4},{6,7},{7,6},{8,9},{9,8},{10,11... | collective-permute-start | bytes 1032200 | tf_op jit(solution)/shard_map/ppermute | solution.py:340
  58.4 11.0 %copy-start.16 = (bf16[3,7,32,256]{3,2,1,0:T(8,128)(2,1)}, bf16[3,7,32,256]{3,2,1,0:T(8,128)(2,1)S(1)}, u32[]{:S(2)}) copy-start(bf16[3,7,32,256]{3,2,1,0:T(8,128)(2,1)S(1)} %collective-permute-done.13.refs_7_) | copy-start | bytes 1032196
  64.9 3.3 %collective-permute-start.14 = (bf16[3,7,32,256]{3,2,1,0:T(8,128)(2,1)S(1)}, bf16[3,7,32,256]{3,2,1,0:T(8,128)(2,1)S(1)}, u32[]{:S(2)}, u32[]{:S(2)}) collective-permute-start(bf16[3,7,32,256]{3,2,1,0:T(8,128)(2,1)S(1)} %collective-permute-done.13.refs_7_), channel_id=1, source_target_pairs={{0,1},{1,0},{2,3},{3,2},{4,5},{5,4},{6,7},{7,6},{8,9},{9,8},{10,11... | collective-permute-start | bytes 1032200 | tf_op jit(solution)/shard_map/ppermute | solution.py:340
  64.9 4.5 %collective-permute-start.16 = (bf16[3,7,32,256]{3,2,1,0:T(8,128)(2,1)}, bf16[3,7,32,256]{3,2,1,0:T(8,128)(2,1)S(1)}, u32[]{:S(2)}, u32[]{:S(2)}) collective-permute-start(bf16[3,7,32,256]{3,2,1,0:T(8,128)(2,1)} %collective-permute-done.15.refs_8_), channel_id=1, source_target_pairs={{0,1},{1,0},{2,3},{3,2},{4,5},{5,4},{6,7},{7,6},{8,9},{9,8},{10,11... | collective-permute-start | bytes 1032200 | tf_op jit(solution)/shard_map/ppermute | solution.py:340
  65.8 3.6 %collective-permute-start.18 = (bf16[3,7,32,256]{3,2,1,0:T(8,128)(2,1)}, bf16[3,7,32,256]{3,2,1,0:T(8,128)(2,1)S(1)}, u32[]{:S(2)}, u32[]{:S(2)}) collective-permute-start(bf16[3,7,32,256]{3,2,1,0:T(8,128)(2,1)} %collective-permute-done.17.refs_9_), channel_id=1, source_target_pairs={{0,1},{1,0},{2,3},{3,2},{4,5},{5,4},{6,7},{7,6},{8,9},{9,8},{10,11... | collective-permute-start | bytes 1032200 | tf_op jit(solution)/shard_map/ppermute | solution.py:340
  65.9 16.9 %collective-permute-start.21 = (bf16[3,7,32,256]{3,2,1,0:T(8,128)(2,1)S(1)}, bf16[3,7,32,256]{3,2,1,0:T(8,128)(2,1)S(1)}, u32[]{:S(2)}, u32[]{:S(2)}) collective-permute-start(bf16[3,7,32,256]{3,2,1,0:T(8,128)(2,1)S(1)} %get-tuple-element.53.refs_6_), channel_id=1, source_target_pairs={{0,2},{2,0},{1,3},{3,1},{4,6},{6,4},{5,7},{7,5},{8,10},{10,8},{9,1... | collective-permute-start | bytes 1032200 | tf_op jit(solution)/shard_map/ppermute | solution.py:333
  67.0 2.4 %copy-start.13 = (bf16[7,128,256]{2,1,0:T(8,128)(2,1)}, bf16[7,128,256]{2,1,0:T(8,128)(2,1)S(1)}, u32[]{:S(2)}) copy-start(bf16[7,128,256]{2,1,0:T(8,128)(2,1)S(1)} %collective-permute-done.19.refs_10_) | copy-start | bytes 1376260
  67.0 22.1 %collective-permute-start.23 = (bf16[3,7,32,256]{3,2,1,0:T(8,128)(2,1)S(1)}, bf16[3,7,32,256]{3,2,1,0:T(8,128)(2,1)S(1)}, u32[]{:S(2)}, u32[]{:S(2)}) collective-permute-start(bf16[3,7,32,256]{3,2,1,0:T(8,128)(2,1)S(1)} %get-tuple-element.53.refs_6_), channel_id=1, source_target_pairs={{0,16},{16,0},{1,17},{17,1},{2,18},{18,2},{3,19},{19,3},{4,20},{20... | collective-permute-start | bytes 1032200 | tf_op jit(solution)/shard_map/ppermute | solution.py:334
  68.2 21.4 %collective-permute-start.25 = (bf16[3,7,32,256]{3,2,1,0:T(8,128)(2,1)S(1)}, bf16[3,7,32,256]{3,2,1,0:T(8,128)(2,1)}, u32[]{:S(2)}, u32[]{:S(2)}) collective-permute-start(bf16[3,7,32,256]{3,2,1,0:T(8,128)(2,1)S(1)} %get-tuple-element.53.refs_6_), channel_id=1, source_target_pairs={{0,18},{18,0},{2,16},{16,2},{1,19},{19,1},{3,17},{17,3},{4,22},{22... | collective-permute-start | bytes 1032200 | tf_op jit(solution)/shard_map/ppermute | solution.py:335
  76.0 13.1 %all-to-all-start.1 = ((bf16[8,8,512]{2,1,0:T(8,128)(2,1)}), bf16[8,8,512]{2,1,0:T(8,128)(2,1)S(1)}, u32[]{:S(2)}, u32[]{:S(2)}) async-start(bf16[8,8,512]{2,1,0:T(8,128)(2,1)} %bitcast.4), calls=%async_computation.1 | async-start | bytes 131072 | tf_op jit(solution)/shard_map/all_to_all | solution.py:452
  82.2 7.5 %collective-permute-start.27 = (bf16[7,128,256]{2,1,0:T(8,128)(2,1)S(1)}, bf16[7,128,256]{2,1,0:T(8,128)(2,1)S(1)}, u32[]{:S(2)}, u32[]{:S(2)}) collective-permute-start(bf16[7,128,256]{2,1,0:T(8,128)(2,1)S(1)} %get-tuple-element.60.refs_5_), channel_id=1, source_target_pairs={{0,1},{1,0},{2,3},{3,2},{4,5},{5,4},{6,7},{7,6},{8,9},{9,8},{10,11... | collective-permute-start | bytes 1376264 | tf_op jit(solution)/shard_map/ppermute | solution.py:340
  82.3 7.4 %collective-permute-start.28 = (bf16[3,7,32,256]{3,2,1,0:T(8,128)(2,1)S(1)}, bf16[3,7,32,256]{3,2,1,0:T(8,128)(2,1)S(1)}, u32[]{:S(2)}, u32[]{:S(2)}) collective-permute-start(bf16[3,7,32,256]{3,2,1,0:T(8,128)(2,1)S(1)} %get-tuple-element.53.refs_6_), channel_id=1, source_target_pairs={{0,1},{1,0},{2,3},{3,2},{4,5},{5,4},{6,7},{7,6},{8,9},{9,8},{10,11... | collective-permute-start | bytes 1032200 | tf_op jit(solution)/shard_map/ppermute | solution.py:340
  82.8 9.2 %copy-start.15 = (bf16[3,7,32,256]{3,2,1,0:T(8,128)(2,1)}, bf16[3,7,32,256]{3,2,1,0:T(8,128)(2,1)S(1)}, u32[]{:S(2)}) copy-start(bf16[3,7,32,256]{3,2,1,0:T(8,128)(2,1)S(1)} %collective-permute-done.21.refs_7_) | copy-start | bytes 1032196
  89.1 1.7 %collective-permute-start.22 = (bf16[3,7,32,256]{3,2,1,0:T(8,128)(2,1)S(1)}, bf16[3,7,32,256]{3,2,1,0:T(8,128)(2,1)S(1)}, u32[]{:S(2)}, u32[]{:S(2)}) collective-permute-start(bf16[3,7,32,256]{3,2,1,0:T(8,128)(2,1)S(1)} %collective-permute-done.21.refs_7_), channel_id=1, source_target_pairs={{0,1},{1,0},{2,3},{3,2},{4,5},{5,4},{6,7},{7,6},{8,9},{9,8},{10,11... | collective-permute-start | bytes 1032200 | tf_op jit(solution)/shard_map/ppermute | solution.py:340
  89.1 2.8 %copy-start.17 = (bf16[3,7,32,256]{3,2,1,0:T(8,128)(2,1)}, bf16[3,7,32,256]{3,2,1,0:T(8,128)(2,1)S(1)}, u32[]{:S(2)}) copy-start(bf16[3,7,32,256]{3,2,1,0:T(8,128)(2,1)S(1)} %collective-permute-done.23.refs_8_) | copy-start | bytes 1032196
  89.1 2.1 %collective-permute-start.24 = (bf16[3,7,32,256]{3,2,1,0:T(8,128)(2,1)S(1)}, bf16[3,7,32,256]{3,2,1,0:T(8,128)(2,1)S(1)}, u32[]{:S(2)}, u32[]{:S(2)}) collective-permute-start(bf16[3,7,32,256]{3,2,1,0:T(8,128)(2,1)S(1)} %collective-permute-done.23.refs_8_), channel_id=1, source_target_pairs={{0,1},{1,0},{2,3},{3,2},{4,5},{5,4},{6,7},{7,6},{8,9},{9,8},{10,11... | collective-permute-start | bytes 1032200 | tf_op jit(solution)/shard_map/ppermute | solution.py:340
  89.6 2.3 %collective-permute-start.26 = (bf16[3,7,32,256]{3,2,1,0:T(8,128)(2,1)}, bf16[3,7,32,256]{3,2,1,0:T(8,128)(2,1)S(1)}, u32[]{:S(2)}, u32[]{:S(2)}) collective-permute-start(bf16[3,7,32,256]{3,2,1,0:T(8,128)(2,1)} %collective-permute-done.25.refs_9_), channel_id=1, source_target_pairs={{0,1},{1,0},{2,3},{3,2},{4,5},{5,4},{6,7},{7,6},{8,9},{9,8},{10,11... | collective-permute-start | bytes 1032200 | tf_op jit(solution)/shard_map/ppermute | solution.py:340
  89.7 2.3 %copy-start.18 = (bf16[3,7,32,256]{3,2,1,0:T(8,128)(2,1)}, bf16[3,7,32,256]{3,2,1,0:T(8,128)(2,1)S(1)}, u32[]{:S(2)}) copy-start(bf16[3,7,32,256]{3,2,1,0:T(8,128)(2,1)S(1)} %collective-permute-done.28.refs_11_) | copy-start | bytes 1032196
  89.7 2.3 %copy-start.14 = (bf16[7,128,256]{2,1,0:T(8,128)(2,1)}, bf16[7,128,256]{2,1,0:T(8,128)(2,1)S(1)}, u32[]{:S(2)}) copy-start(bf16[7,128,256]{2,1,0:T(8,128)(2,1)S(1)} %collective-permute-done.27.refs_10_) | copy-start | bytes 1376260

commit v4 on v3

--- a/solution.py
+++ b/solution.py
@@ -203,9 +203,9 @@
             block[k] = ref[i * block.shape[1] : (i + 1) * block.shape[1]]
 
 
-def join(arrays, blocks):
+def join(arrays, blocks, cost=0.5):
     count, rows, cols = arrays[0].shape
-    return call(join_body, [(len(arrays), count // blocks, rows, cols)] * blocks, [], arrays)
+    return call(join_body, [(len(arrays), count // blocks, rows, cols)] * blocks, [], arrays, cost=cost)
 
 
 def lend_body(grid, down, up, low, high):
@@ -246,32 +246,52 @@
 
 def half_edges_body(pack, gathered, *refs):
     count = len(pack.near_operands)
-    edges, out, buffer, sem, *scratch = refs[count:]
-    fetch = pltpu.make_async_copy(edges, buffer, sem)
+    operands, edges, out, refs = refs[:count], refs[count], refs[count + 1], refs[count + 2 :]
+    saved, refs = (refs[:2], refs[2:]) if len(pack.kind) == 2 else ((), refs)
+    buffer, sems, *scratch = refs
+    fetch = pltpu.make_async_copy(edges, buffer, sems.at[0])
     fetch.start()
-    weights, place = pack.load(refs[:count], (), scratch)
+    weights, place = pack.load(operands, (), scratch)
+    saves = []
+    if saved:
+        place("n")
+        saves = [pltpu.make_async_copy(weights[n], to, sems.at[1 + i]) for i, (n, to) in enumerate(zip(("nm", "nb"), saved))]
+    for save in saves:
+        save.start()
     place("e")
     fetch.wait()
     for at in range(0, edges.shape[0], ROWS):
         rows = slice(at, at + ROWS)
         pre = dot(jnp.concatenate([gathered[rows, :], buffer[rows, :]], axis=1), weights["em"][...])
         out[rows, :] = dot(silu(pre).astype(BF), weights["eb"][...]).astype(BF)
-
-
-def half_nodes_body(pack, targets, nodes, mine, other, *refs):
-    count = len(pack.near_operands)
-    out, message, *scratch = refs[count:]
-    weights, place = pack.load(refs[:count], (), scratch)
-    place("n")
+    for save in saves:
+        save.wait()
+
+
+def half_nodes_body(targets, mine, other, nodes_in, nm_in, nb_in, out, message, nodes, nm, nb, sems):
+    pairs = ((nodes_in, nodes), (nm_in, nm), (nb_in, nb))
+    fetches = [pltpu.make_async_copy(src, dst, sems.at[i]) for i, (src, dst) in enumerate(pairs)]
+    for fetch in fetches:
+        fetch.start()
     for at in range(0, message.shape[0], ROWS):
         rows = slice(at, at + ROWS)
         message[rows, :] = normalize(sum_of((mine, other), rows)).astype(BF)
     incoming = dot(one_hot_rows(targets[...], nodes.shape[0]), message[...]).astype(BF)
-    pre = dot(jnp.concatenate([nodes[...], incoming], axis=1), weights["nm"][...])
-    out[...] = dot(silu(pre).astype(BF), weights["nb"][...]).astype(BF)
-
-
-def first_next_body(nodes, lists, mine, other, packed, out, buffer, sem):
+    for fetch in fetches:
+        fetch.wait()
+    pre = dot(jnp.concatenate([nodes[...], incoming], axis=1), nm[...])
+    out[...] = dot(silu(pre).astype(BF), nb[...]).astype(BF)
+
+
+def mark_body(source, out):
+    out[...] = source[0 : out.shape[0], 0 : out.shape[1]]
+
+
+def mark(source, cost):
+    return call(mark_body, (16, 128), [], [source], cost=cost)
+
+
+def first_next_body(nodes, lists, mine, other, piece, packed, out, buffer, sem):
     buffer[...] = (nodes[...].astype(F32) + normalize(sum_of((mine, other)))).astype(BF)
     save = pltpu.make_async_copy(buffer, out, sem)
     save.start()
@@ -329,11 +349,10 @@
 
 
 def over_plane(own):
-    return [
-        lax.ppermute(own, "band", SWAP),
-        lax.ppermute(own, "groups", SWAP),
-        lax.ppermute(own, ("groups", "band"), DIAGONAL),
-    ]
+    across = lax.ppermute(own, ("groups", "band"), DIAGONAL)
+    along_y = lax.ppermute(own, "groups", SWAP)
+    along_x = lax.ppermute(own, "band", SWAP)
+    return [along_x, along_y, across]
 
 
 def swap_width(array):
@@ -405,8 +424,7 @@
         [joined0] = join(turned0[:-1] + [after(turned0[-1], from_upper, from_lower, cut12)], 1)
         plane0 = over_plane(joined0)
         side0 = [own0, joined0] + plane0
-        joined1, joined2 = join(over_slices(after(cut12, joined0)), 2)
-        from_lower = after(from_lower, joined1)
+        joined1, joined2 = join(over_slices(after(cut12, joined0)), 2, 3.0)
     else:
         packs = weights_whole(edge_mats, node_mats, edge_back, node_back)
     gathered = call(
@@ -417,30 +435,37 @@
         cost=1.2,
     )
     if by_parts:
-        packs = [Parts([side0], [], "e"), Parts([side0], [], "n")]
-    term = call(
-        functools.partial(half_edges_body, packs[0]),
-        (grid_edges, depth),
-        [pltpu.VMEM((grid_edges, depth), BF), pltpu.SemaphoreType.DMA(())] + packs[0].scratch(hidden // 2, depth),
-        [gathered] + packs[0].near_operands,
+        packs = [Parts([[after(own0, joined1)] + side0[1:]], [])]
+    pack = packs[0]
+    term, *node_weights = call(
+        functools.partial(half_edges_body, pack),
+        [((grid_edges, depth), BF)] + [(shape, BF) for shape in (weight_shapes("n", hidden // 2, depth) if by_parts else [])],
+        [pltpu.VMEM((grid_edges, depth), BF), pltpu.SemaphoreType.DMA((3,))] + pack.scratch(hidden // 2, depth),
+        [gathered] + pack.near_operands,
         [grid_edge],
         cost=3.0,
+        far=2 if by_parts else 0,
     )
     if by_parts:
         plane1 = over_plane(after(joined1, term))
+    else:
+        node_weights = packs[1].near_operands
     before = term
     term = call(
-        functools.partial(half_nodes_body, packs[1]),
+        half_nodes_body,
         (nodes, depth),
-        [pltpu.VMEM((grid_edges, depth), BF)] + packs[1].scratch(hidden // 2, depth),
-        [encoder_target[None, :], mesh_latent, term, swap_width(term)] + packs[1].near_operands,
+        [pltpu.VMEM((grid_edges, depth), BF), node_buffer]
+        + [pltpu.VMEM(shape, BF) for shape in weight_shapes("n", hidden // 2, depth)]
+        + [pltpu.SemaphoreType.DMA((3,))],
+        [encoder_target[None, :], term, swap_width(term)],
+        [mesh_latent] + node_weights,
         cost=1.6,
     )
     packed, rows = call(
         first_next_body,
         [(sent_rows, depth), (nodes, depth)],
         [node_buffer, pltpu.SemaphoreType.DMA(())],
-        [mesh_latent, lists, term, swap_width(term)],
+        [mesh_latent, lists, term, swap_width(term), mark(term, 5.0)],
         cost=1.6,
         far=1,
     )

time: 98.6 us -> 94.9 us (0.962)
  starting transfers between devices: 47.4 us -> 39.1 us
  waiting for transfers between devices: 27 us -> 30 us
  Pallas kernels: 23.1 us -> 24.7 us
    ppermute x9, starting transfers between devices: 16.7 us -> 11.6 us  [the longest x3 7.05 us: over_plane(): across = lax.ppermute(own, ('groups', 'band'), DIAGONAL)]
    ppermute x6, waiting for transfers between devices: 6.17 us -> 9.73 us  [over_slices(): lax.ppermute(chunk, 'mesh', [(i, i ^ k) for i in range(count)])]
    all_to_all x2, starting transfers between devices: 12.3 us -> 8.91 us  [on_device(): lax.all_to_all(cut_rows, ('mesh', 'band'), split_axis=0, concat_axis=0, t...]
    pallas_call x11 -> x12, Pallas kernels: 23.1 us -> 24.7 us  [call(): pl.pallas_call(body, out_shape=shapes if many else shapes[0], in_specs=sp...]
  transfers between devices with their start and end apart: 31 -> 31, of which waited for: 13 -> 13; matrix products, arithmetic and copies ran while one was open for 0% -> 0% of each run, Pallas kernels for 12% -> 15%
where the time goes in v4:
time: 94.9 us; the launch traced here: 94.4 us
  starting transfers between devices  39.1 us (41%)
  waiting for transfers between devices  30 us (32%)
  Pallas kernels  24.7 us (26%)
    pallas_call x12, Pallas kernels, call(): pl.pallas_call(body, out_shape=shapes if many else shapes[0], in_specs=sp...  24.7 us
    all_to_all x2, waiting for transfers between devices, on_device(): lax.all_to_all(cut_rows, ('mesh', 'band'), split_axis=0, concat_axis=0, t...  12.4 us
    ppermute x6, starting transfers between devices, over_slices(): lax.ppermute(chunk, 'mesh', [(i, i ^ k) for i in range(count)])  11.1 us
    ppermute x6, waiting for transfers between devices, over_slices(): lax.ppermute(chunk, 'mesh', [(i, i ^ k) for i in range(count)])  9.73 us
    all_to_all x2, starting transfers between devices, on_device(): lax.all_to_all(cut_rows, ('mesh', 'band'), split_axis=0, concat_axis=0, t...  8.91 us
    ppermute x3, starting transfers between devices, over_plane(): across = lax.ppermute(own, ('groups', 'band'), DIAGONAL)  7.05 us
    ppermute x12, waiting for transfers between devices, swap_width(): return lax.ppermute(array, 'width', SWAP)  3.84 us
    ppermute x1, starting transfers between devices, on_device(): lax.ppermute(lent_up, ('mesh', 'band'), [(i, i + 1) for i in range(line -...  3.55 us
  transfers between devices with their start and end apart: 31, of which 13 were waited for; matrix products, arithmetic and copies ran while one was open for 0% of the time, Pallas kernels for 15%

profile of v4, /device:TPU:0, one launch (start us, length us, event | category | flops | bytes accessed | tf_op | source)
XLA Modules:
  0.0 94.4 jit_solution(13703421337197885524)
XLA Ops:
  0.0 0.9 shard_map.146
  0.9 3.1 %collective-permute-start = (bf16[7,32,256]{2,1,0:T(8,128)(2,1)S(1)}, bf16[7,32,256]{2,1,0:T(8,128)(2,1)S(1)}, u32[]{:S(2)}, u32[]{:S(2)}) collective-permute-start(bf16[7,32,256]{2,1,0:T(8,128)(2,1)S(1)} %shard_map.146), channel_id=1, source_target_pairs={{0,4},{4,0},{8,12},{12,8},{1,5},{5,1},{9,13},{13,9},{2,6},{6,2},{1... | collective-permute-start | bytes 344072 | tf_op jit(solution)/shard_map/ppermute | solution.py:348
  4.1 2.5 %collective-permute-start.4 = (bf16[7,32,256]{2,1,0:T(8,128)(2,1)S(1)}, bf16[7,32,256]{2,1,0:T(8,128)(2,1)S(1)}, u32[]{:S(2)}, u32[]{:S(2)}) collective-permute-start(bf16[7,32,256]{2,1,0:T(8,128)(2,1)S(1)} %shard_map.146), channel_id=1, source_target_pairs={{0,12},{4,8},{8,4},{12,0},{1,13},{5,9},{9,5},{13,1},{2,14},{6,10},... | collective-permute-start | bytes 344072 | tf_op jit(solution)/shard_map/ppermute | solution.py:348
  6.5 0.1 collective-permute-start.3
  6.7 0.3 shard_map.145
  7.0 0.2 collective-permute-done.refs_0_
  7.2 3.6 %collective-permute-start.1 = (bf16[64,512]{1,0:T(8,128)(2,1)S(1)}, bf16[64,512]{1,0:T(8,128)(2,1)S(1)}, u32[]{:S(2)}, u32[]{:S(2)}) collective-permute-start(bf16[64,512]{1,0:T(8,128)(2,1)S(1)} %get-tuple-element.37), channel_id=1, source_target_pairs={{0,2},{2,4},{4,6},{6,8},{8,10},{10,12},{12,14},{1,3},{3,5},{5,7},{... | collective-permute-start | bytes 196616 | tf_op jit(solution)/shard_map/ppermute | solution.py:422
  10.8 0.0 copy-start.9
  10.8 0.0 copy-start.10
  10.8 0.0 copy-start.5
  10.8 1.4 %collective-permute-start.2 = (bf16[64,512]{1,0:T(8,128)(2,1)S(1)}, bf16[64,512]{1,0:T(8,128)(2,1)S(1)}, u32[]{:S(2)}, u32[]{:S(2)}) collective-permute-start(bf16[64,512]{1,0:T(8,128)(2,1)S(1)} %get-tuple-element.39), channel_id=1, source_target_pairs={{2,0},{4,2},{6,4},{8,6},{10,8},{12,10},{14,12},{3,1},{5,3},{7,5},{... | collective-permute-start | bytes 196616 | tf_op jit(solution)/shard_map/ppermute | solution.py:421
  12.2 1.8 %shard_map.148 = (bf16[14,32,256]{2,1,0:T(8,128)(2,1)S(1)}, bf16[7,128,256]{2,1,0:T(8,128)(2,1)S(1)}, bf16[7,128,256]{2,1,0:T(8,128)(2,1)S(1)}, bf16[7,128,256]{2,1,0:T(8,128)(2,1)S(1)}) custom-call(bf16[3,3,128,256]{3,2,1,0:T(8,128)(2,1)} %refs_0_.3, bf16[3,256,128]{2,1,0:T(8,128)(2,1)} %refs_1_.3, bf16[3,2,128,256]{3,2,1,0:T(8,128)(2,1)} %refs_2_.3, ...), custom_call_target="tpu_custom_call" | custom-call | flops 500000000 | tf_op jit(solution)/shard_map/pallas_call | solution.py:59
  14.1 0.0 collective-permute-done.4.refs_2_
  14.1 3.0 %collective-permute-done.2.high = bf16[64,512]{1,0:T(8,128)(2,1)S(1)} collective-permute-done((bf16[64,512]{1,0:T(8,128)(2,1)S(1)}, bf16[64,512]{1,0:T(8,128)(2,1)S(1)}, u32[]{:S(2)}, u32[]{:S(2)}) %collective-permute-start.2) | collective-permute-done | bytes 65568 | tf_op jit(solution)/shard_map/ppermute | solution.py:421
  17.1 0.5 collective-permute-done.3.refs_1_
  17.6 1.8 %collective-permute-start.5 = (bf16[14,32,256]{2,1,0:T(8,128)(2,1)S(1)}, bf16[14,32,256]{2,1,0:T(8,128)(2,1)S(1)}, u32[]{:S(2)}, u32[]{:S(2)}) collective-permute-start(bf16[14,32,256]{2,1,0:T(8,128)(2,1)S(1)} %get-tuple-element.43), channel_id=1, source_target_pairs={{0,4},{4,0},{8,12},{12,8},{1,5},{5,1},{9,13},{13,9},{2,6},{6,2},{1... | collective-permute-start | bytes 688136 | tf_op jit(solution)/shard_map/ppermute | solution.py:348
  19.4 3.3 %collective-permute-start.6 = (bf16[14,32,256]{2,1,0:T(8,128)(2,1)S(1)}, bf16[14,32,256]{2,1,0:T(8,128)(2,1)S(1)}, u32[]{:S(2)}, u32[]{:S(2)}) collective-permute-start(bf16[14,32,256]{2,1,0:T(8,128)(2,1)S(1)} %get-tuple-element.43), channel_id=1, source_target_pairs={{0,8},{4,12},{8,0},{12,4},{1,9},{5,13},{9,1},{13,5},{2,10},{6,14},... | collective-permute-start | bytes 688136 | tf_op jit(solution)/shard_map/ppermute | solution.py:348
  22.7 0.4 collective-permute-start.7
  23.1 3.0 %collective-permute-start.10 = (bf16[3,7,32,256]{3,2,1,0:T(8,128)(2,1)S(1)}, bf16[3,7,32,256]{3,2,1,0:T(8,128)(2,1)S(1)}, u32[]{:S(2)}, u32[]{:S(2)}) collective-permute-start(bf16[3,7,32,256]{3,2,1,0:T(8,128)(2,1)S(1)} %shard_map.149.refs_1_), channel_id=1, source_target_pairs={{0,18},{18,0},{2,16},{16,2},{1,19},{19,1},{3,17},{17,3},{4,22},{22... | collective-permute-start | bytes 1032200 | tf_op jit(solution)/shard_map/ppermute | solution.py:352
  26.1 0.1 collective-permute-start.8
  26.2 0.7 collective-permute-done.5.refs_0_
  26.9 1.5 %collective-permute-start.9 = (bf16[3,7,32,256]{3,2,1,0:T(8,128)(2,1)S(1)}, bf16[3,7,32,256]{3,2,1,0:T(8,128)(2,1)S(1)}, u32[]{:S(2)}, u32[]{:S(2)}) collective-permute-start(bf16[3,7,32,256]{3,2,1,0:T(8,128)(2,1)S(1)} %shard_map.149.refs_1_), channel_id=1, source_target_pairs={{0,16},{16,0},{1,17},{17,1},{2,18},{18,2},{3,19},{19,3},{4,20},{20... | collective-permute-start | bytes 1032200 | tf_op jit(solution)/shard_map/ppermute | solution.py:353
  28.4 1.2 %shard_map.147.gathered = bf16[768,1024]{1,0:T(8,128)(2,1)S(1)} custom-call(bf16[512,512]{1,0:T(8,128)(2,1)S(1)} %copy-done, bf16[64,512]{1,0:T(8,128)(2,1)S(1)} %collective-permute-done.1.low, bf16[64,512]{1,0:T(8,128)(2,1)S(1)} %collective-permute-done.2.high, bf16[320,512]{1,0:T(8,128)(2,1)S(1)} %copy-done.5, s32[1,768]{1,0:T(1,128)S(1)} %broadcast_in_dim.22.slots, ...), custom_call_target="tpu_custom_call" | custom-call | flops 1200000000 | tf_op jit(solution)/shard_map/pallas_call | solution.py:59
  29.6 8.3 %collective-permute-done.6.refs_1_ = bf16[14,32,256]{2,1,0:T(8,128)(2,1)S(1)} collective-permute-done((bf16[14,32,256]{2,1,0:T(8,128)(2,1)S(1)}, bf16[14,32,256]{2,1,0:T(8,128)(2,1)S(1)}, u32[]{:S(2)}, u32[]{:S(2)}) %collective-permute-start.6) | collective-permute-done | bytes 229408 | tf_op jit(solution)/shard_map/ppermute | solution.py:348
  37.9 0.0 collective-permute-done.7.refs_2_
  38.0 0.0 copy-start.13
  38.0 1.0 %collective-permute-done.8.refs_2_ = bf16[3,7,32,256]{3,2,1,0:T(8,128)(2,1)S(1)} collective-permute-done((bf16[3,7,32,256]{3,2,1,0:T(8,128)(2,1)S(1)}, bf16[3,7,32,256]{3,2,1,0:T(8,128)(2,1)S(1)}, u32[]{:S(2)}, u32[]{:S(2)}) %collective-permute-start.8) | collective-permute-done | bytes 344096 | tf_op jit(solution)/shard_map/ppermute | solution.py:354
  39.0 0.1 collective-permute-done.9.refs_3_
  39.0 3.5 %shard_map.151 = (bf16[768,512]{1,0:T(8,128)(2,1)S(1)}, bf16[1024,256]{1,0:T(8,128)(2,1)}, bf16[256,512]{1,0:T(8,128)(2,1)}) custom-call(bf16[768,1024]{1,0:T(8,128)(2,1)S(1)} %shard_map.147.gathered, bf16[7,128,256]{2,1,0:T(8,128)(2,1)S(1)} %get-tuple-element.45.refs_0_, bf16[3,7,32,256]{3,2,1,0:T(8,128)(2,1)S(1)} %shard_map.149.refs_1_, ...), custom_call_target="tpu_custom_call" | custom-call | flops 3000000000 | tf_op jit(solution)/shard_map/pallas_call | solution.py:59
  42.5 0.1 collective-permute-start.11
  42.6 0.1 reshape.15.lists
  42.7 2.6 %collective-permute-start.17 = (bf16[3,7,32,256]{3,2,1,0:T(8,128)(2,1)S(1)}, bf16[3,7,32,256]{3,2,1,0:T(8,128)(2,1)}, u32[]{:S(2)}, u32[]{:S(2)}) collective-permute-start(bf16[3,7,32,256]{3,2,1,0:T(8,128)(2,1)S(1)} %get-tuple-element.50.refs_6_), channel_id=1, source_target_pairs={{0,18},{18,0},{2,16},{16,2},{1,19},{19,1},{3,17},{17,3},{4,22},{22... | collective-permute-start | bytes 1032200 | tf_op jit(solution)/shard_map/ppermute | solution.py:352
  45.3 0.6 collective-permute-start.15
  45.9 0.3 collective-permute-start.13
  46.2 2.5 %shard_map.152.source.mine = bf16[320,512]{1,0:T(8,128)(2,1)S(1)} custom-call(s32[1,768]{1,0:T(1,128)S(1)} %broadcast_in_dim.19.targets, bf16[768,512]{1,0:T(8,128)(2,1)S(1)} %get-tuple-element.46.mine, bf16[768,512]{1,0:T(8,128)(2,1)S(1)} %collective-permute-done.11.other, bf16[320,512]{1,0:T(8,128)(2,1)} %nodes.3, ...), custom_call_target="tpu_custom_call" | custom-call | flops 1600000000 | tf_op jit(solution)/shard_map/pallas_call | solution.py:59
  48.7 0.0 copy-start.6
  48.7 0.1 collective-permute-start.12
  48.8 0.0 copy-start.11
  48.8 0.0 copy-start.12
  48.8 1.6 %collective-permute-done.12.other = bf16[320,512]{1,0:T(8,128)(2,1)S(1)} collective-permute-done((bf16[320,512]{1,0:T(8,128)(2,1)S(1)}, bf16[320,512]{1,0:T(8,128)(2,1)S(1)}, u32[]{:S(2)}, u32[]{:S(2)}) %collective-permute-start.12) | collective-permute-done | bytes 327712 | tf_op jit(solution)/shard_map/ppermute | solution.py:359
  50.4 1.6 %shard_map.154 = (bf16[64,512]{1,0:T(8,128)(2,1)}, bf16[320,512]{1,0:T(8,128)(2,1)}) custom-call(bf16[320,512]{1,0:T(8,128)(2,1)S(1)} %copy-done.6, s32[1,64]{1,0:T(1,128)S(1)} %reshape.15.lists, bf16[320,512]{1,0:T(8,128)(2,1)S(1)} %shard_map.152.source.mine, bf16[320,512]{1,0:T(8,128)(2,1)S(1)} %collective-permute-done.12.other, ...), custom_call_target="tpu_custom_call" | custom-call | flops 1600000000 | tf_op jit(solution)/shard_map/pallas_call | solution.py:59
  52.1 5.4 %all-to-all-start = ((bf16[8,8,512]{2,1,0:T(8,128)(2,1)}), bf16[8,8,512]{2,1,0:T(8,128)(2,1)S(1)}, u32[]{:S(2)}, u32[]{:S(2)}) async-start(bf16[8,8,512]{2,1,0:T(8,128)(2,1)} %bitcast.2), calls=%async_computation | async-start | bytes 131072 | tf_op jit(solution)/shard_map/all_to_all | solution.py:477
  57.4 0.1 collective-permute-start.19
  57.5 0.5 collective-permute-start.20
  58.0 6.3 %all-to-all-done = bf16[8,8,512]{2,1,0:T(8,128)(2,1)S(1)} async-done(((bf16[8,8,512]{2,1,0:T(8,128)(2,1)}), bf16[8,8,512]{2,1,0:T(8,128)(2,1)S(1)}, u32[]{:S(2)}, u32[]{:S(2)}) %all-to-all-start) | async-done | bytes 65568 | tf_op jit(solution)/shard_map/all_to_all | solution.py:477
  64.3 0.0 collective-permute-start.18
  64.3 0.0 collective-permute-done.15.refs_8_
  64.3 0.5 collective-permute-start.16
  64.8 0.0 collective-permute-done.13.refs_7_
  64.8 0.1 collective-permute-start.14
  65.0 1.4 %collective-permute-start.25 = (bf16[3,7,32,256]{3,2,1,0:T(8,128)(2,1)S(1)}, bf16[3,7,32,256]{3,2,1,0:T(8,128)(2,1)S(1)}, u32[]{:S(2)}, u32[]{:S(2)}) collective-permute-start(bf16[3,7,32,256]{3,2,1,0:T(8,128)(2,1)S(1)} %get-tuple-element.59.refs_6_), channel_id=1, source_target_pairs={{0,18},{18,0},{2,16},{16,2},{1,19},{19,1},{3,17},{17,3},{4,22},{22... | collective-permute-start | bytes 1032200 | tf_op jit(solution)/shard_map/ppermute | solution.py:352
  66.4 0.5 collective-permute-start.23
  66.9 1.6 %collective-permute-start.21 = (bf16[3,7,32,256]{3,2,1,0:T(8,128)(2,1)S(1)}, bf16[3,7,32,256]{3,2,1,0:T(8,128)(2,1)}, u32[]{:S(2)}, u32[]{:S(2)}) collective-permute-start(bf16[3,7,32,256]{3,2,1,0:T(8,128)(2,1)S(1)} %get-tuple-element.59.refs_6_), channel_id=1, source_target_pairs={{0,2},{2,0},{1,3},{3,1},{4,6},{6,4},{5,7},{7,5},{8,10},{10,8},{9,1... | collective-permute-start | bytes 1032200 | tf_op jit(solution)/shard_map/ppermute | solution.py:354
  68.5 6.6 %shard_map.155 = (bf16[64,512]{1,0:T(8,128)(2,1)}, bf16[320,512]{1,0:T(8,128)(2,1)}, bf16[768,512]{1,0:T(8,128)(2,1)}) custom-call(bf16[64,512]{1,0:T(8,128)(2,1)S(1)} %bitcast.6, s32[1,768]{1,0:T(1,128)S(1)} %broadcast_in_dim.23.slots, s32[1,768]{1,0:T(1,128)S(1)} %broadcast_in_dim.24.targets, s32[1,64]{1,0:T(1,128)S(1)} %reshape.15.lists, ...), custom_call_target="tpu_custom_call" | custom-call | flops 6499999744 | tf_op jit(solution)/shard_map/pallas_call | solution.py:59
  75.1 3.5 %all-to-all-start.1 = ((bf16[8,8,512]{2,1,0:T(8,128)(2,1)}), bf16[8,8,512]{2,1,0:T(8,128)(2,1)S(1)}, u32[]{:S(2)}, u32[]{:S(2)}) async-start(bf16[8,8,512]{2,1,0:T(8,128)(2,1)} %bitcast.4), calls=%async_computation.1 | async-start | bytes 131072 | tf_op jit(solution)/shard_map/all_to_all | solution.py:477
  78.7 0.1 collective-permute-start.27
  78.8 0.5 collective-permute-start.28
  79.2 6.1 %all-to-all-done.1 = bf16[8,8,512]{2,1,0:T(8,128)(2,1)S(1)} async-done(((bf16[8,8,512]{2,1,0:T(8,128)(2,1)}), bf16[8,8,512]{2,1,0:T(8,128)(2,1)S(1)}, u32[]{:S(2)}, u32[]{:S(2)}) %all-to-all-start.1) | async-done | bytes 65568 | tf_op jit(solution)/shard_map/all_to_all | solution.py:477
  85.3 0.5 collective-permute-start.24
  85.8 0.1 collective-permute-start.22
  85.9 1.0 %collective-permute-done.26.refs_2_ = bf16[3,7,32,256]{3,2,1,0:T(8,128)(2,1)S(1)} collective-permute-done((bf16[3,7,32,256]{3,2,1,0:T(8,128)(2,1)S(1)}, bf16[3,7,32,256]{3,2,1,0:T(8,128)(2,1)S(1)}, u32[]{:S(2)}, u32[]{:S(2)}) %collective-permute-start.26) | collective-permute-done | bytes 344096 | tf_op jit(solution)/shard_map/ppermute | solution.py:359
  87.0 0.5 collective-permute-done.24.refs_1_
  87.5 0.7 collective-permute-done.22.refs_0_
  88.2 6.1 %shard_map.156 = bf16[320,512]{1,0:T(8,128)(2,1)} custom-call(bf16[64,512]{1,0:T(8,128)(2,1)S(1)} %bitcast.7, s32[1,768]{1,0:T(1,128)S(1)} %broadcast_in_dim.23.slots, s32[1,768]{1,0:T(1,128)S(1)} %broadcast_in_dim.24.targets, s32[1,64]{1,0:T(1,128)S(1)} %reshape.15.lists, bf16[3,7,32,256]{3,2,1,0:T(8,128)(2,1)S(1)} %collective-permute-done.22.refs_0_, ...), custom_call_target="tpu_custom_call" | custom-call | flops 6499999744 | tf_op jit(solution)/shard_map/pallas_call | solution.py:59
  (51 shorter events, 0.2 us)
Async XLA Ops:
  0.0 6.6 %copy-start.7 = (s32[64]{0:T(128)S(1)}, s32[64]{0:T(128)}, u32[]{:S(2)}) copy-start(s32[64]{0:T(128)} %param.21) | copy-start | bytes 772
  0.0 6.6 %copy-start.8 = (s32[64]{0:T(128)S(1)}, s32[64]{0:T(128)}, u32[]{:S(2)}) copy-start(s32[64]{0:T(128)} %param.22) | copy-start | bytes 772
  0.0 6.6 %copy-start = (bf16[512,512]{1,0:T(8,128)(2,1)S(1)}, bf16[512,512]{1,0:T(8,128)(2,1)}, u32[]{:S(2)}) copy-start(bf16[512,512]{1,0:T(8,128)(2,1)} %grid.3) | copy-start | bytes 1572868
  0.9 6.3 %collective-permute-start = (bf16[7,32,256]{2,1,0:T(8,128)(2,1)S(1)}, bf16[7,32,256]{2,1,0:T(8,128)(2,1)S(1)}, u32[]{:S(2)}, u32[]{:S(2)}) collective-permute-start(bf16[7,32,256]{2,1,0:T(8,128)(2,1)S(1)} %shard_map.146), channel_id=1, source_target_pairs={{0,4},{4,0},{8,12},{12,8},{1,5},{5,1},{9,13},{13,9},{2,6},{6,2},{1... | collective-permute-start | bytes 344072 | tf_op jit(solution)/shard_map/ppermute | solution.py:348
  4.1 10.0 %collective-permute-start.4 = (bf16[7,32,256]{2,1,0:T(8,128)(2,1)S(1)}, bf16[7,32,256]{2,1,0:T(8,128)(2,1)S(1)}, u32[]{:S(2)}, u32[]{:S(2)}) collective-permute-start(bf16[7,32,256]{2,1,0:T(8,128)(2,1)S(1)} %shard_map.146), channel_id=1, source_target_pairs={{0,12},{4,8},{8,4},{12,0},{1,13},{5,9},{9,5},{13,1},{2,14},{6,10},... | collective-permute-start | bytes 344072 | tf_op jit(solution)/shard_map/ppermute | solution.py:348
  6.5 11.1 %collective-permute-start.3 = (bf16[7,32,256]{2,1,0:T(8,128)(2,1)S(1)}, bf16[7,32,256]{2,1,0:T(8,128)(2,1)S(1)}, u32[]{:S(2)}, u32[]{:S(2)}) collective-permute-start(bf16[7,32,256]{2,1,0:T(8,128)(2,1)S(1)} %shard_map.146), channel_id=1, source_target_pairs={{0,8},{4,12},{8,0},{12,4},{1,9},{5,13},{9,1},{13,5},{2,10},{6,14},... | collective-permute-start | bytes 344072 | tf_op jit(solution)/shard_map/ppermute | solution.py:348
  7.2 6.9 %collective-permute-start.1 = (bf16[64,512]{1,0:T(8,128)(2,1)S(1)}, bf16[64,512]{1,0:T(8,128)(2,1)S(1)}, u32[]{:S(2)}, u32[]{:S(2)}) collective-permute-start(bf16[64,512]{1,0:T(8,128)(2,1)S(1)} %get-tuple-element.37), channel_id=1, source_target_pairs={{0,2},{2,4},{4,6},{6,8},{8,10},{10,12},{12,14},{1,3},{3,5},{5,7},{... | collective-permute-start | bytes 196616 | tf_op jit(solution)/shard_map/ppermute | solution.py:422
  10.8 12.3 %copy-start.9 = (s32[768]{0:T(1024)S(1)}, s32[768]{0:T(1024)}, u32[]{:S(2)}) copy-start(s32[768]{0:T(1024)} %param.20) | copy-start | bytes 9220
  10.8 12.3 %copy-start.10 = (s32[768]{0:T(1024)S(1)}, s32[768]{0:T(1024)}, u32[]{:S(2)}) copy-start(s32[768]{0:T(1024)} %param.19) | copy-start | bytes 9220
  10.8 17.6 %copy-start.5 = (bf16[320,512]{1,0:T(8,128)(2,1)S(1)}, bf16[320,512]{1,0:T(8,128)(2,1)}, u32[]{:S(2)}) copy-start(bf16[320,512]{1,0:T(8,128)(2,1)} %nodes.3) | copy-start | bytes 983044
  10.8 6.3 %collective-permute-start.2 = (bf16[64,512]{1,0:T(8,128)(2,1)S(1)}, bf16[64,512]{1,0:T(8,128)(2,1)S(1)}, u32[]{:S(2)}, u32[]{:S(2)}) collective-permute-start(bf16[64,512]{1,0:T(8,128)(2,1)S(1)} %get-tuple-element.39), channel_id=1, source_target_pairs={{2,0},{4,2},{6,4},{8,6},{10,8},{12,10},{14,12},{3,1},{5,3},{7,5},{... | collective-permute-start | bytes 196616 | tf_op jit(solution)/shard_map/ppermute | solution.py:421
  14.0 43.4 %copy-start.2 = (bf16[7,128,256]{2,1,0:T(8,128)(2,1)}, bf16[7,128,256]{2,1,0:T(8,128)(2,1)S(1)}, u32[]{:S(2)}) copy-start(bf16[7,128,256]{2,1,0:T(8,128)(2,1)S(1)} %get-tuple-element.56.refs_5_) | copy-start | bytes 1376260
  14.0 64.6 %copy-start.1 = (bf16[7,128,256]{2,1,0:T(8,128)(2,1)}, bf16[7,128,256]{2,1,0:T(8,128)(2,1)S(1)}, u32[]{:S(2)}) copy-start(bf16[7,128,256]{2,1,0:T(8,128)(2,1)S(1)} %get-tuple-element.66.refs_5_) | copy-start | bytes 1376260
  17.6 9.2 %collective-permute-start.5 = (bf16[14,32,256]{2,1,0:T(8,128)(2,1)S(1)}, bf16[14,32,256]{2,1,0:T(8,128)(2,1)S(1)}, u32[]{:S(2)}, u32[]{:S(2)}) collective-permute-start(bf16[14,32,256]{2,1,0:T(8,128)(2,1)S(1)} %get-tuple-element.43), channel_id=1, source_target_pairs={{0,4},{4,0},{8,12},{12,8},{1,5},{5,1},{9,13},{13,9},{2,6},{6,2},{1... | collective-permute-start | bytes 688136 | tf_op jit(solution)/shard_map/ppermute | solution.py:348
  19.4 18.5 %collective-permute-start.6 = (bf16[14,32,256]{2,1,0:T(8,128)(2,1)S(1)}, bf16[14,32,256]{2,1,0:T(8,128)(2,1)S(1)}, u32[]{:S(2)}, u32[]{:S(2)}) collective-permute-start(bf16[14,32,256]{2,1,0:T(8,128)(2,1)S(1)} %get-tuple-element.43), channel_id=1, source_target_pairs={{0,8},{4,12},{8,0},{12,4},{1,9},{5,13},{9,1},{13,5},{2,10},{6,14},... | collective-permute-start | bytes 688136 | tf_op jit(solution)/shard_map/ppermute | solution.py:348
  22.7 15.2 %collective-permute-start.7 = (bf16[14,32,256]{2,1,0:T(8,128)(2,1)S(1)}, bf16[14,32,256]{2,1,0:T(8,128)(2,1)S(1)}, u32[]{:S(2)}, u32[]{:S(2)}) collective-permute-start(bf16[14,32,256]{2,1,0:T(8,128)(2,1)S(1)} %get-tuple-element.43), channel_id=1, source_target_pairs={{0,12},{4,8},{8,4},{12,0},{1,13},{5,9},{9,5},{13,1},{2,14},{6,10},... | collective-permute-start | bytes 688136 | tf_op jit(solution)/shard_map/ppermute | solution.py:348
  23.1 14.9 %collective-permute-start.10 = (bf16[3,7,32,256]{3,2,1,0:T(8,128)(2,1)S(1)}, bf16[3,7,32,256]{3,2,1,0:T(8,128)(2,1)S(1)}, u32[]{:S(2)}, u32[]{:S(2)}) collective-permute-start(bf16[3,7,32,256]{3,2,1,0:T(8,128)(2,1)S(1)} %shard_map.149.refs_1_), channel_id=1, source_target_pairs={{0,18},{18,0},{2,16},{16,2},{1,19},{19,1},{3,17},{17,3},{4,22},{22... | collective-permute-start | bytes 1032200 | tf_op jit(solution)/shard_map/ppermute | solution.py:352
  26.1 12.9 %collective-permute-start.8 = (bf16[3,7,32,256]{3,2,1,0:T(8,128)(2,1)S(1)}, bf16[3,7,32,256]{3,2,1,0:T(8,128)(2,1)S(1)}, u32[]{:S(2)}, u32[]{:S(2)}) collective-permute-start(bf16[3,7,32,256]{3,2,1,0:T(8,128)(2,1)S(1)} %shard_map.149.refs_1_), channel_id=1, source_target_pairs={{0,2},{2,0},{1,3},{3,1},{4,6},{6,4},{5,7},{7,5},{8,10},{10,8},{9,1... | collective-permute-start | bytes 1032200 | tf_op jit(solution)/shard_map/ppermute | solution.py:354
  26.9 12.2 %collective-permute-start.9 = (bf16[3,7,32,256]{3,2,1,0:T(8,128)(2,1)S(1)}, bf16[3,7,32,256]{3,2,1,0:T(8,128)(2,1)S(1)}, u32[]{:S(2)}, u32[]{:S(2)}) collective-permute-start(bf16[3,7,32,256]{3,2,1,0:T(8,128)(2,1)S(1)} %shard_map.149.refs_1_), channel_id=1, source_target_pairs={{0,16},{16,0},{1,17},{17,1},{2,18},{18,2},{3,19},{19,3},{4,20},{20... | collective-permute-start | bytes 1032200 | tf_op jit(solution)/shard_map/ppermute | solution.py:353
  38.0 19.5 %copy-start.4 = (bf16[3,7,32,256]{3,2,1,0:T(8,128)(2,1)}, bf16[3,7,32,256]{3,2,1,0:T(8,128)(2,1)S(1)}, u32[]{:S(2)}) copy-start(bf16[3,7,32,256]{3,2,1,0:T(8,128)(2,1)S(1)} %get-tuple-element.50.refs_6_) | copy-start | bytes 1032196
  38.0 40.8 %copy-start.3 = (bf16[3,7,32,256]{3,2,1,0:T(8,128)(2,1)}, bf16[3,7,32,256]{3,2,1,0:T(8,128)(2,1)S(1)}, u32[]{:S(2)}) copy-start(bf16[3,7,32,256]{3,2,1,0:T(8,128)(2,1)S(1)} %get-tuple-element.59.refs_6_) | copy-start | bytes 1032196
  38.0 4.6 %copy-start.13 = (s32[1,8,8]{2,1,0:T(8,128)S(1)}, s32[1,8,8]{2,1,0:T(8,128)}, u32[]{:S(2)}) copy-start(s32[1,8,8]{2,1,0:T(8,128)} %param.23) | copy-start | bytes 772
  42.5 3.7 %collective-permute-start.11 = (bf16[768,512]{1,0:T(8,128)(2,1)S(1)}, bf16[768,512]{1,0:T(8,128)(2,1)S(1)}, u32[]{:S(2)}, u32[]{:S(2)}) collective-permute-start(bf16[768,512]{1,0:T(8,128)(2,1)S(1)} %get-tuple-element.46.mine), channel_id=1, source_target_pairs={{0,1},{1,0},{2,3},{3,2},{4,5},{5,4},{6,7},{7,6},{8,9},{9,8},{10,11... | collective-permute-start | bytes 2359304 | tf_op jit(solution)/shard_map/ppermute | solution.py:359
  42.7 15.4 %collective-permute-start.17 = (bf16[3,7,32,256]{3,2,1,0:T(8,128)(2,1)S(1)}, bf16[3,7,32,256]{3,2,1,0:T(8,128)(2,1)}, u32[]{:S(2)}, u32[]{:S(2)}) collective-permute-start(bf16[3,7,32,256]{3,2,1,0:T(8,128)(2,1)S(1)} %get-tuple-element.50.refs_6_), channel_id=1, source_target_pairs={{0,18},{18,0},{2,16},{16,2},{1,19},{19,1},{3,17},{17,3},{4,22},{22... | collective-permute-start | bytes 1032200 | tf_op jit(solution)/shard_map/ppermute | solution.py:352
  45.3 19.0 %collective-permute-start.15 = (bf16[3,7,32,256]{3,2,1,0:T(8,128)(2,1)S(1)}, bf16[3,7,32,256]{3,2,1,0:T(8,128)(2,1)}, u32[]{:S(2)}, u32[]{:S(2)}) collective-permute-start(bf16[3,7,32,256]{3,2,1,0:T(8,128)(2,1)S(1)} %get-tuple-element.50.refs_6_), channel_id=1, source_target_pairs={{0,16},{16,0},{1,17},{17,1},{2,18},{18,2},{3,19},{19,3},{4,20},{20... | collective-permute-start | bytes 1032200 | tf_op jit(solution)/shard_map/ppermute | solution.py:353
  45.9 19.0 %collective-permute-start.13 = (bf16[3,7,32,256]{3,2,1,0:T(8,128)(2,1)S(1)}, bf16[3,7,32,256]{3,2,1,0:T(8,128)(2,1)}, u32[]{:S(2)}, u32[]{:S(2)}) collective-permute-start(bf16[3,7,32,256]{3,2,1,0:T(8,128)(2,1)S(1)} %get-tuple-element.50.refs_6_), channel_id=1, source_target_pairs={{0,2},{2,0},{1,3},{3,1},{4,6},{6,4},{5,7},{7,5},{8,10},{10,8},{9,1... | collective-permute-start | bytes 1032200 | tf_op jit(solution)/shard_map/ppermute | solution.py:354
  48.7 1.7 %copy-start.6 = (bf16[320,512]{1,0:T(8,128)(2,1)S(1)}, bf16[320,512]{1,0:T(8,128)(2,1)}, u32[]{:S(2)}) copy-start(bf16[320,512]{1,0:T(8,128)(2,1)} %nodes.3) | copy-start | bytes 983044
  48.7 1.7 %collective-permute-start.12 = (bf16[320,512]{1,0:T(8,128)(2,1)S(1)}, bf16[320,512]{1,0:T(8,128)(2,1)S(1)}, u32[]{:S(2)}, u32[]{:S(2)}) collective-permute-start(bf16[320,512]{1,0:T(8,128)(2,1)S(1)} %shard_map.152.source.mine), channel_id=1, source_target_pairs={{0,1},{1,0},{2,3},{3,2},{4,5},{5,4},{6,7},{7,6},{8,9},{9,8},{10,11... | collective-permute-start | bytes 983048 | tf_op jit(solution)/shard_map/ppermute | solution.py:359
  48.8 16.1 %copy-start.11 = (s32[768]{0:T(1024)S(1)}, s32[768]{0:T(1024)}, u32[]{:S(2)}) copy-start(s32[768]{0:T(1024)} %param.24) | copy-start | bytes 9220
  48.8 16.1 %copy-start.12 = (s32[768]{0:T(1024)S(1)}, s32[768]{0:T(1024)}, u32[]{:S(2)}) copy-start(s32[768]{0:T(1024)} %param.25) | copy-start | bytes 9220
  52.1 12.3 %all-to-all-start = ((bf16[8,8,512]{2,1,0:T(8,128)(2,1)}), bf16[8,8,512]{2,1,0:T(8,128)(2,1)S(1)}, u32[]{:S(2)}, u32[]{:S(2)}) async-start(bf16[8,8,512]{2,1,0:T(8,128)(2,1)} %bitcast.2), calls=%async_computation | async-start | bytes 131072 | tf_op jit(solution)/shard_map/all_to_all | solution.py:477
  57.4 8.9 %collective-permute-start.19 = (bf16[7,128,256]{2,1,0:T(8,128)(2,1)S(1)}, bf16[7,128,256]{2,1,0:T(8,128)(2,1)S(1)}, u32[]{:S(2)}, u32[]{:S(2)}) collective-permute-start(bf16[7,128,256]{2,1,0:T(8,128)(2,1)S(1)} %get-tuple-element.56.refs_5_), channel_id=1, source_target_pairs={{0,1},{1,0},{2,3},{3,2},{4,5},{5,4},{6,7},{7,6},{8,9},{9,8},{10,11... | collective-permute-start | bytes 1376264 | tf_op jit(solution)/shard_map/ppermute | solution.py:359
  57.5 7.4 %collective-permute-start.20 = (bf16[3,7,32,256]{3,2,1,0:T(8,128)(2,1)S(1)}, bf16[3,7,32,256]{3,2,1,0:T(8,128)(2,1)}, u32[]{:S(2)}, u32[]{:S(2)}) collective-permute-start(bf16[3,7,32,256]{3,2,1,0:T(8,128)(2,1)S(1)} %get-tuple-element.50.refs_6_), channel_id=1, source_target_pairs={{0,1},{1,0},{2,3},{3,2},{4,5},{5,4},{6,7},{7,6},{8,9},{9,8},{10,11... | collective-permute-start | bytes 1032200 | tf_op jit(solution)/shard_map/ppermute | solution.py:359
  64.3 2.5 %collective-permute-start.18 = (bf16[3,7,32,256]{3,2,1,0:T(8,128)(2,1)}, bf16[3,7,32,256]{3,2,1,0:T(8,128)(2,1)S(1)}, u32[]{:S(2)}, u32[]{:S(2)}) collective-permute-start(bf16[3,7,32,256]{3,2,1,0:T(8,128)(2,1)} %collective-permute-done.17.refs_9_), channel_id=1, source_target_pairs={{0,1},{1,0},{2,3},{3,2},{4,5},{5,4},{6,7},{7,6},{8,9},{9,8},{10,11... | collective-permute-start | bytes 1032200 | tf_op jit(solution)/shard_map/ppermute | solution.py:359
  64.3 4.2 %collective-permute-start.16 = (bf16[3,7,32,256]{3,2,1,0:T(8,128)(2,1)}, bf16[3,7,32,256]{3,2,1,0:T(8,128)(2,1)S(1)}, u32[]{:S(2)}, u32[]{:S(2)}) collective-permute-start(bf16[3,7,32,256]{3,2,1,0:T(8,128)(2,1)} %collective-permute-done.15.refs_8_), channel_id=1, source_target_pairs={{0,1},{1,0},{2,3},{3,2},{4,5},{5,4},{6,7},{7,6},{8,9},{9,8},{10,11... | collective-permute-start | bytes 1032200 | tf_op jit(solution)/shard_map/ppermute | solution.py:359
  64.8 3.7 %collective-permute-start.14 = (bf16[3,7,32,256]{3,2,1,0:T(8,128)(2,1)}, bf16[3,7,32,256]{3,2,1,0:T(8,128)(2,1)S(1)}, u32[]{:S(2)}, u32[]{:S(2)}) collective-permute-start(bf16[3,7,32,256]{3,2,1,0:T(8,128)(2,1)} %collective-permute-done.13.refs_7_), channel_id=1, source_target_pairs={{0,1},{1,0},{2,3},{3,2},{4,5},{5,4},{6,7},{7,6},{8,9},{9,8},{10,11... | collective-permute-start | bytes 1032200 | tf_op jit(solution)/shard_map/ppermute | solution.py:359
  65.0 14.3 %collective-permute-start.25 = (bf16[3,7,32,256]{3,2,1,0:T(8,128)(2,1)S(1)}, bf16[3,7,32,256]{3,2,1,0:T(8,128)(2,1)S(1)}, u32[]{:S(2)}, u32[]{:S(2)}) collective-permute-start(bf16[3,7,32,256]{3,2,1,0:T(8,128)(2,1)S(1)} %get-tuple-element.59.refs_6_), channel_id=1, source_target_pairs={{0,18},{18,0},{2,16},{16,2},{1,19},{19,1},{3,17},{17,3},{4,22},{22... | collective-permute-start | bytes 1032200 | tf_op jit(solution)/shard_map/ppermute | solution.py:352
  66.4 2.2 %copy-start.14 = (bf16[7,128,256]{2,1,0:T(8,128)(2,1)}, bf16[7,128,256]{2,1,0:T(8,128)(2,1)S(1)}, u32[]{:S(2)}) copy-start(bf16[7,128,256]{2,1,0:T(8,128)(2,1)S(1)} %collective-permute-done.19.refs_10_) | copy-start | bytes 1376260
  66.4 18.9 %collective-permute-start.23 = (bf16[3,7,32,256]{3,2,1,0:T(8,128)(2,1)S(1)}, bf16[3,7,32,256]{3,2,1,0:T(8,128)(2,1)S(1)}, u32[]{:S(2)}, u32[]{:S(2)}) collective-permute-start(bf16[3,7,32,256]{3,2,1,0:T(8,128)(2,1)S(1)} %get-tuple-element.59.refs_6_), channel_id=1, source_target_pairs={{0,16},{16,0},{1,17},{17,1},{2,18},{18,2},{3,19},{19,3},{4,20},{20... | collective-permute-start | bytes 1032200 | tf_op jit(solution)/shard_map/ppermute | solution.py:353
  66.9 19.0 %collective-permute-start.21 = (bf16[3,7,32,256]{3,2,1,0:T(8,128)(2,1)S(1)}, bf16[3,7,32,256]{3,2,1,0:T(8,128)(2,1)}, u32[]{:S(2)}, u32[]{:S(2)}) collective-permute-start(bf16[3,7,32,256]{3,2,1,0:T(8,128)(2,1)S(1)} %get-tuple-element.59.refs_6_), channel_id=1, source_target_pairs={{0,2},{2,0},{1,3},{3,1},{4,6},{6,4},{5,7},{7,5},{8,10},{10,8},{9,1... | collective-permute-start | bytes 1032200 | tf_op jit(solution)/shard_map/ppermute | solution.py:354
  75.1 10.2 %all-to-all-start.1 = ((bf16[8,8,512]{2,1,0:T(8,128)(2,1)}), bf16[8,8,512]{2,1,0:T(8,128)(2,1)S(1)}, u32[]{:S(2)}, u32[]{:S(2)}) async-start(bf16[8,8,512]{2,1,0:T(8,128)(2,1)} %bitcast.4), calls=%async_computation.1 | async-start | bytes 131072 | tf_op jit(solution)/shard_map/all_to_all | solution.py:477
  78.7 7.3 %collective-permute-start.27 = (bf16[7,128,256]{2,1,0:T(8,128)(2,1)S(1)}, bf16[7,128,256]{2,1,0:T(8,128)(2,1)S(1)}, u32[]{:S(2)}, u32[]{:S(2)}) collective-permute-start(bf16[7,128,256]{2,1,0:T(8,128)(2,1)S(1)} %get-tuple-element.66.refs_5_), channel_id=1, source_target_pairs={{0,1},{1,0},{2,3},{3,2},{4,5},{5,4},{6,7},{7,6},{8,9},{9,8},{10,11... | collective-permute-start | bytes 1376264 | tf_op jit(solution)/shard_map/ppermute | solution.py:359
  78.8 7.2 %collective-permute-start.28 = (bf16[3,7,32,256]{3,2,1,0:T(8,128)(2,1)S(1)}, bf16[3,7,32,256]{3,2,1,0:T(8,128)(2,1)}, u32[]{:S(2)}, u32[]{:S(2)}) collective-permute-start(bf16[3,7,32,256]{3,2,1,0:T(8,128)(2,1)S(1)} %get-tuple-element.59.refs_6_), channel_id=1, source_target_pairs={{0,1},{1,0},{2,3},{3,2},{4,5},{5,4},{6,7},{7,6},{8,9},{9,8},{10,11... | collective-permute-start | bytes 1032200 | tf_op jit(solution)/shard_map/ppermute | solution.py:359
  79.2 8.9 %copy-start.16 = (bf16[3,7,32,256]{3,2,1,0:T(8,128)(2,1)}, bf16[3,7,32,256]{3,2,1,0:T(8,128)(2,1)S(1)}, u32[]{:S(2)}) copy-start(bf16[3,7,32,256]{3,2,1,0:T(8,128)(2,1)S(1)} %collective-permute-done.25.refs_9_) | copy-start | bytes 1032196
  85.3 1.7 %collective-permute-start.26 = (bf16[3,7,32,256]{3,2,1,0:T(8,128)(2,1)S(1)}, bf16[3,7,32,256]{3,2,1,0:T(8,128)(2,1)S(1)}, u32[]{:S(2)}, u32[]{:S(2)}) collective-permute-start(bf16[3,7,32,256]{3,2,1,0:T(8,128)(2,1)S(1)} %collective-permute-done.25.refs_9_), channel_id=1, source_target_pairs={{0,1},{1,0},{2,3},{3,2},{4,5},{5,4},{6,7},{7,6},{8,9},{9,8},{10,11... | collective-permute-start | bytes 1032200 | tf_op jit(solution)/shard_map/ppermute | solution.py:359
  85.3 2.8 %copy-start.17 = (bf16[3,7,32,256]{3,2,1,0:T(8,128)(2,1)}, bf16[3,7,32,256]{3,2,1,0:T(8,128)(2,1)S(1)}, u32[]{:S(2)}) copy-start(bf16[3,7,32,256]{3,2,1,0:T(8,128)(2,1)S(1)} %collective-permute-done.23.refs_8_) | copy-start | bytes 1032196
  85.3 2.1 %collective-permute-start.24 = (bf16[3,7,32,256]{3,2,1,0:T(8,128)(2,1)S(1)}, bf16[3,7,32,256]{3,2,1,0:T(8,128)(2,1)S(1)}, u32[]{:S(2)}, u32[]{:S(2)}) collective-permute-start(bf16[3,7,32,256]{3,2,1,0:T(8,128)(2,1)S(1)} %collective-permute-done.23.refs_8_), channel_id=1, source_target_pairs={{0,1},{1,0},{2,3},{3,2},{4,5},{5,4},{6,7},{7,6},{8,9},{9,8},{10,11... | collective-permute-start | bytes 1032200 | tf_op jit(solution)/shard_map/ppermute | solution.py:359
  85.8 2.3 %collective-permute-start.22 = (bf16[3,7,32,256]{3,2,1,0:T(8,128)(2,1)}, bf16[3,7,32,256]{3,2,1,0:T(8,128)(2,1)S(1)}, u32[]{:S(2)}, u32[]{:S(2)}) collective-permute-start(bf16[3,7,32,256]{3,2,1,0:T(8,128)(2,1)} %collective-permute-done.21.refs_7_), channel_id=1, source_target_pairs={{0,1},{1,0},{2,3},{3,2},{4,5},{5,4},{6,7},{7,6},{8,9},{9,8},{10,11... | collective-permute-start | bytes 1032200 | tf_op jit(solution)/shard_map/ppermute | solution.py:359
  85.9 2.3 %copy-start.15 = (bf16[7,128,256]{2,1,0:T(8,128)(2,1)}, bf16[7,128,256]{2,1,0:T(8,128)(2,1)S(1)}, u32[]{:S(2)}) copy-start(bf16[7,128,256]{2,1,0:T(8,128)(2,1)S(1)} %collective-permute-done.27.refs_10_) | copy-start | bytes 1376260

commit v5 on v4

--- a/solution.py
+++ b/solution.py
@@ -208,18 +208,40 @@
     return call(join_body, [(len(arrays), count // blocks, rows, cols)] * blocks, [], arrays, cost=cost)
 
 
-def lend_body(grid, down, up, low, high):
+class Copies:
+    def __init__(self, sems, at, *plans):
+        self.each = []
+        for src, dst, pieces in plans:
+            rows = src.shape[0] // pieces
+            cuts = [slice(i * rows, (i + 1) * rows) for i in range(pieces)]
+            self.each.append([pltpu.make_async_copy(src.at[cut], dst.at[cut], sems.at[at + i]) for i, cut in enumerate(cuts)])
+            at += pieces
+        for copy in sum(self.each, []):
+            copy.start()
+
+    def wait(self, *which):
+        for i in which:
+            for copy in self.each[i]:
+                copy.wait()
+
+
+def lend_body(grid_in, down_in, up_in, low, high, grid, down, up, sems):
+    copies = Copies(sems, 0, (down_in, down, 1), (up_in, up, 1), (grid_in, grid, 1))
+    copies.wait(0, 1, 2)
     low[...] = dot(one_hot(down[...], grid.shape[0]), grid[...]).astype(BF)
     high[...] = dot(one_hot(up[...], grid.shape[0]), grid[...]).astype(BF)
 
 
-def gather_body(grid, low, high, nodes, slots, targets, out):
+def gather_body(grid, low, high, nodes, slots, targets, edges, out, sem):
+    depth = grid.shape[1]
+    beside = pltpu.make_async_copy(edges, out.at[:, 2 * depth :], sem)
+    beside.start()
     table = jnp.concatenate([grid[...], low[...], high[...]], axis=0)
-    depth = grid.shape[1]
     for at in range(0, out.shape[0], ROWS):
         rows = slice(at, at + ROWS)
         out[rows, 0:depth] = dot(one_hot(slots[:, rows], table.shape[0]), table).astype(BF)
-        out[rows, depth:] = dot(one_hot(targets[:, rows], nodes.shape[0]), nodes[...]).astype(BF)
+        out[rows, depth : 2 * depth] = dot(one_hot(targets[:, rows], nodes.shape[0]), nodes[...]).astype(BF)
+    beside.wait()
 
 
 def edges_to_nodes(weights, inputs, table, edge_buffer, targets, message, keep):
@@ -246,23 +268,20 @@
 
 def half_edges_body(pack, gathered, *refs):
     count = len(pack.near_operands)
-    operands, edges, out, refs = refs[:count], refs[count], refs[count + 1], refs[count + 2 :]
+    operands, out, refs = refs[:count], refs[count], refs[count + 1 :]
     saved, refs = (refs[:2], refs[2:]) if len(pack.kind) == 2 else ((), refs)
-    buffer, sems, *scratch = refs
-    fetch = pltpu.make_async_copy(edges, buffer, sems.at[0])
-    fetch.start()
+    sems, *scratch = refs
     weights, place = pack.load(operands, (), scratch)
     saves = []
     if saved:
         place("n")
-        saves = [pltpu.make_async_copy(weights[n], to, sems.at[1 + i]) for i, (n, to) in enumerate(zip(("nm", "nb"), saved))]
+        saves = [pltpu.make_async_copy(weights[n], to, sems.at[i]) for i, (n, to) in enumerate(zip(("nm", "nb"), saved))]
     for save in saves:
         save.start()
     place("e")
-    fetch.wait()
-    for at in range(0, edges.shape[0], ROWS):
+    for at in range(0, gathered.shape[0], ROWS):
         rows = slice(at, at + ROWS)
-        pre = dot(jnp.concatenate([gathered[rows, :], buffer[rows, :]], axis=1), weights["em"][...])
+        pre = dot(gathered[rows, :], weights["em"][...])
         out[rows, :] = dot(silu(pre).astype(BF), weights["eb"][...]).astype(BF)
     for save in saves:
         save.wait()
@@ -405,10 +424,15 @@
     sent_rows = send_lists.shape[1] * send_lists.shape[2]
     hidden = edge_mats.shape[3] * sizes[3]
     lists = send_lists.reshape(1, -1)
+    lists_back = send_lists[:, ::-1].reshape(1, -1)
     node_buffer, edge_buffer = pltpu.VMEM((nodes, depth), BF), pltpu.VMEM((mesh_edges, depth), BF)
 
     lent_down, lent_up = call(
-        lend_body, [(halo, depth), (halo, depth)], [], [grid_latent, halo_down[None, :], halo_up[None, :]]
+        lend_body,
+        [(halo, depth), (halo, depth)],
+        [pltpu.VMEM(grid_latent.shape, BF)] + [pltpu.VMEM((1, halo), jnp.int32)] * 2 + [pltpu.SemaphoreType.DMA((3,))],
+        [],
+        [grid_latent, halo_down[None, :], halo_up[None, :]],
     )
     if by_parts:
         raws = [edge_mats, edge_back, node_mats, node_back]
@@ -429,9 +453,10 @@
         packs = weights_whole(edge_mats, node_mats, edge_back, node_back)
     gathered = call(
         gather_body,
-        (grid_edges, 2 * depth),
-        [],
+        (grid_edges, 3 * depth),
+        [pltpu.SemaphoreType.DMA(())],
         [grid_latent, from_lower, from_upper, mesh_latent, encoder_slot[None, :], encoder_target[None, :]],
+        [grid_edge],
         cost=1.2,
     )
     if by_parts:
@@ -440,9 +465,8 @@
     term, *node_weights = call(
         functools.partial(half_edges_body, pack),
         [((grid_edges, depth), BF)] + [(shape, BF) for shape in (weight_shapes("n", hidden // 2, depth) if by_parts else [])],
-        [pltpu.VMEM((grid_edges, depth), BF), pltpu.SemaphoreType.DMA((3,))] + pack.scratch(hidden // 2, depth),
+        [pltpu.SemaphoreType.DMA((2,))] + pack.scratch(hidden // 2, depth),
         [gathered] + pack.near_operands,
-        [grid_edge],
         cost=3.0,
         far=2 if by_parts else 0,
     )
@@ -465,16 +489,21 @@
         first_next_body,
         [(sent_rows, depth), (nodes, depth)],
         [node_buffer, pltpu.SemaphoreType.DMA(())],
-        [mesh_latent, lists, term, swap_width(term), mark(term, 5.0)],
+        [mesh_latent, lists_back, term, swap_width(term), mark(term, 5.0)],
         cost=1.6,
         far=1,
     )
     edges = mesh_edge
     slots, targets = mesh_slot[None, :], mesh_target[None, :]
+    room = send_lists.shape[2]
+    slots_back = ((line - 1 - mesh_slot // room) * room + mesh_slot % room)[None, :]
     for block in range(1, edge_mats.shape[0]):
         last = block == edge_mats.shape[0] - 1
         cut_rows = packed.reshape(send_lists.shape[1:] + (depth,))
-        sent = lax.all_to_all(cut_rows, ("mesh", "band"), split_axis=0, concat_axis=0, tiled=True).reshape(-1, depth)
+        order = [list(reversed(range(line)))]
+        sent = lax.all_to_all(
+            cut_rows, ("mesh", "band"), split_axis=0, concat_axis=0, axis_index_groups=order, tiled=True
+        ).reshape(-1, depth)
         if by_parts:
             if not last:
                 plane2 = over_plane(after(joined2, sent))
@@ -491,7 +520,7 @@
             functools.partial(block_body, pack, last),
             (nodes, depth) if last else [(sent_rows, depth), (nodes, depth), (mesh_edges, depth)],
             [edge_buffer, table, node_buffer, edge_buffer, pltpu.SemaphoreType.DMA((4,))] + pack.scratch(hidden, depth),
-            [sent, slots, targets, lists] + pack.near_operands,
+            [sent, slots_back, targets, lists_back] + pack.near_operands,
             [rows, edges] + pack.far_operands,
             cost=6.5,
             far=0 if last else 2,

time: 94.9 us -> 92 us (0.969)
  waiting for transfers between devices: 30 us -> 22.1 us
  starting transfers between devices: 39.1 us -> 44.4 us
    all_to_all x2, waiting for transfers between devices: 12.4 us -> 4.94 us  [on_device(): lax.all_to_all(cut_rows, ('mesh', 'band'), split_axis=0, concat_axis=0, a...]
    all_to_all x2, starting transfers between devices: 8.91 us -> 15 us  [on_device(): lax.all_to_all(cut_rows, ('mesh', 'band'), split_axis=0, concat_axis=0, a...]
  transfers between devices with their start and end apart: 31 -> 31, of which waited for: 13 -> 11; matrix products, arithmetic and copies ran while one was open for 0% -> 0% of each run, Pallas kernels for 15% -> 17%
where the time goes in v5:
time: 92 us; the launch traced here: 91.5 us
  starting transfers between devices  44.4 us (48%)
  Pallas kernels  24.3 us (26%)
  waiting for transfers between devices  22.1 us (24%)
    pallas_call x12, Pallas kernels, call(): pl.pallas_call(body, out_shape=shapes if many else shapes[0], in_specs=sp...  24.3 us
    all_to_all x2, starting transfers between devices, on_device(): lax.all_to_all(cut_rows, ('mesh', 'band'), split_axis=0, concat_axis=0, a...  15 us
    ppermute x6, starting transfers between devices, over_slices(): lax.ppermute(chunk, 'mesh', [(i, i ^ k) for i in range(count)])  10.8 us
    ppermute x6, waiting for transfers between devices, over_slices(): lax.ppermute(chunk, 'mesh', [(i, i ^ k) for i in range(count)])  9.34 us
    ppermute x3, starting transfers between devices, over_plane(): across = lax.ppermute(own, ('groups', 'band'), DIAGONAL)  7.94 us
    all_to_all x2, waiting for transfers between devices, on_device(): lax.all_to_all(cut_rows, ('mesh', 'band'), split_axis=0, concat_axis=0, a...  4.94 us
    ppermute x12, waiting for transfers between devices, swap_width(): return lax.ppermute(array, 'width', SWAP)  3.84 us
    ppermute x1, starting transfers between devices, on_device(): lax.ppermute(lent_up, ('mesh', 'band'), [(i, i + 1) for i in range(line -...  3.4 us
  transfers between devices with their start and end apart: 31, of which 11 were waited for; matrix products, arithmetic and copies ran while one was open for 0% of the time, Pallas kernels for 17%

profile of v5, /device:TPU:0, one launch (start us, length us, event | category | flops | bytes accessed | tf_op | source)
XLA Modules:
  0.0 91.5 jit_solution(5919113951952467315)
XLA Ops:
  0.0 0.9 shard_map.146
  0.9 3.1 %collective-permute-start = (bf16[7,32,256]{2,1,0:T(8,128)(2,1)S(1)}, bf16[7,32,256]{2,1,0:T(8,128)(2,1)S(1)}, u32[]{:S(2)}, u32[]{:S(2)}) collective-permute-start(bf16[7,32,256]{2,1,0:T(8,128)(2,1)S(1)} %shard_map.146), channel_id=1, source_target_pairs={{0,4},{4,0},{8,12},{12,8},{1,5},{5,1},{9,13},{13,9},{2,6},{6,2},{1... | collective-permute-start | bytes 344072 | tf_op jit(solution)/shard_map/ppermute | solution.py:367
  4.0 2.5 %collective-permute-start.4 = (bf16[7,32,256]{2,1,0:T(8,128)(2,1)S(1)}, bf16[7,32,256]{2,1,0:T(8,128)(2,1)S(1)}, u32[]{:S(2)}, u32[]{:S(2)}) collective-permute-start(bf16[7,32,256]{2,1,0:T(8,128)(2,1)S(1)} %shard_map.146), channel_id=1, source_target_pairs={{0,12},{4,8},{8,4},{12,0},{1,13},{5,9},{9,5},{13,1},{2,14},{6,10},... | collective-permute-start | bytes 344072 | tf_op jit(solution)/shard_map/ppermute | solution.py:367
  6.4 0.1 collective-permute-start.3
  6.6 1.5 %shard_map.145 = (bf16[64,512]{1,0:T(8,128)(2,1)S(1)}, bf16[64,512]{1,0:T(8,128)(2,1)S(1)}) custom-call(bf16[512,512]{1,0:T(8,128)(2,1)} %grid.1, s32[1,64]{1,0:T(1,128)} %bitcast.8, s32[1,64]{1,0:T(1,128)} %bitcast.9), custom_call_target="tpu_custom_call" | custom-call | flops 500000000 | tf_op jit(solution)/shard_map/pallas_call | solution.py:59
  8.1 0.0 collective-permute-done.refs_0_
  8.1 3.4 %collective-permute-start.1 = (bf16[64,512]{1,0:T(8,128)(2,1)S(1)}, bf16[64,512]{1,0:T(8,128)(2,1)S(1)}, u32[]{:S(2)}, u32[]{:S(2)}) collective-permute-start(bf16[64,512]{1,0:T(8,128)(2,1)S(1)} %get-tuple-element.37), channel_id=1, source_target_pairs={{0,2},{2,4},{4,6},{6,8},{8,10},{10,12},{12,14},{1,3},{3,5},{5,7},{... | collective-permute-start | bytes 196616 | tf_op jit(solution)/shard_map/ppermute | solution.py:446
  11.5 1.3 %collective-permute-start.2 = (bf16[64,512]{1,0:T(8,128)(2,1)S(1)}, bf16[64,512]{1,0:T(8,128)(2,1)S(1)}, u32[]{:S(2)}, u32[]{:S(2)}) collective-permute-start(bf16[64,512]{1,0:T(8,128)(2,1)S(1)} %get-tuple-element.39), channel_id=1, source_target_pairs={{2,0},{4,2},{6,4},{8,6},{10,8},{12,10},{14,12},{3,1},{5,3},{7,5},{... | collective-permute-start | bytes 196616 | tf_op jit(solution)/shard_map/ppermute | solution.py:445
  12.8 1.8 %shard_map.148 = (bf16[14,32,256]{2,1,0:T(8,128)(2,1)S(1)}, bf16[7,128,256]{2,1,0:T(8,128)(2,1)S(1)}, bf16[7,128,256]{2,1,0:T(8,128)(2,1)S(1)}, bf16[7,128,256]{2,1,0:T(8,128)(2,1)S(1)}) custom-call(bf16[3,3,128,256]{3,2,1,0:T(8,128)(2,1)} %refs_0_.3, bf16[3,256,128]{2,1,0:T(8,128)(2,1)} %refs_1_.3, bf16[3,2,128,256]{3,2,1,0:T(8,128)(2,1)} %refs_2_.3, ...), custom_call_target="tpu_custom_call" | custom-call | flops 500000000 | tf_op jit(solution)/shard_map/pallas_call | solution.py:59
  14.6 0.0 collective-permute-done.4.refs_2_
  14.7 0.0 collective-permute-done.1.low
  14.7 3.0 %collective-permute-done.2.high = bf16[64,512]{1,0:T(8,128)(2,1)S(1)} collective-permute-done((bf16[64,512]{1,0:T(8,128)(2,1)S(1)}, bf16[64,512]{1,0:T(8,128)(2,1)S(1)}, u32[]{:S(2)}, u32[]{:S(2)}) %collective-permute-start.2) | collective-permute-done | bytes 65568 | tf_op jit(solution)/shard_map/ppermute | solution.py:445
  17.7 0.0 collective-permute-done.3.refs_1_
  17.7 1.9 %collective-permute-start.5 = (bf16[14,32,256]{2,1,0:T(8,128)(2,1)S(1)}, bf16[14,32,256]{2,1,0:T(8,128)(2,1)S(1)}, u32[]{:S(2)}, u32[]{:S(2)}) collective-permute-start(bf16[14,32,256]{2,1,0:T(8,128)(2,1)S(1)} %get-tuple-element.43), channel_id=1, source_target_pairs={{0,4},{4,0},{8,12},{12,8},{1,5},{5,1},{9,13},{13,9},{2,6},{6,2},{1... | collective-permute-start | bytes 688136 | tf_op jit(solution)/shard_map/ppermute | solution.py:367
  19.6 2.9 %collective-permute-start.6 = (bf16[14,32,256]{2,1,0:T(8,128)(2,1)S(1)}, bf16[14,32,256]{2,1,0:T(8,128)(2,1)S(1)}, u32[]{:S(2)}, u32[]{:S(2)}) collective-permute-start(bf16[14,32,256]{2,1,0:T(8,128)(2,1)S(1)} %get-tuple-element.43), channel_id=1, source_target_pairs={{0,8},{4,12},{8,0},{12,4},{1,9},{5,13},{9,1},{13,5},{2,10},{6,14},... | collective-permute-start | bytes 688136 | tf_op jit(solution)/shard_map/ppermute | solution.py:367
  22.5 0.4 collective-permute-start.7
  22.9 3.1 %collective-permute-start.10 = (bf16[3,7,32,256]{3,2,1,0:T(8,128)(2,1)S(1)}, bf16[3,7,32,256]{3,2,1,0:T(8,128)(2,1)S(1)}, u32[]{:S(2)}, u32[]{:S(2)}) collective-permute-start(bf16[3,7,32,256]{3,2,1,0:T(8,128)(2,1)S(1)} %shard_map.149.refs_1_), channel_id=1, source_target_pairs={{0,18},{18,0},{2,16},{16,2},{1,19},{19,1},{3,17},{17,3},{4,22},{22... | collective-permute-start | bytes 1032200 | tf_op jit(solution)/shard_map/ppermute | solution.py:371
  25.9 0.9 collective-permute-done.5.refs_0_
  26.8 1.5 %collective-permute-start.9 = (bf16[3,7,32,256]{3,2,1,0:T(8,128)(2,1)S(1)}, bf16[3,7,32,256]{3,2,1,0:T(8,128)(2,1)S(1)}, u32[]{:S(2)}, u32[]{:S(2)}) collective-permute-start(bf16[3,7,32,256]{3,2,1,0:T(8,128)(2,1)S(1)} %shard_map.149.refs_1_), channel_id=1, source_target_pairs={{0,16},{16,0},{1,17},{17,1},{2,18},{18,2},{3,19},{19,3},{4,20},{20... | collective-permute-start | bytes 1032200 | tf_op jit(solution)/shard_map/ppermute | solution.py:372
  28.4 1.3 %shard_map.147.gathered = bf16[768,1536]{1,0:T(8,128)(2,1)S(1)} custom-call(bf16[512,512]{1,0:T(8,128)(2,1)S(1)} %copy-done, bf16[64,512]{1,0:T(8,128)(2,1)S(1)} %collective-permute-done.1.low, bf16[64,512]{1,0:T(8,128)(2,1)S(1)} %collective-permute-done.2.high, bf16[320,512]{1,0:T(8,128)(2,1)S(1)} %copy-done.5, s32[1,768]{1,0:T(1,128)S(1)} %broadcast_in_dim.22.slots, ...), custom_call_target="tpu_custom_call" | custom-call | flops 1200000000 | tf_op jit(solution)/shard_map/pallas_call | solution.py:59
  29.6 8.4 %collective-permute-done.6.refs_1_ = bf16[14,32,256]{2,1,0:T(8,128)(2,1)S(1)} collective-permute-done((bf16[14,32,256]{2,1,0:T(8,128)(2,1)S(1)}, bf16[14,32,256]{2,1,0:T(8,128)(2,1)S(1)}, u32[]{:S(2)}, u32[]{:S(2)}) %collective-permute-start.6) | collective-permute-done | bytes 229408 | tf_op jit(solution)/shard_map/ppermute | solution.py:367
  38.1 0.0 copy-start.10
  38.1 0.0 collective-permute-done.10.refs_4_
  38.1 0.7 collective-permute-done.8.refs_2_
  38.9 0.2 collective-permute-done.9.refs_3_
  39.1 2.0 %shard_map.151 = (bf16[768,512]{1,0:T(8,128)(2,1)S(1)}, bf16[1024,256]{1,0:T(8,128)(2,1)}, bf16[256,512]{1,0:T(8,128)(2,1)}) custom-call(bf16[768,1536]{1,0:T(8,128)(2,1)S(1)} %shard_map.147.gathered, bf16[7,128,256]{2,1,0:T(8,128)(2,1)S(1)} %get-tuple-element.45.refs_0_, bf16[3,7,32,256]{3,2,1,0:T(8,128)(2,1)S(1)} %shard_map.149.refs_1_, ...), custom_call_target="tpu_custom_call" | custom-call | flops 3000000000 | tf_op jit(solution)/shard_map/pallas_call | solution.py:59
  41.1 0.1 collective-permute-start.11
  41.2 0.1 reshape.15.lists
  41.3 2.6 %collective-permute-start.17 = (bf16[3,7,32,256]{3,2,1,0:T(8,128)(2,1)S(1)}, bf16[3,7,32,256]{3,2,1,0:T(8,128)(2,1)}, u32[]{:S(2)}, u32[]{:S(2)}) collective-permute-start(bf16[3,7,32,256]{3,2,1,0:T(8,128)(2,1)S(1)} %get-tuple-element.50.refs_6_), channel_id=1, source_target_pairs={{0,18},{18,0},{2,16},{16,2},{1,19},{19,1},{3,17},{17,3},{4,22},{22... | collective-permute-start | bytes 1032200 | tf_op jit(solution)/shard_map/ppermute | solution.py:371
  43.9 0.6 collective-permute-start.15
  44.5 0.3 collective-permute-start.13
  44.8 0.0 collective-permute-done.11.other
  44.8 2.5 %shard_map.152.source.mine = bf16[320,512]{1,0:T(8,128)(2,1)S(1)} custom-call(s32[1,768]{1,0:T(1,128)S(1)} %broadcast_in_dim.19.targets, bf16[768,512]{1,0:T(8,128)(2,1)S(1)} %get-tuple-element.46.mine, bf16[768,512]{1,0:T(8,128)(2,1)S(1)} %collective-permute-done.11.other, bf16[320,512]{1,0:T(8,128)(2,1)} %nodes.3, ...), custom_call_target="tpu_custom_call" | custom-call | flops 1600000000 | tf_op jit(solution)/shard_map/pallas_call | solution.py:59
  47.3 0.0 copy-start.6
  47.3 0.1 collective-permute-start.12
  47.4 0.0 copy-start.11
  47.4 0.0 copy-start.9
  47.4 1.6 %collective-permute-done.12.other = bf16[320,512]{1,0:T(8,128)(2,1)S(1)} collective-permute-done((bf16[320,512]{1,0:T(8,128)(2,1)S(1)}, bf16[320,512]{1,0:T(8,128)(2,1)S(1)}, u32[]{:S(2)}, u32[]{:S(2)}) %collective-permute-start.12) | collective-permute-done | bytes 327712 | tf_op jit(solution)/shard_map/ppermute | solution.py:378
  49.0 1.6 %shard_map.154 = (bf16[64,512]{1,0:T(8,128)(2,1)}, bf16[320,512]{1,0:T(8,128)(2,1)}) custom-call(bf16[320,512]{1,0:T(8,128)(2,1)S(1)} %copy-done.6, s32[1,64]{1,0:T(1,128)S(1)} %reshape.15.lists, bf16[320,512]{1,0:T(8,128)(2,1)S(1)} %shard_map.152.source.mine, bf16[320,512]{1,0:T(8,128)(2,1)S(1)} %collective-permute-done.12.other, ...), custom_call_target="tpu_custom_call" | custom-call | flops 1600000000 | tf_op jit(solution)/shard_map/pallas_call | solution.py:59
  50.7 7.8 %all-to-all-start = ((bf16[8,8,512]{2,1,0:T(8,128)(2,1)}), bf16[8,8,512]{2,1,0:T(8,128)(2,1)S(1)}, u32[]{:S(2)}, u32[]{:S(2)}) async-start(bf16[8,8,512]{2,1,0:T(8,128)(2,1)} %bitcast.2), calls=%async_computation | async-start | bytes 131072 | tf_op jit(solution)/shard_map/all_to_all | solution.py:504
  58.5 0.5 collective-permute-start.20
  59.0 0.0 collective-permute-done.17.refs_9_
  59.0 2.5 %all-to-all-done = bf16[8,8,512]{2,1,0:T(8,128)(2,1)S(1)} async-done(((bf16[8,8,512]{2,1,0:T(8,128)(2,1)}), bf16[8,8,512]{2,1,0:T(8,128)(2,1)S(1)}, u32[]{:S(2)}, u32[]{:S(2)}) %all-to-all-start) | async-done | bytes 65568 | tf_op jit(solution)/shard_map/all_to_all | solution.py:504
  61.4 0.0 collective-permute-start.18
  61.4 0.0 collective-permute-done.15.refs_8_
  61.5 0.5 collective-permute-start.16
  62.0 0.0 collective-permute-done.13.refs_7_
  62.0 0.1 collective-permute-start.14
  62.1 2.2 %collective-permute-start.25 = (bf16[3,7,32,256]{3,2,1,0:T(8,128)(2,1)S(1)}, bf16[3,7,32,256]{3,2,1,0:T(8,128)(2,1)S(1)}, u32[]{:S(2)}, u32[]{:S(2)}) collective-permute-start(bf16[3,7,32,256]{3,2,1,0:T(8,128)(2,1)S(1)} %get-tuple-element.59.refs_6_), channel_id=1, source_target_pairs={{0,18},{18,0},{2,16},{16,2},{1,19},{19,1},{3,17},{17,3},{4,22},{22... | collective-permute-start | bytes 1032200 | tf_op jit(solution)/shard_map/ppermute | solution.py:371
  64.3 0.5 collective-permute-start.23
  64.8 0.8 collective-permute-start.21
  65.7 6.6 %shard_map.155 = (bf16[64,512]{1,0:T(8,128)(2,1)}, bf16[320,512]{1,0:T(8,128)(2,1)}, bf16[768,512]{1,0:T(8,128)(2,1)}) custom-call(bf16[64,512]{1,0:T(8,128)(2,1)S(1)} %bitcast.6, s32[1,768]{1,0:T(1,128)S(1)} %broadcast_in_dim.23.slots, s32[1,768]{1,0:T(1,128)S(1)} %broadcast_in_dim.24.targets, s32[1,64]{1,0:T(1,128)S(1)} %reshape.15.lists, ...), custom_call_target="tpu_custom_call" | custom-call | flops 6499999744 | tf_op jit(solution)/shard_map/pallas_call | solution.py:59
  72.2 7.2 %all-to-all-start.1 = ((bf16[8,8,512]{2,1,0:T(8,128)(2,1)}), bf16[8,8,512]{2,1,0:T(8,128)(2,1)S(1)}, u32[]{:S(2)}, u32[]{:S(2)}) async-start(bf16[8,8,512]{2,1,0:T(8,128)(2,1)} %bitcast.4), calls=%async_computation.1 | async-start | bytes 131072 | tf_op jit(solution)/shard_map/all_to_all | solution.py:504
  79.4 0.0 collective-permute-start.27
  79.5 0.5 collective-permute-start.28
  80.0 2.5 %all-to-all-done.1 = bf16[8,8,512]{2,1,0:T(8,128)(2,1)S(1)} async-done(((bf16[8,8,512]{2,1,0:T(8,128)(2,1)}), bf16[8,8,512]{2,1,0:T(8,128)(2,1)S(1)}, u32[]{:S(2)}, u32[]{:S(2)}) %all-to-all-start.1) | async-done | bytes 65568 | tf_op jit(solution)/shard_map/all_to_all | solution.py:504
  82.4 0.5 collective-permute-start.24
  82.9 0.1 collective-permute-start.22
  83.0 0.0 collective-permute-done.28.refs_11_
  83.0 0.0 collective-permute-done.27.refs_10_
  83.0 1.0 %collective-permute-done.26.refs_2_ = bf16[3,7,32,256]{3,2,1,0:T(8,128)(2,1)S(1)} collective-permute-done((bf16[3,7,32,256]{3,2,1,0:T(8,128)(2,1)S(1)}, bf16[3,7,32,256]{3,2,1,0:T(8,128)(2,1)S(1)}, u32[]{:S(2)}, u32[]{:S(2)}) %collective-permute-start.26) | collective-permute-done | bytes 344096 | tf_op jit(solution)/shard_map/ppermute | solution.py:378
  84.1 0.5 collective-permute-done.24.refs_1_
  84.6 0.7 collective-permute-done.22.refs_0_
  85.3 6.1 %shard_map.156 = bf16[320,512]{1,0:T(8,128)(2,1)} custom-call(bf16[64,512]{1,0:T(8,128)(2,1)S(1)} %bitcast.7, s32[1,768]{1,0:T(1,128)S(1)} %broadcast_in_dim.23.slots, s32[1,768]{1,0:T(1,128)S(1)} %broadcast_in_dim.24.targets, s32[1,64]{1,0:T(1,128)S(1)} %reshape.15.lists, bf16[3,7,32,256]{3,2,1,0:T(8,128)(2,1)S(1)} %collective-permute-done.22.refs_0_, ...), custom_call_target="tpu_custom_call" | custom-call | flops 6499999744 | tf_op jit(solution)/shard_map/pallas_call | solution.py:59
  (49 shorter events, 0.2 us)
Async XLA Ops:
  0.9 7.2 %collective-permute-start = (bf16[7,32,256]{2,1,0:T(8,128)(2,1)S(1)}, bf16[7,32,256]{2,1,0:T(8,128)(2,1)S(1)}, u32[]{:S(2)}, u32[]{:S(2)}) collective-permute-start(bf16[7,32,256]{2,1,0:T(8,128)(2,1)S(1)} %shard_map.146), channel_id=1, source_target_pairs={{0,4},{4,0},{8,12},{12,8},{1,5},{5,1},{9,13},{13,9},{2,6},{6,2},{1... | collective-permute-start | bytes 344072 | tf_op jit(solution)/shard_map/ppermute | solution.py:367
  4.0 10.7 %collective-permute-start.4 = (bf16[7,32,256]{2,1,0:T(8,128)(2,1)S(1)}, bf16[7,32,256]{2,1,0:T(8,128)(2,1)S(1)}, u32[]{:S(2)}, u32[]{:S(2)}) collective-permute-start(bf16[7,32,256]{2,1,0:T(8,128)(2,1)S(1)} %shard_map.146), channel_id=1, source_target_pairs={{0,12},{4,8},{8,4},{12,0},{1,13},{5,9},{9,5},{13,1},{2,14},{6,10},... | collective-permute-start | bytes 344072 | tf_op jit(solution)/shard_map/ppermute | solution.py:367
  6.4 11.2 %collective-permute-start.3 = (bf16[7,32,256]{2,1,0:T(8,128)(2,1)S(1)}, bf16[7,32,256]{2,1,0:T(8,128)(2,1)S(1)}, u32[]{:S(2)}, u32[]{:S(2)}) collective-permute-start(bf16[7,32,256]{2,1,0:T(8,128)(2,1)S(1)} %shard_map.146), channel_id=1, source_target_pairs={{0,8},{4,12},{8,0},{12,4},{1,9},{5,13},{9,1},{13,5},{2,10},{6,14},... | collective-permute-start | bytes 344072 | tf_op jit(solution)/shard_map/ppermute | solution.py:367
  6.6 16.3 %copy-start.7 = (s32[768]{0:T(1024)S(1)}, s32[768]{0:T(1024)}, u32[]{:S(2)}) copy-start(s32[768]{0:T(1024)} %param.20) | copy-start | bytes 9220
  6.6 16.3 %copy-start.8 = (s32[768]{0:T(1024)S(1)}, s32[768]{0:T(1024)}, u32[]{:S(2)}) copy-start(s32[768]{0:T(1024)} %param.19) | copy-start | bytes 9220
  6.6 21.8 %copy-start = (bf16[512,512]{1,0:T(8,128)(2,1)S(1)}, bf16[512,512]{1,0:T(8,128)(2,1)}, u32[]{:S(2)}) copy-start(bf16[512,512]{1,0:T(8,128)(2,1)} %grid.1) | copy-start | bytes 1572868
  6.6 21.8 %copy-start.5 = (bf16[320,512]{1,0:T(8,128)(2,1)S(1)}, bf16[320,512]{1,0:T(8,128)(2,1)}, u32[]{:S(2)}) copy-start(bf16[320,512]{1,0:T(8,128)(2,1)} %nodes.3) | copy-start | bytes 983044
  8.1 6.5 %collective-permute-start.1 = (bf16[64,512]{1,0:T(8,128)(2,1)S(1)}, bf16[64,512]{1,0:T(8,128)(2,1)S(1)}, u32[]{:S(2)}, u32[]{:S(2)}) collective-permute-start(bf16[64,512]{1,0:T(8,128)(2,1)S(1)} %get-tuple-element.37), channel_id=1, source_target_pairs={{0,2},{2,4},{4,6},{6,8},{8,10},{10,12},{12,14},{1,3},{3,5},{5,7},{... | collective-permute-start | bytes 196616 | tf_op jit(solution)/shard_map/ppermute | solution.py:446
  11.5 6.2 %collective-permute-start.2 = (bf16[64,512]{1,0:T(8,128)(2,1)S(1)}, bf16[64,512]{1,0:T(8,128)(2,1)S(1)}, u32[]{:S(2)}, u32[]{:S(2)}) collective-permute-start(bf16[64,512]{1,0:T(8,128)(2,1)S(1)} %get-tuple-element.39), channel_id=1, source_target_pairs={{2,0},{4,2},{6,4},{8,6},{10,8},{12,10},{14,12},{3,1},{5,3},{7,5},{... | collective-permute-start | bytes 196616 | tf_op jit(solution)/shard_map/ppermute | solution.py:445
  14.6 43.8 %copy-start.2 = (bf16[7,128,256]{2,1,0:T(8,128)(2,1)}, bf16[7,128,256]{2,1,0:T(8,128)(2,1)S(1)}, u32[]{:S(2)}) copy-start(bf16[7,128,256]{2,1,0:T(8,128)(2,1)S(1)} %get-tuple-element.56.refs_5_) | copy-start | bytes 1376260
  14.6 64.8 %copy-start.1 = (bf16[7,128,256]{2,1,0:T(8,128)(2,1)}, bf16[7,128,256]{2,1,0:T(8,128)(2,1)S(1)}, u32[]{:S(2)}) copy-start(bf16[7,128,256]{2,1,0:T(8,128)(2,1)S(1)} %get-tuple-element.66.refs_5_) | copy-start | bytes 1376260
  17.7 9.1 %collective-permute-start.5 = (bf16[14,32,256]{2,1,0:T(8,128)(2,1)S(1)}, bf16[14,32,256]{2,1,0:T(8,128)(2,1)S(1)}, u32[]{:S(2)}, u32[]{:S(2)}) collective-permute-start(bf16[14,32,256]{2,1,0:T(8,128)(2,1)S(1)} %get-tuple-element.43), channel_id=1, source_target_pairs={{0,4},{4,0},{8,12},{12,8},{1,5},{5,1},{9,13},{13,9},{2,6},{6,2},{1... | collective-permute-start | bytes 688136 | tf_op jit(solution)/shard_map/ppermute | solution.py:367
  19.6 18.5 %collective-permute-start.6 = (bf16[14,32,256]{2,1,0:T(8,128)(2,1)S(1)}, bf16[14,32,256]{2,1,0:T(8,128)(2,1)S(1)}, u32[]{:S(2)}, u32[]{:S(2)}) collective-permute-start(bf16[14,32,256]{2,1,0:T(8,128)(2,1)S(1)} %get-tuple-element.43), channel_id=1, source_target_pairs={{0,8},{4,12},{8,0},{12,4},{1,9},{5,13},{9,1},{13,5},{2,10},{6,14},... | collective-permute-start | bytes 688136 | tf_op jit(solution)/shard_map/ppermute | solution.py:367
  22.5 15.6 %collective-permute-start.7 = (bf16[14,32,256]{2,1,0:T(8,128)(2,1)S(1)}, bf16[14,32,256]{2,1,0:T(8,128)(2,1)S(1)}, u32[]{:S(2)}, u32[]{:S(2)}) collective-permute-start(bf16[14,32,256]{2,1,0:T(8,128)(2,1)S(1)} %get-tuple-element.43), channel_id=1, source_target_pairs={{0,12},{4,8},{8,4},{12,0},{1,13},{5,9},{9,5},{13,1},{2,14},{6,10},... | collective-permute-start | bytes 688136 | tf_op jit(solution)/shard_map/ppermute | solution.py:367
  22.9 15.3 %collective-permute-start.10 = (bf16[3,7,32,256]{3,2,1,0:T(8,128)(2,1)S(1)}, bf16[3,7,32,256]{3,2,1,0:T(8,128)(2,1)S(1)}, u32[]{:S(2)}, u32[]{:S(2)}) collective-permute-start(bf16[3,7,32,256]{3,2,1,0:T(8,128)(2,1)S(1)} %shard_map.149.refs_1_), channel_id=1, source_target_pairs={{0,18},{18,0},{2,16},{16,2},{1,19},{19,1},{3,17},{17,3},{4,22},{22... | collective-permute-start | bytes 1032200 | tf_op jit(solution)/shard_map/ppermute | solution.py:371
  25.9 13.0 %collective-permute-start.8 = (bf16[3,7,32,256]{3,2,1,0:T(8,128)(2,1)S(1)}, bf16[3,7,32,256]{3,2,1,0:T(8,128)(2,1)S(1)}, u32[]{:S(2)}, u32[]{:S(2)}) collective-permute-start(bf16[3,7,32,256]{3,2,1,0:T(8,128)(2,1)S(1)} %shard_map.149.refs_1_), channel_id=1, source_target_pairs={{0,2},{2,0},{1,3},{3,1},{4,6},{6,4},{5,7},{7,5},{8,10},{10,8},{9,1... | collective-permute-start | bytes 1032200 | tf_op jit(solution)/shard_map/ppermute | solution.py:373
  26.8 12.2 %collective-permute-start.9 = (bf16[3,7,32,256]{3,2,1,0:T(8,128)(2,1)S(1)}, bf16[3,7,32,256]{3,2,1,0:T(8,128)(2,1)S(1)}, u32[]{:S(2)}, u32[]{:S(2)}) collective-permute-start(bf16[3,7,32,256]{3,2,1,0:T(8,128)(2,1)S(1)} %shard_map.149.refs_1_), channel_id=1, source_target_pairs={{0,16},{16,0},{1,17},{17,1},{2,18},{18,2},{3,19},{19,3},{4,20},{20... | collective-permute-start | bytes 1032200 | tf_op jit(solution)/shard_map/ppermute | solution.py:372
  38.1 20.3 %copy-start.4 = (bf16[3,7,32,256]{3,2,1,0:T(8,128)(2,1)}, bf16[3,7,32,256]{3,2,1,0:T(8,128)(2,1)S(1)}, u32[]{:S(2)}) copy-start(bf16[3,7,32,256]{3,2,1,0:T(8,128)(2,1)S(1)} %get-tuple-element.50.refs_6_) | copy-start | bytes 1032196
  38.1 41.3 %copy-start.3 = (bf16[3,7,32,256]{3,2,1,0:T(8,128)(2,1)}, bf16[3,7,32,256]{3,2,1,0:T(8,128)(2,1)S(1)}, u32[]{:S(2)}) copy-start(bf16[3,7,32,256]{3,2,1,0:T(8,128)(2,1)S(1)} %get-tuple-element.59.refs_6_) | copy-start | bytes 1032196
  38.1 3.1 %copy-start.10 = (s32[1,8,8]{2,1,0:T(8,128)S(1)}, s32[1,8,8]{2,1,0:T(8,128)}, u32[]{:S(2)}) copy-start(s32[1,8,8]{2,1,0:T(8,128)} %param.23) | copy-start | bytes 772
  41.1 3.7 %collective-permute-start.11 = (bf16[768,512]{1,0:T(8,128)(2,1)S(1)}, bf16[768,512]{1,0:T(8,128)(2,1)S(1)}, u32[]{:S(2)}, u32[]{:S(2)}) collective-permute-start(bf16[768,512]{1,0:T(8,128)(2,1)S(1)} %get-tuple-element.46.mine), channel_id=1, source_target_pairs={{0,1},{1,0},{2,3},{3,2},{4,5},{5,4},{6,7},{7,6},{8,9},{9,8},{10,11... | collective-permute-start | bytes 2359304 | tf_op jit(solution)/shard_map/ppermute | solution.py:378
  41.3 17.7 %collective-permute-start.17 = (bf16[3,7,32,256]{3,2,1,0:T(8,128)(2,1)S(1)}, bf16[3,7,32,256]{3,2,1,0:T(8,128)(2,1)}, u32[]{:S(2)}, u32[]{:S(2)}) collective-permute-start(bf16[3,7,32,256]{3,2,1,0:T(8,128)(2,1)S(1)} %get-tuple-element.50.refs_6_), channel_id=1, source_target_pairs={{0,18},{18,0},{2,16},{16,2},{1,19},{19,1},{3,17},{17,3},{4,22},{22... | collective-permute-start | bytes 1032200 | tf_op jit(solution)/shard_map/ppermute | solution.py:371
  43.9 17.5 %collective-permute-start.15 = (bf16[3,7,32,256]{3,2,1,0:T(8,128)(2,1)S(1)}, bf16[3,7,32,256]{3,2,1,0:T(8,128)(2,1)}, u32[]{:S(2)}, u32[]{:S(2)}) collective-permute-start(bf16[3,7,32,256]{3,2,1,0:T(8,128)(2,1)S(1)} %get-tuple-element.50.refs_6_), channel_id=1, source_target_pairs={{0,16},{16,0},{1,17},{17,1},{2,18},{18,2},{3,19},{19,3},{4,20},{20... | collective-permute-start | bytes 1032200 | tf_op jit(solution)/shard_map/ppermute | solution.py:372
  44.5 17.5 %collective-permute-start.13 = (bf16[3,7,32,256]{3,2,1,0:T(8,128)(2,1)S(1)}, bf16[3,7,32,256]{3,2,1,0:T(8,128)(2,1)}, u32[]{:S(2)}, u32[]{:S(2)}) collective-permute-start(bf16[3,7,32,256]{3,2,1,0:T(8,128)(2,1)S(1)} %get-tuple-element.50.refs_6_), channel_id=1, source_target_pairs={{0,2},{2,0},{1,3},{3,1},{4,6},{6,4},{5,7},{7,5},{8,10},{10,8},{9,1... | collective-permute-start | bytes 1032200 | tf_op jit(solution)/shard_map/ppermute | solution.py:373
  47.3 1.7 %copy-start.6 = (bf16[320,512]{1,0:T(8,128)(2,1)S(1)}, bf16[320,512]{1,0:T(8,128)(2,1)}, u32[]{:S(2)}) copy-start(bf16[320,512]{1,0:T(8,128)(2,1)} %nodes.3) | copy-start | bytes 983044
  47.3 1.7 %collective-permute-start.12 = (bf16[320,512]{1,0:T(8,128)(2,1)S(1)}, bf16[320,512]{1,0:T(8,128)(2,1)S(1)}, u32[]{:S(2)}, u32[]{:S(2)}) collective-permute-start(bf16[320,512]{1,0:T(8,128)(2,1)S(1)} %shard_map.152.source.mine), channel_id=1, source_target_pairs={{0,1},{1,0},{2,3},{3,2},{4,5},{5,4},{6,7},{7,6},{8,9},{9,8},{10,11... | collective-permute-start | bytes 983048 | tf_op jit(solution)/shard_map/ppermute | solution.py:378
  47.4 14.6 %copy-start.11 = (s32[768]{0:T(1024)S(1)}, s32[768]{0:T(1024)}, u32[]{:S(2)}) copy-start(s32[768]{0:T(1024)} %param.24) | copy-start | bytes 9220
  47.4 14.6 %copy-start.9 = (s32[768]{0:T(1024)S(1)}, s32[768]{0:T(1024)}, u32[]{:S(2)}) copy-start(s32[768]{0:T(1024)} %param.25) | copy-start | bytes 9220
  50.7 10.8 %all-to-all-start = ((bf16[8,8,512]{2,1,0:T(8,128)(2,1)}), bf16[8,8,512]{2,1,0:T(8,128)(2,1)S(1)}, u32[]{:S(2)}, u32[]{:S(2)}) async-start(bf16[8,8,512]{2,1,0:T(8,128)(2,1)} %bitcast.2), calls=%async_computation | async-start | bytes 131072 | tf_op jit(solution)/shard_map/all_to_all | solution.py:504
  58.4 5.9 %collective-permute-start.19 = (bf16[7,128,256]{2,1,0:T(8,128)(2,1)S(1)}, bf16[7,128,256]{2,1,0:T(8,128)(2,1)S(1)}, u32[]{:S(2)}, u32[]{:S(2)}) collective-permute-start(bf16[7,128,256]{2,1,0:T(8,128)(2,1)S(1)} %get-tuple-element.56.refs_5_), channel_id=1, source_target_pairs={{0,1},{1,0},{2,3},{3,2},{4,5},{5,4},{6,7},{7,6},{8,9},{9,8},{10,11... | collective-permute-start | bytes 1376264 | tf_op jit(solution)/shard_map/ppermute | solution.py:378
  58.5 3.6 %collective-permute-start.20 = (bf16[3,7,32,256]{3,2,1,0:T(8,128)(2,1)S(1)}, bf16[3,7,32,256]{3,2,1,0:T(8,128)(2,1)}, u32[]{:S(2)}, u32[]{:S(2)}) collective-permute-start(bf16[3,7,32,256]{3,2,1,0:T(8,128)(2,1)S(1)} %get-tuple-element.50.refs_6_), channel_id=1, source_target_pairs={{0,1},{1,0},{2,3},{3,2},{4,5},{5,4},{6,7},{7,6},{8,9},{9,8},{10,11... | collective-permute-start | bytes 1032200 | tf_op jit(solution)/shard_map/ppermute | solution.py:378
  61.4 3.4 %collective-permute-start.18 = (bf16[3,7,32,256]{3,2,1,0:T(8,128)(2,1)}, bf16[3,7,32,256]{3,2,1,0:T(8,128)(2,1)S(1)}, u32[]{:S(2)}, u32[]{:S(2)}) collective-permute-start(bf16[3,7,32,256]{3,2,1,0:T(8,128)(2,1)} %collective-permute-done.17.refs_9_), channel_id=1, source_target_pairs={{0,1},{1,0},{2,3},{3,2},{4,5},{5,4},{6,7},{7,6},{8,9},{9,8},{10,11... | collective-permute-start | bytes 1032200 | tf_op jit(solution)/shard_map/ppermute | solution.py:378
  61.5 4.2 %collective-permute-start.16 = (bf16[3,7,32,256]{3,2,1,0:T(8,128)(2,1)}, bf16[3,7,32,256]{3,2,1,0:T(8,128)(2,1)S(1)}, u32[]{:S(2)}, u32[]{:S(2)}) collective-permute-start(bf16[3,7,32,256]{3,2,1,0:T(8,128)(2,1)} %collective-permute-done.15.refs_8_), channel_id=1, source_target_pairs={{0,1},{1,0},{2,3},{3,2},{4,5},{5,4},{6,7},{7,6},{8,9},{9,8},{10,11... | collective-permute-start | bytes 1032200 | tf_op jit(solution)/shard_map/ppermute | solution.py:378
  62.0 3.7 %collective-permute-start.14 = (bf16[3,7,32,256]{3,2,1,0:T(8,128)(2,1)}, bf16[3,7,32,256]{3,2,1,0:T(8,128)(2,1)S(1)}, u32[]{:S(2)}, u32[]{:S(2)}) collective-permute-start(bf16[3,7,32,256]{3,2,1,0:T(8,128)(2,1)} %collective-permute-done.13.refs_7_), channel_id=1, source_target_pairs={{0,1},{1,0},{2,3},{3,2},{4,5},{5,4},{6,7},{7,6},{8,9},{9,8},{10,11... | collective-permute-start | bytes 1032200 | tf_op jit(solution)/shard_map/ppermute | solution.py:378
  62.1 17.9 %collective-permute-start.25 = (bf16[3,7,32,256]{3,2,1,0:T(8,128)(2,1)S(1)}, bf16[3,7,32,256]{3,2,1,0:T(8,128)(2,1)S(1)}, u32[]{:S(2)}, u32[]{:S(2)}) collective-permute-start(bf16[3,7,32,256]{3,2,1,0:T(8,128)(2,1)S(1)} %get-tuple-element.59.refs_6_), channel_id=1, source_target_pairs={{0,18},{18,0},{2,16},{16,2},{1,19},{19,1},{3,17},{17,3},{4,22},{22... | collective-permute-start | bytes 1032200 | tf_op jit(solution)/shard_map/ppermute | solution.py:371
  64.3 1.3 %copy-start.12 = (bf16[7,128,256]{2,1,0:T(8,128)(2,1)}, bf16[7,128,256]{2,1,0:T(8,128)(2,1)S(1)}, u32[]{:S(2)}) copy-start(bf16[7,128,256]{2,1,0:T(8,128)(2,1)S(1)} %collective-permute-done.19.refs_10_) | copy-start | bytes 1376260
  64.3 18.1 %collective-permute-start.23 = (bf16[3,7,32,256]{3,2,1,0:T(8,128)(2,1)S(1)}, bf16[3,7,32,256]{3,2,1,0:T(8,128)(2,1)S(1)}, u32[]{:S(2)}, u32[]{:S(2)}) collective-permute-start(bf16[3,7,32,256]{3,2,1,0:T(8,128)(2,1)S(1)} %get-tuple-element.59.refs_6_), channel_id=1, source_target_pairs={{0,16},{16,0},{1,17},{17,1},{2,18},{18,2},{3,19},{19,3},{4,20},{20... | collective-permute-start | bytes 1032200 | tf_op jit(solution)/shard_map/ppermute | solution.py:372
  64.8 18.1 %collective-permute-start.21 = (bf16[3,7,32,256]{3,2,1,0:T(8,128)(2,1)S(1)}, bf16[3,7,32,256]{3,2,1,0:T(8,128)(2,1)}, u32[]{:S(2)}, u32[]{:S(2)}) collective-permute-start(bf16[3,7,32,256]{3,2,1,0:T(8,128)(2,1)S(1)} %get-tuple-element.59.refs_6_), channel_id=1, source_target_pairs={{0,2},{2,0},{1,3},{3,1},{4,6},{6,4},{5,7},{7,5},{8,10},{10,8},{9,1... | collective-permute-start | bytes 1032200 | tf_op jit(solution)/shard_map/ppermute | solution.py:373
  72.2 10.2 %all-to-all-start.1 = ((bf16[8,8,512]{2,1,0:T(8,128)(2,1)}), bf16[8,8,512]{2,1,0:T(8,128)(2,1)S(1)}, u32[]{:S(2)}, u32[]{:S(2)}) async-start(bf16[8,8,512]{2,1,0:T(8,128)(2,1)} %bitcast.4), calls=%async_computation.1 | async-start | bytes 131072 | tf_op jit(solution)/shard_map/all_to_all | solution.py:504
  79.4 3.6 %collective-permute-start.27 = (bf16[7,128,256]{2,1,0:T(8,128)(2,1)S(1)}, bf16[7,128,256]{2,1,0:T(8,128)(2,1)S(1)}, u32[]{:S(2)}, u32[]{:S(2)}) collective-permute-start(bf16[7,128,256]{2,1,0:T(8,128)(2,1)S(1)} %get-tuple-element.66.refs_5_), channel_id=1, source_target_pairs={{0,1},{1,0},{2,3},{3,2},{4,5},{5,4},{6,7},{7,6},{8,9},{9,8},{10,11... | collective-permute-start | bytes 1376264 | tf_op jit(solution)/shard_map/ppermute | solution.py:378
  79.5 3.6 %collective-permute-start.28 = (bf16[3,7,32,256]{3,2,1,0:T(8,128)(2,1)S(1)}, bf16[3,7,32,256]{3,2,1,0:T(8,128)(2,1)}, u32[]{:S(2)}, u32[]{:S(2)}) collective-permute-start(bf16[3,7,32,256]{3,2,1,0:T(8,128)(2,1)S(1)} %get-tuple-element.59.refs_6_), channel_id=1, source_target_pairs={{0,1},{1,0},{2,3},{3,2},{4,5},{5,4},{6,7},{7,6},{8,9},{9,8},{10,11... | collective-permute-start | bytes 1032200 | tf_op jit(solution)/shard_map/ppermute | solution.py:378
  80.0 5.3 %copy-start.14 = (bf16[3,7,32,256]{3,2,1,0:T(8,128)(2,1)}, bf16[3,7,32,256]{3,2,1,0:T(8,128)(2,1)S(1)}, u32[]{:S(2)}) copy-start(bf16[3,7,32,256]{3,2,1,0:T(8,128)(2,1)S(1)} %collective-permute-done.25.refs_9_) | copy-start | bytes 1032196
  82.4 1.7 %collective-permute-start.26 = (bf16[3,7,32,256]{3,2,1,0:T(8,128)(2,1)S(1)}, bf16[3,7,32,256]{3,2,1,0:T(8,128)(2,1)S(1)}, u32[]{:S(2)}, u32[]{:S(2)}) collective-permute-start(bf16[3,7,32,256]{3,2,1,0:T(8,128)(2,1)S(1)} %collective-permute-done.25.refs_9_), channel_id=1, source_target_pairs={{0,1},{1,0},{2,3},{3,2},{4,5},{5,4},{6,7},{7,6},{8,9},{9,8},{10,11... | collective-permute-start | bytes 1032200 | tf_op jit(solution)/shard_map/ppermute | solution.py:378
  82.4 2.8 %copy-start.15 = (bf16[3,7,32,256]{3,2,1,0:T(8,128)(2,1)}, bf16[3,7,32,256]{3,2,1,0:T(8,128)(2,1)S(1)}, u32[]{:S(2)}) copy-start(bf16[3,7,32,256]{3,2,1,0:T(8,128)(2,1)S(1)} %collective-permute-done.23.refs_8_) | copy-start | bytes 1032196
  82.4 2.1 %collective-permute-start.24 = (bf16[3,7,32,256]{3,2,1,0:T(8,128)(2,1)S(1)}, bf16[3,7,32,256]{3,2,1,0:T(8,128)(2,1)S(1)}, u32[]{:S(2)}, u32[]{:S(2)}) collective-permute-start(bf16[3,7,32,256]{3,2,1,0:T(8,128)(2,1)S(1)} %collective-permute-done.23.refs_8_), channel_id=1, source_target_pairs={{0,1},{1,0},{2,3},{3,2},{4,5},{5,4},{6,7},{7,6},{8,9},{9,8},{10,11... | collective-permute-start | bytes 1032200 | tf_op jit(solution)/shard_map/ppermute | solution.py:378
  82.9 2.3 %collective-permute-start.22 = (bf16[3,7,32,256]{3,2,1,0:T(8,128)(2,1)}, bf16[3,7,32,256]{3,2,1,0:T(8,128)(2,1)S(1)}, u32[]{:S(2)}, u32[]{:S(2)}) collective-permute-start(bf16[3,7,32,256]{3,2,1,0:T(8,128)(2,1)} %collective-permute-done.21.refs_7_), channel_id=1, source_target_pairs={{0,1},{1,0},{2,3},{3,2},{4,5},{5,4},{6,7},{7,6},{8,9},{9,8},{10,11... | collective-permute-start | bytes 1032200 | tf_op jit(solution)/shard_map/ppermute | solution.py:378
  83.0 2.3 %copy-start.13 = (bf16[7,128,256]{2,1,0:T(8,128)(2,1)}, bf16[7,128,256]{2,1,0:T(8,128)(2,1)S(1)}, u32[]{:S(2)}) copy-start(bf16[7,128,256]{2,1,0:T(8,128)(2,1)S(1)} %collective-permute-done.27.refs_10_) | copy-start | bytes 1376260

commit v6 on v5

--- a/solution.py
+++ b/solution.py
@@ -48,14 +48,16 @@
     return jnp.where(spots == ids, 1.0, 0.0).astype(BF)
 
 
-def call(body, outs, scratch, fast, slow=(), cost=0.5, far=0, keep=True):
+def call(body, outs, scratch, fast, slow=(), free=(), cost=0.5, far=0, keep=True):
     many = isinstance(outs, list)
     full = [(o if isinstance(o[1], tuple) or not isinstance(o[0], int) else (o, BF)) for o in (outs if many else [outs])]
     places = [pltpu.VMEM] * (len(full) - far) + [pltpu.HBM] * far
     shapes = [(place if keep else jax.ShapeDtypeStruct)(shape, dtype) for place, (shape, dtype) in zip(places, full)]
     operands = [pltpu.with_memory_space_constraint(a, pltpu.VMEM) for a in fast]
     operands += [pltpu.with_memory_space_constraint(a, pltpu.HBM) for a in slow]
+    operands += list(free)
     specs = [pl.BlockSpec(memory_space=pltpu.VMEM)] * len(fast) + [pl.BlockSpec(memory_space=pltpu.HBM)] * len(slow)
+    specs += [pl.BlockSpec(memory_space=pl.ANY)] * len(free)
     return pl.pallas_call(
         body,
         out_shape=shapes if many else shapes[0],
@@ -279,10 +281,8 @@
     for save in saves:
         save.start()
     place("e")
-    for at in range(0, gathered.shape[0], ROWS):
-        rows = slice(at, at + ROWS)
-        pre = dot(gathered[rows, :], weights["em"][...])
-        out[rows, :] = dot(silu(pre).astype(BF), weights["eb"][...]).astype(BF)
+    pre = dot(gathered[...], weights["em"][...])
+    out[...] = dot(silu(pre).astype(BF), weights["eb"][...]).astype(BF)
     for save in saves:
         save.wait()
 
@@ -360,6 +360,60 @@
     packed[...] = dot(one_hot(lists[...], count), new).astype(BF)
     save_edges.wait()
     save_nodes.wait()
+
+
+def picks_of(targets, slots, rows, count, room):
+    return [one_hot(targets[:, rows], count), one_hot(slots[:, rows], room)]
+
+
+def fill_table(table, weights, nodes, sent):
+    em, depth, count = weights["em"], sent.shape[1], nodes.shape[0]
+    table[0:depth, :] = em[2 * depth :, :]
+    table[depth : depth + count, :] = dot(nodes[...], em[depth : 2 * depth, :]).astype(BF)
+    table[depth + count :, :] = dot(sent[...], em[0:depth, :]).astype(BF)
+
+
+def own_half_body(pack, sent, slots, targets, nodes_in, edges_in, *refs):
+    far, refs = refs[:7], refs[7:]
+    total, nm, nb, own_there, joined_there, nodes, edges, table, sems, *scratch = refs
+    pairs = ((nodes_in, nodes), (edges_in, edges), (far[5], own_there), (far[6], joined_there))
+    copies = [pltpu.make_async_copy(src, dst, sems.at[i]) for i, (src, dst) in enumerate(pairs)]
+    weights, place = pack.load((), far[:5], scratch)
+    for copy in copies:
+        copy.start()
+    place("e")
+    copies[0].wait()
+    fill_table(table, weights, nodes, sent)
+    copies[1].wait()
+    for at in range(0, edges.shape[0], edges.shape[0]):
+        rows = slice(at, at + edges.shape[0])
+        picks = picks_of(targets, slots, rows, nodes.shape[0], sent.shape[0])
+        pre = dot(jnp.concatenate([edges[rows, :]] + picks, axis=1), table[...])
+        total[rows, :] = dot(silu(pre).astype(BF), weights["eb"][...])
+    place("n")
+    nm[...] = weights["nm"][...]
+    nb[...] = weights["nb"][...]
+    copies[2].wait()
+    copies[3].wait()
+
+
+def other_half_body(pack, sent, slots, targets, total, nm, nb, nodes, edges, *refs):
+    near, out, message, table, scratch = refs[:5], refs[5], refs[6], refs[7], refs[8:]
+    weights, place = pack.load(near, (), scratch)
+    place("e")
+    fill_table(table, weights, nodes, sent)
+    for at in range(0, edges.shape[0], edges.shape[0]):
+        rows = slice(at, at + edges.shape[0])
+        picks = picks_of(targets, slots, rows, nodes.shape[0], sent.shape[0])
+        pre = dot(jnp.concatenate([edges[rows, :]] + picks, axis=1), table[...])
+        sums = total[rows, :] + dot(silu(pre).astype(BF), weights["eb"][...])
+        message[rows, :] = normalize(sums).astype(BF)
+    place("n")
+    incoming = dot(one_hot_rows(targets[...], nodes.shape[0]), message[...]).astype(BF)
+    both = jnp.concatenate([nodes[...], incoming], axis=1)
+    sums = dot(silu(dot(both, nm[...])).astype(BF), nb[...])
+    sums = sums + dot(silu(dot(both, weights["nm"][...])).astype(BF), weights["nb"][...])
+    out[...] = (nodes[...].astype(F32) + normalize(sums)).astype(BF)
 
 
 def over_slices(chunk):
@@ -515,6 +569,30 @@
             before = sent
         else:
             pack = packs[block + 1]
+        if by_parts and last:
+            half = hidden // 2
+            mine, there = Parts([side], range(5)), Parts([other], [])
+            table = pltpu.VMEM((depth + nodes + sent_rows, half), BF)
+            total, *kept = call(
+                functools.partial(own_half_body, mine),
+                [((mesh_edges, depth), F32)]
+                + [(shape, BF) for shape in weight_shapes("n", half, depth) + [other[0].shape, other[1].shape]]
+                + [((nodes, depth), BF), ((mesh_edges, depth), BF)],
+                [table, pltpu.SemaphoreType.DMA((4,))] + mine.scratch(half, depth),
+                [sent, slots_back, targets],
+                [rows, edges],
+                side + other[:2],
+                cost=3.5,
+            )
+            nm, nb, own_there, joined_there, node_rows, edge_rows = kept
+            return call(
+                functools.partial(other_half_body, there),
+                (nodes, depth),
+                [edge_buffer, table] + there.scratch(half, depth),
+                [sent, slots_back, targets, total, nm, nb, node_rows, edge_rows, own_there, joined_there] + other[2:],
+                cost=3.5,
+                keep=False,
+            )
         table = pltpu.VMEM((depth + nodes + sent_rows, hidden), BF)
         got = call(
             functools.partial(block_body, pack, last),

time: 92 us -> 91.1 us (level)
  waiting for transfers between devices: 22.1 us -> 15.3 us
  starting transfers between devices: 44.4 us -> 49.8 us
    ppermute x6, waiting for transfers between devices: 9.34 us -> 3.75 us  [over_slices(): lax.ppermute(chunk, 'mesh', [(i, i ^ k) for i in range(count)])]
    ppermute x3, starting transfers between devices: 1.11 us -> 4.61 us  [over_plane(): along_x = lax.ppermute(own, 'band', SWAP)]
    ppermute x12, waiting for transfers between devices: 3.84 us -> 1.61 us  [swap_width(): return lax.ppermute(array, 'width', SWAP)]
    ppermute x3, starting transfers between devices: 2.59 us -> 4.34 us  [over_plane(): along_y = lax.ppermute(own, 'groups', SWAP)]
    ppermute x3, waiting for transfers between devices: 0.19 us -> 1.45 us  [over_plane(): along_y = lax.ppermute(own, 'groups', SWAP)]
    pallas_call x12 -> x13, Pallas kernels: 24.3 us -> 24.9 us  [call(): pl.pallas_call(body, out_shape=shapes if many else shapes[0], in_specs=sp...]
  transfers between devices with their start and end apart: 31 -> 31, of which waited for: 11 -> 7; matrix products, arithmetic and copies ran while one was open for 0% -> 0% of each run, Pallas kernels for 17% -> 21%
where the time goes in v6:
time: 91.1 us; the launch traced here: 90.7 us
  starting transfers between devices  49.8 us (55%)
  Pallas kernels  24.9 us (27%)
  waiting for transfers between devices  15.3 us (17%)
    pallas_call x13, Pallas kernels, call(): pl.pallas_call(body, out_shape=shapes if many else shapes[0], in_specs=sp...  24.9 us
    all_to_all x2, starting transfers between devices, on_device(): lax.all_to_all(cut_rows, ('mesh', 'band'), split_axis=0, concat_axis=0, a...  14.5 us
    ppermute x6, starting transfers between devices, over_slices(): lax.ppermute(chunk, 'mesh', [(i, i ^ k) for i in range(count)])  10.8 us
    ppermute x3, starting transfers between devices, over_plane(): across = lax.ppermute(own, ('groups', 'band'), DIAGONAL)  8.54 us
    all_to_all x2, waiting for transfers between devices, on_device(): lax.all_to_all(cut_rows, ('mesh', 'band'), split_axis=0, concat_axis=0, a...  5.46 us
    ppermute x3, starting transfers between devices, over_plane(): along_x = lax.ppermute(own, 'band', SWAP)  4.61 us
    ppermute x3, starting transfers between devices, over_plane(): along_y = lax.ppermute(own, 'groups', SWAP)  4.34 us
    ppermute x6, waiting for transfers between devices, over_slices(): lax.ppermute(chunk, 'mesh', [(i, i ^ k) for i in range(count)])  3.75 us
  transfers between devices with their start and end apart: 31, of which 7 were waited for; matrix products, arithmetic and copies ran while one was open for 0% of the time, Pallas kernels for 21%

profile of v6, /device:TPU:0, one launch (start us, length us, event | category | flops | bytes accessed | tf_op | source)
XLA Modules:
  0.0 90.7 jit_solution(16405044566742500384)
XLA Ops:
  0.0 0.9 shard_map.146
  0.9 3.1 %collective-permute-start = (bf16[7,32,256]{2,1,0:T(8,128)(2,1)S(1)}, bf16[7,32,256]{2,1,0:T(8,128)(2,1)S(1)}, u32[]{:S(2)}, u32[]{:S(2)}) collective-permute-start(bf16[7,32,256]{2,1,0:T(8,128)(2,1)S(1)} %shard_map.146), channel_id=1, source_target_pairs={{0,4},{4,0},{8,12},{12,8},{1,5},{5,1},{9,13},{13,9},{2,6},{6,2},{1... | collective-permute-start | bytes 344072 | tf_op jit(solution)/shard_map/ppermute | solution.py:421
  4.0 2.5 %collective-permute-start.4 = (bf16[7,32,256]{2,1,0:T(8,128)(2,1)S(1)}, bf16[7,32,256]{2,1,0:T(8,128)(2,1)S(1)}, u32[]{:S(2)}, u32[]{:S(2)}) collective-permute-start(bf16[7,32,256]{2,1,0:T(8,128)(2,1)S(1)} %shard_map.146), channel_id=1, source_target_pairs={{0,12},{4,8},{8,4},{12,0},{1,13},{5,9},{9,5},{13,1},{2,14},{6,10},... | collective-permute-start | bytes 344072 | tf_op jit(solution)/shard_map/ppermute | solution.py:421
  6.4 0.1 collective-permute-start.3
  6.6 1.5 %shard_map.145 = (bf16[64,512]{1,0:T(8,128)(2,1)S(1)}, bf16[64,512]{1,0:T(8,128)(2,1)S(1)}) custom-call(bf16[512,512]{1,0:T(8,128)(2,1)} %grid.1, s32[1,64]{1,0:T(1,128)} %bitcast.9, s32[1,64]{1,0:T(1,128)} %bitcast.10), custom_call_target="tpu_custom_call" | custom-call | flops 500000000 | tf_op jit(solution)/shard_map/pallas_call | solution.py:61
  8.1 0.0 collective-permute-done.refs_0_
  8.1 3.4 %collective-permute-start.1 = (bf16[64,512]{1,0:T(8,128)(2,1)S(1)}, bf16[64,512]{1,0:T(8,128)(2,1)S(1)}, u32[]{:S(2)}, u32[]{:S(2)}) collective-permute-start(bf16[64,512]{1,0:T(8,128)(2,1)S(1)} %get-tuple-element.44), channel_id=1, source_target_pairs={{0,2},{2,4},{4,6},{6,8},{8,10},{10,12},{12,14},{1,3},{3,5},{5,7},{... | collective-permute-start | bytes 196616 | tf_op jit(solution)/shard_map/ppermute | solution.py:500
  11.5 1.3 %collective-permute-start.2 = (bf16[64,512]{1,0:T(8,128)(2,1)S(1)}, bf16[64,512]{1,0:T(8,128)(2,1)S(1)}, u32[]{:S(2)}, u32[]{:S(2)}) collective-permute-start(bf16[64,512]{1,0:T(8,128)(2,1)S(1)} %get-tuple-element.46), channel_id=1, source_target_pairs={{2,0},{4,2},{6,4},{8,6},{10,8},{12,10},{14,12},{3,1},{5,3},{7,5},{... | collective-permute-start | bytes 196616 | tf_op jit(solution)/shard_map/ppermute | solution.py:499
  12.8 1.8 %shard_map.148 = (bf16[14,32,256]{2,1,0:T(8,128)(2,1)S(1)}, bf16[7,128,256]{2,1,0:T(8,128)(2,1)S(1)}, bf16[7,128,256]{2,1,0:T(8,128)(2,1)S(1)}, bf16[7,128,256]{2,1,0:T(8,128)(2,1)S(1)}) custom-call(bf16[3,3,128,256]{3,2,1,0:T(8,128)(2,1)} %refs_0_.3, bf16[3,256,128]{2,1,0:T(8,128)(2,1)} %refs_1_.3, bf16[3,2,128,256]{3,2,1,0:T(8,128)(2,1)} %refs_2_.3, ...), custom_call_target="tpu_custom_call" | custom-call | flops 500000000 | tf_op jit(solution)/shard_map/pallas_call | solution.py:61
  14.6 0.0 collective-permute-done.4.refs_2_
  14.7 3.0 %collective-permute-done.2.high = bf16[64,512]{1,0:T(8,128)(2,1)S(1)} collective-permute-done((bf16[64,512]{1,0:T(8,128)(2,1)S(1)}, bf16[64,512]{1,0:T(8,128)(2,1)S(1)}, u32[]{:S(2)}, u32[]{:S(2)}) %collective-permute-start.2) | collective-permute-done | bytes 65568 | tf_op jit(solution)/shard_map/ppermute | solution.py:499
  17.7 0.0 collective-permute-done.3.refs_1_
  17.7 1.9 %collective-permute-start.5 = (bf16[14,32,256]{2,1,0:T(8,128)(2,1)S(1)}, bf16[14,32,256]{2,1,0:T(8,128)(2,1)S(1)}, u32[]{:S(2)}, u32[]{:S(2)}) collective-permute-start(bf16[14,32,256]{2,1,0:T(8,128)(2,1)S(1)} %get-tuple-element.50), channel_id=1, source_target_pairs={{0,4},{4,0},{8,12},{12,8},{1,5},{5,1},{9,13},{13,9},{2,6},{6,2},{1... | collective-permute-start | bytes 688136 | tf_op jit(solution)/shard_map/ppermute | solution.py:421
  19.6 2.9 %collective-permute-start.6 = (bf16[14,32,256]{2,1,0:T(8,128)(2,1)S(1)}, bf16[14,32,256]{2,1,0:T(8,128)(2,1)S(1)}, u32[]{:S(2)}, u32[]{:S(2)}) collective-permute-start(bf16[14,32,256]{2,1,0:T(8,128)(2,1)S(1)} %get-tuple-element.50), channel_id=1, source_target_pairs={{0,8},{4,12},{8,0},{12,4},{1,9},{5,13},{9,1},{13,5},{2,10},{6,14},... | collective-permute-start | bytes 688136 | tf_op jit(solution)/shard_map/ppermute | solution.py:421
  22.5 0.4 collective-permute-start.7
  22.9 2.1 %collective-permute-start.8 = (bf16[3,7,32,256]{3,2,1,0:T(8,128)(2,1)S(1)}, bf16[3,7,32,256]{3,2,1,0:T(8,128)(2,1)S(1)}, u32[]{:S(2)}, u32[]{:S(2)}) collective-permute-start(bf16[3,7,32,256]{3,2,1,0:T(8,128)(2,1)S(1)} %shard_map.149.refs_1_), channel_id=1, source_target_pairs={{0,2},{2,0},{1,3},{3,1},{4,6},{6,4},{5,7},{7,5},{8,10},{10,8},{9,1... | collective-permute-start | bytes 1032200 | tf_op jit(solution)/shard_map/ppermute | solution.py:427
  25.0 1.5 %collective-permute-start.9 = (bf16[3,7,32,256]{3,2,1,0:T(8,128)(2,1)S(1)}, bf16[3,7,32,256]{3,2,1,0:T(8,128)(2,1)S(1)}, u32[]{:S(2)}, u32[]{:S(2)}) collective-permute-start(bf16[3,7,32,256]{3,2,1,0:T(8,128)(2,1)S(1)} %shard_map.149.refs_1_), channel_id=1, source_target_pairs={{0,16},{16,0},{1,17},{17,1},{2,18},{18,2},{3,19},{19,3},{4,20},{20... | collective-permute-start | bytes 1032200 | tf_op jit(solution)/shard_map/ppermute | solution.py:426
  26.5 0.4 collective-permute-done.5.refs_0_
  26.8 6.5 %collective-permute-start.10 = (bf16[3,7,32,256]{3,2,1,0:T(8,128)(2,1)S(1)}, bf16[3,7,32,256]{3,2,1,0:T(8,128)(2,1)S(1)}, u32[]{:S(2)}, u32[]{:S(2)}) collective-permute-start(bf16[3,7,32,256]{3,2,1,0:T(8,128)(2,1)S(1)} %shard_map.149.refs_1_), channel_id=1, source_target_pairs={{0,18},{18,0},{2,16},{16,2},{1,19},{19,1},{3,17},{17,3},{4,22},{22... | collective-permute-start | bytes 1032200 | tf_op jit(solution)/shard_map/ppermute | solution.py:425
  33.4 1.3 %shard_map.147.gathered = bf16[768,1536]{1,0:T(8,128)(2,1)S(1)} custom-call(bf16[512,512]{1,0:T(8,128)(2,1)S(1)} %copy-done, bf16[64,512]{1,0:T(8,128)(2,1)S(1)} %collective-permute-done.1.low, bf16[64,512]{1,0:T(8,128)(2,1)S(1)} %collective-permute-done.2.high, bf16[320,512]{1,0:T(8,128)(2,1)S(1)} %copy-done.3, s32[1,768]{1,0:T(1,128)S(1)} %broadcast_in_dim.22.slots, ...), custom_call_target="tpu_custom_call" | custom-call | flops 1200000000 | tf_op jit(solution)/shard_map/pallas_call | solution.py:61
  34.7 3.4 %collective-permute-done.6.refs_1_ = bf16[14,32,256]{2,1,0:T(8,128)(2,1)S(1)} collective-permute-done((bf16[14,32,256]{2,1,0:T(8,128)(2,1)S(1)}, bf16[14,32,256]{2,1,0:T(8,128)(2,1)S(1)}, u32[]{:S(2)}, u32[]{:S(2)}) %collective-permute-start.6) | collective-permute-done | bytes 229408 | tf_op jit(solution)/shard_map/ppermute | solution.py:421
  38.0 0.0 collective-permute-done.7.refs_2_
  38.1 0.0 copy-start.8
  38.1 1.4 %collective-permute-done.9.refs_3_ = bf16[3,7,32,256]{3,2,1,0:T(8,128)(2,1)S(1)} collective-permute-done((bf16[3,7,32,256]{3,2,1,0:T(8,128)(2,1)S(1)}, bf16[3,7,32,256]{3,2,1,0:T(8,128)(2,1)S(1)}, u32[]{:S(2)}, u32[]{:S(2)}) %collective-permute-start.9) | collective-permute-done | bytes 344096 | tf_op jit(solution)/shard_map/ppermute | solution.py:426
  39.6 0.0 collective-permute-done.10.refs_4_
  39.6 1.6 %shard_map.151 = (bf16[768,512]{1,0:T(8,128)(2,1)S(1)}, bf16[1024,256]{1,0:T(8,128)(2,1)}, bf16[256,512]{1,0:T(8,128)(2,1)}) custom-call(bf16[768,1536]{1,0:T(8,128)(2,1)S(1)} %shard_map.147.gathered, bf16[7,128,256]{2,1,0:T(8,128)(2,1)S(1)} %get-tuple-element.52.refs_0_, bf16[3,7,32,256]{3,2,1,0:T(8,128)(2,1)S(1)} %shard_map.149.refs_1_, ...), custom_call_target="tpu_custom_call" | custom-call | flops 3000000000 | tf_op jit(solution)/shard_map/pallas_call | solution.py:61
  41.2 0.1 collective-permute-start.11
  41.3 0.1 reshape.15.lists
  41.4 1.2 %collective-permute-start.13 = (bf16[3,7,32,256]{3,2,1,0:T(8,128)(2,1)S(1)}, bf16[3,7,32,256]{3,2,1,0:T(8,128)(2,1)}, u32[]{:S(2)}, u32[]{:S(2)}) collective-permute-start(bf16[3,7,32,256]{3,2,1,0:T(8,128)(2,1)S(1)} %get-tuple-element.57.refs_6_), channel_id=1, source_target_pairs={{0,2},{2,0},{1,3},{3,1},{4,6},{6,4},{5,7},{7,5},{8,10},{10,8},{9,1... | collective-permute-start | bytes 1032200 | tf_op jit(solution)/shard_map/ppermute | solution.py:427
  42.6 1.3 %collective-permute-start.15 = (bf16[3,7,32,256]{3,2,1,0:T(8,128)(2,1)S(1)}, bf16[3,7,32,256]{3,2,1,0:T(8,128)(2,1)}, u32[]{:S(2)}, u32[]{:S(2)}) collective-permute-start(bf16[3,7,32,256]{3,2,1,0:T(8,128)(2,1)S(1)} %get-tuple-element.57.refs_6_), channel_id=1, source_target_pairs={{0,16},{16,0},{1,17},{17,1},{2,18},{18,2},{3,19},{19,3},{4,20},{20... | collective-permute-start | bytes 1032200 | tf_op jit(solution)/shard_map/ppermute | solution.py:426
  43.9 1.0 %collective-permute-start.17 = (bf16[3,7,32,256]{3,2,1,0:T(8,128)(2,1)S(1)}, bf16[3,7,32,256]{3,2,1,0:T(8,128)(2,1)}, u32[]{:S(2)}, u32[]{:S(2)}) collective-permute-start(bf16[3,7,32,256]{3,2,1,0:T(8,128)(2,1)S(1)} %get-tuple-element.57.refs_6_), channel_id=1, source_target_pairs={{0,18},{18,0},{2,16},{16,2},{1,19},{19,1},{3,17},{17,3},{4,22},{22... | collective-permute-start | bytes 1032200 | tf_op jit(solution)/shard_map/ppermute | solution.py:425
  44.9 2.5 %shard_map.152.source.mine = bf16[320,512]{1,0:T(8,128)(2,1)S(1)} custom-call(s32[1,768]{1,0:T(1,128)S(1)} %broadcast_in_dim.19.targets, bf16[768,512]{1,0:T(8,128)(2,1)S(1)} %get-tuple-element.53.mine, bf16[768,512]{1,0:T(8,128)(2,1)S(1)} %collective-permute-done.11.other, bf16[320,512]{1,0:T(8,128)(2,1)} %nodes.3, ...), custom_call_target="tpu_custom_call" | custom-call | flops 1600000000 | tf_op jit(solution)/shard_map/pallas_call | solution.py:61
  47.4 0.0 copy-start.4
  47.4 0.1 collective-permute-start.12
  47.5 0.0 copy-start.9
  47.5 0.0 copy-start.7
  47.6 1.6 %collective-permute-done.12.other = bf16[320,512]{1,0:T(8,128)(2,1)S(1)} collective-permute-done((bf16[320,512]{1,0:T(8,128)(2,1)S(1)}, bf16[320,512]{1,0:T(8,128)(2,1)S(1)}, u32[]{:S(2)}, u32[]{:S(2)}) %collective-permute-start.12) | collective-permute-done | bytes 327712 | tf_op jit(solution)/shard_map/ppermute | solution.py:432
  49.1 1.6 %shard_map.154 = (bf16[64,512]{1,0:T(8,128)(2,1)}, bf16[320,512]{1,0:T(8,128)(2,1)}) custom-call(bf16[320,512]{1,0:T(8,128)(2,1)S(1)} %copy-done.4, s32[1,64]{1,0:T(1,128)S(1)} %reshape.15.lists, bf16[320,512]{1,0:T(8,128)(2,1)S(1)} %shard_map.152.source.mine, bf16[320,512]{1,0:T(8,128)(2,1)S(1)} %collective-permute-done.12.other, ...), custom_call_target="tpu_custom_call" | custom-call | flops 1600000000 | tf_op jit(solution)/shard_map/pallas_call | solution.py:61
  50.8 7.2 %all-to-all-start = ((bf16[8,8,512]{2,1,0:T(8,128)(2,1)}), bf16[8,8,512]{2,1,0:T(8,128)(2,1)S(1)}, u32[]{:S(2)}, u32[]{:S(2)}) async-start(bf16[8,8,512]{2,1,0:T(8,128)(2,1)} %bitcast.2), calls=%async_computation | async-start | bytes 131072 | tf_op jit(solution)/shard_map/all_to_all | solution.py:558
  58.1 0.5 collective-permute-start.20
  58.6 2.5 %all-to-all-done = bf16[8,8,512]{2,1,0:T(8,128)(2,1)S(1)} async-done(((bf16[8,8,512]{2,1,0:T(8,128)(2,1)}), bf16[8,8,512]{2,1,0:T(8,128)(2,1)S(1)}, u32[]{:S(2)}, u32[]{:S(2)}) %all-to-all-start) | async-done | bytes 65568 | tf_op jit(solution)/shard_map/all_to_all | solution.py:558
  61.0 0.0 collective-permute-start.14
  61.0 0.0 collective-permute-done.15.refs_8_
  61.0 0.5 collective-permute-start.16
  61.6 0.0 collective-permute-done.17.refs_9_
  61.6 0.1 collective-permute-start.18
  61.7 0.0 collective-permute-done.20.refs_11_
  61.7 1.3 %collective-permute-start.21 = (bf16[3,7,32,256]{3,2,1,0:T(8,128)(2,1)S(1)}, bf16[3,7,32,256]{3,2,1,0:T(8,128)(2,1)S(1)}, u32[]{:S(2)}, u32[]{:S(2)}) collective-permute-start(bf16[3,7,32,256]{3,2,1,0:T(8,128)(2,1)S(1)} %get-tuple-element.69.refs_1_), channel_id=1, source_target_pairs={{0,2},{2,0},{1,3},{3,1},{4,6},{6,4},{5,7},{7,5},{8,10},{10,8},{9,1... | collective-permute-start | bytes 1032200 | tf_op jit(solution)/shard_map/ppermute | solution.py:427
  63.0 1.5 %collective-permute-start.22 = (bf16[3,7,32,256]{3,2,1,0:T(8,128)(2,1)S(1)}, bf16[3,7,32,256]{3,2,1,0:T(8,128)(2,1)S(1)}, u32[]{:S(2)}, u32[]{:S(2)}) collective-permute-start(bf16[3,7,32,256]{3,2,1,0:T(8,128)(2,1)S(1)} %get-tuple-element.69.refs_1_), channel_id=1, source_target_pairs={{0,16},{16,0},{1,17},{17,1},{2,18},{18,2},{3,19},{19,3},{4,20},{20... | collective-permute-start | bytes 1032200 | tf_op jit(solution)/shard_map/ppermute | solution.py:426
  64.5 0.0 collective-permute-done.14.refs_0_
  64.5 1.0 %collective-permute-start.23 = (bf16[3,7,32,256]{3,2,1,0:T(8,128)(2,1)S(1)}, bf16[3,7,32,256]{3,2,1,0:T(8,128)(2,1)S(1)}, u32[]{:S(2)}, u32[]{:S(2)}) collective-permute-start(bf16[3,7,32,256]{3,2,1,0:T(8,128)(2,1)S(1)} %get-tuple-element.69.refs_1_), channel_id=1, source_target_pairs={{0,18},{18,0},{2,16},{16,2},{1,19},{19,1},{3,17},{17,3},{4,22},{22... | collective-permute-start | bytes 1032200 | tf_op jit(solution)/shard_map/ppermute | solution.py:425
  65.5 0.0 collective-permute-done.16.refs_1_
  65.5 0.0 collective-permute-start.25
  65.5 0.0 collective-permute-done.18.refs_2_
  65.5 0.5 collective-permute-start.24
  66.0 6.5 %shard_map.155 = (bf16[64,512]{1,0:T(8,128)(2,1)}, bf16[320,512]{1,0:T(8,128)(2,1)}, bf16[768,512]{1,0:T(8,128)(2,1)}) custom-call(bf16[64,512]{1,0:T(8,128)(2,1)S(1)} %bitcast.6, s32[1,768]{1,0:T(1,128)S(1)} %broadcast_in_dim.23.slots, s32[1,768]{1,0:T(1,128)S(1)} %broadcast_in_dim.24.targets, s32[1,64]{1,0:T(1,128)S(1)} %reshape.15.lists, ...), custom_call_target="tpu_custom_call" | custom-call | flops 6499999744 | tf_op jit(solution)/shard_map/pallas_call | solution.py:61
  72.5 7.2 %all-to-all-start.1 = ((bf16[8,8,512]{2,1,0:T(8,128)(2,1)}), bf16[8,8,512]{2,1,0:T(8,128)(2,1)S(1)}, u32[]{:S(2)}, u32[]{:S(2)}) async-start(bf16[8,8,512]{2,1,0:T(8,128)(2,1)} %bitcast.4), calls=%async_computation.1 | async-start | bytes 131072 | tf_op jit(solution)/shard_map/all_to_all | solution.py:558
  79.8 3.0 %all-to-all-done.1 = bf16[8,8,512]{2,1,0:T(8,128)(2,1)S(1)} async-done(((bf16[8,8,512]{2,1,0:T(8,128)(2,1)}), bf16[8,8,512]{2,1,0:T(8,128)(2,1)S(1)}, u32[]{:S(2)}, u32[]{:S(2)}) %all-to-all-start.1) | async-done | bytes 65568 | tf_op jit(solution)/shard_map/all_to_all | solution.py:558
  82.7 0.0 collective-permute-start.26
  82.7 0.5 collective-permute-start.27
  83.2 0.1 collective-permute-start.28
  83.3 0.0 collective-permute-done.25.refs_6_
  83.3 3.4 %shard_map.156 = (f32[768,512]{1,0:T(8,128)S(1)}, bf16[1024,256]{1,0:T(8,128)(2,1)S(1)}, bf16[256,512]{1,0:T(8,128)(2,1)S(1)}, bf16[7,128,256]{2,1,0:T(8,128)(2,...) custom-call(bf16[64,512]{1,0:T(8,128)(2,1)S(1)} %bitcast.7, ...), custom_call_target="tpu_custom_call" | custom-call | flops 3500000000 | tf_op jit(solution)/shard_map/pallas_call | solution.py:61
  86.7 3.8 %shard_map.157 = bf16[320,512]{1,0:T(8,128)(2,1)} custom-call(bf16[64,512]{1,0:T(8,128)(2,1)S(1)} %bitcast.8, s32[1,768]{1,0:T(1,128)S(1)} %broadcast_in_dim.23.slots, s32[1,768]{1,0:T(1,128)S(1)} %broadcast_in_dim.24.targets, f32[768,512]{1,0:T(8,128)S(1)} %get-tuple-element.71.total, bf16[1024,256]{1,0:T(8,128)(2,1)S(1)} %get-tuple-element.72.nm, ...), custom_call_target="tpu_custom_call" | custom-call | flops 3500000000 | tf_op jit(solution)/shard_map/pallas_call | solution.py:61
  (40 shorter events, 0.2 us)
Async XLA Ops:
  0.9 7.2 %collective-permute-start = (bf16[7,32,256]{2,1,0:T(8,128)(2,1)S(1)}, bf16[7,32,256]{2,1,0:T(8,128)(2,1)S(1)}, u32[]{:S(2)}, u32[]{:S(2)}) collective-permute-start(bf16[7,32,256]{2,1,0:T(8,128)(2,1)S(1)} %shard_map.146), channel_id=1, source_target_pairs={{0,4},{4,0},{8,12},{12,8},{1,5},{5,1},{9,13},{13,9},{2,6},{6,2},{1... | collective-permute-start | bytes 344072 | tf_op jit(solution)/shard_map/ppermute | solution.py:421
  4.0 10.7 %collective-permute-start.4 = (bf16[7,32,256]{2,1,0:T(8,128)(2,1)S(1)}, bf16[7,32,256]{2,1,0:T(8,128)(2,1)S(1)}, u32[]{:S(2)}, u32[]{:S(2)}) collective-permute-start(bf16[7,32,256]{2,1,0:T(8,128)(2,1)S(1)} %shard_map.146), channel_id=1, source_target_pairs={{0,12},{4,8},{8,4},{12,0},{1,13},{5,9},{9,5},{13,1},{2,14},{6,10},... | collective-permute-start | bytes 344072 | tf_op jit(solution)/shard_map/ppermute | solution.py:421
  6.4 11.2 %collective-permute-start.3 = (bf16[7,32,256]{2,1,0:T(8,128)(2,1)S(1)}, bf16[7,32,256]{2,1,0:T(8,128)(2,1)S(1)}, u32[]{:S(2)}, u32[]{:S(2)}) collective-permute-start(bf16[7,32,256]{2,1,0:T(8,128)(2,1)S(1)} %shard_map.146), channel_id=1, source_target_pairs={{0,8},{4,12},{8,0},{12,4},{1,9},{5,13},{9,1},{13,5},{2,10},{6,14},... | collective-permute-start | bytes 344072 | tf_op jit(solution)/shard_map/ppermute | solution.py:421
  6.6 16.3 %copy-start.5 = (s32[768]{0:T(1024)S(1)}, s32[768]{0:T(1024)}, u32[]{:S(2)}) copy-start(s32[768]{0:T(1024)} %param.20) | copy-start | bytes 9220
  6.6 16.3 %copy-start.6 = (s32[768]{0:T(1024)S(1)}, s32[768]{0:T(1024)}, u32[]{:S(2)}) copy-start(s32[768]{0:T(1024)} %param.19) | copy-start | bytes 9220
  6.6 26.8 %copy-start = (bf16[512,512]{1,0:T(8,128)(2,1)S(1)}, bf16[512,512]{1,0:T(8,128)(2,1)}, u32[]{:S(2)}) copy-start(bf16[512,512]{1,0:T(8,128)(2,1)} %grid.1) | copy-start | bytes 1572868
  6.6 26.8 %copy-start.3 = (bf16[320,512]{1,0:T(8,128)(2,1)S(1)}, bf16[320,512]{1,0:T(8,128)(2,1)}, u32[]{:S(2)}) copy-start(bf16[320,512]{1,0:T(8,128)(2,1)} %nodes.3) | copy-start | bytes 983044
  8.1 6.5 %collective-permute-start.1 = (bf16[64,512]{1,0:T(8,128)(2,1)S(1)}, bf16[64,512]{1,0:T(8,128)(2,1)S(1)}, u32[]{:S(2)}, u32[]{:S(2)}) collective-permute-start(bf16[64,512]{1,0:T(8,128)(2,1)S(1)} %get-tuple-element.44), channel_id=1, source_target_pairs={{0,2},{2,4},{4,6},{6,8},{8,10},{10,12},{12,14},{1,3},{3,5},{5,7},{... | collective-permute-start | bytes 196616 | tf_op jit(solution)/shard_map/ppermute | solution.py:500
  11.5 6.2 %collective-permute-start.2 = (bf16[64,512]{1,0:T(8,128)(2,1)S(1)}, bf16[64,512]{1,0:T(8,128)(2,1)S(1)}, u32[]{:S(2)}, u32[]{:S(2)}) collective-permute-start(bf16[64,512]{1,0:T(8,128)(2,1)S(1)} %get-tuple-element.46), channel_id=1, source_target_pairs={{2,0},{4,2},{6,4},{8,6},{10,8},{12,10},{14,12},{3,1},{5,3},{7,5},{... | collective-permute-start | bytes 196616 | tf_op jit(solution)/shard_map/ppermute | solution.py:499
  14.6 43.4 %copy-start.1 = (bf16[7,128,256]{2,1,0:T(8,128)(2,1)}, bf16[7,128,256]{2,1,0:T(8,128)(2,1)S(1)}, u32[]{:S(2)}) copy-start(bf16[7,128,256]{2,1,0:T(8,128)(2,1)S(1)} %get-tuple-element.63.refs_5_) | copy-start | bytes 1376260
  17.7 9.1 %collective-permute-start.5 = (bf16[14,32,256]{2,1,0:T(8,128)(2,1)S(1)}, bf16[14,32,256]{2,1,0:T(8,128)(2,1)S(1)}, u32[]{:S(2)}, u32[]{:S(2)}) collective-permute-start(bf16[14,32,256]{2,1,0:T(8,128)(2,1)S(1)} %get-tuple-element.50), channel_id=1, source_target_pairs={{0,4},{4,0},{8,12},{12,8},{1,5},{5,1},{9,13},{13,9},{2,6},{6,2},{1... | collective-permute-start | bytes 688136 | tf_op jit(solution)/shard_map/ppermute | solution.py:421
  19.6 18.5 %collective-permute-start.6 = (bf16[14,32,256]{2,1,0:T(8,128)(2,1)S(1)}, bf16[14,32,256]{2,1,0:T(8,128)(2,1)S(1)}, u32[]{:S(2)}, u32[]{:S(2)}) collective-permute-start(bf16[14,32,256]{2,1,0:T(8,128)(2,1)S(1)} %get-tuple-element.50), channel_id=1, source_target_pairs={{0,8},{4,12},{8,0},{12,4},{1,9},{5,13},{9,1},{13,5},{2,10},{6,14},... | collective-permute-start | bytes 688136 | tf_op jit(solution)/shard_map/ppermute | solution.py:421
  22.5 15.6 %collective-permute-start.7 = (bf16[14,32,256]{2,1,0:T(8,128)(2,1)S(1)}, bf16[14,32,256]{2,1,0:T(8,128)(2,1)S(1)}, u32[]{:S(2)}, u32[]{:S(2)}) collective-permute-start(bf16[14,32,256]{2,1,0:T(8,128)(2,1)S(1)} %get-tuple-element.50), channel_id=1, source_target_pairs={{0,12},{4,8},{8,4},{12,0},{1,13},{5,9},{9,5},{13,1},{2,14},{6,10},... | collective-permute-start | bytes 688136 | tf_op jit(solution)/shard_map/ppermute | solution.py:421
  22.9 15.3 %collective-permute-start.8 = (bf16[3,7,32,256]{3,2,1,0:T(8,128)(2,1)S(1)}, bf16[3,7,32,256]{3,2,1,0:T(8,128)(2,1)S(1)}, u32[]{:S(2)}, u32[]{:S(2)}) collective-permute-start(bf16[3,7,32,256]{3,2,1,0:T(8,128)(2,1)S(1)} %shard_map.149.refs_1_), channel_id=1, source_target_pairs={{0,2},{2,0},{1,3},{3,1},{4,6},{6,4},{5,7},{7,5},{8,10},{10,8},{9,1... | collective-permute-start | bytes 1032200 | tf_op jit(solution)/shard_map/ppermute | solution.py:427
  25.0 14.6 %collective-permute-start.9 = (bf16[3,7,32,256]{3,2,1,0:T(8,128)(2,1)S(1)}, bf16[3,7,32,256]{3,2,1,0:T(8,128)(2,1)S(1)}, u32[]{:S(2)}, u32[]{:S(2)}) collective-permute-start(bf16[3,7,32,256]{3,2,1,0:T(8,128)(2,1)S(1)} %shard_map.149.refs_1_), channel_id=1, source_target_pairs={{0,16},{16,0},{1,17},{17,1},{2,18},{18,2},{3,19},{19,3},{4,20},{20... | collective-permute-start | bytes 1032200 | tf_op jit(solution)/shard_map/ppermute | solution.py:426
  26.8 12.7 %collective-permute-start.10 = (bf16[3,7,32,256]{3,2,1,0:T(8,128)(2,1)S(1)}, bf16[3,7,32,256]{3,2,1,0:T(8,128)(2,1)S(1)}, u32[]{:S(2)}, u32[]{:S(2)}) collective-permute-start(bf16[3,7,32,256]{3,2,1,0:T(8,128)(2,1)S(1)} %shard_map.149.refs_1_), channel_id=1, source_target_pairs={{0,18},{18,0},{2,16},{16,2},{1,19},{19,1},{3,17},{17,3},{4,22},{22... | collective-permute-start | bytes 1032200 | tf_op jit(solution)/shard_map/ppermute | solution.py:425
  38.1 19.9 %copy-start.2 = (bf16[3,7,32,256]{3,2,1,0:T(8,128)(2,1)}, bf16[3,7,32,256]{3,2,1,0:T(8,128)(2,1)S(1)}, u32[]{:S(2)}) copy-start(bf16[3,7,32,256]{3,2,1,0:T(8,128)(2,1)S(1)} %get-tuple-element.57.refs_6_) | copy-start | bytes 1032196
  38.1 3.2 %copy-start.8 = (s32[1,8,8]{2,1,0:T(8,128)S(1)}, s32[1,8,8]{2,1,0:T(8,128)}, u32[]{:S(2)}) copy-start(s32[1,8,8]{2,1,0:T(8,128)} %param.23) | copy-start | bytes 772
  41.2 3.7 %collective-permute-start.11 = (bf16[768,512]{1,0:T(8,128)(2,1)S(1)}, bf16[768,512]{1,0:T(8,128)(2,1)S(1)}, u32[]{:S(2)}, u32[]{:S(2)}) collective-permute-start(bf16[768,512]{1,0:T(8,128)(2,1)S(1)} %get-tuple-element.53.mine), channel_id=1, source_target_pairs={{0,1},{1,0},{2,3},{3,2},{4,5},{5,4},{6,7},{7,6},{8,9},{9,8},{10,11... | collective-permute-start | bytes 2359304 | tf_op jit(solution)/shard_map/ppermute | solution.py:432
  41.4 17.2 %collective-permute-start.13 = (bf16[3,7,32,256]{3,2,1,0:T(8,128)(2,1)S(1)}, bf16[3,7,32,256]{3,2,1,0:T(8,128)(2,1)}, u32[]{:S(2)}, u32[]{:S(2)}) collective-permute-start(bf16[3,7,32,256]{3,2,1,0:T(8,128)(2,1)S(1)} %get-tuple-element.57.refs_6_), channel_id=1, source_target_pairs={{0,2},{2,0},{1,3},{3,1},{4,6},{6,4},{5,7},{7,5},{8,10},{10,8},{9,1... | collective-permute-start | bytes 1032200 | tf_op jit(solution)/shard_map/ppermute | solution.py:427
  42.6 18.4 %collective-permute-start.15 = (bf16[3,7,32,256]{3,2,1,0:T(8,128)(2,1)S(1)}, bf16[3,7,32,256]{3,2,1,0:T(8,128)(2,1)}, u32[]{:S(2)}, u32[]{:S(2)}) collective-permute-start(bf16[3,7,32,256]{3,2,1,0:T(8,128)(2,1)S(1)} %get-tuple-element.57.refs_6_), channel_id=1, source_target_pairs={{0,16},{16,0},{1,17},{17,1},{2,18},{18,2},{3,19},{19,3},{4,20},{20... | collective-permute-start | bytes 1032200 | tf_op jit(solution)/shard_map/ppermute | solution.py:426
  43.9 17.6 %collective-permute-start.17 = (bf16[3,7,32,256]{3,2,1,0:T(8,128)(2,1)S(1)}, bf16[3,7,32,256]{3,2,1,0:T(8,128)(2,1)}, u32[]{:S(2)}, u32[]{:S(2)}) collective-permute-start(bf16[3,7,32,256]{3,2,1,0:T(8,128)(2,1)S(1)} %get-tuple-element.57.refs_6_), channel_id=1, source_target_pairs={{0,18},{18,0},{2,16},{16,2},{1,19},{19,1},{3,17},{17,3},{4,22},{22... | collective-permute-start | bytes 1032200 | tf_op jit(solution)/shard_map/ppermute | solution.py:425
  47.4 1.7 %copy-start.4 = (bf16[320,512]{1,0:T(8,128)(2,1)S(1)}, bf16[320,512]{1,0:T(8,128)(2,1)}, u32[]{:S(2)}) copy-start(bf16[320,512]{1,0:T(8,128)(2,1)} %nodes.3) | copy-start | bytes 983044
  47.4 1.7 %collective-permute-start.12 = (bf16[320,512]{1,0:T(8,128)(2,1)S(1)}, bf16[320,512]{1,0:T(8,128)(2,1)S(1)}, u32[]{:S(2)}, u32[]{:S(2)}) collective-permute-start(bf16[320,512]{1,0:T(8,128)(2,1)S(1)} %shard_map.152.source.mine), channel_id=1, source_target_pairs={{0,1},{1,0},{2,3},{3,2},{4,5},{5,4},{6,7},{7,6},{8,9},{9,8},{10,11... | collective-permute-start | bytes 983048 | tf_op jit(solution)/shard_map/ppermute | solution.py:432
  47.5 14.1 %copy-start.9 = (s32[768]{0:T(1024)S(1)}, s32[768]{0:T(1024)}, u32[]{:S(2)}) copy-start(s32[768]{0:T(1024)} %param.24) | copy-start | bytes 9220
  47.5 14.1 %copy-start.7 = (s32[768]{0:T(1024)S(1)}, s32[768]{0:T(1024)}, u32[]{:S(2)}) copy-start(s32[768]{0:T(1024)} %param.25) | copy-start | bytes 9220
  50.8 10.3 %all-to-all-start = ((bf16[8,8,512]{2,1,0:T(8,128)(2,1)}), bf16[8,8,512]{2,1,0:T(8,128)(2,1)S(1)}, u32[]{:S(2)}, u32[]{:S(2)}) async-start(bf16[8,8,512]{2,1,0:T(8,128)(2,1)} %bitcast.2), calls=%async_computation | async-start | bytes 131072 | tf_op jit(solution)/shard_map/all_to_all | solution.py:558
  58.0 4.9 %collective-permute-start.19 = (bf16[7,128,256]{2,1,0:T(8,128)(2,1)S(1)}, bf16[7,128,256]{2,1,0:T(8,128)(2,1)S(1)}, u32[]{:S(2)}, u32[]{:S(2)}) collective-permute-start(bf16[7,128,256]{2,1,0:T(8,128)(2,1)S(1)} %get-tuple-element.63.refs_5_), channel_id=1, source_target_pairs={{0,1},{1,0},{2,3},{3,2},{4,5},{5,4},{6,7},{7,6},{8,9},{9,8},{10,11... | collective-permute-start | bytes 1376264 | tf_op jit(solution)/shard_map/ppermute | solution.py:432
  58.1 3.6 %collective-permute-start.20 = (bf16[3,7,32,256]{3,2,1,0:T(8,128)(2,1)S(1)}, bf16[3,7,32,256]{3,2,1,0:T(8,128)(2,1)}, u32[]{:S(2)}, u32[]{:S(2)}) collective-permute-start(bf16[3,7,32,256]{3,2,1,0:T(8,128)(2,1)S(1)} %get-tuple-element.57.refs_6_), channel_id=1, source_target_pairs={{0,1},{1,0},{2,3},{3,2},{4,5},{5,4},{6,7},{7,6},{8,9},{9,8},{10,11... | collective-permute-start | bytes 1032200 | tf_op jit(solution)/shard_map/ppermute | solution.py:432
  61.0 3.4 %collective-permute-start.14 = (bf16[3,7,32,256]{3,2,1,0:T(8,128)(2,1)}, bf16[3,7,32,256]{3,2,1,0:T(8,128)(2,1)S(1)}, u32[]{:S(2)}, u32[]{:S(2)}) collective-permute-start(bf16[3,7,32,256]{3,2,1,0:T(8,128)(2,1)} %collective-permute-done.13.refs_7_), channel_id=1, source_target_pairs={{0,1},{1,0},{2,3},{3,2},{4,5},{5,4},{6,7},{7,6},{8,9},{9,8},{10,11... | collective-permute-start | bytes 1032200 | tf_op jit(solution)/shard_map/ppermute | solution.py:432
  61.0 4.5 %collective-permute-start.16 = (bf16[3,7,32,256]{3,2,1,0:T(8,128)(2,1)}, bf16[3,7,32,256]{3,2,1,0:T(8,128)(2,1)S(1)}, u32[]{:S(2)}, u32[]{:S(2)}) collective-permute-start(bf16[3,7,32,256]{3,2,1,0:T(8,128)(2,1)} %collective-permute-done.15.refs_8_), channel_id=1, source_target_pairs={{0,1},{1,0},{2,3},{3,2},{4,5},{5,4},{6,7},{7,6},{8,9},{9,8},{10,11... | collective-permute-start | bytes 1032200 | tf_op jit(solution)/shard_map/ppermute | solution.py:432
  61.6 4.0 %collective-permute-start.18 = (bf16[3,7,32,256]{3,2,1,0:T(8,128)(2,1)}, bf16[3,7,32,256]{3,2,1,0:T(8,128)(2,1)S(1)}, u32[]{:S(2)}, u32[]{:S(2)}) collective-permute-start(bf16[3,7,32,256]{3,2,1,0:T(8,128)(2,1)} %collective-permute-done.17.refs_9_), channel_id=1, source_target_pairs={{0,1},{1,0},{2,3},{3,2},{4,5},{5,4},{6,7},{7,6},{8,9},{9,8},{10,11... | collective-permute-start | bytes 1032200 | tf_op jit(solution)/shard_map/ppermute | solution.py:432
  61.7 18.1 %collective-permute-start.21 = (bf16[3,7,32,256]{3,2,1,0:T(8,128)(2,1)S(1)}, bf16[3,7,32,256]{3,2,1,0:T(8,128)(2,1)S(1)}, u32[]{:S(2)}, u32[]{:S(2)}) collective-permute-start(bf16[3,7,32,256]{3,2,1,0:T(8,128)(2,1)S(1)} %get-tuple-element.69.refs_1_), channel_id=1, source_target_pairs={{0,2},{2,0},{1,3},{3,1},{4,6},{6,4},{5,7},{7,5},{8,10},{10,8},{9,1... | collective-permute-start | bytes 1032200 | tf_op jit(solution)/shard_map/ppermute | solution.py:427
  63.0 1.5 %copy-start.10 = (bf16[7,128,256]{2,1,0:T(8,128)(2,1)}, bf16[7,128,256]{2,1,0:T(8,128)(2,1)S(1)}, u32[]{:S(2)}) copy-start(bf16[7,128,256]{2,1,0:T(8,128)(2,1)S(1)} %collective-permute-done.19.refs_10_) | copy-start | bytes 1376260
  63.0 19.8 %collective-permute-start.22 = (bf16[3,7,32,256]{3,2,1,0:T(8,128)(2,1)S(1)}, bf16[3,7,32,256]{3,2,1,0:T(8,128)(2,1)S(1)}, u32[]{:S(2)}, u32[]{:S(2)}) collective-permute-start(bf16[3,7,32,256]{3,2,1,0:T(8,128)(2,1)S(1)} %get-tuple-element.69.refs_1_), channel_id=1, source_target_pairs={{0,16},{16,0},{1,17},{17,1},{2,18},{18,2},{3,19},{19,3},{4,20},{20... | collective-permute-start | bytes 1032200 | tf_op jit(solution)/shard_map/ppermute | solution.py:426
  64.5 18.7 %collective-permute-start.23 = (bf16[3,7,32,256]{3,2,1,0:T(8,128)(2,1)S(1)}, bf16[3,7,32,256]{3,2,1,0:T(8,128)(2,1)S(1)}, u32[]{:S(2)}, u32[]{:S(2)}) collective-permute-start(bf16[3,7,32,256]{3,2,1,0:T(8,128)(2,1)S(1)} %get-tuple-element.69.refs_1_), channel_id=1, source_target_pairs={{0,18},{18,0},{2,16},{16,2},{1,19},{19,1},{3,17},{17,3},{4,22},{22... | collective-permute-start | bytes 1032200 | tf_op jit(solution)/shard_map/ppermute | solution.py:425
  65.5 17.8 %collective-permute-start.25 = (bf16[3,7,32,256]{3,2,1,0:T(8,128)(2,1)S(1)}, bf16[3,7,32,256]{3,2,1,0:T(8,128)(2,1)S(1)}, u32[]{:S(2)}, u32[]{:S(2)}) collective-permute-start(bf16[3,7,32,256]{3,2,1,0:T(8,128)(2,1)S(1)} %get-tuple-element.69.refs_1_), channel_id=1, source_target_pairs={{0,1},{1,0},{2,3},{3,2},{4,5},{5,4},{6,7},{7,6},{8,9},{9,8},{10,11... | collective-permute-start | bytes 1032200 | tf_op jit(solution)/shard_map/ppermute | solution.py:432
  65.5 17.8 %collective-permute-start.24 = (bf16[7,128,256]{2,1,0:T(8,128)(2,1)S(1)}, bf16[7,128,256]{2,1,0:T(8,128)(2,1)S(1)}, u32[]{:S(2)}, u32[]{:S(2)}) collective-permute-start(bf16[7,128,256]{2,1,0:T(8,128)(2,1)S(1)} %get-tuple-element.70.refs_0_), channel_id=1, source_target_pairs={{0,1},{1,0},{2,3},{3,2},{4,5},{5,4},{6,7},{7,6},{8,9},{9,8},{10,11... | collective-permute-start | bytes 1376264 | tf_op jit(solution)/shard_map/ppermute | solution.py:432
  72.5 10.2 %all-to-all-start.1 = ((bf16[8,8,512]{2,1,0:T(8,128)(2,1)}), bf16[8,8,512]{2,1,0:T(8,128)(2,1)S(1)}, u32[]{:S(2)}, u32[]{:S(2)}) async-start(bf16[8,8,512]{2,1,0:T(8,128)(2,1)} %bitcast.4), calls=%async_computation.1 | async-start | bytes 131072 | tf_op jit(solution)/shard_map/all_to_all | solution.py:558
  82.7 4.0 %collective-permute-start.26 = (bf16[3,7,32,256]{3,2,1,0:T(8,128)(2,1)S(1)}, bf16[3,7,32,256]{3,2,1,0:T(8,128)(2,1)S(1)}, u32[]{:S(2)}, u32[]{:S(2)}) collective-permute-start(bf16[3,7,32,256]{3,2,1,0:T(8,128)(2,1)S(1)} %collective-permute-done.21.refs_2_), channel_id=1, source_target_pairs={{0,1},{1,0},{2,3},{3,2},{4,5},{5,4},{6,7},{7,6},{8,9},{9,8},{10,11... | collective-permute-start | bytes 1032200 | tf_op jit(solution)/shard_map/ppermute | solution.py:432
  82.7 4.0 %collective-permute-start.27 = (bf16[3,7,32,256]{3,2,1,0:T(8,128)(2,1)S(1)}, bf16[3,7,32,256]{3,2,1,0:T(8,128)(2,1)S(1)}, u32[]{:S(2)}, u32[]{:S(2)}) collective-permute-start(bf16[3,7,32,256]{3,2,1,0:T(8,128)(2,1)S(1)} %collective-permute-done.22.refs_3_), channel_id=1, source_target_pairs={{0,1},{1,0},{2,3},{3,2},{4,5},{5,4},{6,7},{7,6},{8,9},{9,8},{10,11... | collective-permute-start | bytes 1032200 | tf_op jit(solution)/shard_map/ppermute | solution.py:432
  83.2 3.5 %collective-permute-start.28 = (bf16[3,7,32,256]{3,2,1,0:T(8,128)(2,1)S(1)}, bf16[3,7,32,256]{3,2,1,0:T(8,128)(2,1)S(1)}, u32[]{:S(2)}, u32[]{:S(2)}) collective-permute-start(bf16[3,7,32,256]{3,2,1,0:T(8,128)(2,1)S(1)} %collective-permute-done.23.refs_4_), channel_id=1, source_target_pairs={{0,1},{1,0},{2,3},{3,2},{4,5},{5,4},{6,7},{7,6},{8,9},{9,8},{10,11... | collective-permute-start | bytes 1032200 | tf_op jit(solution)/shard_map/ppermute | solution.py:432

commit v7 on v6

--- a/solution.py
+++ b/solution.py
@@ -495,7 +495,7 @@
         [cut0] = cut([((0,), "quarter", quarter)], raws)
         cut12, own0, own1, own2 = cut([((1, 2), "quarter", quarter)] + [((block,), "whole", slab) for block in range(3)], raws)
         turned0 = over_slices(cut0)
-        lent_down, lent_up = after(lent_down, turned0[0]), after(lent_up, turned0[0])
+        lent_down, lent_up = after(lent_down, cut0), after(lent_up, cut0)
     from_upper = lax.ppermute(lent_down, ("mesh", "band"), [(i + 1, i) for i in range(line - 1)])
     from_lower = lax.ppermute(lent_up, ("mesh", "band"), [(i, i + 1) for i in range(line - 1)])
     if by_parts:
@@ -528,7 +528,7 @@
         plane1 = over_plane(after(joined1, term))
     else:
         node_weights = packs[1].near_operands
-    before = term
+    before = gathered
     term = call(
         half_nodes_body,
         (nodes, depth),

time: 91.1 us -> 90.6 us (level)
  starting transfers between devices: 49.8 us -> 45.4 us
  waiting for transfers between devices: 15.3 us -> 19.1 us
    ppermute x6, waiting for transfers between devices: 3.75 us -> 7.94 us  [over_slices(): lax.ppermute(chunk, 'mesh', [(i, i ^ k) for i in range(count)])]
    ppermute x3, starting transfers between devices: 8.54 us -> 4.52 us  [over_plane(): across = lax.ppermute(own, ('groups', 'band'), DIAGONAL)]
where the time goes in v7:
time: 90.6 us; the launch traced here: 90.1 us
  starting transfers between devices  45.4 us (50%)
  Pallas kernels  24.9 us (27%)
  waiting for transfers between devices  19.1 us (21%)
    pallas_call x13, Pallas kernels, call(): pl.pallas_call(body, out_shape=shapes if many else shapes[0], in_specs=sp...  24.9 us
    all_to_all x2, starting transfers between devices, on_device(): lax.all_to_all(cut_rows, ('mesh', 'band'), split_axis=0, concat_axis=0, a...  14.6 us
    ppermute x6, starting transfers between devices, over_slices(): lax.ppermute(chunk, 'mesh', [(i, i ^ k) for i in range(count)])  10.2 us
    ppermute x6, waiting for transfers between devices, over_slices(): lax.ppermute(chunk, 'mesh', [(i, i ^ k) for i in range(count)])  7.94 us
    all_to_all x2, waiting for transfers between devices, on_device(): lax.all_to_all(cut_rows, ('mesh', 'band'), split_axis=0, concat_axis=0, a...  5.46 us
    ppermute x3, starting transfers between devices, over_plane(): along_x = lax.ppermute(own, 'band', SWAP)  4.71 us
    ppermute x3, starting transfers between devices, over_plane(): across = lax.ppermute(own, ('groups', 'band'), DIAGONAL)  4.52 us
    ppermute x3, starting transfers between devices, over_plane(): along_y = lax.ppermute(own, 'groups', SWAP)  4.26 us
  transfers between devices with their start and end apart: 31, of which 7 were waited for; matrix products, arithmetic and copies ran while one was open for 0% of the time, Pallas kernels for 21%

profile of v7, /device:TPU:0, one launch (start us, length us, event | category | flops | bytes accessed | tf_op | source)
XLA Modules:
  0.0 90.1 jit_solution(15239730363116307552)
XLA Ops:
  0.0 0.9 shard_map.146
  0.9 5.1 %collective-permute-start.4 = (bf16[7,32,256]{2,1,0:T(8,128)(2,1)S(1)}, bf16[7,32,256]{2,1,0:T(8,128)(2,1)S(1)}, u32[]{:S(2)}, u32[]{:S(2)}) collective-permute-start(bf16[7,32,256]{2,1,0:T(8,128)(2,1)S(1)} %shard_map.146), channel_id=1, source_target_pairs={{0,12},{4,8},{8,4},{12,0},{1,13},{5,9},{9,5},{13,1},{2,14},{6,10},... | collective-permute-start | bytes 344072 | tf_op jit(solution)/shard_map/ppermute | solution.py:421
  6.0 0.6 collective-permute-start.3
  6.6 1.5 %shard_map.145 = (bf16[64,512]{1,0:T(8,128)(2,1)S(1)}, bf16[64,512]{1,0:T(8,128)(2,1)S(1)}) custom-call(bf16[512,512]{1,0:T(8,128)(2,1)} %grid.1, s32[1,64]{1,0:T(1,128)} %bitcast.9, s32[1,64]{1,0:T(1,128)} %bitcast.10), custom_call_target="tpu_custom_call" | custom-call | flops 500000000 | tf_op jit(solution)/shard_map/pallas_call | solution.py:61
  8.2 3.5 %collective-permute-start = (bf16[64,512]{1,0:T(8,128)(2,1)S(1)}, bf16[64,512]{1,0:T(8,128)(2,1)S(1)}, u32[]{:S(2)}, u32[]{:S(2)}) collective-permute-start(bf16[64,512]{1,0:T(8,128)(2,1)S(1)} %get-tuple-element.45), channel_id=1, source_target_pairs={{0,2},{2,4},{4,6},{6,8},{8,10},{10,12},{12,14},{1,3},{3,5},{5,7},{... | collective-permute-start | bytes 196616 | tf_op jit(solution)/shard_map/ppermute | solution.py:500
  11.7 1.3 %collective-permute-start.1 = (bf16[64,512]{1,0:T(8,128)(2,1)S(1)}, bf16[64,512]{1,0:T(8,128)(2,1)S(1)}, u32[]{:S(2)}, u32[]{:S(2)}) collective-permute-start(bf16[64,512]{1,0:T(8,128)(2,1)S(1)} %get-tuple-element.47), channel_id=1, source_target_pairs={{2,0},{4,2},{6,4},{8,6},{10,8},{12,10},{14,12},{3,1},{5,3},{7,5},{... | collective-permute-start | bytes 196616 | tf_op jit(solution)/shard_map/ppermute | solution.py:499
  13.0 1.8 %shard_map.148 = (bf16[14,32,256]{2,1,0:T(8,128)(2,1)S(1)}, bf16[7,128,256]{2,1,0:T(8,128)(2,1)S(1)}, bf16[7,128,256]{2,1,0:T(8,128)(2,1)S(1)}, bf16[7,128,256]{2,1,0:T(8,128)(2,1)S(1)}) custom-call(bf16[3,3,128,256]{3,2,1,0:T(8,128)(2,1)} %refs_0_.3, bf16[3,256,128]{2,1,0:T(8,128)(2,1)} %refs_1_.3, bf16[3,2,128,256]{3,2,1,0:T(8,128)(2,1)} %refs_2_.3, ...), custom_call_target="tpu_custom_call" | custom-call | flops 500000000 | tf_op jit(solution)/shard_map/pallas_call | solution.py:61
  14.9 3.0 %collective-permute-done.1.high = bf16[64,512]{1,0:T(8,128)(2,1)S(1)} collective-permute-done((bf16[64,512]{1,0:T(8,128)(2,1)S(1)}, bf16[64,512]{1,0:T(8,128)(2,1)S(1)}, u32[]{:S(2)}, u32[]{:S(2)}) %collective-permute-start.1) | collective-permute-done | bytes 65568 | tf_op jit(solution)/shard_map/ppermute | solution.py:499
  17.9 0.0 collective-permute-done.2.refs_0_
  17.9 0.0 collective-permute-done.3.refs_1_
  17.9 1.3 %collective-permute-start.5 = (bf16[14,32,256]{2,1,0:T(8,128)(2,1)S(1)}, bf16[14,32,256]{2,1,0:T(8,128)(2,1)S(1)}, u32[]{:S(2)}, u32[]{:S(2)}) collective-permute-start(bf16[14,32,256]{2,1,0:T(8,128)(2,1)S(1)} %get-tuple-element.51), channel_id=1, source_target_pairs={{0,4},{4,0},{8,12},{12,8},{1,5},{5,1},{9,13},{13,9},{2,6},{6,2},{1... | collective-permute-start | bytes 688136 | tf_op jit(solution)/shard_map/ppermute | solution.py:421
  19.2 2.9 %collective-permute-start.6 = (bf16[14,32,256]{2,1,0:T(8,128)(2,1)S(1)}, bf16[14,32,256]{2,1,0:T(8,128)(2,1)S(1)}, u32[]{:S(2)}, u32[]{:S(2)}) collective-permute-start(bf16[14,32,256]{2,1,0:T(8,128)(2,1)S(1)} %get-tuple-element.51), channel_id=1, source_target_pairs={{0,8},{4,12},{8,0},{12,4},{1,9},{5,13},{9,1},{13,5},{2,10},{6,14},... | collective-permute-start | bytes 688136 | tf_op jit(solution)/shard_map/ppermute | solution.py:421
  22.2 0.2 collective-permute-start.7
  22.4 2.3 %collective-permute-start.8 = (bf16[3,7,32,256]{3,2,1,0:T(8,128)(2,1)S(1)}, bf16[3,7,32,256]{3,2,1,0:T(8,128)(2,1)S(1)}, u32[]{:S(2)}, u32[]{:S(2)}) collective-permute-start(bf16[3,7,32,256]{3,2,1,0:T(8,128)(2,1)S(1)} %shard_map.149.refs_1_), channel_id=1, source_target_pairs={{0,2},{2,0},{1,3},{3,1},{4,6},{6,4},{5,7},{7,5},{8,10},{10,8},{9,1... | collective-permute-start | bytes 1032200 | tf_op jit(solution)/shard_map/ppermute | solution.py:427
  24.7 1.5 %collective-permute-start.9 = (bf16[3,7,32,256]{3,2,1,0:T(8,128)(2,1)S(1)}, bf16[3,7,32,256]{3,2,1,0:T(8,128)(2,1)S(1)}, u32[]{:S(2)}, u32[]{:S(2)}) collective-permute-start(bf16[3,7,32,256]{3,2,1,0:T(8,128)(2,1)S(1)} %shard_map.149.refs_1_), channel_id=1, source_target_pairs={{0,16},{16,0},{1,17},{17,1},{2,18},{18,2},{3,19},{19,3},{4,20},{20... | collective-permute-start | bytes 1032200 | tf_op jit(solution)/shard_map/ppermute | solution.py:426
  26.2 0.6 collective-permute-done.5.refs_0_
  26.8 2.6 %collective-permute-start.10 = (bf16[3,7,32,256]{3,2,1,0:T(8,128)(2,1)S(1)}, bf16[3,7,32,256]{3,2,1,0:T(8,128)(2,1)S(1)}, u32[]{:S(2)}, u32[]{:S(2)}) collective-permute-start(bf16[3,7,32,256]{3,2,1,0:T(8,128)(2,1)S(1)} %shard_map.149.refs_1_), channel_id=1, source_target_pairs={{0,18},{18,0},{2,16},{16,2},{1,19},{19,1},{3,17},{17,3},{4,22},{22... | collective-permute-start | bytes 1032200 | tf_op jit(solution)/shard_map/ppermute | solution.py:425
  29.4 1.3 %shard_map.147.gathered = bf16[768,1536]{1,0:T(8,128)(2,1)S(1)} custom-call(bf16[512,512]{1,0:T(8,128)(2,1)S(1)} %copy-done, bf16[64,512]{1,0:T(8,128)(2,1)S(1)} %collective-permute-done.low, bf16[64,512]{1,0:T(8,128)(2,1)S(1)} %collective-permute-done.1.high, bf16[320,512]{1,0:T(8,128)(2,1)S(1)} %copy-done.3, s32[1,768]{1,0:T(1,128)S(1)} %broadcast_in_dim.22.slots, ...), custom_call_target="tpu_custom_call" | custom-call | flops 1200000000 | tf_op jit(solution)/shard_map/pallas_call | solution.py:61
  30.7 7.4 %collective-permute-done.6.refs_1_ = bf16[14,32,256]{2,1,0:T(8,128)(2,1)S(1)} collective-permute-done((bf16[14,32,256]{2,1,0:T(8,128)(2,1)S(1)}, bf16[14,32,256]{2,1,0:T(8,128)(2,1)S(1)}, u32[]{:S(2)}, u32[]{:S(2)}) %collective-permute-start.6) | collective-permute-done | bytes 229408 | tf_op jit(solution)/shard_map/ppermute | solution.py:421
  38.1 0.0 copy-start.8
  38.1 1.0 %collective-permute-done.9.refs_3_ = bf16[3,7,32,256]{3,2,1,0:T(8,128)(2,1)S(1)} collective-permute-done((bf16[3,7,32,256]{3,2,1,0:T(8,128)(2,1)S(1)}, bf16[3,7,32,256]{3,2,1,0:T(8,128)(2,1)S(1)}, u32[]{:S(2)}, u32[]{:S(2)}) %collective-permute-start.9) | collective-permute-done | bytes 344096 | tf_op jit(solution)/shard_map/ppermute | solution.py:426
  39.2 0.0 collective-permute-done.10.refs_4_
  39.2 1.6 %shard_map.151 = (bf16[768,512]{1,0:T(8,128)(2,1)S(1)}, bf16[1024,256]{1,0:T(8,128)(2,1)}, bf16[256,512]{1,0:T(8,128)(2,1)}) custom-call(bf16[768,1536]{1,0:T(8,128)(2,1)S(1)} %shard_map.147.gathered, bf16[7,128,256]{2,1,0:T(8,128)(2,1)S(1)} %get-tuple-element.53.refs_0_, bf16[3,7,32,256]{3,2,1,0:T(8,128)(2,1)S(1)} %shard_map.149.refs_1_, ...), custom_call_target="tpu_custom_call" | custom-call | flops 3000000000 | tf_op jit(solution)/shard_map/pallas_call | solution.py:61
  40.8 0.1 collective-permute-start.11
  40.9 0.1 reshape.15.lists
  41.0 1.1 %collective-permute-start.13 = (bf16[3,7,32,256]{3,2,1,0:T(8,128)(2,1)S(1)}, bf16[3,7,32,256]{3,2,1,0:T(8,128)(2,1)}, u32[]{:S(2)}, u32[]{:S(2)}) collective-permute-start(bf16[3,7,32,256]{3,2,1,0:T(8,128)(2,1)S(1)} %get-tuple-element.65.refs_6_), channel_id=1, source_target_pairs={{0,2},{2,0},{1,3},{3,1},{4,6},{6,4},{5,7},{7,5},{8,10},{10,8},{9,1... | collective-permute-start | bytes 1032200 | tf_op jit(solution)/shard_map/ppermute | solution.py:427
  42.1 1.2 %collective-permute-start.15 = (bf16[3,7,32,256]{3,2,1,0:T(8,128)(2,1)S(1)}, bf16[3,7,32,256]{3,2,1,0:T(8,128)(2,1)}, u32[]{:S(2)}, u32[]{:S(2)}) collective-permute-start(bf16[3,7,32,256]{3,2,1,0:T(8,128)(2,1)S(1)} %get-tuple-element.65.refs_6_), channel_id=1, source_target_pairs={{0,16},{16,0},{1,17},{17,1},{2,18},{18,2},{3,19},{19,3},{4,20},{20... | collective-permute-start | bytes 1032200 | tf_op jit(solution)/shard_map/ppermute | solution.py:426
  43.3 1.1 %collective-permute-start.17 = (bf16[3,7,32,256]{3,2,1,0:T(8,128)(2,1)S(1)}, bf16[3,7,32,256]{3,2,1,0:T(8,128)(2,1)}, u32[]{:S(2)}, u32[]{:S(2)}) collective-permute-start(bf16[3,7,32,256]{3,2,1,0:T(8,128)(2,1)S(1)} %get-tuple-element.65.refs_6_), channel_id=1, source_target_pairs={{0,18},{18,0},{2,16},{16,2},{1,19},{19,1},{3,17},{17,3},{4,22},{22... | collective-permute-start | bytes 1032200 | tf_op jit(solution)/shard_map/ppermute | solution.py:425
  44.5 2.5 %shard_map.152.source.mine = bf16[320,512]{1,0:T(8,128)(2,1)S(1)} custom-call(s32[1,768]{1,0:T(1,128)S(1)} %broadcast_in_dim.19.targets, bf16[768,512]{1,0:T(8,128)(2,1)S(1)} %get-tuple-element.54.mine, bf16[768,512]{1,0:T(8,128)(2,1)S(1)} %collective-permute-done.11.other, bf16[320,512]{1,0:T(8,128)(2,1)} %nodes.3, ...), custom_call_target="tpu_custom_call" | custom-call | flops 1600000000 | tf_op jit(solution)/shard_map/pallas_call | solution.py:61
  47.0 0.0 copy-start.4
  47.0 0.1 collective-permute-start.12
  47.1 0.0 copy-start.9
  47.1 0.0 copy-start.7
  47.1 1.6 %collective-permute-done.12.other = bf16[320,512]{1,0:T(8,128)(2,1)S(1)} collective-permute-done((bf16[320,512]{1,0:T(8,128)(2,1)S(1)}, bf16[320,512]{1,0:T(8,128)(2,1)S(1)}, u32[]{:S(2)}, u32[]{:S(2)}) %collective-permute-start.12) | collective-permute-done | bytes 327712 | tf_op jit(solution)/shard_map/ppermute | solution.py:432
  48.7 1.6 %shard_map.154 = (bf16[64,512]{1,0:T(8,128)(2,1)}, bf16[320,512]{1,0:T(8,128)(2,1)}) custom-call(bf16[320,512]{1,0:T(8,128)(2,1)S(1)} %copy-done.4, s32[1,64]{1,0:T(1,128)S(1)} %reshape.15.lists, bf16[320,512]{1,0:T(8,128)(2,1)S(1)} %shard_map.152.source.mine, bf16[320,512]{1,0:T(8,128)(2,1)S(1)} %collective-permute-done.12.other, ...), custom_call_target="tpu_custom_call" | custom-call | flops 1600000000 | tf_op jit(solution)/shard_map/pallas_call | solution.py:61
  50.4 7.4 %all-to-all-start = ((bf16[8,8,512]{2,1,0:T(8,128)(2,1)}), bf16[8,8,512]{2,1,0:T(8,128)(2,1)S(1)}, u32[]{:S(2)}, u32[]{:S(2)}) async-start(bf16[8,8,512]{2,1,0:T(8,128)(2,1)} %bitcast.2), calls=%async_computation | async-start | bytes 131072 | tf_op jit(solution)/shard_map/all_to_all | solution.py:558
  57.8 0.5 collective-permute-start.20
  58.3 0.0 collective-permute-done.13.refs_7_
  58.3 2.5 %all-to-all-done = bf16[8,8,512]{2,1,0:T(8,128)(2,1)S(1)} async-done(((bf16[8,8,512]{2,1,0:T(8,128)(2,1)}), bf16[8,8,512]{2,1,0:T(8,128)(2,1)S(1)}, u32[]{:S(2)}, u32[]{:S(2)}) %all-to-all-start) | async-done | bytes 65568 | tf_op jit(solution)/shard_map/all_to_all | solution.py:558
  60.8 0.0 collective-permute-start.14
  60.8 0.0 collective-permute-done.15.refs_8_
  60.8 0.5 collective-permute-start.16
  61.3 0.0 collective-permute-done.17.refs_9_
  61.3 0.1 collective-permute-start.18
  61.4 1.3 %collective-permute-start.21 = (bf16[3,7,32,256]{3,2,1,0:T(8,128)(2,1)S(1)}, bf16[3,7,32,256]{3,2,1,0:T(8,128)(2,1)S(1)}, u32[]{:S(2)}, u32[]{:S(2)}) collective-permute-start(bf16[3,7,32,256]{3,2,1,0:T(8,128)(2,1)S(1)} %get-tuple-element.71.refs_1_), channel_id=1, source_target_pairs={{0,2},{2,0},{1,3},{3,1},{4,6},{6,4},{5,7},{7,5},{8,10},{10,8},{9,1... | collective-permute-start | bytes 1032200 | tf_op jit(solution)/shard_map/ppermute | solution.py:427
  62.7 0.0 collective-permute-done.20.refs_11_
  62.7 1.5 %collective-permute-start.22 = (bf16[3,7,32,256]{3,2,1,0:T(8,128)(2,1)S(1)}, bf16[3,7,32,256]{3,2,1,0:T(8,128)(2,1)S(1)}, u32[]{:S(2)}, u32[]{:S(2)}) collective-permute-start(bf16[3,7,32,256]{3,2,1,0:T(8,128)(2,1)S(1)} %get-tuple-element.71.refs_1_), channel_id=1, source_target_pairs={{0,16},{16,0},{1,17},{17,1},{2,18},{18,2},{3,19},{19,3},{4,20},{20... | collective-permute-start | bytes 1032200 | tf_op jit(solution)/shard_map/ppermute | solution.py:426
  64.2 0.0 collective-permute-done.14.refs_0_
  64.2 0.8 collective-permute-start.23
  65.0 0.0 collective-permute-done.16.refs_1_
  65.0 0.0 collective-permute-start.25
  65.0 0.5 collective-permute-start.24
  65.5 6.5 %shard_map.155 = (bf16[64,512]{1,0:T(8,128)(2,1)}, bf16[320,512]{1,0:T(8,128)(2,1)}, bf16[768,512]{1,0:T(8,128)(2,1)}) custom-call(bf16[64,512]{1,0:T(8,128)(2,1)S(1)} %bitcast.6, s32[1,768]{1,0:T(1,128)S(1)} %broadcast_in_dim.23.slots, s32[1,768]{1,0:T(1,128)S(1)} %broadcast_in_dim.24.targets, s32[1,64]{1,0:T(1,128)S(1)} %reshape.15.lists, ...), custom_call_target="tpu_custom_call" | custom-call | flops 6499999744 | tf_op jit(solution)/shard_map/pallas_call | solution.py:61
  72.0 7.2 %all-to-all-start.1 = ((bf16[8,8,512]{2,1,0:T(8,128)(2,1)}), bf16[8,8,512]{2,1,0:T(8,128)(2,1)S(1)}, u32[]{:S(2)}, u32[]{:S(2)}) async-start(bf16[8,8,512]{2,1,0:T(8,128)(2,1)} %bitcast.4), calls=%async_computation.1 | async-start | bytes 131072 | tf_op jit(solution)/shard_map/all_to_all | solution.py:558
  79.2 0.0 collective-permute-done.21.refs_2_
  79.2 3.0 %all-to-all-done.1 = bf16[8,8,512]{2,1,0:T(8,128)(2,1)S(1)} async-done(((bf16[8,8,512]{2,1,0:T(8,128)(2,1)}), bf16[8,8,512]{2,1,0:T(8,128)(2,1)S(1)}, u32[]{:S(2)}, u32[]{:S(2)}) %all-to-all-start.1) | async-done | bytes 65568 | tf_op jit(solution)/shard_map/all_to_all | solution.py:558
  82.2 0.0 collective-permute-start.26
  82.2 0.0 collective-permute-done.22.refs_3_
  82.2 0.5 collective-permute-start.27
  82.7 0.0 collective-permute-done.23.refs_4_
  82.7 0.1 collective-permute-start.28
  82.8 0.0 collective-permute-done.25.refs_6_
  82.8 3.4 %shard_map.156 = (f32[768,512]{1,0:T(8,128)S(1)}, bf16[1024,256]{1,0:T(8,128)(2,1)S(1)}, bf16[256,512]{1,0:T(8,128)(2,1)S(1)}, bf16[7,128,256]{2,1,0:T(8,128)(2,...) custom-call(bf16[64,512]{1,0:T(8,128)(2,1)S(1)} %bitcast.7, ...), custom_call_target="tpu_custom_call" | custom-call | flops 3500000000 | tf_op jit(solution)/shard_map/pallas_call | solution.py:61
  86.2 3.8 %shard_map.157 = bf16[320,512]{1,0:T(8,128)(2,1)} custom-call(bf16[64,512]{1,0:T(8,128)(2,1)S(1)} %bitcast.8, s32[1,768]{1,0:T(1,128)S(1)} %broadcast_in_dim.23.slots, s32[1,768]{1,0:T(1,128)S(1)} %broadcast_in_dim.24.targets, f32[768,512]{1,0:T(8,128)S(1)} %get-tuple-element.73.total, bf16[1024,256]{1,0:T(8,128)(2,1)S(1)} %get-tuple-element.74.nm, ...), custom_call_target="tpu_custom_call" | custom-call | flops 3500000000 | tf_op jit(solution)/shard_map/pallas_call | solution.py:61
  (40 shorter events, 0.2 us)
Async XLA Ops:
  0.9 17.0 %collective-permute-start.4 = (bf16[7,32,256]{2,1,0:T(8,128)(2,1)S(1)}, bf16[7,32,256]{2,1,0:T(8,128)(2,1)S(1)}, u32[]{:S(2)}, u32[]{:S(2)}) collective-permute-start(bf16[7,32,256]{2,1,0:T(8,128)(2,1)S(1)} %shard_map.146), channel_id=1, source_target_pairs={{0,12},{4,8},{8,4},{12,0},{1,13},{5,9},{9,5},{13,1},{2,14},{6,10},... | collective-permute-start | bytes 344072 | tf_op jit(solution)/shard_map/ppermute | solution.py:421
  6.0 11.9 %collective-permute-start.2 = (bf16[7,32,256]{2,1,0:T(8,128)(2,1)S(1)}, bf16[7,32,256]{2,1,0:T(8,128)(2,1)S(1)}, u32[]{:S(2)}, u32[]{:S(2)}) collective-permute-start(bf16[7,32,256]{2,1,0:T(8,128)(2,1)S(1)} %shard_map.146), channel_id=1, source_target_pairs={{0,4},{4,0},{8,12},{12,8},{1,5},{5,1},{9,13},{13,9},{2,6},{6,2},{1... | collective-permute-start | bytes 344072 | tf_op jit(solution)/shard_map/ppermute | solution.py:421
  6.0 11.9 %collective-permute-start.3 = (bf16[7,32,256]{2,1,0:T(8,128)(2,1)S(1)}, bf16[7,32,256]{2,1,0:T(8,128)(2,1)S(1)}, u32[]{:S(2)}, u32[]{:S(2)}) collective-permute-start(bf16[7,32,256]{2,1,0:T(8,128)(2,1)S(1)} %shard_map.146), channel_id=1, source_target_pairs={{0,8},{4,12},{8,0},{12,4},{1,9},{5,13},{9,1},{13,5},{2,10},{6,14},... | collective-permute-start | bytes 344072 | tf_op jit(solution)/shard_map/ppermute | solution.py:421
  6.6 15.7 %copy-start.5 = (s32[768]{0:T(1024)S(1)}, s32[768]{0:T(1024)}, u32[]{:S(2)}) copy-start(s32[768]{0:T(1024)} %param.20) | copy-start | bytes 9220
  6.6 15.8 %copy-start.6 = (s32[768]{0:T(1024)S(1)}, s32[768]{0:T(1024)}, u32[]{:S(2)}) copy-start(s32[768]{0:T(1024)} %param.19) | copy-start | bytes 9220
  6.6 22.8 %copy-start = (bf16[512,512]{1,0:T(8,128)(2,1)S(1)}, bf16[512,512]{1,0:T(8,128)(2,1)}, u32[]{:S(2)}) copy-start(bf16[512,512]{1,0:T(8,128)(2,1)} %grid.1) | copy-start | bytes 1572868
  6.6 22.8 %copy-start.3 = (bf16[320,512]{1,0:T(8,128)(2,1)S(1)}, bf16[320,512]{1,0:T(8,128)(2,1)}, u32[]{:S(2)}) copy-start(bf16[320,512]{1,0:T(8,128)(2,1)} %nodes.3) | copy-start | bytes 983044
  8.2 6.7 %collective-permute-start = (bf16[64,512]{1,0:T(8,128)(2,1)S(1)}, bf16[64,512]{1,0:T(8,128)(2,1)S(1)}, u32[]{:S(2)}, u32[]{:S(2)}) collective-permute-start(bf16[64,512]{1,0:T(8,128)(2,1)S(1)} %get-tuple-element.45), channel_id=1, source_target_pairs={{0,2},{2,4},{4,6},{6,8},{8,10},{10,12},{12,14},{1,3},{3,5},{5,7},{... | collective-permute-start | bytes 196616 | tf_op jit(solution)/shard_map/ppermute | solution.py:500
  11.7 6.2 %collective-permute-start.1 = (bf16[64,512]{1,0:T(8,128)(2,1)S(1)}, bf16[64,512]{1,0:T(8,128)(2,1)S(1)}, u32[]{:S(2)}, u32[]{:S(2)}) collective-permute-start(bf16[64,512]{1,0:T(8,128)(2,1)S(1)} %get-tuple-element.47), channel_id=1, source_target_pairs={{2,0},{4,2},{6,4},{8,6},{10,8},{12,10},{14,12},{3,1},{5,3},{7,5},{... | collective-permute-start | bytes 196616 | tf_op jit(solution)/shard_map/ppermute | solution.py:499
  14.8 42.9 %copy-start.1 = (bf16[7,128,256]{2,1,0:T(8,128)(2,1)}, bf16[7,128,256]{2,1,0:T(8,128)(2,1)S(1)}, u32[]{:S(2)}) copy-start(bf16[7,128,256]{2,1,0:T(8,128)(2,1)S(1)} %get-tuple-element.64.refs_5_) | copy-start | bytes 1376260
  17.9 8.9 %collective-permute-start.5 = (bf16[14,32,256]{2,1,0:T(8,128)(2,1)S(1)}, bf16[14,32,256]{2,1,0:T(8,128)(2,1)S(1)}, u32[]{:S(2)}, u32[]{:S(2)}) collective-permute-start(bf16[14,32,256]{2,1,0:T(8,128)(2,1)S(1)} %get-tuple-element.51), channel_id=1, source_target_pairs={{0,4},{4,0},{8,12},{12,8},{1,5},{5,1},{9,13},{13,9},{2,6},{6,2},{1... | collective-permute-start | bytes 688136 | tf_op jit(solution)/shard_map/ppermute | solution.py:421
  19.2 18.8 %collective-permute-start.6 = (bf16[14,32,256]{2,1,0:T(8,128)(2,1)S(1)}, bf16[14,32,256]{2,1,0:T(8,128)(2,1)S(1)}, u32[]{:S(2)}, u32[]{:S(2)}) collective-permute-start(bf16[14,32,256]{2,1,0:T(8,128)(2,1)S(1)} %get-tuple-element.51), channel_id=1, source_target_pairs={{0,8},{4,12},{8,0},{12,4},{1,9},{5,13},{9,1},{13,5},{2,10},{6,14},... | collective-permute-start | bytes 688136 | tf_op jit(solution)/shard_map/ppermute | solution.py:421
  22.2 15.9 %collective-permute-start.7 = (bf16[14,32,256]{2,1,0:T(8,128)(2,1)S(1)}, bf16[14,32,256]{2,1,0:T(8,128)(2,1)S(1)}, u32[]{:S(2)}, u32[]{:S(2)}) collective-permute-start(bf16[14,32,256]{2,1,0:T(8,128)(2,1)S(1)} %get-tuple-element.51), channel_id=1, source_target_pairs={{0,12},{4,8},{8,4},{12,0},{1,13},{5,9},{9,5},{13,1},{2,14},{6,10},... | collective-permute-start | bytes 688136 | tf_op jit(solution)/shard_map/ppermute | solution.py:421
  22.4 15.7 %collective-permute-start.8 = (bf16[3,7,32,256]{3,2,1,0:T(8,128)(2,1)S(1)}, bf16[3,7,32,256]{3,2,1,0:T(8,128)(2,1)S(1)}, u32[]{:S(2)}, u32[]{:S(2)}) collective-permute-start(bf16[3,7,32,256]{3,2,1,0:T(8,128)(2,1)S(1)} %shard_map.149.refs_1_), channel_id=1, source_target_pairs={{0,2},{2,0},{1,3},{3,1},{4,6},{6,4},{5,7},{7,5},{8,10},{10,8},{9,1... | collective-permute-start | bytes 1032200 | tf_op jit(solution)/shard_map/ppermute | solution.py:427
  24.7 14.4 %collective-permute-start.9 = (bf16[3,7,32,256]{3,2,1,0:T(8,128)(2,1)S(1)}, bf16[3,7,32,256]{3,2,1,0:T(8,128)(2,1)S(1)}, u32[]{:S(2)}, u32[]{:S(2)}) collective-permute-start(bf16[3,7,32,256]{3,2,1,0:T(8,128)(2,1)S(1)} %shard_map.149.refs_1_), channel_id=1, source_target_pairs={{0,16},{16,0},{1,17},{17,1},{2,18},{18,2},{3,19},{19,3},{4,20},{20... | collective-permute-start | bytes 1032200 | tf_op jit(solution)/shard_map/ppermute | solution.py:426
  26.8 12.4 %collective-permute-start.10 = (bf16[3,7,32,256]{3,2,1,0:T(8,128)(2,1)S(1)}, bf16[3,7,32,256]{3,2,1,0:T(8,128)(2,1)S(1)}, u32[]{:S(2)}, u32[]{:S(2)}) collective-permute-start(bf16[3,7,32,256]{3,2,1,0:T(8,128)(2,1)S(1)} %shard_map.149.refs_1_), channel_id=1, source_target_pairs={{0,18},{18,0},{2,16},{16,2},{1,19},{19,1},{3,17},{17,3},{4,22},{22... | collective-permute-start | bytes 1032200 | tf_op jit(solution)/shard_map/ppermute | solution.py:425
  38.1 19.7 %copy-start.2 = (bf16[3,7,32,256]{3,2,1,0:T(8,128)(2,1)}, bf16[3,7,32,256]{3,2,1,0:T(8,128)(2,1)S(1)}, u32[]{:S(2)}) copy-start(bf16[3,7,32,256]{3,2,1,0:T(8,128)(2,1)S(1)} %get-tuple-element.65.refs_6_) | copy-start | bytes 1032196
  38.1 2.7 %copy-start.8 = (s32[1,8,8]{2,1,0:T(8,128)S(1)}, s32[1,8,8]{2,1,0:T(8,128)}, u32[]{:S(2)}) copy-start(s32[1,8,8]{2,1,0:T(8,128)} %param.23) | copy-start | bytes 772
  40.8 3.7 %collective-permute-start.11 = (bf16[768,512]{1,0:T(8,128)(2,1)S(1)}, bf16[768,512]{1,0:T(8,128)(2,1)S(1)}, u32[]{:S(2)}, u32[]{:S(2)}) collective-permute-start(bf16[768,512]{1,0:T(8,128)(2,1)S(1)} %get-tuple-element.54.mine), channel_id=1, source_target_pairs={{0,1},{1,0},{2,3},{3,2},{4,5},{5,4},{6,7},{7,6},{8,9},{9,8},{10,11... | collective-permute-start | bytes 2359304 | tf_op jit(solution)/shard_map/ppermute | solution.py:432
  41.0 17.3 %collective-permute-start.13 = (bf16[3,7,32,256]{3,2,1,0:T(8,128)(2,1)S(1)}, bf16[3,7,32,256]{3,2,1,0:T(8,128)(2,1)}, u32[]{:S(2)}, u32[]{:S(2)}) collective-permute-start(bf16[3,7,32,256]{3,2,1,0:T(8,128)(2,1)S(1)} %get-tuple-element.65.refs_6_), channel_id=1, source_target_pairs={{0,2},{2,0},{1,3},{3,1},{4,6},{6,4},{5,7},{7,5},{8,10},{10,8},{9,1... | collective-permute-start | bytes 1032200 | tf_op jit(solution)/shard_map/ppermute | solution.py:427
  42.1 18.7 %collective-permute-start.15 = (bf16[3,7,32,256]{3,2,1,0:T(8,128)(2,1)S(1)}, bf16[3,7,32,256]{3,2,1,0:T(8,128)(2,1)}, u32[]{:S(2)}, u32[]{:S(2)}) collective-permute-start(bf16[3,7,32,256]{3,2,1,0:T(8,128)(2,1)S(1)} %get-tuple-element.65.refs_6_), channel_id=1, source_target_pairs={{0,16},{16,0},{1,17},{17,1},{2,18},{18,2},{3,19},{19,3},{4,20},{20... | collective-permute-start | bytes 1032200 | tf_op jit(solution)/shard_map/ppermute | solution.py:426
  43.3 18.0 %collective-permute-start.17 = (bf16[3,7,32,256]{3,2,1,0:T(8,128)(2,1)S(1)}, bf16[3,7,32,256]{3,2,1,0:T(8,128)(2,1)}, u32[]{:S(2)}, u32[]{:S(2)}) collective-permute-start(bf16[3,7,32,256]{3,2,1,0:T(8,128)(2,1)S(1)} %get-tuple-element.65.refs_6_), channel_id=1, source_target_pairs={{0,18},{18,0},{2,16},{16,2},{1,19},{19,1},{3,17},{17,3},{4,22},{22... | collective-permute-start | bytes 1032200 | tf_op jit(solution)/shard_map/ppermute | solution.py:425
  47.0 1.7 %copy-start.4 = (bf16[320,512]{1,0:T(8,128)(2,1)S(1)}, bf16[320,512]{1,0:T(8,128)(2,1)}, u32[]{:S(2)}) copy-start(bf16[320,512]{1,0:T(8,128)(2,1)} %nodes.3) | copy-start | bytes 983044
  47.0 1.7 %collective-permute-start.12 = (bf16[320,512]{1,0:T(8,128)(2,1)S(1)}, bf16[320,512]{1,0:T(8,128)(2,1)S(1)}, u32[]{:S(2)}, u32[]{:S(2)}) collective-permute-start(bf16[320,512]{1,0:T(8,128)(2,1)S(1)} %shard_map.152.source.mine), channel_id=1, source_target_pairs={{0,1},{1,0},{2,3},{3,2},{4,5},{5,4},{6,7},{7,6},{8,9},{9,8},{10,11... | collective-permute-start | bytes 983048 | tf_op jit(solution)/shard_map/ppermute | solution.py:432
  47.1 14.3 %copy-start.9 = (s32[768]{0:T(1024)S(1)}, s32[768]{0:T(1024)}, u32[]{:S(2)}) copy-start(s32[768]{0:T(1024)} %param.24) | copy-start | bytes 9220
  47.1 14.3 %copy-start.7 = (s32[768]{0:T(1024)S(1)}, s32[768]{0:T(1024)}, u32[]{:S(2)}) copy-start(s32[768]{0:T(1024)} %param.25) | copy-start | bytes 9220
  50.4 10.4 %all-to-all-start = ((bf16[8,8,512]{2,1,0:T(8,128)(2,1)}), bf16[8,8,512]{2,1,0:T(8,128)(2,1)S(1)}, u32[]{:S(2)}, u32[]{:S(2)}) async-start(bf16[8,8,512]{2,1,0:T(8,128)(2,1)} %bitcast.2), calls=%async_computation | async-start | bytes 131072 | tf_op jit(solution)/shard_map/all_to_all | solution.py:558
  57.8 3.6 %collective-permute-start.19 = (bf16[7,128,256]{2,1,0:T(8,128)(2,1)S(1)}, bf16[7,128,256]{2,1,0:T(8,128)(2,1)S(1)}, u32[]{:S(2)}, u32[]{:S(2)}) collective-permute-start(bf16[7,128,256]{2,1,0:T(8,128)(2,1)S(1)} %get-tuple-element.64.refs_5_), channel_id=1, source_target_pairs={{0,1},{1,0},{2,3},{3,2},{4,5},{5,4},{6,7},{7,6},{8,9},{9,8},{10,11... | collective-permute-start | bytes 1376264 | tf_op jit(solution)/shard_map/ppermute | solution.py:432
  57.8 4.9 %collective-permute-start.20 = (bf16[3,7,32,256]{3,2,1,0:T(8,128)(2,1)S(1)}, bf16[3,7,32,256]{3,2,1,0:T(8,128)(2,1)}, u32[]{:S(2)}, u32[]{:S(2)}) collective-permute-start(bf16[3,7,32,256]{3,2,1,0:T(8,128)(2,1)S(1)} %get-tuple-element.65.refs_6_), channel_id=1, source_target_pairs={{0,1},{1,0},{2,3},{3,2},{4,5},{5,4},{6,7},{7,6},{8,9},{9,8},{10,11... | collective-permute-start | bytes 1032200 | tf_op jit(solution)/shard_map/ppermute | solution.py:432
  60.8 3.5 %collective-permute-start.14 = (bf16[3,7,32,256]{3,2,1,0:T(8,128)(2,1)}, bf16[3,7,32,256]{3,2,1,0:T(8,128)(2,1)S(1)}, u32[]{:S(2)}, u32[]{:S(2)}) collective-permute-start(bf16[3,7,32,256]{3,2,1,0:T(8,128)(2,1)} %collective-permute-done.13.refs_7_), channel_id=1, source_target_pairs={{0,1},{1,0},{2,3},{3,2},{4,5},{5,4},{6,7},{7,6},{8,9},{9,8},{10,11... | collective-permute-start | bytes 1032200 | tf_op jit(solution)/shard_map/ppermute | solution.py:432
  60.8 4.2 %collective-permute-start.16 = (bf16[3,7,32,256]{3,2,1,0:T(8,128)(2,1)}, bf16[3,7,32,256]{3,2,1,0:T(8,128)(2,1)S(1)}, u32[]{:S(2)}, u32[]{:S(2)}) collective-permute-start(bf16[3,7,32,256]{3,2,1,0:T(8,128)(2,1)} %collective-permute-done.15.refs_8_), channel_id=1, source_target_pairs={{0,1},{1,0},{2,3},{3,2},{4,5},{5,4},{6,7},{7,6},{8,9},{9,8},{10,11... | collective-permute-start | bytes 1032200 | tf_op jit(solution)/shard_map/ppermute | solution.py:432
  61.3 3.7 %collective-permute-start.18 = (bf16[3,7,32,256]{3,2,1,0:T(8,128)(2,1)}, bf16[3,7,32,256]{3,2,1,0:T(8,128)(2,1)S(1)}, u32[]{:S(2)}, u32[]{:S(2)}) collective-permute-start(bf16[3,7,32,256]{3,2,1,0:T(8,128)(2,1)} %collective-permute-done.17.refs_9_), channel_id=1, source_target_pairs={{0,1},{1,0},{2,3},{3,2},{4,5},{5,4},{6,7},{7,6},{8,9},{9,8},{10,11... | collective-permute-start | bytes 1032200 | tf_op jit(solution)/shard_map/ppermute | solution.py:432
  61.4 1.3 %copy-start.10 = (bf16[7,128,256]{2,1,0:T(8,128)(2,1)}, bf16[7,128,256]{2,1,0:T(8,128)(2,1)S(1)}, u32[]{:S(2)}) copy-start(bf16[7,128,256]{2,1,0:T(8,128)(2,1)S(1)} %collective-permute-done.19.refs_10_) | copy-start | bytes 1376260
  61.4 17.8 %collective-permute-start.21 = (bf16[3,7,32,256]{3,2,1,0:T(8,128)(2,1)S(1)}, bf16[3,7,32,256]{3,2,1,0:T(8,128)(2,1)S(1)}, u32[]{:S(2)}, u32[]{:S(2)}) collective-permute-start(bf16[3,7,32,256]{3,2,1,0:T(8,128)(2,1)S(1)} %get-tuple-element.71.refs_1_), channel_id=1, source_target_pairs={{0,2},{2,0},{1,3},{3,1},{4,6},{6,4},{5,7},{7,5},{8,10},{10,8},{9,1... | collective-permute-start | bytes 1032200 | tf_op jit(solution)/shard_map/ppermute | solution.py:427
  62.7 19.5 %collective-permute-start.22 = (bf16[3,7,32,256]{3,2,1,0:T(8,128)(2,1)S(1)}, bf16[3,7,32,256]{3,2,1,0:T(8,128)(2,1)S(1)}, u32[]{:S(2)}, u32[]{:S(2)}) collective-permute-start(bf16[3,7,32,256]{3,2,1,0:T(8,128)(2,1)S(1)} %get-tuple-element.71.refs_1_), channel_id=1, source_target_pairs={{0,16},{16,0},{1,17},{17,1},{2,18},{18,2},{3,19},{19,3},{4,20},{20... | collective-permute-start | bytes 1032200 | tf_op jit(solution)/shard_map/ppermute | solution.py:426
  64.2 18.5 %collective-permute-start.23 = (bf16[3,7,32,256]{3,2,1,0:T(8,128)(2,1)S(1)}, bf16[3,7,32,256]{3,2,1,0:T(8,128)(2,1)S(1)}, u32[]{:S(2)}, u32[]{:S(2)}) collective-permute-start(bf16[3,7,32,256]{3,2,1,0:T(8,128)(2,1)S(1)} %get-tuple-element.71.refs_1_), channel_id=1, source_target_pairs={{0,18},{18,0},{2,16},{16,2},{1,19},{19,1},{3,17},{17,3},{4,22},{22... | collective-permute-start | bytes 1032200 | tf_op jit(solution)/shard_map/ppermute | solution.py:425
  65.0 17.8 %collective-permute-start.25 = (bf16[3,7,32,256]{3,2,1,0:T(8,128)(2,1)S(1)}, bf16[3,7,32,256]{3,2,1,0:T(8,128)(2,1)S(1)}, u32[]{:S(2)}, u32[]{:S(2)}) collective-permute-start(bf16[3,7,32,256]{3,2,1,0:T(8,128)(2,1)S(1)} %get-tuple-element.71.refs_1_), channel_id=1, source_target_pairs={{0,1},{1,0},{2,3},{3,2},{4,5},{5,4},{6,7},{7,6},{8,9},{9,8},{10,11... | collective-permute-start | bytes 1032200 | tf_op jit(solution)/shard_map/ppermute | solution.py:432
  65.0 17.8 %collective-permute-start.24 = (bf16[7,128,256]{2,1,0:T(8,128)(2,1)S(1)}, bf16[7,128,256]{2,1,0:T(8,128)(2,1)S(1)}, u32[]{:S(2)}, u32[]{:S(2)}) collective-permute-start(bf16[7,128,256]{2,1,0:T(8,128)(2,1)S(1)} %get-tuple-element.72.refs_0_), channel_id=1, source_target_pairs={{0,1},{1,0},{2,3},{3,2},{4,5},{5,4},{6,7},{7,6},{8,9},{9,8},{10,11... | collective-permute-start | bytes 1376264 | tf_op jit(solution)/shard_map/ppermute | solution.py:432
  72.0 10.2 %all-to-all-start.1 = ((bf16[8,8,512]{2,1,0:T(8,128)(2,1)}), bf16[8,8,512]{2,1,0:T(8,128)(2,1)S(1)}, u32[]{:S(2)}, u32[]{:S(2)}) async-start(bf16[8,8,512]{2,1,0:T(8,128)(2,1)} %bitcast.4), calls=%async_computation.1 | async-start | bytes 131072 | tf_op jit(solution)/shard_map/all_to_all | solution.py:558
  82.2 4.0 %collective-permute-start.26 = (bf16[3,7,32,256]{3,2,1,0:T(8,128)(2,1)S(1)}, bf16[3,7,32,256]{3,2,1,0:T(8,128)(2,1)S(1)}, u32[]{:S(2)}, u32[]{:S(2)}) collective-permute-start(bf16[3,7,32,256]{3,2,1,0:T(8,128)(2,1)S(1)} %collective-permute-done.21.refs_2_), channel_id=1, source_target_pairs={{0,1},{1,0},{2,3},{3,2},{4,5},{5,4},{6,7},{7,6},{8,9},{9,8},{10,11... | collective-permute-start | bytes 1032200 | tf_op jit(solution)/shard_map/ppermute | solution.py:432
  82.2 4.0 %collective-permute-start.27 = (bf16[3,7,32,256]{3,2,1,0:T(8,128)(2,1)S(1)}, bf16[3,7,32,256]{3,2,1,0:T(8,128)(2,1)S(1)}, u32[]{:S(2)}, u32[]{:S(2)}) collective-permute-start(bf16[3,7,32,256]{3,2,1,0:T(8,128)(2,1)S(1)} %collective-permute-done.22.refs_3_), channel_id=1, source_target_pairs={{0,1},{1,0},{2,3},{3,2},{4,5},{5,4},{6,7},{7,6},{8,9},{9,8},{10,11... | collective-permute-start | bytes 1032200 | tf_op jit(solution)/shard_map/ppermute | solution.py:432
  82.7 3.5 %collective-permute-start.28 = (bf16[3,7,32,256]{3,2,1,0:T(8,128)(2,1)S(1)}, bf16[3,7,32,256]{3,2,1,0:T(8,128)(2,1)S(1)}, u32[]{:S(2)}, u32[]{:S(2)}) collective-permute-start(bf16[3,7,32,256]{3,2,1,0:T(8,128)(2,1)S(1)} %collective-permute-done.23.refs_4_), channel_id=1, source_target_pairs={{0,1},{1,0},{2,3},{3,2},{4,5},{5,4},{6,7},{7,6},{8,9},{9,8},{10,11... | collective-permute-start | bytes 1032200 | tf_op jit(solution)/shard_map/ppermute | solution.py:432

commit v8 on v7

--- a/solution.py
+++ b/solution.py
@@ -318,7 +318,7 @@
     save.wait()
 
 
-def block_body(pack, last, sent, slots, targets, lists, *refs):
+def block_body(pack, last, sent, slots, targets, lists, piece, *refs):
     near, far = len(pack.near_operands), len(pack.far_operands)
     near, refs = refs[:near], refs[near:]
     nodes, edges, far, refs = refs[0], refs[1], refs[2 : 2 + far], refs[2 + far :]
@@ -528,7 +528,7 @@
         plane1 = over_plane(after(joined1, term))
     else:
         node_weights = packs[1].near_operands
-    before = gathered
+    before = term
     term = call(
         half_nodes_body,
         (nodes, depth),
@@ -560,7 +560,7 @@
         ).reshape(-1, depth)
         if by_parts:
             if not last:
-                plane2 = over_plane(after(joined2, sent))
+                plane2 = over_plane(after(joined2, packed))
                 side = [own1, joined1] + plane1
             else:
                 side = [own2, joined2] + plane2
@@ -598,7 +598,7 @@
             functools.partial(block_body, pack, last),
             (nodes, depth) if last else [(sent_rows, depth), (nodes, depth), (mesh_edges, depth)],
             [edge_buffer, table, node_buffer, edge_buffer, pltpu.SemaphoreType.DMA((4,))] + pack.scratch(hidden, depth),
-            [sent, slots_back, targets, lists_back] + pack.near_operands,
+            [sent, slots_back, targets, lists_back, mark(sent, 8.0)] + pack.near_operands,
             [rows, edges] + pack.far_operands,
             cost=6.5,
             far=0 if last else 2,

time: 90.6 us -> 90.5 us (level)
    pallas_call x13 -> x14, Pallas kernels: 24.9 us -> 24.9 us  [call(): pl.pallas_call(body, out_shape=shapes if many else shapes[0], in_specs=sp...]
where the time goes in v8:
time: 90.5 us; the launch traced here: 90 us
  starting transfers between devices  45.4 us (50%)
  Pallas kernels  24.9 us (28%)
  waiting for transfers between devices  18.9 us (21%)
    pallas_call x14, Pallas kernels, call(): pl.pallas_call(body, out_shape=shapes if many else shapes[0], in_specs=sp...  24.9 us
    all_to_all x2, starting transfers between devices, on_device(): lax.all_to_all(cut_rows, ('mesh', 'band'), split_axis=0, concat_axis=0, a...  14.6 us
    ppermute x6, starting transfers between devices, over_slices(): lax.ppermute(chunk, 'mesh', [(i, i ^ k) for i in range(count)])  10.2 us
    ppermute x6, waiting for transfers between devices, over_slices(): lax.ppermute(chunk, 'mesh', [(i, i ^ k) for i in range(count)])  7.94 us
    all_to_all x2, waiting for transfers between devices, on_device(): lax.all_to_all(cut_rows, ('mesh', 'band'), split_axis=0, concat_axis=0, a...  5.33 us
    ppermute x3, starting transfers between devices, over_plane(): along_x = lax.ppermute(own, 'band', SWAP)  4.66 us
    ppermute x3, starting transfers between devices, over_plane(): across = lax.ppermute(own, ('groups', 'band'), DIAGONAL)  4.52 us
    ppermute x3, starting transfers between devices, over_plane(): along_y = lax.ppermute(own, 'groups', SWAP)  4.26 us
  transfers between devices with their start and end apart: 31, of which 7 were waited for; matrix products, arithmetic and copies ran while one was open for 0% of the time, Pallas kernels for 21%

profile of v8, /device:TPU:0, one launch (start us, length us, event | category | flops | bytes accessed | tf_op | source)
XLA Modules:
  0.0 90.0 jit_solution(3831183010787898579)
XLA Ops:
  0.0 0.9 shard_map.146
  0.9 5.1 %collective-permute-start.4 = (bf16[7,32,256]{2,1,0:T(8,128)(2,1)S(1)}, bf16[7,32,256]{2,1,0:T(8,128)(2,1)S(1)}, u32[]{:S(2)}, u32[]{:S(2)}) collective-permute-start(bf16[7,32,256]{2,1,0:T(8,128)(2,1)S(1)} %shard_map.146), channel_id=1, source_target_pairs={{0,12},{4,8},{8,4},{12,0},{1,13},{5,9},{9,5},{13,1},{2,14},{6,10},... | collective-permute-start | bytes 344072 | tf_op jit(solution)/shard_map/ppermute | solution.py:421
  6.0 0.0 collective-permute-start.2
  6.0 0.6 collective-permute-start.3
  6.6 1.5 %shard_map.145 = (bf16[64,512]{1,0:T(8,128)(2,1)S(1)}, bf16[64,512]{1,0:T(8,128)(2,1)S(1)}) custom-call(bf16[512,512]{1,0:T(8,128)(2,1)} %grid.1, s32[1,64]{1,0:T(1,128)} %bitcast.10, s32[1,64]{1,0:T(1,128)} %bitcast.11), custom_call_target="tpu_custom_call" | custom-call | flops 500000000 | tf_op jit(solution)/shard_map/pallas_call | solution.py:61
  8.2 3.5 %collective-permute-start = (bf16[64,512]{1,0:T(8,128)(2,1)S(1)}, bf16[64,512]{1,0:T(8,128)(2,1)S(1)}, u32[]{:S(2)}, u32[]{:S(2)}) collective-permute-start(bf16[64,512]{1,0:T(8,128)(2,1)S(1)} %get-tuple-element.45), channel_id=1, source_target_pairs={{0,2},{2,4},{4,6},{6,8},{8,10},{10,12},{12,14},{1,3},{3,5},{5,7},{... | collective-permute-start | bytes 196616 | tf_op jit(solution)/shard_map/ppermute | solution.py:500
  11.7 1.3 %collective-permute-start.1 = (bf16[64,512]{1,0:T(8,128)(2,1)S(1)}, bf16[64,512]{1,0:T(8,128)(2,1)S(1)}, u32[]{:S(2)}, u32[]{:S(2)}) collective-permute-start(bf16[64,512]{1,0:T(8,128)(2,1)S(1)} %get-tuple-element.47), channel_id=1, source_target_pairs={{2,0},{4,2},{6,4},{8,6},{10,8},{12,10},{14,12},{3,1},{5,3},{7,5},{... | collective-permute-start | bytes 196616 | tf_op jit(solution)/shard_map/ppermute | solution.py:499
  13.0 1.8 %shard_map.148 = (bf16[14,32,256]{2,1,0:T(8,128)(2,1)S(1)}, bf16[7,128,256]{2,1,0:T(8,128)(2,1)S(1)}, bf16[7,128,256]{2,1,0:T(8,128)(2,1)S(1)}, bf16[7,128,256]{2,1,0:T(8,128)(2,1)S(1)}) custom-call(bf16[3,3,128,256]{3,2,1,0:T(8,128)(2,1)} %refs_0_.3, bf16[3,256,128]{2,1,0:T(8,128)(2,1)} %refs_1_.3, bf16[3,2,128,256]{3,2,1,0:T(8,128)(2,1)} %refs_2_.3, ...), custom_call_target="tpu_custom_call" | custom-call | flops 500000000 | tf_op jit(solution)/shard_map/pallas_call | solution.py:61
  14.8 0.0 collective-permute-done.low
  14.9 3.0 %collective-permute-done.1.high = bf16[64,512]{1,0:T(8,128)(2,1)S(1)} collective-permute-done((bf16[64,512]{1,0:T(8,128)(2,1)S(1)}, bf16[64,512]{1,0:T(8,128)(2,1)S(1)}, u32[]{:S(2)}, u32[]{:S(2)}) %collective-permute-start.1) | collective-permute-done | bytes 65568 | tf_op jit(solution)/shard_map/ppermute | solution.py:499
  17.9 0.0 collective-permute-done.4.refs_2_
  17.9 0.0 collective-permute-done.3.refs_1_
  17.9 1.3 %collective-permute-start.5 = (bf16[14,32,256]{2,1,0:T(8,128)(2,1)S(1)}, bf16[14,32,256]{2,1,0:T(8,128)(2,1)S(1)}, u32[]{:S(2)}, u32[]{:S(2)}) collective-permute-start(bf16[14,32,256]{2,1,0:T(8,128)(2,1)S(1)} %get-tuple-element.51), channel_id=1, source_target_pairs={{0,4},{4,0},{8,12},{12,8},{1,5},{5,1},{9,13},{13,9},{2,6},{6,2},{1... | collective-permute-start | bytes 688136 | tf_op jit(solution)/shard_map/ppermute | solution.py:421
  19.2 2.9 %collective-permute-start.6 = (bf16[14,32,256]{2,1,0:T(8,128)(2,1)S(1)}, bf16[14,32,256]{2,1,0:T(8,128)(2,1)S(1)}, u32[]{:S(2)}, u32[]{:S(2)}) collective-permute-start(bf16[14,32,256]{2,1,0:T(8,128)(2,1)S(1)} %get-tuple-element.51), channel_id=1, source_target_pairs={{0,8},{4,12},{8,0},{12,4},{1,9},{5,13},{9,1},{13,5},{2,10},{6,14},... | collective-permute-start | bytes 688136 | tf_op jit(solution)/shard_map/ppermute | solution.py:421
  22.2 0.2 collective-permute-start.7
  22.4 2.3 %collective-permute-start.8 = (bf16[3,7,32,256]{3,2,1,0:T(8,128)(2,1)S(1)}, bf16[3,7,32,256]{3,2,1,0:T(8,128)(2,1)S(1)}, u32[]{:S(2)}, u32[]{:S(2)}) collective-permute-start(bf16[3,7,32,256]{3,2,1,0:T(8,128)(2,1)S(1)} %shard_map.149.refs_1_), channel_id=1, source_target_pairs={{0,2},{2,0},{1,3},{3,1},{4,6},{6,4},{5,7},{7,5},{8,10},{10,8},{9,1... | collective-permute-start | bytes 1032200 | tf_op jit(solution)/shard_map/ppermute | solution.py:427
  24.7 1.5 %collective-permute-start.9 = (bf16[3,7,32,256]{3,2,1,0:T(8,128)(2,1)S(1)}, bf16[3,7,32,256]{3,2,1,0:T(8,128)(2,1)S(1)}, u32[]{:S(2)}, u32[]{:S(2)}) collective-permute-start(bf16[3,7,32,256]{3,2,1,0:T(8,128)(2,1)S(1)} %shard_map.149.refs_1_), channel_id=1, source_target_pairs={{0,16},{16,0},{1,17},{17,1},{2,18},{18,2},{3,19},{19,3},{4,20},{20... | collective-permute-start | bytes 1032200 | tf_op jit(solution)/shard_map/ppermute | solution.py:426
  26.2 0.6 collective-permute-done.5.refs_0_
  26.8 2.6 %collective-permute-start.10 = (bf16[3,7,32,256]{3,2,1,0:T(8,128)(2,1)S(1)}, bf16[3,7,32,256]{3,2,1,0:T(8,128)(2,1)S(1)}, u32[]{:S(2)}, u32[]{:S(2)}) collective-permute-start(bf16[3,7,32,256]{3,2,1,0:T(8,128)(2,1)S(1)} %shard_map.149.refs_1_), channel_id=1, source_target_pairs={{0,18},{18,0},{2,16},{16,2},{1,19},{19,1},{3,17},{17,3},{4,22},{22... | collective-permute-start | bytes 1032200 | tf_op jit(solution)/shard_map/ppermute | solution.py:425
  29.4 1.3 %shard_map.147.gathered = bf16[768,1536]{1,0:T(8,128)(2,1)S(1)} custom-call(bf16[512,512]{1,0:T(8,128)(2,1)S(1)} %copy-done, bf16[64,512]{1,0:T(8,128)(2,1)S(1)} %collective-permute-done.low, bf16[64,512]{1,0:T(8,128)(2,1)S(1)} %collective-permute-done.1.high, bf16[320,512]{1,0:T(8,128)(2,1)S(1)} %copy-done.3, s32[1,768]{1,0:T(1,128)S(1)} %broadcast_in_dim.22.slots, ...), custom_call_target="tpu_custom_call" | custom-call | flops 1200000000 | tf_op jit(solution)/shard_map/pallas_call | solution.py:61
  30.7 7.4 %collective-permute-done.6.refs_1_ = bf16[14,32,256]{2,1,0:T(8,128)(2,1)S(1)} collective-permute-done((bf16[14,32,256]{2,1,0:T(8,128)(2,1)S(1)}, bf16[14,32,256]{2,1,0:T(8,128)(2,1)S(1)}, u32[]{:S(2)}, u32[]{:S(2)}) %collective-permute-start.6) | collective-permute-done | bytes 229408 | tf_op jit(solution)/shard_map/ppermute | solution.py:421
  38.1 0.0 copy-start.8
  38.1 0.0 collective-permute-done.8.refs_2_
  38.1 1.0 %collective-permute-done.9.refs_3_ = bf16[3,7,32,256]{3,2,1,0:T(8,128)(2,1)S(1)} collective-permute-done((bf16[3,7,32,256]{3,2,1,0:T(8,128)(2,1)S(1)}, bf16[3,7,32,256]{3,2,1,0:T(8,128)(2,1)S(1)}, u32[]{:S(2)}, u32[]{:S(2)}) %collective-permute-start.9) | collective-permute-done | bytes 344096 | tf_op jit(solution)/shard_map/ppermute | solution.py:426
  39.2 0.0 collective-permute-done.10.refs_4_
  39.2 1.6 %shard_map.151 = (bf16[768,512]{1,0:T(8,128)(2,1)S(1)}, bf16[1024,256]{1,0:T(8,128)(2,1)}, bf16[256,512]{1,0:T(8,128)(2,1)}) custom-call(bf16[768,1536]{1,0:T(8,128)(2,1)S(1)} %shard_map.147.gathered, bf16[7,128,256]{2,1,0:T(8,128)(2,1)S(1)} %get-tuple-element.53.refs_0_, bf16[3,7,32,256]{3,2,1,0:T(8,128)(2,1)S(1)} %shard_map.149.refs_1_, ...), custom_call_target="tpu_custom_call" | custom-call | flops 3000000000 | tf_op jit(solution)/shard_map/pallas_call | solution.py:61
  40.8 0.1 collective-permute-start.11
  40.9 0.1 reshape.15.lists
  41.0 1.1 %collective-permute-start.13 = (bf16[3,7,32,256]{3,2,1,0:T(8,128)(2,1)S(1)}, bf16[3,7,32,256]{3,2,1,0:T(8,128)(2,1)}, u32[]{:S(2)}, u32[]{:S(2)}) collective-permute-start(bf16[3,7,32,256]{3,2,1,0:T(8,128)(2,1)S(1)} %get-tuple-element.58.refs_6_), channel_id=1, source_target_pairs={{0,2},{2,0},{1,3},{3,1},{4,6},{6,4},{5,7},{7,5},{8,10},{10,8},{9,1... | collective-permute-start | bytes 1032200 | tf_op jit(solution)/shard_map/ppermute | solution.py:427
  42.1 1.2 %collective-permute-start.15 = (bf16[3,7,32,256]{3,2,1,0:T(8,128)(2,1)S(1)}, bf16[3,7,32,256]{3,2,1,0:T(8,128)(2,1)}, u32[]{:S(2)}, u32[]{:S(2)}) collective-permute-start(bf16[3,7,32,256]{3,2,1,0:T(8,128)(2,1)S(1)} %get-tuple-element.58.refs_6_), channel_id=1, source_target_pairs={{0,16},{16,0},{1,17},{17,1},{2,18},{18,2},{3,19},{19,3},{4,20},{20... | collective-permute-start | bytes 1032200 | tf_op jit(solution)/shard_map/ppermute | solution.py:426
  43.3 1.1 %collective-permute-start.17 = (bf16[3,7,32,256]{3,2,1,0:T(8,128)(2,1)S(1)}, bf16[3,7,32,256]{3,2,1,0:T(8,128)(2,1)}, u32[]{:S(2)}, u32[]{:S(2)}) collective-permute-start(bf16[3,7,32,256]{3,2,1,0:T(8,128)(2,1)S(1)} %get-tuple-element.58.refs_6_), channel_id=1, source_target_pairs={{0,18},{18,0},{2,16},{16,2},{1,19},{19,1},{3,17},{17,3},{4,22},{22... | collective-permute-start | bytes 1032200 | tf_op jit(solution)/shard_map/ppermute | solution.py:425
  44.5 2.5 %shard_map.152.source.mine = bf16[320,512]{1,0:T(8,128)(2,1)S(1)} custom-call(s32[1,768]{1,0:T(1,128)S(1)} %broadcast_in_dim.19.targets, bf16[768,512]{1,0:T(8,128)(2,1)S(1)} %get-tuple-element.54.mine, bf16[768,512]{1,0:T(8,128)(2,1)S(1)} %collective-permute-done.11.other, bf16[320,512]{1,0:T(8,128)(2,1)} %nodes.3, ...), custom_call_target="tpu_custom_call" | custom-call | flops 1600000000 | tf_op jit(solution)/shard_map/pallas_call | solution.py:61
  47.0 0.0 copy-start.4
  47.0 0.1 collective-permute-start.12
  47.1 0.0 copy-start.9
  47.1 0.0 copy-start.7
  47.1 1.6 %collective-permute-done.12.other = bf16[320,512]{1,0:T(8,128)(2,1)S(1)} collective-permute-done((bf16[320,512]{1,0:T(8,128)(2,1)S(1)}, bf16[320,512]{1,0:T(8,128)(2,1)S(1)}, u32[]{:S(2)}, u32[]{:S(2)}) %collective-permute-start.12) | collective-permute-done | bytes 327712 | tf_op jit(solution)/shard_map/ppermute | solution.py:432
  48.7 1.6 %shard_map.154 = (bf16[64,512]{1,0:T(8,128)(2,1)}, bf16[320,512]{1,0:T(8,128)(2,1)}) custom-call(bf16[320,512]{1,0:T(8,128)(2,1)S(1)} %copy-done.4, s32[1,64]{1,0:T(1,128)S(1)} %reshape.15.lists, bf16[320,512]{1,0:T(8,128)(2,1)S(1)} %shard_map.152.source.mine, bf16[320,512]{1,0:T(8,128)(2,1)S(1)} %collective-permute-done.12.other, ...), custom_call_target="tpu_custom_call" | custom-call | flops 1600000000 | tf_op jit(solution)/shard_map/pallas_call | solution.py:61
  50.4 7.4 %all-to-all-start = ((bf16[8,8,512]{2,1,0:T(8,128)(2,1)}), bf16[8,8,512]{2,1,0:T(8,128)(2,1)S(1)}, u32[]{:S(2)}, u32[]{:S(2)}) async-start(bf16[8,8,512]{2,1,0:T(8,128)(2,1)} %bitcast.2), calls=%async_computation | async-start | bytes 131072 | tf_op jit(solution)/shard_map/all_to_all | solution.py:558
  57.8 0.1 collective-permute-start.20
  57.9 0.5 collective-permute-start.19
  58.4 2.4 %all-to-all-done = bf16[8,8,512]{2,1,0:T(8,128)(2,1)S(1)} async-done(((bf16[8,8,512]{2,1,0:T(8,128)(2,1)}), bf16[8,8,512]{2,1,0:T(8,128)(2,1)S(1)}, u32[]{:S(2)}, u32[]{:S(2)}) %all-to-all-start) | async-done | bytes 65568 | tf_op jit(solution)/shard_map/all_to_all | solution.py:558
  60.8 0.0 collective-permute-start.14
  60.8 0.0 collective-permute-done.15.refs_8_
  60.8 0.5 collective-permute-start.16
  61.3 0.0 collective-permute-done.17.refs_9_
  61.3 0.1 collective-permute-start.18
  61.4 1.2 %collective-permute-start.21 = (bf16[3,7,32,256]{3,2,1,0:T(8,128)(2,1)S(1)}, bf16[3,7,32,256]{3,2,1,0:T(8,128)(2,1)S(1)}, u32[]{:S(2)}, u32[]{:S(2)}) collective-permute-start(bf16[3,7,32,256]{3,2,1,0:T(8,128)(2,1)S(1)} %get-tuple-element.72.refs_1_), channel_id=1, source_target_pairs={{0,2},{2,0},{1,3},{3,1},{4,6},{6,4},{5,7},{7,5},{8,10},{10,8},{9,1... | collective-permute-start | bytes 1032200 | tf_op jit(solution)/shard_map/ppermute | solution.py:427
  62.6 1.5 %collective-permute-start.22 = (bf16[3,7,32,256]{3,2,1,0:T(8,128)(2,1)S(1)}, bf16[3,7,32,256]{3,2,1,0:T(8,128)(2,1)S(1)}, u32[]{:S(2)}, u32[]{:S(2)}) collective-permute-start(bf16[3,7,32,256]{3,2,1,0:T(8,128)(2,1)S(1)} %get-tuple-element.72.refs_1_), channel_id=1, source_target_pairs={{0,16},{16,0},{1,17},{17,1},{2,18},{18,2},{3,19},{19,3},{4,20},{20... | collective-permute-start | bytes 1032200 | tf_op jit(solution)/shard_map/ppermute | solution.py:426
  64.1 0.8 collective-permute-start.23
  64.9 0.0 collective-permute-done.16.refs_1_
  64.9 0.0 collective-permute-start.24
  64.9 0.5 collective-permute-start.25
  65.4 6.5 %shard_map.156 = (bf16[64,512]{1,0:T(8,128)(2,1)}, bf16[320,512]{1,0:T(8,128)(2,1)}, bf16[768,512]{1,0:T(8,128)(2,1)}) custom-call(bf16[64,512]{1,0:T(8,128)(2,1)S(1)} %bitcast.7, s32[1,768]{1,0:T(1,128)S(1)} %broadcast_in_dim.23.slots, s32[1,768]{1,0:T(1,128)S(1)} %broadcast_in_dim.24.targets, s32[1,64]{1,0:T(1,128)S(1)} %reshape.15.lists, ...), custom_call_target="tpu_custom_call" | custom-call | flops 6499999744 | tf_op jit(solution)/shard_map/pallas_call | solution.py:61
  71.9 7.2 %all-to-all-start.1 = ((bf16[8,8,512]{2,1,0:T(8,128)(2,1)}), bf16[8,8,512]{2,1,0:T(8,128)(2,1)S(1)}, u32[]{:S(2)}, u32[]{:S(2)}) async-start(bf16[8,8,512]{2,1,0:T(8,128)(2,1)} %bitcast.4), calls=%async_computation.1 | async-start | bytes 131072 | tf_op jit(solution)/shard_map/all_to_all | solution.py:558
  79.1 0.0 collective-permute-done.21.refs_2_
  79.1 3.0 %all-to-all-done.1 = bf16[8,8,512]{2,1,0:T(8,128)(2,1)S(1)} async-done(((bf16[8,8,512]{2,1,0:T(8,128)(2,1)}), bf16[8,8,512]{2,1,0:T(8,128)(2,1)S(1)}, u32[]{:S(2)}, u32[]{:S(2)}) %all-to-all-start.1) | async-done | bytes 65568 | tf_op jit(solution)/shard_map/all_to_all | solution.py:558
  82.1 0.5 collective-permute-start.27
  82.6 0.0 collective-permute-done.23.refs_4_
  82.6 0.1 collective-permute-start.28
  82.6 3.4 %shard_map.157 = (f32[768,512]{1,0:T(8,128)S(1)}, bf16[1024,256]{1,0:T(8,128)(2,1)S(1)}, bf16[256,512]{1,0:T(8,128)(2,1)S(1)}, bf16[7,128,256]{2,1,0:T(8,128)(2,...) custom-call(bf16[64,512]{1,0:T(8,128)(2,1)S(1)} %bitcast.8, ...), custom_call_target="tpu_custom_call" | custom-call | flops 3500000000 | tf_op jit(solution)/shard_map/pallas_call | solution.py:61
  86.0 0.0 collective-permute-done.26.refs_2_
  86.1 0.0 collective-permute-done.27.refs_3_
  86.1 3.8 %shard_map.158 = bf16[320,512]{1,0:T(8,128)(2,1)} custom-call(bf16[64,512]{1,0:T(8,128)(2,1)S(1)} %bitcast.9, s32[1,768]{1,0:T(1,128)S(1)} %broadcast_in_dim.23.slots, s32[1,768]{1,0:T(1,128)S(1)} %broadcast_in_dim.24.targets, f32[768,512]{1,0:T(8,128)S(1)} %get-tuple-element.73.total, bf16[1024,256]{1,0:T(8,128)(2,1)S(1)} %get-tuple-element.74.nm, ...), custom_call_target="tpu_custom_call" | custom-call | flops 3500000000 | tf_op jit(solution)/shard_map/pallas_call | solution.py:61
  (41 shorter events, 0.2 us)
Async XLA Ops:
  0.9 17.0 %collective-permute-start.4 = (bf16[7,32,256]{2,1,0:T(8,128)(2,1)S(1)}, bf16[7,32,256]{2,1,0:T(8,128)(2,1)S(1)}, u32[]{:S(2)}, u32[]{:S(2)}) collective-permute-start(bf16[7,32,256]{2,1,0:T(8,128)(2,1)S(1)} %shard_map.146), channel_id=1, source_target_pairs={{0,12},{4,8},{8,4},{12,0},{1,13},{5,9},{9,5},{13,1},{2,14},{6,10},... | collective-permute-start | bytes 344072 | tf_op jit(solution)/shard_map/ppermute | solution.py:421
  6.0 11.9 %collective-permute-start.2 = (bf16[7,32,256]{2,1,0:T(8,128)(2,1)S(1)}, bf16[7,32,256]{2,1,0:T(8,128)(2,1)S(1)}, u32[]{:S(2)}, u32[]{:S(2)}) collective-permute-start(bf16[7,32,256]{2,1,0:T(8,128)(2,1)S(1)} %shard_map.146), channel_id=1, source_target_pairs={{0,4},{4,0},{8,12},{12,8},{1,5},{5,1},{9,13},{13,9},{2,6},{6,2},{1... | collective-permute-start | bytes 344072 | tf_op jit(solution)/shard_map/ppermute | solution.py:421
  6.0 11.9 %collective-permute-start.3 = (bf16[7,32,256]{2,1,0:T(8,128)(2,1)S(1)}, bf16[7,32,256]{2,1,0:T(8,128)(2,1)S(1)}, u32[]{:S(2)}, u32[]{:S(2)}) collective-permute-start(bf16[7,32,256]{2,1,0:T(8,128)(2,1)S(1)} %shard_map.146), channel_id=1, source_target_pairs={{0,8},{4,12},{8,0},{12,4},{1,9},{5,13},{9,1},{13,5},{2,10},{6,14},... | collective-permute-start | bytes 344072 | tf_op jit(solution)/shard_map/ppermute | solution.py:421
  6.6 15.7 %copy-start.5 = (s32[768]{0:T(1024)S(1)}, s32[768]{0:T(1024)}, u32[]{:S(2)}) copy-start(s32[768]{0:T(1024)} %param.20) | copy-start | bytes 9220
  6.6 15.8 %copy-start.6 = (s32[768]{0:T(1024)S(1)}, s32[768]{0:T(1024)}, u32[]{:S(2)}) copy-start(s32[768]{0:T(1024)} %param.19) | copy-start | bytes 9220
  6.6 22.8 %copy-start = (bf16[512,512]{1,0:T(8,128)(2,1)S(1)}, bf16[512,512]{1,0:T(8,128)(2,1)}, u32[]{:S(2)}) copy-start(bf16[512,512]{1,0:T(8,128)(2,1)} %grid.1) | copy-start | bytes 1572868
  6.6 22.8 %copy-start.3 = (bf16[320,512]{1,0:T(8,128)(2,1)S(1)}, bf16[320,512]{1,0:T(8,128)(2,1)}, u32[]{:S(2)}) copy-start(bf16[320,512]{1,0:T(8,128)(2,1)} %nodes.3) | copy-start | bytes 983044
  8.2 6.7 %collective-permute-start = (bf16[64,512]{1,0:T(8,128)(2,1)S(1)}, bf16[64,512]{1,0:T(8,128)(2,1)S(1)}, u32[]{:S(2)}, u32[]{:S(2)}) collective-permute-start(bf16[64,512]{1,0:T(8,128)(2,1)S(1)} %get-tuple-element.45), channel_id=1, source_target_pairs={{0,2},{2,4},{4,6},{6,8},{8,10},{10,12},{12,14},{1,3},{3,5},{5,7},{... | collective-permute-start | bytes 196616 | tf_op jit(solution)/shard_map/ppermute | solution.py:500
  11.7 6.2 %collective-permute-start.1 = (bf16[64,512]{1,0:T(8,128)(2,1)S(1)}, bf16[64,512]{1,0:T(8,128)(2,1)S(1)}, u32[]{:S(2)}, u32[]{:S(2)}) collective-permute-start(bf16[64,512]{1,0:T(8,128)(2,1)S(1)} %get-tuple-element.47), channel_id=1, source_target_pairs={{2,0},{4,2},{6,4},{8,6},{10,8},{12,10},{14,12},{3,1},{5,3},{7,5},{... | collective-permute-start | bytes 196616 | tf_op jit(solution)/shard_map/ppermute | solution.py:499
  14.8 43.1 %copy-start.1 = (bf16[7,128,256]{2,1,0:T(8,128)(2,1)}, bf16[7,128,256]{2,1,0:T(8,128)(2,1)S(1)}, u32[]{:S(2)}) copy-start(bf16[7,128,256]{2,1,0:T(8,128)(2,1)S(1)} %get-tuple-element.64.refs_5_) | copy-start | bytes 1376260
  17.9 8.9 %collective-permute-start.5 = (bf16[14,32,256]{2,1,0:T(8,128)(2,1)S(1)}, bf16[14,32,256]{2,1,0:T(8,128)(2,1)S(1)}, u32[]{:S(2)}, u32[]{:S(2)}) collective-permute-start(bf16[14,32,256]{2,1,0:T(8,128)(2,1)S(1)} %get-tuple-element.51), channel_id=1, source_target_pairs={{0,4},{4,0},{8,12},{12,8},{1,5},{5,1},{9,13},{13,9},{2,6},{6,2},{1... | collective-permute-start | bytes 688136 | tf_op jit(solution)/shard_map/ppermute | solution.py:421
  19.2 18.8 %collective-permute-start.6 = (bf16[14,32,256]{2,1,0:T(8,128)(2,1)S(1)}, bf16[14,32,256]{2,1,0:T(8,128)(2,1)S(1)}, u32[]{:S(2)}, u32[]{:S(2)}) collective-permute-start(bf16[14,32,256]{2,1,0:T(8,128)(2,1)S(1)} %get-tuple-element.51), channel_id=1, source_target_pairs={{0,8},{4,12},{8,0},{12,4},{1,9},{5,13},{9,1},{13,5},{2,10},{6,14},... | collective-permute-start | bytes 688136 | tf_op jit(solution)/shard_map/ppermute | solution.py:421
  22.2 15.9 %collective-permute-start.7 = (bf16[14,32,256]{2,1,0:T(8,128)(2,1)S(1)}, bf16[14,32,256]{2,1,0:T(8,128)(2,1)S(1)}, u32[]{:S(2)}, u32[]{:S(2)}) collective-permute-start(bf16[14,32,256]{2,1,0:T(8,128)(2,1)S(1)} %get-tuple-element.51), channel_id=1, source_target_pairs={{0,12},{4,8},{8,4},{12,0},{1,13},{5,9},{9,5},{13,1},{2,14},{6,10},... | collective-permute-start | bytes 688136 | tf_op jit(solution)/shard_map/ppermute | solution.py:421
  22.4 15.7 %collective-permute-start.8 = (bf16[3,7,32,256]{3,2,1,0:T(8,128)(2,1)S(1)}, bf16[3,7,32,256]{3,2,1,0:T(8,128)(2,1)S(1)}, u32[]{:S(2)}, u32[]{:S(2)}) collective-permute-start(bf16[3,7,32,256]{3,2,1,0:T(8,128)(2,1)S(1)} %shard_map.149.refs_1_), channel_id=1, source_target_pairs={{0,2},{2,0},{1,3},{3,1},{4,6},{6,4},{5,7},{7,5},{8,10},{10,8},{9,1... | collective-permute-start | bytes 1032200 | tf_op jit(solution)/shard_map/ppermute | solution.py:427
  24.7 14.4 %collective-permute-start.9 = (bf16[3,7,32,256]{3,2,1,0:T(8,128)(2,1)S(1)}, bf16[3,7,32,256]{3,2,1,0:T(8,128)(2,1)S(1)}, u32[]{:S(2)}, u32[]{:S(2)}) collective-permute-start(bf16[3,7,32,256]{3,2,1,0:T(8,128)(2,1)S(1)} %shard_map.149.refs_1_), channel_id=1, source_target_pairs={{0,16},{16,0},{1,17},{17,1},{2,18},{18,2},{3,19},{19,3},{4,20},{20... | collective-permute-start | bytes 1032200 | tf_op jit(solution)/shard_map/ppermute | solution.py:426
  26.8 12.4 %collective-permute-start.10 = (bf16[3,7,32,256]{3,2,1,0:T(8,128)(2,1)S(1)}, bf16[3,7,32,256]{3,2,1,0:T(8,128)(2,1)S(1)}, u32[]{:S(2)}, u32[]{:S(2)}) collective-permute-start(bf16[3,7,32,256]{3,2,1,0:T(8,128)(2,1)S(1)} %shard_map.149.refs_1_), channel_id=1, source_target_pairs={{0,18},{18,0},{2,16},{16,2},{1,19},{19,1},{3,17},{17,3},{4,22},{22... | collective-permute-start | bytes 1032200 | tf_op jit(solution)/shard_map/ppermute | solution.py:425
  38.1 19.7 %copy-start.2 = (bf16[3,7,32,256]{3,2,1,0:T(8,128)(2,1)}, bf16[3,7,32,256]{3,2,1,0:T(8,128)(2,1)S(1)}, u32[]{:S(2)}) copy-start(bf16[3,7,32,256]{3,2,1,0:T(8,128)(2,1)S(1)} %get-tuple-element.58.refs_6_) | copy-start | bytes 1032196
  38.1 2.7 %copy-start.8 = (s32[1,8,8]{2,1,0:T(8,128)S(1)}, s32[1,8,8]{2,1,0:T(8,128)}, u32[]{:S(2)}) copy-start(s32[1,8,8]{2,1,0:T(8,128)} %param.23) | copy-start | bytes 772
  40.8 3.7 %collective-permute-start.11 = (bf16[768,512]{1,0:T(8,128)(2,1)S(1)}, bf16[768,512]{1,0:T(8,128)(2,1)S(1)}, u32[]{:S(2)}, u32[]{:S(2)}) collective-permute-start(bf16[768,512]{1,0:T(8,128)(2,1)S(1)} %get-tuple-element.54.mine), channel_id=1, source_target_pairs={{0,1},{1,0},{2,3},{3,2},{4,5},{5,4},{6,7},{7,6},{8,9},{9,8},{10,11... | collective-permute-start | bytes 2359304 | tf_op jit(solution)/shard_map/ppermute | solution.py:432
  41.0 17.4 %collective-permute-start.13 = (bf16[3,7,32,256]{3,2,1,0:T(8,128)(2,1)S(1)}, bf16[3,7,32,256]{3,2,1,0:T(8,128)(2,1)}, u32[]{:S(2)}, u32[]{:S(2)}) collective-permute-start(bf16[3,7,32,256]{3,2,1,0:T(8,128)(2,1)S(1)} %get-tuple-element.58.refs_6_), channel_id=1, source_target_pairs={{0,2},{2,0},{1,3},{3,1},{4,6},{6,4},{5,7},{7,5},{8,10},{10,8},{9,1... | collective-permute-start | bytes 1032200 | tf_op jit(solution)/shard_map/ppermute | solution.py:427
  42.1 18.7 %collective-permute-start.15 = (bf16[3,7,32,256]{3,2,1,0:T(8,128)(2,1)S(1)}, bf16[3,7,32,256]{3,2,1,0:T(8,128)(2,1)}, u32[]{:S(2)}, u32[]{:S(2)}) collective-permute-start(bf16[3,7,32,256]{3,2,1,0:T(8,128)(2,1)S(1)} %get-tuple-element.58.refs_6_), channel_id=1, source_target_pairs={{0,16},{16,0},{1,17},{17,1},{2,18},{18,2},{3,19},{19,3},{4,20},{20... | collective-permute-start | bytes 1032200 | tf_op jit(solution)/shard_map/ppermute | solution.py:426
  43.3 18.0 %collective-permute-start.17 = (bf16[3,7,32,256]{3,2,1,0:T(8,128)(2,1)S(1)}, bf16[3,7,32,256]{3,2,1,0:T(8,128)(2,1)}, u32[]{:S(2)}, u32[]{:S(2)}) collective-permute-start(bf16[3,7,32,256]{3,2,1,0:T(8,128)(2,1)S(1)} %get-tuple-element.58.refs_6_), channel_id=1, source_target_pairs={{0,18},{18,0},{2,16},{16,2},{1,19},{19,1},{3,17},{17,3},{4,22},{22... | collective-permute-start | bytes 1032200 | tf_op jit(solution)/shard_map/ppermute | solution.py:425
  47.0 1.7 %copy-start.4 = (bf16[320,512]{1,0:T(8,128)(2,1)S(1)}, bf16[320,512]{1,0:T(8,128)(2,1)}, u32[]{:S(2)}) copy-start(bf16[320,512]{1,0:T(8,128)(2,1)} %nodes.3) | copy-start | bytes 983044
  47.0 1.7 %collective-permute-start.12 = (bf16[320,512]{1,0:T(8,128)(2,1)S(1)}, bf16[320,512]{1,0:T(8,128)(2,1)S(1)}, u32[]{:S(2)}, u32[]{:S(2)}) collective-permute-start(bf16[320,512]{1,0:T(8,128)(2,1)S(1)} %shard_map.152.source.mine), channel_id=1, source_target_pairs={{0,1},{1,0},{2,3},{3,2},{4,5},{5,4},{6,7},{7,6},{8,9},{9,8},{10,11... | collective-permute-start | bytes 983048 | tf_op jit(solution)/shard_map/ppermute | solution.py:432
  47.1 10.7 %copy-start.9 = (s32[768]{0:T(1024)S(1)}, s32[768]{0:T(1024)}, u32[]{:S(2)}) copy-start(s32[768]{0:T(1024)} %param.24) | copy-start | bytes 9220
  47.1 10.7 %copy-start.7 = (s32[768]{0:T(1024)S(1)}, s32[768]{0:T(1024)}, u32[]{:S(2)}) copy-start(s32[768]{0:T(1024)} %param.25) | copy-start | bytes 9220
  50.4 10.4 %all-to-all-start = ((bf16[8,8,512]{2,1,0:T(8,128)(2,1)}), bf16[8,8,512]{2,1,0:T(8,128)(2,1)S(1)}, u32[]{:S(2)}, u32[]{:S(2)}) async-start(bf16[8,8,512]{2,1,0:T(8,128)(2,1)} %bitcast.2), calls=%async_computation | async-start | bytes 131072 | tf_op jit(solution)/shard_map/all_to_all | solution.py:558
  57.8 3.5 %collective-permute-start.20 = (bf16[3,7,32,256]{3,2,1,0:T(8,128)(2,1)S(1)}, bf16[3,7,32,256]{3,2,1,0:T(8,128)(2,1)}, u32[]{:S(2)}, u32[]{:S(2)}) collective-permute-start(bf16[3,7,32,256]{3,2,1,0:T(8,128)(2,1)S(1)} %get-tuple-element.58.refs_6_), channel_id=1, source_target_pairs={{0,1},{1,0},{2,3},{3,2},{4,5},{5,4},{6,7},{7,6},{8,9},{9,8},{10,11... | collective-permute-start | bytes 1032200 | tf_op jit(solution)/shard_map/ppermute | solution.py:432
  57.9 4.7 %collective-permute-start.19 = (bf16[7,128,256]{2,1,0:T(8,128)(2,1)S(1)}, bf16[7,128,256]{2,1,0:T(8,128)(2,1)S(1)}, u32[]{:S(2)}, u32[]{:S(2)}) collective-permute-start(bf16[7,128,256]{2,1,0:T(8,128)(2,1)S(1)} %get-tuple-element.64.refs_5_), channel_id=1, source_target_pairs={{0,1},{1,0},{2,3},{3,2},{4,5},{5,4},{6,7},{7,6},{8,9},{9,8},{10,11... | collective-permute-start | bytes 1376264 | tf_op jit(solution)/shard_map/ppermute | solution.py:432
  60.8 3.3 %collective-permute-start.14 = (bf16[3,7,32,256]{3,2,1,0:T(8,128)(2,1)}, bf16[3,7,32,256]{3,2,1,0:T(8,128)(2,1)S(1)}, u32[]{:S(2)}, u32[]{:S(2)}) collective-permute-start(bf16[3,7,32,256]{3,2,1,0:T(8,128)(2,1)} %collective-permute-done.13.refs_7_), channel_id=1, source_target_pairs={{0,1},{1,0},{2,3},{3,2},{4,5},{5,4},{6,7},{7,6},{8,9},{9,8},{10,11... | collective-permute-start | bytes 1032200 | tf_op jit(solution)/shard_map/ppermute | solution.py:432
  60.8 4.1 %collective-permute-start.16 = (bf16[3,7,32,256]{3,2,1,0:T(8,128)(2,1)}, bf16[3,7,32,256]{3,2,1,0:T(8,128)(2,1)S(1)}, u32[]{:S(2)}, u32[]{:S(2)}) collective-permute-start(bf16[3,7,32,256]{3,2,1,0:T(8,128)(2,1)} %collective-permute-done.15.refs_8_), channel_id=1, source_target_pairs={{0,1},{1,0},{2,3},{3,2},{4,5},{5,4},{6,7},{7,6},{8,9},{9,8},{10,11... | collective-permute-start | bytes 1032200 | tf_op jit(solution)/shard_map/ppermute | solution.py:432
  61.3 3.6 %collective-permute-start.18 = (bf16[3,7,32,256]{3,2,1,0:T(8,128)(2,1)}, bf16[3,7,32,256]{3,2,1,0:T(8,128)(2,1)S(1)}, u32[]{:S(2)}, u32[]{:S(2)}) collective-permute-start(bf16[3,7,32,256]{3,2,1,0:T(8,128)(2,1)} %collective-permute-done.17.refs_9_), channel_id=1, source_target_pairs={{0,1},{1,0},{2,3},{3,2},{4,5},{5,4},{6,7},{7,6},{8,9},{9,8},{10,11... | collective-permute-start | bytes 1032200 | tf_op jit(solution)/shard_map/ppermute | solution.py:432
  61.4 17.7 %collective-permute-start.21 = (bf16[3,7,32,256]{3,2,1,0:T(8,128)(2,1)S(1)}, bf16[3,7,32,256]{3,2,1,0:T(8,128)(2,1)S(1)}, u32[]{:S(2)}, u32[]{:S(2)}) collective-permute-start(bf16[3,7,32,256]{3,2,1,0:T(8,128)(2,1)S(1)} %get-tuple-element.72.refs_1_), channel_id=1, source_target_pairs={{0,2},{2,0},{1,3},{3,1},{4,6},{6,4},{5,7},{7,5},{8,10},{10,8},{9,1... | collective-permute-start | bytes 1032200 | tf_op jit(solution)/shard_map/ppermute | solution.py:427
  62.6 2.3 %copy-start.10 = (bf16[7,128,256]{2,1,0:T(8,128)(2,1)}, bf16[7,128,256]{2,1,0:T(8,128)(2,1)S(1)}, u32[]{:S(2)}) copy-start(bf16[7,128,256]{2,1,0:T(8,128)(2,1)S(1)} %collective-permute-done.19.refs_10_) | copy-start | bytes 1376260
  62.6 19.5 %collective-permute-start.22 = (bf16[3,7,32,256]{3,2,1,0:T(8,128)(2,1)S(1)}, bf16[3,7,32,256]{3,2,1,0:T(8,128)(2,1)S(1)}, u32[]{:S(2)}, u32[]{:S(2)}) collective-permute-start(bf16[3,7,32,256]{3,2,1,0:T(8,128)(2,1)S(1)} %get-tuple-element.72.refs_1_), channel_id=1, source_target_pairs={{0,16},{16,0},{1,17},{17,1},{2,18},{18,2},{3,19},{19,3},{4,20},{20... | collective-permute-start | bytes 1032200 | tf_op jit(solution)/shard_map/ppermute | solution.py:426
  64.1 18.5 %collective-permute-start.23 = (bf16[3,7,32,256]{3,2,1,0:T(8,128)(2,1)S(1)}, bf16[3,7,32,256]{3,2,1,0:T(8,128)(2,1)S(1)}, u32[]{:S(2)}, u32[]{:S(2)}) collective-permute-start(bf16[3,7,32,256]{3,2,1,0:T(8,128)(2,1)S(1)} %get-tuple-element.72.refs_1_), channel_id=1, source_target_pairs={{0,18},{18,0},{2,16},{16,2},{1,19},{19,1},{3,17},{17,3},{4,22},{22... | collective-permute-start | bytes 1032200 | tf_op jit(solution)/shard_map/ppermute | solution.py:425
  64.9 17.8 %collective-permute-start.24 = (bf16[7,128,256]{2,1,0:T(8,128)(2,1)S(1)}, bf16[7,128,256]{2,1,0:T(8,128)(2,1)S(1)}, u32[]{:S(2)}, u32[]{:S(2)}) collective-permute-start(bf16[7,128,256]{2,1,0:T(8,128)(2,1)S(1)} %get-tuple-element.71.refs_0_), channel_id=1, source_target_pairs={{0,1},{1,0},{2,3},{3,2},{4,5},{5,4},{6,7},{7,6},{8,9},{9,8},{10,11... | collective-permute-start | bytes 1376264 | tf_op jit(solution)/shard_map/ppermute | solution.py:432
  64.9 17.7 %collective-permute-start.25 = (bf16[3,7,32,256]{3,2,1,0:T(8,128)(2,1)S(1)}, bf16[3,7,32,256]{3,2,1,0:T(8,128)(2,1)S(1)}, u32[]{:S(2)}, u32[]{:S(2)}) collective-permute-start(bf16[3,7,32,256]{3,2,1,0:T(8,128)(2,1)S(1)} %get-tuple-element.72.refs_1_), channel_id=1, source_target_pairs={{0,1},{1,0},{2,3},{3,2},{4,5},{5,4},{6,7},{7,6},{8,9},{9,8},{10,11... | collective-permute-start | bytes 1032200 | tf_op jit(solution)/shard_map/ppermute | solution.py:432
  71.9 10.2 %all-to-all-start.1 = ((bf16[8,8,512]{2,1,0:T(8,128)(2,1)}), bf16[8,8,512]{2,1,0:T(8,128)(2,1)S(1)}, u32[]{:S(2)}, u32[]{:S(2)}) async-start(bf16[8,8,512]{2,1,0:T(8,128)(2,1)} %bitcast.4), calls=%async_computation.1 | async-start | bytes 131072 | tf_op jit(solution)/shard_map/all_to_all | solution.py:558
  82.1 4.0 %collective-permute-start.26 = (bf16[3,7,32,256]{3,2,1,0:T(8,128)(2,1)S(1)}, bf16[3,7,32,256]{3,2,1,0:T(8,128)(2,1)S(1)}, u32[]{:S(2)}, u32[]{:S(2)}) collective-permute-start(bf16[3,7,32,256]{3,2,1,0:T(8,128)(2,1)S(1)} %collective-permute-done.21.refs_2_), channel_id=1, source_target_pairs={{0,1},{1,0},{2,3},{3,2},{4,5},{5,4},{6,7},{7,6},{8,9},{9,8},{10,11... | collective-permute-start | bytes 1032200 | tf_op jit(solution)/shard_map/ppermute | solution.py:432
  82.1 4.0 %collective-permute-start.27 = (bf16[3,7,32,256]{3,2,1,0:T(8,128)(2,1)S(1)}, bf16[3,7,32,256]{3,2,1,0:T(8,128)(2,1)S(1)}, u32[]{:S(2)}, u32[]{:S(2)}) collective-permute-start(bf16[3,7,32,256]{3,2,1,0:T(8,128)(2,1)S(1)} %collective-permute-done.22.refs_3_), channel_id=1, source_target_pairs={{0,1},{1,0},{2,3},{3,2},{4,5},{5,4},{6,7},{7,6},{8,9},{9,8},{10,11... | collective-permute-start | bytes 1032200 | tf_op jit(solution)/shard_map/ppermute | solution.py:432
  82.6 3.5 %collective-permute-start.28 = (bf16[3,7,32,256]{3,2,1,0:T(8,128)(2,1)S(1)}, bf16[3,7,32,256]{3,2,1,0:T(8,128)(2,1)S(1)}, u32[]{:S(2)}, u32[]{:S(2)}) collective-permute-start(bf16[3,7,32,256]{3,2,1,0:T(8,128)(2,1)S(1)} %collective-permute-done.23.refs_4_), channel_id=1, source_target_pairs={{0,1},{1,0},{2,3},{3,2},{4,5},{5,4},{6,7},{7,6},{8,9},{9,8},{10,11... | collective-permute-start | bytes 1032200 | tf_op jit(solution)/shard_map/ppermute | solution.py:432
